TPU v7x, 128 devices: a whole 4x4x4 slice. The times are simulated.
128 devices in a mesh: sec: 2 (over core), tile: 32 (over x, y_lo, z), lev: 2 (over y_hi).
Axes of the slice: x: 4, y: 4 (y_hi: 2, y_lo: 2; y = y_hi * 2 + y_lo), z: 4, core: 2. Of those that a mesh axis runs over, the one named last changes fastest.
Arguments:
- state: float32 [3, 80, 512, 128], P(None, 'lev', 'tile'), may hold values from -6 to 6
- sound: float32 [80, 512, 128], P('lev', 'tile'), may hold values from 0.5 to 2
- target: float32 [3, 80, 512, 128], P(None, 'lev', 'tile'), may hold values from -6 to 6
- edge_turn: int32 [32, 2], P('tile'), may hold values from 0 to 3
- w_first: bfloat16 [240, 512], replicated, may hold values from -0.375 to 0.375
- b_first: float32 [512], replicated, may hold values from -3 to 3
- w_second: bfloat16 [512, 512], replicated, may hold values from -0.25 to 0.25
- w_third: bfloat16 [512, 240], replicated, may hold values from -0.25 to 0.25
Outputs:
- state_grad: float32 [3, 80, 512, 128], P(None, 'lev', 'tile')
- grad_first: float32 [240, 512], replicated
- grad_bias: float32 [512], replicated
- grad_second: float32 [512, 512], replicated
- grad_third: float32 [512, 240], replicated
Inputs may be any that keep to these rules, and one draw needn't show every extreme that they name: `edge_turn`: entry [t, 0] is the quarter turn from strip t - 1 into strip t, entry [t, 1] from strip t + 1.
All inputs are finite; a program needn't handle non-finite values.
Results may differ from a plain program's by a relative error of at most 0.0024.
Values may be sent and summed in bfloat16 or wider, within the bound.
No kernel may reach another device: no remote copies, remote signals or barrier semaphores. Data moves between devices by JAX's collectives and lax.ppermute only.
A program may use at most 128 MiB of HBM per device.

v0:
```python
import jax
import jax.numpy as jnp
from jax import lax
from jax.sharding import PartitionSpec as P

SUBSTEPS = 4


courant = 0.3
diffusion = 0.08


def from_behind(value, axis, steps):
    count = lax.axis_size(axis)
    first, last = (max(0, -steps), min(count, count - steps))
    return lax.ppermute(value, axis, [(source, source + steps) for source in range(first, last)])


def extended(array, sides, width):
    for axis, dim in sides:
        peers, length = (lax.axis_size(axis), array.shape[dim])
        up = [(i, (i + 1) % peers) for i in range(peers - 1)]
        down = [(j, i) for i, j in up]
        last = lax.slice_in_dim(array, length - width, length, axis=dim)
        first = lax.slice_in_dim(array, 0, width, axis=dim)
        before = lax.ppermute(last, axis, up)
        after = lax.ppermute(first, axis, down)
        array = jnp.concatenate([before, array, after], axis=dim)
    return array


def from_partner(value, axis, apart):
    mask = 2**apart
    pairs = [(source, source ^ mask) for source in range(lax.axis_size(axis))]
    return lax.ppermute(value, axis, pairs)


def pad_along(values, along, before, after):
    widths = [(0, 0)] * values.ndim
    widths[along] = (before, after)
    return jnp.pad(values, widths)


def diff_padded(padded, along, length):

    def take(offset):
        return lax.slice_in_dim(padded, offset, offset + length, axis=along)

    return (8.0 * (take(3) - take(1)) - (take(4) - take(0))) / 12.0


def diff_padded_t(weighted, along):
    return (
        8.0 * (pad_along(weighted, along, 3, 1) - pad_along(weighted, along, 1, 3))
        - (pad_along(weighted, along, 4, 0) - pad_along(weighted, along, 0, 4))
    ) / 12.0


def diff_periodic(values, along):
    return (
        8.0 * (jnp.roll(values, -1, along) - jnp.roll(values, 1, along))
        - (jnp.roll(values, -2, along) - jnp.roll(values, 2, along))
    ) / 12.0


def vertical_mix(padded, length):

    def take(offset):
        return padded[offset : offset + length]

    return (16.0 * (take(3) + take(1)) - (take(4) + take(0)) - 30.0 * take(2)) / 12.0


def vertical_mix_t(weighted):
    return (
        16.0 * (pad_along(weighted, 0, 3, 1) + pad_along(weighted, 0, 1, 3))
        - (pad_along(weighted, 0, 4, 0) + pad_along(weighted, 0, 0, 4))
        - 30.0 * pad_along(weighted, 0, 2, 2)
    ) / 12.0


def turn_factors(quarter):
    cosine = jnp.where(quarter == 0, 1.0, 0.0) - jnp.where(quarter == 2, 1.0, 0.0)
    sine = jnp.where(quarter == 1, 1.0, 0.0) - jnp.where(quarter == 3, 1.0, 0.0)
    return (cosine, sine)


def return_rows(lower_part, upper_part, along, rows):
    from_above = from_behind(lower_part.astype(jnp.bfloat16), "tile", -1).astype(lower_part.dtype)
    from_below = from_behind(upper_part.astype(jnp.bfloat16), "tile", 1).astype(upper_part.dtype)
    return pad_along(from_below, along, 0, rows - 2) + pad_along(from_above, along, rows - 2, 0)


def send_back(lower_part, upper_part, along, rows):
    result = return_rows(lower_part, upper_part, along, rows)
    return result


def return_levels(padded, levels):
    from_above = from_behind(padded[:2], "lev", -1)
    from_below = from_behind(padded[levels + 2 :], "lev", 1)
    return (
        padded[2 : levels + 2]
        + pad_along(from_below, 0, 0, levels - 2)
        + pad_along(from_above, 0, levels - 2, 0)
    )


def forward_step(state, coeff, turns):
    cos_low, sin_low, cos_high, sin_high = turns
    height, wind_x, wind_y = (state[0], state[1], state[2])
    levels, rows = (height.shape[0], height.shape[1])
    row_padded = extended(height, (("tile", 1),), 2)
    level_padded = extended(height, (("lev", 0),), 2)
    wind_x = wind_x - coeff * diff_padded(row_padded, 1, rows)
    wind_y = wind_y - coeff * diff_periodic(height, 2)
    mixing = vertical_mix(level_padded, levels)
    framed_wind = extended(jnp.stack([wind_x, wind_y]), (("tile", 2),), 2)
    wind_below = framed_wind[:, :, :2]
    wind_above = framed_wind[:, :, rows + 2 :]
    padded_x = jnp.concatenate(
        [
            cos_low * wind_below[0] - sin_low * wind_below[1],
            wind_x,
            cos_high * wind_above[0] - sin_high * wind_above[1],
        ],
        axis=1,
    )
    height = (
        height
        - coeff * (diff_padded(padded_x, 1, rows) + diff_periodic(wind_y, 2))
        + diffusion * mixing
    )
    return jnp.stack([height, wind_x, wind_y])


def adjoint_step(grads, coeff, turns):
    cos_low, sin_low, cos_high, sin_high = turns
    grad_height, grad_x, grad_y = (grads[0], grads[1], grads[2])
    levels, rows = (grad_height.shape[0], grad_height.shape[1])
    weighted = coeff * grad_height
    spread = diff_padded_t(weighted, 1)
    ghosts_below = jnp.stack([cos_low * spread[:, :2], -sin_low * spread[:, :2]])
    ghosts_above = jnp.stack([cos_high * spread[:, rows + 2 :], -sin_high * spread[:, rows + 2 :]])
    returned = send_back(ghosts_below, ghosts_above, 2, rows)
    grad_x = grad_x - spread[:, 2 : rows + 2] - returned[0]
    grad_y = grad_y + diff_periodic(weighted, 2) - returned[1]
    total = grad_height + diffusion * return_levels(vertical_mix_t(grad_height), levels)
    spread_x = diff_padded_t(coeff * grad_x, 1)
    total = (
        total
        - spread_x[:, 2 : rows + 2]
        - send_back(spread_x[:, :2], spread_x[:, rows + 2 :], 1, rows)
    )
    total = total + diff_periodic(coeff * grad_y, 2)
    return jnp.stack([total, grad_x, grad_y])


def slope(values):
    sigma = jax.nn.sigmoid(values)
    return sigma * (1.0 + values * (1.0 - sigma))


def product(left, right, left_dim, right_dim):
    return lax.dot_general(
        left, right, (((left_dim,), (right_dim,)), ((), ())), preferred_element_type=jnp.float32
    )


def local(state, sound, target, edge_turn, w_first, b_first, w_second, w_third):
    section = lax.axis_index("sec")
    rows = state.shape[2]
    width = state.shape[3]
    half_rows = rows // 2
    coeff_full = courant * sound
    cos_low, sin_low = turn_factors(edge_turn[0, 0])
    cos_high, sin_high = turn_factors(edge_turn[0, 1])
    own_state = lax.dynamic_slice_in_dim(state, section * half_rows, half_rows, 2)
    target_own = lax.dynamic_slice_in_dim(target, section * half_rows, half_rows, 2)
    columns = lax.all_to_all(
        own_state.astype(jnp.bfloat16), "lev", split_axis=2, concat_axis=1, tiled=True
    )
    col_shape = columns.shape
    features = col_shape[0] * col_shape[1]
    feat = columns.reshape(features, -1)
    first = product(w_first, feat, 0, 0) + b_first[:, None]
    hidden_one = jax.nn.silu(first).astype(jnp.bfloat16)
    second = product(w_second, hidden_one, 0, 0)
    hidden_two = jax.nn.silu(second).astype(jnp.bfloat16)
    tendency = product(w_third, hidden_two, 0, 0)
    tend_cells = lax.all_to_all(
        tendency.reshape(col_shape), "lev", split_axis=1, concat_axis=2, tiled=True
    )
    turns = (cos_low, sin_low, cos_high, sin_high)
    evolved = state
    for step in range(SUBSTEPS):
        evolved = forward_step(evolved, coeff_full, turns)
    outgoing = jnp.where(section == 0, evolved[:, :, half_rows:], tend_cells)
    received = from_partner(outgoing, "sec", 0)
    evolved_own = jnp.where(section == 0, evolved[:, :, :half_rows], received)
    resid_own = evolved_own + tend_cells - target_own
    resid_other = evolved[:, :, half_rows:] + received - target[:, :, half_rows:]
    resid_full = jnp.concatenate([resid_own, resid_other], axis=2)
    resid_cols = lax.all_to_all(
        resid_own.astype(jnp.bfloat16), "lev", split_axis=2, concat_axis=1, tiled=True
    ).reshape(features, -1)
    grad_third = product(hidden_two, resid_cols, 1, 1)
    err_two = (product(w_third, resid_cols, 1, 0) * slope(second)).astype(jnp.bfloat16)
    grad_second = product(hidden_one, err_two, 1, 1)
    err_one = (product(w_second, err_two, 1, 0) * slope(first)).astype(jnp.bfloat16)
    grad_first = product(feat, err_one, 1, 1)
    grad_bias = jnp.sum(err_one.astype(jnp.float32), axis=1)
    input_grad = product(w_first, err_one, 1, 0)
    input_cells = lax.all_to_all(
        input_grad.reshape(col_shape), "lev", split_axis=1, concat_axis=2, tiled=True
    )
    adjoint = resid_full
    for step in range(SUBSTEPS):
        adjoint = adjoint_step(adjoint, coeff_full, turns)
    adjoint = jnp.where(section == 0, adjoint, 0.0)
    blank = jnp.zeros_like(input_cells)
    placed = jnp.where(
        section == 0,
        jnp.concatenate([input_cells, blank], axis=2),
        jnp.concatenate([blank, input_cells], axis=2),
    )
    state_grad = lax.psum(adjoint + placed, "sec")
    sum_first, sum_bias, sum_second, sum_third = lax.psum(
        (grad_first, grad_bias, grad_second, grad_third), ("sec", "tile", "lev")
    )
    ncols = rows * lax.axis_size("tile") * width
    return (state_grad, sum_first / ncols, sum_bias / ncols, sum_second / ncols, sum_third / ncols)


def solution(mesh):
    placed = (
        P(None, "lev", "tile", None),
        P("lev", "tile", None),
        P(None, "lev", "tile", None),
        P("tile", None),
        P(),
        P(),
        P(),
        P(),
    )
    return jax.shard_map(
        local,
        mesh=mesh,
        in_specs=placed,
        out_specs=(P(None, "lev", "tile", None), P(), P(), P(), P()),
        check_vma=False,
    )
```

profile of v0, /device:TPU:1, one launch (start us, length us, event | category | flops | bytes accessed | tf_op | source)
XLA Modules:
  0.0 646.7 jit_solution(14541283882861324732)
XLA Ops:
  9.1 5.0 all-to-all-start
  17.4 4.2 collective-permute-start.1
  23.5 5.5 collective-permute-start.5
  48.4 4.1 fusion.76
  53.2 4.3 collective-permute-start.3
  60.8 3.8 collective-permute-done.2
  64.7 3.1 fusion.68
  81.6 6.7 %collective-permute-start.11 = (f32[2,16,128]{2,1,0:T(8,128)}, f32[2,16,128]{2,1,0:T(8,128)}, u32[]{:S(2)}, u32[]{:S(2)}) collective-permute-start(f32[2,16,128]{2,1,0:T(8,128)} %copy.519), channel_id=1, source_target_pairs={{0,1},{2,3},{4,5},{6,7},{8,9},{10,11},{12,13},{14,15},{16,17},{18,... | collective-permute-start | bytes 49160 | tf_op jit(solution)/shard_map/ppermute | solution.py:26
  99.3 5.9 all-to-all-start.1
  109.6 3.9 fusion.58
  114.1 5.0 collective-permute-start.9
  122.5 5.4 collective-permute-done.8
  136.6 3.5 collective-permute-start.13
  143.1 5.6 collective-permute-start.17
  154.4 3.6 collective-permute-done.16
  160.2 3.9 fusion.40
  164.7 4.2 collective-permute-start.15
  172.3 5.6 collective-permute-done.14
  186.5 3.6 collective-permute-start.19
  193.1 3.9 collective-permute-start.23
  207.6 3.9 fusion.22
  215.7 5.0 collective-permute-start.21
  227.9 6.4 collective-permute-done.20
  234.4 8.1 %fusion.14 = f32[1,40,16,128]{1,2,3,0:T(8,128)} fusion(f32[40,16,128]{0,1,2:T(8,128)S(1)} %fusion.32, f32[40,2,128]{0,1,2:T(2,128)S(1)} %fusion.228, f32[40,16,128]{0,1,2:T(8,128)} %copy-done.25, f32[40,2,128]{0,1,2:T(2,128)S(1)} %fusion.230, f32[2,16,128]{0,1,2:T(8,128)} %copy.528, f32[2,16,128]{0,1,2:T(8,128)} %copy.526, ...), kind=kLoop, calls=%fused_computation.68 | loop fusion | flops 2703360 | bytes 2736128 | tf_op jit(solution)/shard_map/stack | solution.py:134
  246.9 11.5 %collective-permute-start.24 = (f32[3,40,8,128]{3,2,1,0:T(8,128)}, f32[3,40,8,128]{3,2,1,0:T(8,128)}, u32[]{:S(2)}, u32[]{:S(2)}) collective-permute-start(f32[3,40,8,128]{3,2,1,0:T(8,128)} %slice_select_fusion.1), channel_id=1, source_target_pairs={{0,64},{64,0},{1,65},{65,1},{2,66},{66,2},{3,67},{67,3},{4,68},{68... | collective-permute-start | bytes 1474568 | tf_op jit(solution)/shard_map/ppermute | solution.py:35
  274.8 4.9 collective-permute-start.27
  287.7 6.3 collective-permute-start.25
  300.1 4.1 all-to-all-start.2
  309.3 4.9 fusion.268
  316.7 4.1 collective-permute-start.29
  332.4 7.0 %collective-permute-start.33 = (bf16[2,40,2,128]{1,2,3,0:T(2,128)(2,1)}, bf16[2,40,2,128]{1,2,3,0:T(2,128)(2,1)}, u32[]{:S(2)}, u32[]{:S(2)}) collective-permute-start(bf16[2,40,2,128]{1,2,3,0:T(2,128)(2,1)} %pad_maximum_fusion.36), channel_id=1, source_target_pairs={{0,2},{2,4},{4,6},{6,8},{8,10},{10,12},{12,14},{14,16},{16,18},{18... | collective-permute-start | bytes 122888 | tf_op jit(solution)/shard_map/ppermute | solution.py:16
  347.4 7.0 %collective-permute-start.31 = (f32[2,16,128]{2,1,0:T(8,128)}, f32[2,16,128]{2,1,0:T(8,128)}, u32[]{:S(2)}, u32[]{:S(2)}) collective-permute-start(f32[2,16,128]{2,1,0:T(8,128)} %copy.543), channel_id=1, source_target_pairs={{0,1},{2,3},{4,5},{6,7},{8,9},{10,11},{12,13},{14,15},{16,17},{18,... | collective-permute-start | bytes 49160 | tf_op jit(solution)/shard_map/ppermute | solution.py:16
  361.2 6.2 fusion.266
  370.0 5.5 collective-permute-start.35
  398.5 6.1 collective-permute-start.39
  412.6 6.1 collective-permute-start.37
  420.4 4.3 all-to-all-start.3
  425.5 90.8 %psum.37 = f32[512]{0:T(512)} all-reduce(f32[512]{0:T(512)S(1)} %copy-done.116), channel_id=1, replica_groups=mesh['sec'=2,'tile'=32,'lev'=2] {'sec','tile','lev'}, use_global_device_ids=true, to_apply=%region_3.4 | all-reduce | flops 512 | bytes 4096 | tf_op jit(solution)/shard_map/psum | solution.py:228
  521.2 4.1 fusion.263
  527.9 4.0 collective-permute-start.41
  542.6 4.3 collective-permute-start.45
  555.0 6.8 %collective-permute-start.43 = (f32[2,16,128]{2,1,0:T(8,128)}, f32[2,16,128]{2,1,0:T(8,128)}, u32[]{:S(2)}, u32[]{:S(2)}) collective-permute-start(f32[2,16,128]{2,1,0:T(8,128)} %copy.551), channel_id=1, source_target_pairs={{0,1},{2,3},{4,5},{6,7},{8,9},{10,11},{12,13},{14,15},{16,17},{18,... | collective-permute-start | bytes 49160 | tf_op jit(solution)/shard_map/ppermute | solution.py:16
  568.6 5.5 fusion.261
  579.1 4.6 collective-permute-start.47
  584.0 4.2 fusion.202
  593.4 5.2 fusion.80
  603.1 6.3 all-reduce.84.cloned.1.call-done
  614.3 23.2 %all-reduce.82.cloned.1.call-done = f32[3,40,16,128]{3,2,1,0:T(8,128)} async-done(((f32[3,40,16,128]{3,2,1,0:T(8,128)}), f32[3,40,16,128]{3,2,1,0:T(8,128)}) %all-reduce.82.cloned.1.call-update) | async-done | bytes 983056 | tf_op jit(solution)/shard_map/psum | solution.py:227
  (514 shorter events, 273.8 us)
Async XLA Ops:
  9.1 64.2 %all-to-all-start = ((bf16[3,40,8,128]{3,1,0,2:T(8,128)(2,1)}), bf16[3,40,8,128]{3,1,0,2:T(8,128)(2,1)S(1)}, u32[]{:S(2)}, u32[]{:S(2)}) async-start(bf16[3,40,8,128]{3,1,0,2:T(8,128)(2,1)} %copy.588), calls=%async_computation | async-start | bytes 491520 | tf_op jit(solution)/shard_map/all_to_all | solution.py:180
  17.4 31.0 %collective-permute-start.1 = (f32[40,2,128]{0,1,2:T(2,128)}, f32[40,2,128]{0,1,2:T(2,128)}, u32[]{:S(2)}, u32[]{:S(2)}) collective-permute-start(f32[40,2,128]{0,1,2:T(2,128)} %get-tuple-element.250), channel_id=1, source_target_pairs={{0,2},{2,4},{4,6},{6,8},{8,10},{10,12},{12,14},{14,16},{16,18},{18... | collective-permute-start | bytes 122888 | tf_op jit(solution)/shard_map/ppermute | solution.py:26
  21.6 26.8 %collective-permute-start = (f32[40,2,128]{0,1,2:T(2,128)}, f32[40,2,128]{0,1,2:T(2,128)}, u32[]{:S(2)}, u32[]{:S(2)}) collective-permute-start(f32[40,2,128]{0,1,2:T(2,128)} %get-tuple-element.249), channel_id=1, source_target_pairs={{2,0},{4,2},{6,4},{8,6},{10,8},{12,10},{14,12},{16,14},{18,16},{20... | collective-permute-start | bytes 122888 | tf_op jit(solution)/shard_map/ppermute | solution.py:27
  23.5 20.5 %collective-permute-start.5 = (f32[2,16,128]{2,1,0:T(8,128)}, f32[2,16,128]{2,1,0:T(8,128)}, u32[]{:S(2)}, u32[]{:S(2)}) collective-permute-start(f32[2,16,128]{2,1,0:T(8,128)} %get-tuple-element.263), channel_id=1, source_target_pairs={{0,1},{2,3},{4,5},{6,7},{8,9},{10,11},{12,13},{14,15},{16,17},{18,... | collective-permute-start | bytes 49160 | tf_op jit(solution)/shard_map/ppermute | solution.py:26
  28.9 17.3 %collective-permute-start.4 = (f32[2,16,128]{2,1,0:T(8,128)}, f32[2,16,128]{2,1,0:T(8,128)}, u32[]{:S(2)}, u32[]{:S(2)}) collective-permute-start(f32[2,16,128]{2,1,0:T(8,128)} %get-tuple-element.262), channel_id=1, source_target_pairs={{1,0},{3,2},{5,4},{7,6},{9,8},{11,10},{13,12},{15,14},{17,16},{19,... | collective-permute-start | bytes 49160 | tf_op jit(solution)/shard_map/ppermute | solution.py:27
  53.2 7.6 %collective-permute-start.3 = (f32[2,40,2,128]{1,2,3,0:T(2,128)S(1)}, f32[2,40,2,128]{1,2,3,0:T(2,128)S(1)}, u32[]{:S(2)}, u32[]{:S(2)}) collective-permute-start(f32[2,40,2,128]{1,2,3,0:T(2,128)S(1)} %get-tuple-element.44), channel_id=1, source_target_pairs={{0,2},{2,4},{4,6},{6,8},{8,10},{10,12},{12,14},{14,16},{16,18},{18... | collective-permute-start | bytes 245768 | tf_op jit(solution)/shard_map/ppermute | solution.py:26
  57.5 7.1 %collective-permute-start.2 = (f32[2,40,2,128]{1,2,3,0:T(2,128)S(1)}, f32[2,40,2,128]{1,2,3,0:T(2,128)S(1)}, u32[]{:S(2)}, u32[]{:S(2)}) collective-permute-start(f32[2,40,2,128]{1,2,3,0:T(2,128)S(1)} %get-tuple-element.43), channel_id=1, source_target_pairs={{2,0},{4,2},{6,4},{8,6},{10,8},{12,10},{14,12},{16,14},{18,16},{20... | collective-permute-start | bytes 245768 | tf_op jit(solution)/shard_map/ppermute | solution.py:27
  75.0 34.5 %collective-permute-start.7 = (f32[40,2,128]{0,1,2:T(2,128)}, f32[40,2,128]{0,1,2:T(2,128)S(1)}, u32[]{:S(2)}, u32[]{:S(2)}) collective-permute-start(f32[40,2,128]{0,1,2:T(2,128)} %get-tuple-element.230), channel_id=1, source_target_pairs={{0,2},{2,4},{4,6},{6,8},{8,10},{10,12},{12,14},{14,16},{16,18},{18... | collective-permute-start | bytes 122888 | tf_op jit(solution)/shard_map/ppermute | solution.py:26
  78.1 31.5 %collective-permute-start.6 = (f32[40,2,128]{0,1,2:T(2,128)}, f32[40,2,128]{0,1,2:T(2,128)}, u32[]{:S(2)}, u32[]{:S(2)}) collective-permute-start(f32[40,2,128]{0,1,2:T(2,128)} %get-tuple-element.229), channel_id=1, source_target_pairs={{2,0},{4,2},{6,4},{8,6},{10,8},{12,10},{14,12},{16,14},{18,16},{20... | collective-permute-start | bytes 122888 | tf_op jit(solution)/shard_map/ppermute | solution.py:27
  81.6 23.6 %collective-permute-start.11 = (f32[2,16,128]{2,1,0:T(8,128)}, f32[2,16,128]{2,1,0:T(8,128)}, u32[]{:S(2)}, u32[]{:S(2)}) collective-permute-start(f32[2,16,128]{2,1,0:T(8,128)} %copy.519), channel_id=1, source_target_pairs={{0,1},{2,3},{4,5},{6,7},{8,9},{10,11},{12,13},{14,15},{16,17},{18,... | collective-permute-start | bytes 49160 | tf_op jit(solution)/shard_map/ppermute | solution.py:26
  90.5 16.8 %collective-permute-start.10 = (f32[2,16,128]{2,1,0:T(8,128)}, f32[2,16,128]{2,1,0:T(8,128)}, u32[]{:S(2)}, u32[]{:S(2)}) collective-permute-start(f32[2,16,128]{2,1,0:T(8,128)} %copy.517), channel_id=1, source_target_pairs={{1,0},{3,2},{5,4},{7,6},{9,8},{11,10},{13,12},{15,14},{17,16},{19,... | collective-permute-start | bytes 49160 | tf_op jit(solution)/shard_map/ppermute | solution.py:27
  99.3 101.4 %all-to-all-start.1 = ((f32[3,80,4,128]{3,2,0,1:T(4,128)}), f32[3,80,4,128]{3,2,0,1:T(4,128)S(1)}, u32[]{:S(2)}, u32[]{:S(2)}) async-start(f32[3,80,4,128]{3,2,0,1:T(4,128)} %copy.534), calls=%async_computation.1 | async-start | bytes 983040 | tf_op jit(solution)/shard_map/all_to_all | solution.py:191
  114.1 8.3 %collective-permute-start.9 = (f32[2,40,2,128]{1,2,3,0:T(2,128)S(1)}, f32[2,40,2,128]{1,2,3,0:T(2,128)S(1)}, u32[]{:S(2)}, u32[]{:S(2)}) collective-permute-start(f32[2,40,2,128]{1,2,3,0:T(2,128)S(1)} %get-tuple-element.42), channel_id=1, source_target_pairs={{0,2},{2,4},{4,6},{6,8},{8,10},{10,12},{12,14},{14,16},{16,18},{18... | collective-permute-start | bytes 245768 | tf_op jit(solution)/shard_map/ppermute | solution.py:26
  119.2 8.7 %collective-permute-start.8 = (f32[2,40,2,128]{1,2,3,0:T(2,128)S(1)}, f32[2,40,2,128]{1,2,3,0:T(2,128)S(1)}, u32[]{:S(2)}, u32[]{:S(2)}) collective-permute-start(f32[2,40,2,128]{1,2,3,0:T(2,128)S(1)} %get-tuple-element.41), channel_id=1, source_target_pairs={{2,0},{4,2},{6,4},{8,6},{10,8},{12,10},{14,12},{16,14},{18,16},{20... | collective-permute-start | bytes 245768 | tf_op jit(solution)/shard_map/ppermute | solution.py:27
  136.6 23.5 %collective-permute-start.13 = (f32[40,2,128]{0,1,2:T(2,128)}, f32[40,2,128]{0,1,2:T(2,128)S(1)}, u32[]{:S(2)}, u32[]{:S(2)}) collective-permute-start(f32[40,2,128]{0,1,2:T(2,128)} %get-tuple-element.208), channel_id=1, source_target_pairs={{0,2},{2,4},{4,6},{6,8},{8,10},{10,12},{12,14},{14,16},{16,18},{18... | collective-permute-start | bytes 122888 | tf_op jit(solution)/shard_map/ppermute | solution.py:26
  140.1 20.0 %collective-permute-start.12 = (f32[40,2,128]{0,1,2:T(2,128)}, f32[40,2,128]{0,1,2:T(2,128)}, u32[]{:S(2)}, u32[]{:S(2)}) collective-permute-start(f32[40,2,128]{0,1,2:T(2,128)} %get-tuple-element.207), channel_id=1, source_target_pairs={{2,0},{4,2},{6,4},{8,6},{10,8},{12,10},{14,12},{16,14},{18,16},{20... | collective-permute-start | bytes 122888 | tf_op jit(solution)/shard_map/ppermute | solution.py:27
  143.1 9.2 %collective-permute-start.17 = (f32[2,16,128]{2,1,0:T(8,128)S(1)}, f32[2,16,128]{2,1,0:T(8,128)}, u32[]{:S(2)}, u32[]{:S(2)}) collective-permute-start(f32[2,16,128]{2,1,0:T(8,128)S(1)} %copy.523), channel_id=1, source_target_pairs={{0,1},{2,3},{4,5},{6,7},{8,9},{10,11},{12,13},{14,15},{16,17},{18,... | collective-permute-start | bytes 49160 | tf_op jit(solution)/shard_map/ppermute | solution.py:26
  150.9 7.1 %collective-permute-start.16 = (f32[2,16,128]{2,1,0:T(8,128)}, f32[2,16,128]{2,1,0:T(8,128)}, u32[]{:S(2)}, u32[]{:S(2)}) collective-permute-start(f32[2,16,128]{2,1,0:T(8,128)} %copy.521), channel_id=1, source_target_pairs={{1,0},{3,2},{5,4},{7,6},{9,8},{11,10},{13,12},{15,14},{17,16},{19,... | collective-permute-start | bytes 49160 | tf_op jit(solution)/shard_map/ppermute | solution.py:27
  164.7 7.5 %collective-permute-start.15 = (f32[2,40,2,128]{1,2,3,0:T(2,128)S(1)}, f32[2,40,2,128]{1,2,3,0:T(2,128)S(1)}, u32[]{:S(2)}, u32[]{:S(2)}) collective-permute-start(f32[2,40,2,128]{1,2,3,0:T(2,128)S(1)} %get-tuple-element.40), channel_id=1, source_target_pairs={{0,2},{2,4},{4,6},{6,8},{8,10},{10,12},{12,14},{14,16},{16,18},{18... | collective-permute-start | bytes 245768 | tf_op jit(solution)/shard_map/ppermute | solution.py:26
  169.0 8.9 %collective-permute-start.14 = (f32[2,40,2,128]{1,2,3,0:T(2,128)S(1)}, f32[2,40,2,128]{1,2,3,0:T(2,128)S(1)}, u32[]{:S(2)}, u32[]{:S(2)}) collective-permute-start(f32[2,40,2,128]{1,2,3,0:T(2,128)S(1)} %get-tuple-element.39), channel_id=1, source_target_pairs={{2,0},{4,2},{6,4},{8,6},{10,8},{12,10},{14,12},{16,14},{18,16},{20... | collective-permute-start | bytes 245768 | tf_op jit(solution)/shard_map/ppermute | solution.py:27
  186.5 21.1 %collective-permute-start.19 = (f32[40,2,128]{0,1,2:T(2,128)}, f32[40,2,128]{0,1,2:T(2,128)S(1)}, u32[]{:S(2)}, u32[]{:S(2)}) collective-permute-start(f32[40,2,128]{0,1,2:T(2,128)} %get-tuple-element.186), channel_id=1, source_target_pairs={{0,2},{2,4},{4,6},{6,8},{8,10},{10,12},{12,14},{14,16},{16,18},{18... | collective-permute-start | bytes 122888 | tf_op jit(solution)/shard_map/ppermute | solution.py:26
  190.2 17.4 %collective-permute-start.18 = (f32[40,2,128]{0,1,2:T(2,128)}, f32[40,2,128]{0,1,2:T(2,128)}, u32[]{:S(2)}, u32[]{:S(2)}) collective-permute-start(f32[40,2,128]{0,1,2:T(2,128)} %get-tuple-element.185), channel_id=1, source_target_pairs={{2,0},{4,2},{6,4},{8,6},{10,8},{12,10},{14,12},{16,14},{18,16},{20... | collective-permute-start | bytes 122888 | tf_op jit(solution)/shard_map/ppermute | solution.py:27
  193.1 9.5 %collective-permute-start.23 = (f32[2,16,128]{2,1,0:T(8,128)S(1)}, f32[2,16,128]{2,1,0:T(8,128)}, u32[]{:S(2)}, u32[]{:S(2)}) collective-permute-start(f32[2,16,128]{2,1,0:T(8,128)S(1)} %copy.527), channel_id=1, source_target_pairs={{0,1},{2,3},{4,5},{6,7},{8,9},{10,11},{12,13},{14,15},{16,17},{18,... | collective-permute-start | bytes 49160 | tf_op jit(solution)/shard_map/ppermute | solution.py:26
  215.7 11.1 %collective-permute-start.21 = (f32[2,40,2,128]{1,2,3,0:T(2,128)}, f32[2,40,2,128]{1,2,3,0:T(2,128)}, u32[]{:S(2)}, u32[]{:S(2)}) collective-permute-start(f32[2,40,2,128]{1,2,3,0:T(2,128)} %get-tuple-element.38), channel_id=1, source_target_pairs={{0,2},{2,4},{4,6},{6,8},{8,10},{10,12},{12,14},{14,16},{16,18},{18... | collective-permute-start | bytes 245768 | tf_op jit(solution)/shard_map/ppermute | solution.py:26
  225.5 8.8 %collective-permute-start.20 = (f32[2,40,2,128]{1,2,3,0:T(2,128)}, f32[2,40,2,128]{1,2,3,0:T(2,128)S(1)}, u32[]{:S(2)}, u32[]{:S(2)}) collective-permute-start(f32[2,40,2,128]{1,2,3,0:T(2,128)} %get-tuple-element.37), channel_id=1, source_target_pairs={{2,0},{4,2},{6,4},{8,6},{10,8},{12,10},{14,12},{16,14},{18,16},{20... | collective-permute-start | bytes 245768 | tf_op jit(solution)/shard_map/ppermute | solution.py:27
  246.9 13.3 %collective-permute-start.24 = (f32[3,40,8,128]{3,2,1,0:T(8,128)}, f32[3,40,8,128]{3,2,1,0:T(8,128)}, u32[]{:S(2)}, u32[]{:S(2)}) collective-permute-start(f32[3,40,8,128]{3,2,1,0:T(8,128)} %slice_select_fusion.1), channel_id=1, source_target_pairs={{0,64},{64,0},{1,65},{65,1},{2,66},{66,2},{3,67},{67,3},{4,68},{68... | collective-permute-start | bytes 1474568 | tf_op jit(solution)/shard_map/ppermute | solution.py:35
  272.6 35.2 %collective-permute-start.28 = (bf16[2,40,2,128]{1,2,3,0:T(2,128)(2,1)}, bf16[2,40,2,128]{1,2,3,0:T(2,128)(2,1)S(1)}, u32[]{:S(2)}, u32[]{:S(2)}) collective-permute-start(bf16[2,40,2,128]{1,2,3,0:T(2,128)(2,1)} %pad_maximum_fusion.35), channel_id=1, source_target_pairs={{2,0},{4,2},{6,4},{8,6},{10,8},{12,10},{14,12},{16,14},{18,16},{20... | collective-permute-start | bytes 122888 | tf_op jit(solution)/shard_map/ppermute | solution.py:16
  274.8 33.1 %collective-permute-start.27 = (bf16[2,40,2,128]{1,2,3,0:T(2,128)(2,1)}, bf16[2,40,2,128]{1,2,3,0:T(2,128)(2,1)}, u32[]{:S(2)}, u32[]{:S(2)}) collective-permute-start(bf16[2,40,2,128]{1,2,3,0:T(2,128)(2,1)} %pad_maximum_fusion.34), channel_id=1, source_target_pairs={{0,2},{2,4},{4,6},{6,8},{8,10},{10,12},{12,14},{14,16},{16,18},{18... | collective-permute-start | bytes 122888 | tf_op jit(solution)/shard_map/ppermute | solution.py:16
  284.2 20.0 %collective-permute-start.26 = (f32[2,16,128]{2,1,0:T(8,128)S(1)}, f32[2,16,128]{2,1,0:T(8,128)S(1)}, u32[]{:S(2)}, u32[]{:S(2)}) collective-permute-start(f32[2,16,128]{2,1,0:T(8,128)S(1)} %copy.539), channel_id=1, source_target_pairs={{1,0},{3,2},{5,4},{7,6},{9,8},{11,10},{13,12},{15,14},{17,16},{19,... | collective-permute-start | bytes 49160 | tf_op jit(solution)/shard_map/ppermute | solution.py:16
  287.7 17.9 %collective-permute-start.25 = (f32[2,16,128]{2,1,0:T(8,128)}, f32[2,16,128]{2,1,0:T(8,128)}, u32[]{:S(2)}, u32[]{:S(2)}) collective-permute-start(f32[2,16,128]{2,1,0:T(8,128)} %copy.537), channel_id=1, source_target_pairs={{0,1},{2,3},{4,5},{6,7},{8,9},{10,11},{12,13},{14,15},{16,17},{18,... | collective-permute-start | bytes 49160 | tf_op jit(solution)/shard_map/ppermute | solution.py:16
  300.1 85.5 %all-to-all-start.2 = ((bf16[3,40,8,128]{3,1,0,2:T(8,128)(2,1)}), bf16[3,40,8,128]{3,1,0,2:T(8,128)(2,1)}, u32[]{:S(2)}, u32[]{:S(2)}) async-start(bf16[3,40,8,128]{3,1,0,2:T(8,128)(2,1)} %copy.558), calls=%async_computation.2 | async-start | bytes 491520 | tf_op jit(solution)/shard_map/all_to_all | solution.py:204
  330.2 29.3 %collective-permute-start.34 = (bf16[2,40,2,128]{1,2,3,0:T(2,128)(2,1)}, bf16[2,40,2,128]{1,2,3,0:T(2,128)(2,1)S(1)}, u32[]{:S(2)}, u32[]{:S(2)}) collective-permute-start(bf16[2,40,2,128]{1,2,3,0:T(2,128)(2,1)} %pad_maximum_fusion.37), channel_id=1, source_target_pairs={{2,0},{4,2},{6,4},{8,6},{10,8},{12,10},{14,12},{16,14},{18,16},{20... | collective-permute-start | bytes 122888 | tf_op jit(solution)/shard_map/ppermute | solution.py:16
  332.4 27.1 %collective-permute-start.33 = (bf16[2,40,2,128]{1,2,3,0:T(2,128)(2,1)}, bf16[2,40,2,128]{1,2,3,0:T(2,128)(2,1)}, u32[]{:S(2)}, u32[]{:S(2)}) collective-permute-start(bf16[2,40,2,128]{1,2,3,0:T(2,128)(2,1)} %pad_maximum_fusion.36), channel_id=1, source_target_pairs={{0,2},{2,4},{4,6},{6,8},{8,10},{10,12},{12,14},{14,16},{16,18},{18... | collective-permute-start | bytes 122888 | tf_op jit(solution)/shard_map/ppermute | solution.py:16
  343.9 11.2 %collective-permute-start.32 = (f32[2,16,128]{2,1,0:T(8,128)S(1)}, f32[2,16,128]{2,1,0:T(8,128)}, u32[]{:S(2)}, u32[]{:S(2)}) collective-permute-start(f32[2,16,128]{2,1,0:T(8,128)S(1)} %copy.545), channel_id=1, source_target_pairs={{1,0},{3,2},{5,4},{7,6},{9,8},{11,10},{13,12},{15,14},{17,16},{19,... | collective-permute-start | bytes 49160 | tf_op jit(solution)/shard_map/ppermute | solution.py:16
  347.4 9.9 %collective-permute-start.31 = (f32[2,16,128]{2,1,0:T(8,128)}, f32[2,16,128]{2,1,0:T(8,128)}, u32[]{:S(2)}, u32[]{:S(2)}) collective-permute-start(f32[2,16,128]{2,1,0:T(8,128)} %copy.543), channel_id=1, source_target_pairs={{0,1},{2,3},{4,5},{6,7},{8,9},{10,11},{12,13},{14,15},{16,17},{18,... | collective-permute-start | bytes 49160 | tf_op jit(solution)/shard_map/ppermute | solution.py:16
  396.4 123.6 %collective-permute-start.40 = (bf16[2,40,2,128]{1,2,3,0:T(2,128)(2,1)S(1)}, bf16[2,40,2,128]{1,2,3,0:T(2,128)(2,1)S(1)}, u32[]{:S(2)}, u32[]{:S(2)}) collective-permute-start(bf16[2,40,2,128]{1,2,3,0:T(2,128)(2,1)S(1)} %pad_maximum_fusion.39), channel_id=1, source_target_pairs={{2,0},{4,2},{6,4},{8,6},{10,8},{12,10},{14,12},{16,14},{18,16},{20... | collective-permute-start | bytes 122888 | tf_op jit(solution)/shard_map/ppermute | solution.py:16
  398.5 121.5 %collective-permute-start.39 = (bf16[2,40,2,128]{1,2,3,0:T(2,128)(2,1)}, bf16[2,40,2,128]{1,2,3,0:T(2,128)(2,1)S(1)}, u32[]{:S(2)}, u32[]{:S(2)}) collective-permute-start(bf16[2,40,2,128]{1,2,3,0:T(2,128)(2,1)} %pad_maximum_fusion.38), channel_id=1, source_target_pairs={{0,2},{2,4},{4,6},{6,8},{8,10},{10,12},{12,14},{14,16},{16,18},{18... | collective-permute-start | bytes 122888 | tf_op jit(solution)/shard_map/ppermute | solution.py:16
  409.1 107.1 %collective-permute-start.38 = (f32[2,16,128]{2,1,0:T(8,128)S(1)}, f32[2,16,128]{2,1,0:T(8,128)S(1)}, u32[]{:S(2)}, u32[]{:S(2)}) collective-permute-start(f32[2,16,128]{2,1,0:T(8,128)S(1)} %copy.549), channel_id=1, source_target_pairs={{1,0},{3,2},{5,4},{7,6},{9,8},{11,10},{13,12},{15,14},{17,16},{19,... | collective-permute-start | bytes 49160 | tf_op jit(solution)/shard_map/ppermute | solution.py:16
  412.6 105.1 %collective-permute-start.37 = (f32[2,16,128]{2,1,0:T(8,128)}, f32[2,16,128]{2,1,0:T(8,128)}, u32[]{:S(2)}, u32[]{:S(2)}) collective-permute-start(f32[2,16,128]{2,1,0:T(8,128)} %copy.547), channel_id=1, source_target_pairs={{0,1},{2,3},{4,5},{6,7},{8,9},{10,11},{12,13},{14,15},{16,17},{18,... | collective-permute-start | bytes 49160 | tf_op jit(solution)/shard_map/ppermute | solution.py:16
  420.4 179.9 %all-to-all-start.3 = ((f32[3,80,4,128]{3,2,0,1:T(4,128)}), f32[3,80,4,128]{3,2,0,1:T(4,128)}, u32[]{:S(2)}, u32[]{:S(2)}) async-start(f32[3,80,4,128]{3,2,0,1:T(4,128)} %copy.560), calls=%async_computation.3 | async-start | bytes 983040 | tf_op jit(solution)/shard_map/all_to_all | solution.py:214
  424.7 184.7 %all-reduce.84.cloned.1.call-start = ((), (), s32[]{:S(2)}) async-start(), calls=%async_computation.5 | async-start | bytes 4063232 | tf_op jit(solution)/shard_map/psum | solution.py:228
  425.4 212.0 %all-reduce.82.cloned.1.call-start = ((), (), s32[]{:S(2)}) async-start(), calls=%async_computation.4 | async-start | bytes 1966080 | tf_op jit(solution)/shard_map/psum | solution.py:227
  540.5 26.5 %collective-permute-start.46 = (bf16[2,40,2,128]{1,2,3,0:T(2,128)(2,1)S(1)}, bf16[2,40,2,128]{1,2,3,0:T(2,128)(2,1)S(1)}, u32[]{:S(2)}, u32[]{:S(2)}) collective-permute-start(bf16[2,40,2,128]{1,2,3,0:T(2,128)(2,1)S(1)} %pad_maximum_fusion.41), channel_id=1, source_target_pairs={{2,0},{4,2},{6,4},{8,6},{10,8},{12,10},{14,12},{16,14},{18,16},{20... | collective-permute-start | bytes 122888 | tf_op jit(solution)/shard_map/ppermute | solution.py:16
  542.6 24.3 %collective-permute-start.45 = (bf16[2,40,2,128]{1,2,3,0:T(2,128)(2,1)}, bf16[2,40,2,128]{1,2,3,0:T(2,128)(2,1)S(1)}, u32[]{:S(2)}, u32[]{:S(2)}) collective-permute-start(bf16[2,40,2,128]{1,2,3,0:T(2,128)(2,1)} %pad_maximum_fusion.40), channel_id=1, source_target_pairs={{0,2},{2,4},{4,6},{6,8},{8,10},{10,12},{12,14},{14,16},{16,18},{18... | collective-permute-start | bytes 122888 | tf_op jit(solution)/shard_map/ppermute | solution.py:16
  551.5 11.0 %collective-permute-start.44 = (f32[2,16,128]{2,1,0:T(8,128)S(1)}, f32[2,16,128]{2,1,0:T(8,128)}, u32[]{:S(2)}, u32[]{:S(2)}) collective-permute-start(f32[2,16,128]{2,1,0:T(8,128)S(1)} %copy.553), channel_id=1, source_target_pairs={{1,0},{3,2},{5,4},{7,6},{9,8},{11,10},{13,12},{15,14},{17,16},{19,... | collective-permute-start | bytes 49160 | tf_op jit(solution)/shard_map/ppermute | solution.py:16
  555.0 9.7 %collective-permute-start.43 = (f32[2,16,128]{2,1,0:T(8,128)}, f32[2,16,128]{2,1,0:T(8,128)}, u32[]{:S(2)}, u32[]{:S(2)}) collective-permute-start(f32[2,16,128]{2,1,0:T(8,128)} %copy.551), channel_id=1, source_target_pairs={{0,1},{2,3},{4,5},{6,7},{8,9},{10,11},{12,13},{14,15},{16,17},{18,... | collective-permute-start | bytes 49160 | tf_op jit(solution)/shard_map/ppermute | solution.py:16
  577.7 15.6 %collective-permute-start.48 = (bf16[40,2,128]{0,1,2:T(2,128)(2,1)S(1)}, bf16[40,2,128]{0,1,2:T(2,128)(2,1)S(1)}, u32[]{:S(2)}, u32[]{:S(2)}) collective-permute-start(bf16[40,2,128]{0,1,2:T(2,128)(2,1)S(1)} %get-tuple-element.268), channel_id=1, source_target_pairs={{2,0},{4,2},{6,4},{8,6},{10,8},{12,10},{14,12},{16,14},{18,16},{20... | collective-permute-start | bytes 61448 | tf_op jit(solution)/shard_map/ppermute | solution.py:16
  579.1 14.2 %collective-permute-start.47 = (bf16[40,2,128]{0,1,2:T(2,128)(2,1)S(1)}, bf16[40,2,128]{0,1,2:T(2,128)(2,1)}, u32[]{:S(2)}, u32[]{:S(2)}) collective-permute-start(bf16[40,2,128]{0,1,2:T(2,128)(2,1)S(1)} %get-tuple-element.267), channel_id=1, source_target_pairs={{0,2},{2,4},{4,6},{6,8},{8,10},{10,12},{12,14},{14,16},{16,18},{18... | collective-permute-start | bytes 61448 | tf_op jit(solution)/shard_map/ppermute | solution.py:16
  (125 other events, 1016.6 us)
Sparse Core Ops, SparseCore 0:
  431.5 177.8 all-reduce.83
  612.4 24.9 all-reduce.81
where the time goes:
time: 658 us; the launch traced here: 647 us
  starting transfers between devices  184 us (28%)
  local copies, waits for them, and re-layouts  165 us (25%)
  other arithmetic  107 us (16%)
  blocking collectives  90.8 us (14%)
  waiting for transfers between devices  67.4 us (10%)
  between operations  21.8 us (3%)
  matrix products  10.9 us (2%)
    psum x1, blocking collectives, local(): lax.psum((grad_first, grad_bias, grad_second, grad_third), ('sec', 'tile'...  90.8 us
    ppermute x24, starting transfers between devices, from_behind(): lax.ppermute(value, axis, [(source, source + steps) for source in range(f...  82.7 us
    ppermute x12, starting transfers between devices, extended(): before = lax.ppermute(last, axis, up)  54.5 us
    ppermute x12, waiting for transfers between devices, extended(): after = lax.ppermute(first, axis, down)  25.5 us
    psum x1, waiting for transfers between devices, local(): state_grad = lax.psum(adjoint + placed, 'sec')  23.2 us
    unnamed x245, local copies, waits for them, and re-layouts  18.2 us
    ppermute x8, local copies, waits for them, and re-layouts, from_behind(): lax.ppermute(value, axis, [(source, source + steps) for source in range(f...  16.1 us
    sub x4, other arithmetic, forward_step(): wind_x = wind_x - coeff * diff_padded(row_padded, 1, rows)  15.8 us
  transfers between devices with their start and end apart: 55, of which 16 were waited for; matrix products, arithmetic and copies ran while one was open for 36% of the time, Pallas kernels for 0%

commit v1 on v0

v1 whole, which is shorter than its diff:
```python
import jax
import jax.numpy as jnp
from jax import lax
from jax.experimental import pallas as pl
from jax.experimental.pallas import tpu as pltpu
from jax.sharding import PartitionSpec as P

SUBSTEPS = 4
COURANT = 0.3
DIFFUSION = 0.08
NEAR = 8.0 / 12.0
FAR = 1.0 / 12.0

BLK = 8
OWN = 40
EDGE = 8
EXT = OWN + EDGE
ROWS = 7 * BLK
CHUNK = 4
WIND_BLOCKS = ((0, 5), (0, 5), (1, 4), (1, 4))
MASS_BLOCKS = ((0, 5), (1, 4), (1, 4), (2, 3))


def roll(values, steps, axis):
    return pltpu.roll(values, steps % values.shape[axis], axis)


def across(values):
    return NEAR * (roll(values, -1, 2) - roll(values, 1, 2)) - FAR * (
        roll(values, -2, 2) - roll(values, 2, 2)
    )


def along(ref, levels, row):
    def take(steps):
        return ref[levels, row + steps : row + steps + BLK, :]

    return NEAR * (take(1) - take(-1)) - FAR * (take(2) - take(-2))


def vertical(ref, k, row):
    v = ref[pl.ds(k, CHUNK + 4), row : row + BLK, :]
    mid = v[2 : 2 + CHUNK]
    near = v[3 : 3 + CHUNK] + v[1 : 1 + CHUNK]
    far = v[4 : 4 + CHUNK] + v[0:CHUNK]
    return mid, DIFFUSION * (16.0 / 12.0) * near - (DIFFUSION / 12.0) * far - (
        DIFFUSION * 30.0 / 12.0
    ) * mid


def edge_masks():
    i = lax.broadcasted_iota(jnp.int32, (1, 2 * BLK, 128), 1)

    def at(row, value):
        return jnp.where(i == row, value, 0.0)

    return at(8, -NEAR), at(8, FAR) + at(9, FAR), at(7, NEAR), at(7, -FAR) + at(6, -FAR)


def crossing(values, masks):
    m1, m2, m3, m4 = masks
    return (
        m1 * roll(values, 1, 1)
        + m2 * roll(values, 2, 1)
        + m3 * roll(values, -1, 1)
        + m4 * roll(values, -2, 1)
    )


def turn_rows(turn_ref, edge):
    i = lax.broadcasted_iota(jnp.int32, (1, 2 * BLK, 128), 1)
    low = i < BLK
    cosine = jnp.where(low, turn_ref[4 * edge], turn_ref[4 * edge + 2])
    sine = jnp.where(low, turn_ref[4 * edge + 1], turn_ref[4 * edge + 3])
    return cosine, sine


def clear(ref, levels):
    zeros = jnp.zeros((levels, BLK, 128), jnp.float32)
    ref[:, 0:BLK, :] = zeros
    ref[:, ROWS - BLK : ROWS, :] = zeros


def spread_block(src, comp, count, dst, level, row, scale):
    def body(i, _):
        rows = src[comp, pl.ds(pl.multiple_of(i * 16, 16), 16), :].astype(jnp.float32)
        if scale != 1.0:
            rows = rows * scale
        dst[pl.ds(level + 2 * i, 2), pl.ds(row, BLK), :] = rows.reshape(2, BLK, 128)
        return 0

    lax.fori_loop(0, count // 2, body, 0, unroll=4)


def places(place_ref):
    sec, lev = place_ref[0], place_ref[1]
    own_level = EDGE * lev
    edge_level = OWN * (1 - lev)
    partner_row = pl.multiple_of(16 + 16 * sec, BLK)
    other_row = pl.multiple_of(32 - 16 * sec, BLK)
    tile_row = pl.multiple_of(24 - 8 * sec, BLK)
    near_edge = pl.multiple_of(16 + 8 * sec, BLK)
    far_edge = pl.multiple_of(32 - 24 * sec, BLK)
    return own_level, edge_level, partner_row, other_row, tile_row, near_edge, far_edge


def forward_kernel(
    place_ref, turn_ref, state_ref, sound_ref, low_ref, high_ref, low_edge_ref, high_edge_ref,
    partner_ref, partner_edge_ref, other_edge_ref, own_edge_ref,
    out_ref, c_ref, pa, pb, u, v,
):
    own_level, edge_level, partner_row, other_row, tile_row, near_edge, far_edge = places(place_ref)
    for ref, levels in ((pa, EXT + 4), (pb, EXT + 4), (u, EXT), (v, EXT), (c_ref, EXT)):
        clear(ref, levels)
    for ref in (pa, pb):
        ref[0:2] = jnp.zeros((2, ROWS, 128), jnp.float32)
        ref[EXT + 2 : EXT + 4] = jnp.zeros((2, ROWS, 128), jnp.float32)
    for comp, dst, shift, scale in ((0, pa, 2, 1.0), (1, u, 0, 1.0), (2, v, 0, 1.0), (3, c_ref, 0, COURANT)):
        at = own_level + shift
        for src, edge, row in (
            (low_ref, low_edge_ref, BLK),
            (high_ref, high_edge_ref, 5 * BLK),
            (partner_ref, partner_edge_ref, partner_row),
        ):
            spread_block(src, comp, OWN, dst, at, row, scale)
            spread_block(edge, comp, EDGE, dst, edge_level + shift, row, scale)
        spread_block(other_edge_ref, comp, EDGE, dst, edge_level + shift, other_row, scale)
        spread_block(own_edge_ref, comp, EDGE, dst, edge_level + shift, 3 * BLK, scale)
        if comp < 3:
            dst[pl.ds(at, OWN), pl.ds(tile_row, 16), :] = state_ref[comp]
        else:
            dst[pl.ds(at, OWN), pl.ds(tile_row, 16), :] = COURANT * sound_ref[...]
    masks = edge_masks()
    turns = [turn_rows(turn_ref, 0), turn_rows(turn_ref, 1)]
    for step in range(SUBSTEPS):
        old, new = (pa, pb) if step % 2 == 0 else (pb, pa)

        def body(i, _, step=step, old=old, new=new):
            k = i * CHUNK
            levels = pl.ds(k, CHUNK)
            inner = pl.ds(k + 2, CHUNK)
            for block in range(*WIND_BLOCKS[step]):
                row = BLK + BLK * block
                rows = slice(row, row + BLK)
                c = c_ref[levels, rows, :]
                u[levels, rows, :] = u[levels, rows, :] - c * along(old, inner, row)
                v[levels, rows, :] = v[levels, rows, :] - c * across(old[inner, rows, :])
            for block in range(*MASS_BLOCKS[step]):
                row = BLK + BLK * block
                rows = slice(row, row + BLK)
                c = c_ref[levels, rows, :]
                mid, mixing = vertical(old, k, row)
                spread = along(u, levels, row) + across(v[levels, rows, :])
                new[inner, rows, :] = mid - c * spread + mixing
            for edge, start in enumerate((near_edge, far_edge)[: 2 if step < 2 else 1]):
                window = pl.ds(start, 2 * BLK)
                cosine, sine = turns[edge]
                delta = cosine * u[levels, window, :] - sine * v[levels, window, :]
                c = c_ref[levels, window, :]
                new[inner, window, :] = new[inner, window, :] - c * crossing(delta, masks)
            return 0

        lax.fori_loop(0, EXT // CHUNK, body, 0)
    final = pa if SUBSTEPS % 2 == 0 else pb
    own = slice(3 * BLK, 4 * BLK)
    out_ref[0] = final[pl.ds(own_level + 2, OWN), own, :]
    out_ref[1] = u[pl.ds(own_level, OWN), own, :]
    out_ref[2] = v[pl.ds(own_level, OWN), own, :]


def adjoint_kernel(
    place_ref, turn_ref, resid_ref, other_ref, low_ref, high_ref, low_edge_ref, high_edge_ref,
    partner_ref, partner_edge_ref, other_edge_ref, own_edge_ref, c_ref,
    out_ref, pa, pb, u, v, w,
):
    own_level, edge_level, partner_row, other_row, tile_row, near_edge, far_edge = places(place_ref)
    for ref, levels in ((pa, EXT + 4), (pb, EXT + 4), (u, EXT), (v, EXT), (w, CHUNK)):
        clear(ref, levels)
    for ref in (pa, pb):
        ref[0:2] = jnp.zeros((2, ROWS, 128), jnp.float32)
        ref[EXT + 2 : EXT + 4] = jnp.zeros((2, ROWS, 128), jnp.float32)
    for comp, dst, shift in ((0, pa, 2), (1, u, 0), (2, v, 0)):
        at = own_level + shift
        for src, edge, row in (
            (low_ref, low_edge_ref, BLK),
            (high_ref, high_edge_ref, 5 * BLK),
            (partner_ref, partner_edge_ref, partner_row),
        ):
            spread_block(src, comp, OWN, dst, at, row, 1.0)
            spread_block(edge, comp, EDGE, dst, edge_level + shift, row, 1.0)
        spread_block(other_edge_ref, comp, EDGE, dst, edge_level + shift, other_row, 1.0)
        spread_block(own_edge_ref, comp, EDGE, dst, edge_level + shift, 3 * BLK, 1.0)
        dst[pl.ds(at, OWN), 3 * BLK : 4 * BLK, :] = resid_ref[comp]
        dst[pl.ds(at, OWN), pl.ds(other_row, BLK), :] = other_ref[comp]
    masks = edge_masks()
    turns = [turn_rows(turn_ref, 0), turn_rows(turn_ref, 1)]
    whole = pl.ds(0, CHUNK)
    for step in range(SUBSTEPS):
        old, new = (pa, pb) if step % 2 == 0 else (pb, pa)

        def body(i, _, step=step, old=old, new=new):
            k = i * CHUNK
            levels = pl.ds(k, CHUNK)
            inner = pl.ds(k + 2, CHUNK)
            w[:, BLK : 6 * BLK, :] = c_ref[levels, BLK : 6 * BLK, :] * old[inner, BLK : 6 * BLK, :]
            for block in range(*WIND_BLOCKS[step]):
                row = BLK + BLK * block
                rows = slice(row, row + BLK)
                u[levels, rows, :] = u[levels, rows, :] + along(w, whole, row)
                v[levels, rows, :] = v[levels, rows, :] + across(w[:, rows, :])
            for edge, start in enumerate((near_edge, far_edge)[: 2 if step < 2 else 1]):
                window = pl.ds(start, 2 * BLK)
                cosine, sine = turns[edge]
                cross = crossing(w[:, window, :], masks)
                u[levels, window, :] = u[levels, window, :] + cosine * cross
                v[levels, window, :] = v[levels, window, :] - sine * cross
            w[:, BLK : 6 * BLK, :] = c_ref[levels, BLK : 6 * BLK, :] * u[levels, BLK : 6 * BLK, :]
            for block in range(*MASS_BLOCKS[step]):
                row = BLK + BLK * block
                rows = slice(row, row + BLK)
                mid, mixing = vertical(old, k, row)
                cv = c_ref[levels, rows, :] * v[levels, rows, :]
                new[inner, rows, :] = mid + mixing + along(w, whole, row) + across(cv)
            return 0

        lax.fori_loop(0, EXT // CHUNK, body, 0)
    final = pa if SUBSTEPS % 2 == 0 else pb
    own = slice(3 * BLK, 4 * BLK)
    out_ref[0] = final[pl.ds(own_level + 2, OWN), own, :]
    out_ref[1] = u[pl.ds(own_level, OWN), own, :]
    out_ref[2] = v[pl.ds(own_level, OWN), own, :]


def scratch(extra=()):
    mass = pltpu.VMEM((EXT + 4, ROWS, 128), jnp.float32)
    wind = pltpu.VMEM((EXT, ROWS, 128), jnp.float32)
    return [mass, mass, wind, wind, *extra]


def call(kernel, n_smem, n_vmem, outs, extra=()):
    vmem = pl.BlockSpec(memory_space=pltpu.VMEM)
    smem = pl.BlockSpec(memory_space=pltpu.SMEM)
    return pl.pallas_call(
        kernel,
        out_shape=outs,
        in_specs=[smem] * n_smem + [vmem] * n_vmem,
        out_specs=jax.tree.map(lambda _: vmem, outs),
        scratch_shapes=scratch(extra),
        compiler_params=pltpu.CompilerParams(vmem_limit_bytes=48 * 1024 * 1024),
        cost_estimate=pl.CostEstimate(flops=40_000_000, bytes_accessed=10_000_000, transcendentals=0),
    )


def swap(value, axis):
    return lax.ppermute(value, axis, [(0, 1), (1, 0)])


def strip_swaps(value, edges, tiles):
    odd = lax.rem(lax.axis_index("tile"), 2) == 1
    first = [(t, t ^ 1) for t in range(tiles)]
    second = [(t, ((t + 1) ^ 1) - 1) for t in range(1, tiles - 1)]

    def cross(pairs):
        return [(2 * a + lev, 2 * b + 1 - lev) for a, b in pairs for lev in range(2)]

    a = lax.ppermute(value, "tile", first)
    b = lax.ppermute(value, "tile", second)
    a_edge = lax.ppermute(edges, ("tile", "lev"), cross(first))
    b_edge = lax.ppermute(edges, ("tile", "lev"), cross(second))
    return (
        jnp.where(odd, a, b),
        jnp.where(odd, b, a),
        jnp.where(odd, a_edge, b_edge),
        jnp.where(odd, b_edge, a_edge),
    )


def turn_factors(quarter):
    cosine = jnp.where(quarter == 0, 1.0, 0.0) - jnp.where(quarter == 2, 1.0, 0.0)
    sine = jnp.where(quarter == 1, 1.0, 0.0) - jnp.where(quarter == 3, 1.0, 0.0)
    return (cosine, sine)


def slope(values):
    sigma = jax.nn.sigmoid(values)
    return sigma * (1.0 + values * (1.0 - sigma))


def product(left, right, left_dim, right_dim):
    return lax.dot_general(
        left, right, (((left_dim,), (right_dim,)), ((), ())), preferred_element_type=jnp.float32
    )


def local(state, sound, target, edge_turn, w_first, b_first, w_second, w_third):
    sec, lev = lax.axis_index("sec"), lax.axis_index("lev")
    tiles = lax.axis_size("tile")
    bf = jnp.bfloat16
    width = state.shape[3]
    hid = w_second.shape[0]
    feats = w_first.shape[0]
    cols = BLK * width

    def own_rows(values):
        return lax.dynamic_slice_in_dim(values, sec * BLK, BLK, values.ndim - 2)

    def edge_levels(values):
        return lax.dynamic_slice_in_dim(values, (OWN - EDGE) * (1 - lev), EDGE, 1)

    def packed(values):
        return values.reshape(values.shape[0], -1, width)

    def both_levels(own, other):
        own = own.reshape(3, OWN, cols)
        other = other.reshape(3, OWN, cols)
        low = jnp.where(lev == 0, own, other)
        high = jnp.where(lev == 0, other, own)
        return jnp.concatenate([low, high], axis=1).reshape(feats, cols)

    def near_far(value):
        low, high = value
        return jnp.where(sec == 0, high, low)

    own_state = own_rows(state)
    own_sound = own_rows(sound)
    block = jnp.concatenate([own_state, own_sound[None]], axis=0).astype(bf)
    cos_low, sin_low = turn_factors(edge_turn[0, 0])
    cos_high, sin_high = turn_factors(edge_turn[0, 1])
    factors = jnp.stack([cos_low, sin_low, cos_high, sin_high])
    turn_block = jnp.broadcast_to(
        jnp.concatenate([factors, jnp.zeros((12,), factors.dtype)])[:, None], (16, width)
    ).astype(bf)
    edges = edge_levels(block)
    payload = jnp.concatenate([block.reshape(-1, width), turn_block], axis=0)
    low, high, low_edge, high_edge = strip_swaps(payload, packed(edges), tiles)
    columns = swap(
        jnp.concatenate([block[:3].reshape(-1, width), edges[3].reshape(-1, width)], axis=0), "lev"
    )
    n_state = 3 * OWN * BLK
    other_state = columns[:n_state].reshape(3, OWN, BLK, width)
    lev_edge = lax.dynamic_slice_in_dim(other_state, (OWN - EDGE) * lev, EDGE, 1)
    own_edge = jnp.concatenate(
        [packed(lev_edge), columns[n_state:].reshape(1, EDGE * BLK, width)], axis=0
    )
    low_turn, high_turn = low[4 * OWN * BLK :, 0], high[4 * OWN * BLK :, 0]
    low = low[: 4 * OWN * BLK].reshape(4, OWN * BLK, width)
    high = high[: 4 * OWN * BLK].reshape(4, OWN * BLK, width)
    partner, partner_edge, other_edge = swap(
        (near_far((low, high)), near_far((low_edge, high_edge)), own_edge), "sec"
    )
    f32 = jnp.float32
    lower = jnp.stack([cos_low - 1, sin_low, low_turn[2].astype(f32) - 1, low_turn[3].astype(f32)])
    upper = jnp.stack(
        [high_turn[0].astype(f32) - 1, high_turn[1].astype(f32), cos_high - 1, sin_high]
    )
    turns = jnp.where(sec == 0, jnp.concatenate([lower, upper]), jnp.concatenate([upper, lower]))
    place = jnp.stack([sec, lev]).astype(jnp.int32)

    evolved, coeff = call(
        forward_kernel, 2, 10,
        (jax.ShapeDtypeStruct((3, OWN, BLK, width), f32), jax.ShapeDtypeStruct((EXT, ROWS, width), f32)),
    )(place, turns, state, sound, low, high, low_edge, high_edge, partner, partner_edge, other_edge, own_edge)

    feat = both_levels(block[:3], other_state)
    first = product(w_first, feat, 0, 0) + b_first[:, None]
    hidden_one = jax.nn.silu(first).astype(bf)
    second = product(w_second, hidden_one, 0, 0)
    hidden_two = jax.nn.silu(second).astype(bf)
    w_third_own = lax.dynamic_slice_in_dim(w_third.reshape(hid, 3, 2 * OWN), lev * OWN, OWN, 2)
    w_first_own = lax.dynamic_slice_in_dim(w_first.reshape(3, 2 * OWN, hid), lev * OWN, OWN, 1)
    tendency = product(w_third_own.reshape(hid, 3 * OWN), hidden_two, 0, 0)
    resid = evolved + tendency.reshape(3, OWN, BLK, width) - own_rows(target)

    resid_low = resid.astype(bf)
    other_block = swap(resid, "sec")
    r_edges = packed(edge_levels(resid_low))
    r_low, r_high, r_low_edge, r_high_edge = strip_swaps(packed(resid_low), r_edges, tiles)
    other_resid = swap(packed(resid_low), "lev").reshape(3, OWN, BLK, width)
    r_own_edge = packed(lax.dynamic_slice_in_dim(other_resid, (OWN - EDGE) * lev, EDGE, 1))
    r_partner, r_partner_edge, r_other_edge = swap(
        (near_far((r_low, r_high)), near_far((r_low_edge, r_high_edge)), r_own_edge), "sec"
    )

    resid_cols = both_levels(resid_low, other_resid)
    err_two = (product(w_third, resid_cols, 1, 0) * slope(second)).astype(bf)
    err_one = (product(w_second, err_two, 1, 0) * slope(first)).astype(bf)
    half = hid // 2

    def half_units(values):
        return lax.dynamic_slice_in_dim(values, lev * half, half, 0)

    err_half = half_units(err_one)
    n_rows = 1024
    grads = jnp.concatenate(
        [
            product(feat, err_half, 1, 1),
            product(hidden_one, half_units(err_two), 1, 1),
            product(resid_cols, half_units(hidden_two), 1, 1),
            jnp.sum(err_half.astype(f32), axis=1)[None],
            jnp.zeros((n_rows - 2 * feats - hid - 1, half), f32),
        ],
        axis=0,
    )
    quarter = half // 2
    kept = lax.dynamic_slice_in_dim(grads, sec * quarter, quarter, 1)
    given = lax.dynamic_slice_in_dim(grads, (1 - sec) * quarter, quarter, 1)
    kept = kept + swap(given, "sec")
    share = n_rows // tiles
    parts = lax.all_to_all(kept.astype(bf).reshape(tiles, share, quarter), "tile", 0, 0)
    ncols = cols * 2 * tiles
    total = jnp.sum(parts.astype(f32), axis=0) / ncols
    everywhere = jnp.broadcast_to(total[None], (2 * tiles, share, quarter))
    gathered = lax.all_to_all(everywhere, ("tile", "lev"), 0, 0)
    partner_half = swap(gathered, "sec")
    halves = jnp.stack(
        [jnp.where(sec == 0, gathered, partner_half), jnp.where(sec == 0, partner_half, gathered)]
    ).reshape(2, tiles, 2, share, quarter)
    full = halves.transpose(1, 3, 2, 0, 4).reshape(n_rows, hid)

    input_grad = product(w_first_own.reshape(3 * OWN, hid), err_one, 1, 0)
    adjoint = call(
        adjoint_kernel, 2, 11, jax.ShapeDtypeStruct((3, OWN, BLK, width), f32),
        (pltpu.VMEM((CHUNK, ROWS, 128), f32),),
    )(place, turns, resid, other_block, r_low, r_high, r_low_edge, r_high_edge, r_partner, r_partner_edge, r_other_edge, r_own_edge, coeff)
    mine = adjoint + input_grad.reshape(3, OWN, BLK, width)
    theirs = swap(mine, "sec")
    state_grad = jnp.concatenate(
        [jnp.where(sec == 0, mine, theirs), jnp.where(sec == 0, theirs, mine)], axis=2
    )
    return (
        state_grad,
        full[:feats],
        full[2 * feats + hid],
        full[feats : feats + hid],
        full[feats + hid : 2 * feats + hid].T,
    )


def solution(mesh):
    placed = (
        P(None, "lev", "tile", None),
        P("lev", "tile", None),
        P(None, "lev", "tile", None),
        P("tile", None),
        P(),
        P(),
        P(),
        P(),
    )
    return jax.shard_map(
        local,
        mesh=mesh,
        in_specs=placed,
        out_specs=(P(None, "lev", "tile", None), P(), P(), P(), P()),
        check_vma=False,
    )
```

time: 658 us -> 179 us (0.27); the launches traced: 647 us -> 178 us
  starting transfers between devices: 184 us -> 41 us
  local copies, waits for them, and re-layouts: 165 us -> 33.7 us
  other arithmetic: 107 us -> 13.5 us
  blocking collectives: 90.8 us -> 13.3 us
  waiting for transfers between devices: 67.4 us -> 27.6 us
  Pallas kernels: 0 us -> 28.1 us
  between operations: 21.8 us -> 7.66 us
    ppermute x49 -> x20, starting transfers between devices: 164 us -> 34.8 us  [the longest x12 13.2 us: swap(): return lax.ppermute(value, axis, [(0, 1), (1, 0)])]
    psum x1 -> x0, blocking collectives: 90.8 us -> none  [local(): lax.psum((grad_first, grad_bias, grad_second, grad_third), ('sec', 'tile'...]
    slice x95 -> x7, local copies, waits for them, and re-layouts: 88.4 us -> 4.19 us  [the longest x1 2.26 us: local(): full[feats:feats + hid]]
    ppermute x16 -> x0, local copies, waits for them, and re-layouts: 33.5 us -> none  [the longest x8 16.1 us: from_behind(): lax.ppermute(value, axis, [(source, source + steps) for source in range(f...]
    psum x2 -> x0, waiting for transfers between devices: 29.5 us -> none  [the longest x1 23.2 us: local(): state_grad = lax.psum(adjoint + placed, 'sec')]
    pallas_call x0 -> x2, Pallas kernels: none -> 28.1 us  [the longest x1 15.2 us: local(): call(adjoint_kernel, 2, 11, jax.ShapeDtypeStruct((3, OWN, BLK, width), f3...]
    mul x8 -> x0, other arithmetic: 26.5 us -> none  [the longest x2 11.7 us: adjoint_step(): spread_x = diff_padded_t(coeff * grad_x, 1)]
    another operation x16 -> x1, other arithmetic: 24.3 us -> 0.07 us  [local(): place = jnp.stack([sec, lev]).astype(jnp.int32)]
  transfers between devices with their start and end apart: 55 -> 21, of which waited for: 16 -> 8; matrix products, arithmetic and copies ran while one was open for 36% -> 10% of each run, Pallas kernels for 0% -> 9%
where the time goes in v1:
time: 179 us; the launch traced here: 178 us
  starting transfers between devices  41 us (23%)
  local copies, waits for them, and re-layouts  33.7 us (19%)
  Pallas kernels  28.1 us (16%)
  waiting for transfers between devices  27.6 us (15%)
  other arithmetic  13.5 us (8%)
  blocking collectives  13.3 us (7%)
  matrix products  12.7 us (7%)
  between operations  7.66 us (4%)
    ppermute x12, waiting for transfers between devices, swap(): return lax.ppermute(value, axis, [(0, 1), (1, 0)])  19.1 us
    pallas_call x1, Pallas kernels, local(): call(adjoint_kernel, 2, 11, jax.ShapeDtypeStruct((3, OWN, BLK, width), f3...  15.2 us
    all_to_all x1, blocking collectives, local(): lax.all_to_all(kept.astype(bf).reshape(tiles, share, quarter), 'tile', 0, 0)  13.3 us
    ppermute x12, starting transfers between devices, swap(): return lax.ppermute(value, axis, [(0, 1), (1, 0)])  13.2 us
    pallas_call x1, Pallas kernels, local(): call(forward_kernel, 2, 10, (jax.ShapeDtypeStruct((3, OWN, BLK, width), f...  12.9 us
    dot_general x9, matrix products, product(): lax.dot_general(left, right, (((left_dim,), (right_dim,)), ((), ())), pre...  12.7 us
    ppermute x2, starting transfers between devices, strip_swaps(): a_edge = lax.ppermute(edges, ('tile', 'lev'), cross(first))  10.9 us
    unnamed x68, local copies, waits for them, and re-layouts  10.4 us
  transfers between devices with their start and end apart: 21, of which 8 were waited for; matrix products, arithmetic and copies ran while one was open for 10% of the time, Pallas kernels for 9%

profile of v1, /device:TPU:1, one launch (start us, length us, event | category | flops | bytes accessed | tf_op | source)
XLA Modules:
  0.0 177.6 jit_solution(18414056362176313191)
XLA Ops:
  0.7 1.3 fusion.25
  7.2 0.9 dynamic-slice_bitcast_fusion
  8.1 1.1 constant_dynamic-slice_fusion.1
  10.3 5.4 %collective-permute-start = (bf16[1296,128]{1,0:T(8,128)(2,1)S(1)}, bf16[1296,128]{1,0:T(8,128)(2,1)}, u32[]{:S(2)}, u32[]{:S(2)}) collective-permute-start(bf16[1296,128]{1,0:T(8,128)(2,1)S(1)} %pad_maximum_fusion.3), channel_id=1, source_target_pairs={{0,2},{2,0},{4,6},{6,4},{8,10},{10,8},{12,14},{14,12},{16,18},{18,... | collective-permute-start | bytes 995336 | tf_op jit(solution)/shard_map/ppermute | solution.py:266
  16.4 5.1 %collective-permute-start.2 = (bf16[4,64,128]{2,1,0:T(8,128)(2,1)S(1)}, bf16[4,64,128]{2,1,0:T(8,128)(2,1)S(1)}, u32[]{:S(2)}, u32[]{:S(2)}) collective-permute-start(bf16[4,64,128]{2,1,0:T(8,128)(2,1)S(1)} %dynamic-slice_bitcast_fusion.1), channel_id=1, source_target_pairs={{0,3},{1,2},{2,1},{3,0},{4,7},{5,6},{6,5},{7,4},{8,11},{9,10},{10,... | collective-permute-start | bytes 196616 | tf_op jit(solution)/shard_map/ppermute | solution.py:268
  21.6 3.0 %collective-permute-start.6 = (bf16[1024,128]{1,0:T(8,128)(2,1)S(1)}, bf16[1024,128]{1,0:T(8,128)(2,1)S(1)}, u32[]{:S(2)}, u32[]{:S(2)}) collective-permute-start(bf16[1024,128]{1,0:T(8,128)(2,1)S(1)} %pad_maximum_fusion.4), channel_id=1, source_target_pairs={{0,1},{1,0},{2,3},{3,2},{4,5},{5,4},{6,7},{7,6},{8,9},{9,8},{10,11... | collective-permute-start | bytes 786440 | tf_op jit(solution)/shard_map/ppermute | solution.py:255
  24.8 2.0 %collective-permute-done.2 = bf16[4,64,128]{2,1,0:T(8,128)(2,1)S(1)} collective-permute-done((bf16[4,64,128]{2,1,0:T(8,128)(2,1)S(1)}, bf16[4,64,128]{2,1,0:T(8,128)(2,1)S(1)}, u32[]{:S(2)}, u32[]{:S(2)}) %collective-permute-start.2) | collective-permute-done | bytes 65568 | tf_op jit(solution)/shard_map/ppermute | solution.py:268
  28.2 7.7 %collective-permute-done.6 = bf16[1024,128]{1,0:T(8,128)(2,1)S(1)} collective-permute-done((bf16[1024,128]{1,0:T(8,128)(2,1)S(1)}, bf16[1024,128]{1,0:T(8,128)(2,1)S(1)}, u32[]{:S(2)}, u32[]{:S(2)}) %collective-permute-start.6) | collective-permute-done | bytes 262176 | tf_op jit(solution)/shard_map/ppermute | solution.py:255
  38.1 2.0 %add_divide_fusion.1 = (f32[512,1024]{0,1:T(8,128)}, f32[512,1024]{0,1:T(8,128)S(1)}) fusion(f32[1024,512]{1,0:T(8,128)S(1)} %fusion.26, f32[512]{0:T(512)S(1)} %copy-done.32), kind=kLoop, calls=%fused_computation.7 | loop fusion | flops 2097152 | bytes 6293504 | tf_op jit(solution)/shard_map/jit(silu)/div | solution.py:366
  40.8 2.3 %multiply_convert_fusion.1 = (bf16[1024,512]{1,0:T(8,128)(2,1)S(1)}, f32[1024,512]{1,0:T(8,128)}) fusion(bf16[512,1024]{0,1:T(8,128)(2,1)S(1)} %multiply_convert_fusion.2, bf16[512,512]{1,0:T(8,128)(2,1)S(1)} %copy-done), kind=kOutput, calls=%fused_computation.5 | convolution fusion | flops 539492352 | bytes 4718592 | tf_op jit(solution)/shard_map/dot_general | solution.py:290
  43.0 1.3 fusion.12
  44.3 1.1 broadcast_select_fusion.2
  48.0 1.4 concatenate.40
  49.4 1.4 concatenate.41
  52.7 1.0 copy-done.2
  53.7 1.0 copy-done.4
  54.7 0.8 copy-done.5
  58.9 12.9 %shard_map.119 = (f32[3,40,8,128]{3,2,1,0:T(8,128)S(1)}, f32[48,56,128]{2,1,0:T(8,128)S(1)}) custom-call(s32[2]{0:T(128)S(1)} %pad_add_fusion.place_ref, f32[8]{0:T(128)S(1)} %broadcast_select_fusion.20.turn_ref, f32[3,40,16,128]{3,2,1,0:T(8,128)S(1)} %copy-done.1, f32[40,16,128]{2,1,0:T(8,128)S(1)} %copy-done.2, bf16[4,320,128]{2,1,0:T(8,128)(2,1)S(1)} %bitcast.102, ...), custom_call_target="tpu_custom_call" | custom-call | flops 40000000 | bytes 10000000 | tf_op jit(solution)/shard_map/pallas_call | solution.py:359
  71.8 1.4 fusion.21
  73.8 1.9 %add_divide_fusion = f32[512,1024]{0,1:T(8,128)} fusion(f32[1024,512]{1,0:T(8,128)S(1)} %copy-done.17), kind=kLoop, calls=%fused_computation.4 | loop fusion | flops 1572864 | bytes 4194304 | tf_op jit(solution)/shard_map/jit(silu)/div | solution.py:368
  75.8 6.3 %collective-permute-done.15 = bf16[3,320,128]{2,1,0:T(8,128)(2,1)S(1)} collective-permute-done((bf16[3,320,128]{2,1,0:T(8,128)(2,1)S(1)}, bf16[3,320,128]{2,1,0:T(8,128)(2,1)S(1)}, u32[]{:S(2)}, u32[]{:S(2)}) %collective-permute-start.15) | collective-permute-done | bytes 245792 | tf_op jit(solution)/shard_map/ppermute | solution.py:255
  82.4 2.8 %fusion = bf16[512,1024]{0,1:T(8,128)(2,1)S(1)} fusion(bf16[240,1024]{1,0:T(8,128)(2,1)S(1)} %bitcast.112, bf16[512,240]{0,1:T(8,128)(2,1)} %param.15, f32[1024,512]{1,0:T(8,128)} %get-tuple-element.43), kind=kOutput, calls=%fused_computation.2 | convolution fusion | flops 256376832 | bytes 3883008 | tf_op jit(solution)/shard_map/dot_general | solution.py:290
  85.2 2.1 %multiply_convert_fusion = (bf16[1024,512]{1,0:T(8,128)(2,1)}, f32[1024,512]{1,0:T(8,128)S(1)}) fusion(f32[1024,512]{1,0:T(8,128)S(1)} %copy-done.16, f32[512]{0:T(512)S(1)} %copy-done.33, bf16[512,1024]{0,1:T(8,128)(2,1)S(1)} %fusion, bf16[512,512]{1,0:T(8,128)(2,1)S(1)} %copy-done), kind=kOutput, calls=%fused_computation.3 | convolution fusion | flops 542113792 | bytes 6817792 | tf_op jit(solution)/shard_map/dot_general | solution.py:290
  87.3 1.3 fusion.7
  89.7 1.0 fusion.27
  91.4 1.1 fusion.5
  92.5 3.2 %concatenate.47 = f32[1024,256]{1,0:T(8,128)S(1)} concatenate(f32[240,256]{1,0:T(8,128)} %fusion.27, f32[512,256]{1,0:T(8,128)} %fusion.7, f32[240,256]{1,0:T(8,128)} %fusion.5, f32[1,256]{1,0:T(1,128)S(1)} %bitcast.125, f32[31,256]{1,0:T(8,128)S(1)} %broadcast_in_dim.25), dimensions={0} | concatenate | bytes 2097152 | tf_op jit(solution)/shard_map/concatenate | solution.py:394
  96.5 1.2 collective-permute-start.18
  97.7 1.9 %collective-permute-done.18 = f32[1024,128]{1,0:T(8,128)} collective-permute-done((f32[1024,128]{1,0:T(8,128)}, f32[1024,128]{1,0:T(8,128)}, u32[]{:S(2)}, u32[]{:S(2)}) %collective-permute-start.18) | collective-permute-done | bytes 524320 | tf_op jit(solution)/shard_map/ppermute | solution.py:255
  99.6 1.1 add_convert_fusion
  100.7 13.3 %all_to_all.10 = bf16[32,32,128]{2,1,0:T(8,128)(2,1)S(1)} all-to-all(bf16[32,32,128]{2,1,0:T(8,128)(2,1)S(1)} %bitcast.120), channel_id=1, replica_groups=mesh['sec'=2,'tile'=32,'lev'=2] {'tile'}, dimensions={0} | all-to-all | bytes 524288 | tf_op jit(solution)/shard_map/all_to_all | solution.py:409
  114.1 1.1 broadcast_in_dim.26
  115.2 6.2 %all-to-all-start.1 = ((f32[64,32,128]{2,1,0:T(8,128)}), f32[64,32,128]{2,1,0:T(8,128)}, u32[]{:S(2)}, u32[]{:S(2)}) async-start(f32[64,32,128]{2,1,0:T(8,128)} %broadcast_in_dim.26), calls=%async_computation.1 | async-start | bytes 2097152 | tf_op jit(solution)/shard_map/all_to_all | solution.py:413
  122.3 5.8 %collective-permute-start.11 = (bf16[3,64,128]{2,1,0:T(8,128)(2,1)S(1)}, bf16[3,64,128]{2,1,0:T(8,128)(2,1)S(1)}, u32[]{:S(2)}, u32[]{:S(2)}) collective-permute-start(bf16[3,64,128]{2,1,0:T(8,128)(2,1)S(1)} %dynamic-slice_bitcast_fusion.3), channel_id=1, source_target_pairs={{0,3},{1,2},{2,1},{3,0},{4,7},{5,6},{6,5},{7,4},{8,11},{9,10},{10,... | collective-permute-start | bytes 147464 | tf_op jit(solution)/shard_map/ppermute | solution.py:268
  128.9 2.5 %collective-permute-start.9 = (bf16[3,320,128]{2,1,0:T(8,128)(2,1)S(1)}, bf16[3,320,128]{2,1,0:T(8,128)(2,1)S(1)}, u32[]{:S(2)}, u32[]{:S(2)}) collective-permute-start(bf16[3,320,128]{2,1,0:T(8,128)(2,1)S(1)} %bitcast.116), channel_id=1, source_target_pairs={{0,2},{2,0},{4,6},{6,4},{8,10},{10,8},{12,14},{14,12},{16,18},{18,... | collective-permute-start | bytes 737288 | tf_op jit(solution)/shard_map/ppermute | solution.py:266
  131.4 3.3 %collective-permute-start.8 = (f32[3,40,8,128]{3,2,1,0:T(8,128)S(1)}, f32[3,40,8,128]{3,2,1,0:T(8,128)S(1)}, u32[]{:S(2)}, u32[]{:S(2)}) collective-permute-start(f32[3,40,8,128]{3,2,1,0:T(8,128)S(1)} %get-tuple-element.20.resid_ref), channel_id=1, source_target_pairs={{0,64},{64,0},{1,65},{65,1},{2,66},{66,2},{3,67},{67,3},{4,68},{68... | collective-permute-start | bytes 1474568 | tf_op jit(solution)/shard_map/ppermute | solution.py:255
  134.6 2.8 %collective-permute-done.11 = bf16[3,64,128]{2,1,0:T(8,128)(2,1)S(1)} collective-permute-done((bf16[3,64,128]{2,1,0:T(8,128)(2,1)S(1)}, bf16[3,64,128]{2,1,0:T(8,128)(2,1)S(1)}, u32[]{:S(2)}, u32[]{:S(2)}) %collective-permute-start.11) | collective-permute-done | bytes 49184 | tf_op jit(solution)/shard_map/ppermute | solution.py:268
  137.5 2.3 %collective-permute-start.14 = (bf16[3,64,128]{2,1,0:T(8,128)(2,1)S(1)}, bf16[3,64,128]{2,1,0:T(8,128)(2,1)S(1)}, u32[]{:S(2)}, u32[]{:S(2)}) collective-permute-start(bf16[3,64,128]{2,1,0:T(8,128)(2,1)S(1)} %get-tuple-element.13), channel_id=1, source_target_pairs={{0,64},{64,0},{1,65},{65,1},{2,66},{66,2},{3,67},{67,3},{4,68},{68... | collective-permute-start | bytes 147464 | tf_op jit(solution)/shard_map/ppermute | solution.py:255
  139.8 3.6 %collective-permute-done.9 = bf16[3,320,128]{2,1,0:T(8,128)(2,1)S(1)} collective-permute-done((bf16[3,320,128]{2,1,0:T(8,128)(2,1)S(1)}, bf16[3,320,128]{2,1,0:T(8,128)(2,1)S(1)}, u32[]{:S(2)}, u32[]{:S(2)}) %collective-permute-start.9) | collective-permute-done | bytes 245792 | tf_op jit(solution)/shard_map/ppermute | solution.py:266
  146.1 15.2 %shard_map.120 = f32[3,40,8,128]{3,2,1,0:T(8,128)S(1)} custom-call(s32[2]{0:T(128)S(1)} %pad_add_fusion.place_ref, f32[8]{0:T(128)S(1)} %broadcast_select_fusion.20.turn_ref, f32[3,40,8,128]{3,2,1,0:T(8,128)S(1)} %get-tuple-element.20.resid_ref, f32[3,40,8,128]{3,2,1,0:T(8,128)S(1)} %collective-permute-done.8.other_ref, ...), custom_call_target="tpu_custom_call" | custom-call | flops 40000000 | bytes 10000000 | tf_op jit(solution)/shard_map/pallas_call | solution.py:421
  162.3 2.4 %collective-permute-done.17 = f32[3,40,8,128]{3,2,1,0:T(8,128)S(1)} collective-permute-done((f32[3,40,8,128]{3,2,1,0:T(8,128)S(1)}, f32[3,40,8,128]{3,2,1,0:T(8,128)S(1)}, u32[]{:S(2)}, u32[]{:S(2)}) %collective-permute-start.17) | collective-permute-done | bytes 491552 | tf_op jit(solution)/shard_map/ppermute | solution.py:255
  164.8 1.0 pad_maximum_fusion
  165.8 1.5 broadcast_select_fusion.1
  167.5 1.7 copy.19
  169.2 2.7 %reshape.185 = f32[1024,512]{1,0:T(8,128)} reshape(f32[32,32,2,2,128]{4,3,2,1,0:T(2,128)S(1)} %copy.19) | data formatting | bytes 4194304 | tf_op jit(solution)/shard_map/reshape | solution.py:418
  171.9 2.2 %slice_bitcast_fusion = (f32[512,240]{0,1:T(8,128)}, f32[240,512]{1,0:T(8,128)}) fusion(f32[1024,512]{1,0:T(8,128)} %reshape.185), kind=kLoop, calls=%fused_computation.26 | loop fusion | bytes 1966080 | tf_op jit(solution)/shard_map/transpose | solution.py:435
  174.1 1.3 slice.85
  175.4 2.3 %slice.86 = f32[512,512]{1,0:T(8,128)} slice(f32[1024,512]{1,0:T(8,128)} %reshape.185), slice={[240:752], [0:512]} | slice | bytes 2097152 | tf_op jit(solution)/shard_map/slice | solution.py:434
  (134 shorter events, 21.8 us)
Async XLA Ops:
  0.6 40.1 %copy-start = (bf16[512,512]{1,0:T(8,128)(2,1)S(1)}, bf16[512,512]{1,0:T(8,128)(2,1)}, u32[]{:S(2)}) copy-start(bf16[512,512]{1,0:T(8,128)(2,1)} %param.14) | copy-start | bytes 1572868
  9.6 34.7 %collective-permute-start.1 = (bf16[1296,128]{1,0:T(8,128)(2,1)S(1)}, bf16[1296,128]{1,0:T(8,128)(2,1)S(1)}, u32[]{:S(2)}, u32[]{:S(2)}) collective-permute-start(bf16[1296,128]{1,0:T(8,128)(2,1)S(1)} %pad_maximum_fusion.3), channel_id=1, source_target_pairs={{2,4},{4,2},{6,8},{8,6},{10,12},{12,10},{14,16},{16,14},{18,20},{2... | collective-permute-start | bytes 995336 | tf_op jit(solution)/shard_map/ppermute | solution.py:267
  10.3 34.0 %collective-permute-start = (bf16[1296,128]{1,0:T(8,128)(2,1)S(1)}, bf16[1296,128]{1,0:T(8,128)(2,1)}, u32[]{:S(2)}, u32[]{:S(2)}) collective-permute-start(bf16[1296,128]{1,0:T(8,128)(2,1)S(1)} %pad_maximum_fusion.3), channel_id=1, source_target_pairs={{0,2},{2,0},{4,6},{6,4},{8,10},{10,8},{12,14},{14,12},{16,18},{18,... | collective-permute-start | bytes 995336 | tf_op jit(solution)/shard_map/ppermute | solution.py:266
  15.7 9.0 %collective-permute-start.3 = (bf16[4,64,128]{2,1,0:T(8,128)(2,1)S(1)}, bf16[4,64,128]{2,1,0:T(8,128)(2,1)S(1)}, u32[]{:S(2)}, u32[]{:S(2)}) collective-permute-start(bf16[4,64,128]{2,1,0:T(8,128)(2,1)S(1)} %dynamic-slice_bitcast_fusion.1), channel_id=1, source_target_pairs={{2,5},{3,4},{4,3},{5,2},{6,9},{7,8},{8,7},{9,6},{10,13},{11,12},{1... | collective-permute-start | bytes 196616 | tf_op jit(solution)/shard_map/ppermute | solution.py:269
  16.4 10.4 %collective-permute-start.2 = (bf16[4,64,128]{2,1,0:T(8,128)(2,1)S(1)}, bf16[4,64,128]{2,1,0:T(8,128)(2,1)S(1)}, u32[]{:S(2)}, u32[]{:S(2)}) collective-permute-start(bf16[4,64,128]{2,1,0:T(8,128)(2,1)S(1)} %dynamic-slice_bitcast_fusion.1), channel_id=1, source_target_pairs={{0,3},{1,2},{2,1},{3,0},{4,7},{5,6},{6,5},{7,4},{8,11},{9,10},{10,... | collective-permute-start | bytes 196616 | tf_op jit(solution)/shard_map/ppermute | solution.py:268
  21.6 16.0 %copy-start.28 = (bf16[240,512]{1,0:T(8,128)(2,1)S(1)}, bf16[240,512]{1,0:T(8,128)(2,1)}, u32[]{:S(2)}) copy-start(bf16[240,512]{1,0:T(8,128)(2,1)} %param.12) | copy-start | bytes 737284
  21.6 14.4 %collective-permute-start.6 = (bf16[1024,128]{1,0:T(8,128)(2,1)S(1)}, bf16[1024,128]{1,0:T(8,128)(2,1)S(1)}, u32[]{:S(2)}, u32[]{:S(2)}) collective-permute-start(bf16[1024,128]{1,0:T(8,128)(2,1)S(1)} %pad_maximum_fusion.4), channel_id=1, source_target_pairs={{0,1},{1,0},{2,3},{3,2},{4,5},{5,4},{6,7},{7,6},{8,9},{9,8},{10,11... | collective-permute-start | bytes 786440 | tf_op jit(solution)/shard_map/ppermute | solution.py:255
  27.5 23.2 %collective-permute-start.5 = (bf16[4,64,128]{2,1,0:T(8,128)(2,1)}, bf16[4,64,128]{2,1,0:T(8,128)(2,1)S(1)}, u32[]{:S(2)}, u32[]{:S(2)}) collective-permute-start(bf16[4,64,128]{2,1,0:T(8,128)(2,1)} %get-tuple-element.21), channel_id=1, source_target_pairs={{0,64},{64,0},{1,65},{65,1},{2,66},{66,2},{3,67},{67,3},{4,68},{68... | collective-permute-start | bytes 196616 | tf_op jit(solution)/shard_map/ppermute | solution.py:255
  36.1 2.0 %copy-start.7 = (bf16[4,64,128]{2,1,0:T(8,128)(2,1)}, bf16[4,64,128]{2,1,0:T(8,128)(2,1)S(1)}, u32[]{:S(2)}) copy-start(bf16[4,64,128]{2,1,0:T(8,128)(2,1)S(1)} %pad_maximum_fusion.5.own_edge_ref) | copy-start | bytes 196612
  36.1 15.3 %collective-permute-start.7 = (bf16[4,64,128]{2,1,0:T(8,128)(2,1)S(1)}, bf16[4,64,128]{2,1,0:T(8,128)(2,1)S(1)}, u32[]{:S(2)}, u32[]{:S(2)}) collective-permute-start(bf16[4,64,128]{2,1,0:T(8,128)(2,1)S(1)} %pad_maximum_fusion.5.own_edge_ref), channel_id=1, source_target_pairs={{0,64},{64,0},{1,65},{65,1},{2,66},{66,2},{3,67},{67,3},{4,68},{68... | collective-permute-start | bytes 196616 | tf_op jit(solution)/shard_map/ppermute | solution.py:255
  36.7 1.3 copy-start.32
  38.1 2.0 %copy-start.15 = (f32[1024,512]{1,0:T(8,128)}, f32[1024,512]{1,0:T(8,128)S(1)}, u32[]{:S(2)}) copy-start(f32[1024,512]{1,0:T(8,128)S(1)} %fusion.26) | copy-start | bytes 6291460
  40.1 2.9 %copy-start.13 = (f32[512,1024]{0,1:T(8,128)}, f32[512,1024]{0,1:T(8,128)S(1)}, u32[]{:S(2)}) copy-start(f32[512,1024]{0,1:T(8,128)S(1)} %get-tuple-element.12) | copy-start | bytes 6291460
  40.7 2.3 %copy-start.25 = (bf16[512,1024]{0,1:T(8,128)(2,1)}, bf16[512,1024]{0,1:T(8,128)(2,1)S(1)}, u32[]{:S(2)}) copy-start(bf16[512,1024]{0,1:T(8,128)(2,1)S(1)} %multiply_convert_fusion.2) | copy-start | bytes 3145732
  40.7 2.3 %copy-start.31 = (bf16[512,240]{0,1:T(8,128)(2,1)S(1)}, bf16[512,240]{0,1:T(8,128)(2,1)}, u32[]{:S(2)}) copy-start(bf16[512,240]{0,1:T(8,128)(2,1)} %param.15) | copy-start | bytes 737284
  44.3 8.5 %copy-start.1 = (f32[3,40,16,128]{3,2,1,0:T(8,128)S(1)}, f32[3,40,16,128]{3,2,1,0:T(8,128)}, u32[]{:S(2)}) copy-start(f32[3,40,16,128]{3,2,1,0:T(8,128)} %state_ref.1) | copy-start | bytes 2949124
  46.2 5.8 %collective-permute-start.4 = (bf16[4,320,128]{2,1,0:T(8,128)(2,1)}, bf16[4,320,128]{2,1,0:T(8,128)(2,1)S(1)}, u32[]{:S(2)}, u32[]{:S(2)}) collective-permute-start(bf16[4,320,128]{2,1,0:T(8,128)(2,1)} %broadcast_select_fusion.4), channel_id=1, source_target_pairs={{0,64},{64,0},{1,65},{65,1},{2,66},{66,2},{3,67},{67,3},{4,68},{68... | collective-permute-start | bytes 983048 | tf_op jit(solution)/shard_map/ppermute | solution.py:255
  52.7 1.0 copy-start.2
  53.7 1.0 copy-start.4
  54.7 0.8 copy-start.5
  55.5 0.8 copy-start.6
  58.9 14.9 %copy-start.17 = (f32[1024,512]{1,0:T(8,128)S(1)}, f32[1024,512]{1,0:T(8,128)}, u32[]{:S(2)}) copy-start(f32[1024,512]{1,0:T(8,128)} %get-tuple-element.43) | copy-start | bytes 6291460
  73.2 2.5 %copy-start.23 = (bf16[3,40,8,128]{3,2,1,0:T(8,128)(2,1)}, bf16[3,40,8,128]{3,2,1,0:T(8,128)(2,1)S(1)}, u32[]{:S(2)}) copy-start(bf16[3,40,8,128]{3,2,1,0:T(8,128)(2,1)S(1)} %get-tuple-element.19) | copy-start | bytes 737284
  73.2 8.9 %collective-permute-start.15 = (bf16[3,320,128]{2,1,0:T(8,128)(2,1)S(1)}, bf16[3,320,128]{2,1,0:T(8,128)(2,1)S(1)}, u32[]{:S(2)}, u32[]{:S(2)}) collective-permute-start(bf16[3,320,128]{2,1,0:T(8,128)(2,1)S(1)} %bitcast.114), channel_id=1, source_target_pairs={{0,1},{1,0},{2,3},{3,2},{4,5},{5,4},{6,7},{7,6},{8,9},{9,8},{10,11... | collective-permute-start | bytes 737288 | tf_op jit(solution)/shard_map/ppermute | solution.py:255
  82.1 3.0 %copy-start.30 = (bf16[3,320,128]{2,1,0:T(8,128)(2,1)}, bf16[3,320,128]{2,1,0:T(8,128)(2,1)S(1)}, u32[]{:S(2)}) copy-start(bf16[3,320,128]{2,1,0:T(8,128)(2,1)S(1)} %collective-permute-done.15) | copy-start | bytes 737284
  82.3 2.8 %copy-start.16 = (f32[1024,512]{1,0:T(8,128)S(1)}, f32[1024,512]{1,0:T(8,128)}, u32[]{:S(2)}) copy-start(f32[1024,512]{1,0:T(8,128)} %copy-done.15) | copy-start | bytes 6291460
  82.4 2.8 %copy-start.33 = (f32[512]{0:T(512)S(1)}, f32[512]{0:T(512)}, u32[]{:S(2)}) copy-start(f32[512]{0:T(512)} %param.13) | copy-start | bytes 6148
  85.2 2.1 %copy-start.26 = (bf16[512,1024]{0,1:T(8,128)(2,1)S(1)}, bf16[512,1024]{0,1:T(8,128)(2,1)}, u32[]{:S(2)}) copy-start(bf16[512,1024]{0,1:T(8,128)(2,1)} %copy-done.25) | copy-start | bytes 3145732
  85.2 3.4 %copy-start.19 = (f32[512,1024]{0,1:T(8,128)S(1)}, f32[512,1024]{0,1:T(8,128)}, u32[]{:S(2)}) copy-start(f32[512,1024]{0,1:T(8,128)} %get-tuple-element.11) | copy-start | bytes 6291460
  87.3 1.8 %copy-start.14 = (f32[512,1024]{0,1:T(8,128)S(1)}, f32[512,1024]{0,1:T(8,128)}, u32[]{:S(2)}) copy-start(f32[512,1024]{0,1:T(8,128)} %copy-done.13) | copy-start | bytes 6291460
  88.6 1.2 copy-start.22
  89.1 1.6 copy-start.18
  89.1 2.3 %copy-start.20 = (f32[512,1024]{0,1:T(8,128)S(1)}, f32[512,1024]{0,1:T(8,128)}, u32[]{:S(2)}) copy-start(f32[512,1024]{0,1:T(8,128)} %add_divide_fusion) | copy-start | bytes 6291460
  96.5 3.1 %collective-permute-start.18 = (f32[1024,128]{1,0:T(8,128)}, f32[1024,128]{1,0:T(8,128)}, u32[]{:S(2)}, u32[]{:S(2)}) collective-permute-start(f32[1024,128]{1,0:T(8,128)} %constant_dynamic-slice_fusion), channel_id=1, source_target_pairs={{0,64},{64,0},{1,65},{65,1},{2,66},{66,2},{3,67},{67,3},{4,68},{68... | collective-permute-start | bytes 1572872 | tf_op jit(solution)/shard_map/ppermute | solution.py:255
  100.7 20.8 %copy-start.24 = (bf16[3,40,8,128]{3,2,1,0:T(8,128)(2,1)S(1)}, bf16[3,40,8,128]{3,2,1,0:T(8,128)(2,1)}, u32[]{:S(2)}) copy-start(bf16[3,40,8,128]{3,2,1,0:T(8,128)(2,1)} %copy-done.23) | copy-start | bytes 737284
  115.2 29.6 %copy-start.29 = (bf16[240,512]{1,0:T(8,128)(2,1)S(1)}, bf16[240,512]{1,0:T(8,128)(2,1)}, u32[]{:S(2)}) copy-start(bf16[240,512]{1,0:T(8,128)(2,1)} %param.12) | copy-start | bytes 737284
  115.2 46.0 %all-to-all-start.1 = ((f32[64,32,128]{2,1,0:T(8,128)}), f32[64,32,128]{2,1,0:T(8,128)}, u32[]{:S(2)}, u32[]{:S(2)}) async-start(f32[64,32,128]{2,1,0:T(8,128)} %broadcast_in_dim.26), calls=%async_computation.1 | async-start | bytes 2097152 | tf_op jit(solution)/shard_map/all_to_all | solution.py:413
  121.5 23.4 %copy-start.27 = (bf16[1024,512]{1,0:T(8,128)(2,1)S(1)}, bf16[1024,512]{1,0:T(8,128)(2,1)}, u32[]{:S(2)}) copy-start(bf16[1024,512]{1,0:T(8,128)(2,1)} %get-tuple-element.44) | copy-start | bytes 3145732
  121.5 13.1 %collective-permute-start.12 = (bf16[3,64,128]{2,1,0:T(8,128)(2,1)S(1)}, bf16[3,64,128]{2,1,0:T(8,128)(2,1)S(1)}, u32[]{:S(2)}, u32[]{:S(2)}) collective-permute-start(bf16[3,64,128]{2,1,0:T(8,128)(2,1)S(1)} %dynamic-slice_bitcast_fusion.3), channel_id=1, source_target_pairs={{2,5},{3,4},{4,3},{5,2},{6,9},{7,8},{8,7},{9,6},{10,13},{11,12},{1... | collective-permute-start | bytes 147464 | tf_op jit(solution)/shard_map/ppermute | solution.py:269
  122.3 15.1 %collective-permute-start.11 = (bf16[3,64,128]{2,1,0:T(8,128)(2,1)S(1)}, bf16[3,64,128]{2,1,0:T(8,128)(2,1)S(1)}, u32[]{:S(2)}, u32[]{:S(2)}) collective-permute-start(bf16[3,64,128]{2,1,0:T(8,128)(2,1)S(1)} %dynamic-slice_bitcast_fusion.3), channel_id=1, source_target_pairs={{0,3},{1,2},{2,1},{3,0},{4,7},{5,6},{6,5},{7,4},{8,11},{9,10},{10,... | collective-permute-start | bytes 147464 | tf_op jit(solution)/shard_map/ppermute | solution.py:268
  128.2 11.6 %collective-permute-start.10 = (bf16[3,320,128]{2,1,0:T(8,128)(2,1)S(1)}, bf16[3,320,128]{2,1,0:T(8,128)(2,1)S(1)}, u32[]{:S(2)}, u32[]{:S(2)}) collective-permute-start(bf16[3,320,128]{2,1,0:T(8,128)(2,1)S(1)} %bitcast.115), channel_id=1, source_target_pairs={{2,4},{4,2},{6,8},{8,6},{10,12},{12,10},{14,16},{16,14},{18,20},{2... | collective-permute-start | bytes 737288 | tf_op jit(solution)/shard_map/ppermute | solution.py:267
  128.9 14.5 %collective-permute-start.9 = (bf16[3,320,128]{2,1,0:T(8,128)(2,1)S(1)}, bf16[3,320,128]{2,1,0:T(8,128)(2,1)S(1)}, u32[]{:S(2)}, u32[]{:S(2)}) collective-permute-start(bf16[3,320,128]{2,1,0:T(8,128)(2,1)S(1)} %bitcast.116), channel_id=1, source_target_pairs={{0,2},{2,0},{4,6},{6,4},{8,10},{10,8},{12,14},{14,12},{16,18},{18,... | collective-permute-start | bytes 737288 | tf_op jit(solution)/shard_map/ppermute | solution.py:266
  131.4 14.7 %collective-permute-start.8 = (f32[3,40,8,128]{3,2,1,0:T(8,128)S(1)}, f32[3,40,8,128]{3,2,1,0:T(8,128)S(1)}, u32[]{:S(2)}, u32[]{:S(2)}) collective-permute-start(f32[3,40,8,128]{3,2,1,0:T(8,128)S(1)} %get-tuple-element.20.resid_ref), channel_id=1, source_target_pairs={{0,64},{64,0},{1,65},{65,1},{2,66},{66,2},{3,67},{67,3},{4,68},{68... | collective-permute-start | bytes 1474568 | tf_op jit(solution)/shard_map/ppermute | solution.py:255
  137.5 7.9 %collective-permute-start.14 = (bf16[3,64,128]{2,1,0:T(8,128)(2,1)S(1)}, bf16[3,64,128]{2,1,0:T(8,128)(2,1)S(1)}, u32[]{:S(2)}, u32[]{:S(2)}) collective-permute-start(bf16[3,64,128]{2,1,0:T(8,128)(2,1)S(1)} %get-tuple-element.13), channel_id=1, source_target_pairs={{0,64},{64,0},{1,65},{65,1},{2,66},{66,2},{3,67},{67,3},{4,68},{68... | collective-permute-start | bytes 147464 | tf_op jit(solution)/shard_map/ppermute | solution.py:255
  143.5 2.6 %collective-permute-start.13 = (bf16[3,320,128]{2,1,0:T(8,128)(2,1)S(1)}, bf16[3,320,128]{2,1,0:T(8,128)(2,1)S(1)}, u32[]{:S(2)}, u32[]{:S(2)}) collective-permute-start(bf16[3,320,128]{2,1,0:T(8,128)(2,1)S(1)} %get-tuple-element.16), channel_id=1, source_target_pairs={{0,64},{64,0},{1,65},{65,1},{2,66},{66,2},{3,67},{67,3},{4,68},{68... | collective-permute-start | bytes 737288 | tf_op jit(solution)/shard_map/ppermute | solution.py:255
  144.8 1.2 collective-permute-start.16
  161.3 4.5 %collective-permute-start.19 = (f32[64,32,128]{2,1,0:T(8,128)}, f32[64,32,128]{2,1,0:T(8,128)S(1)}, u32[]{:S(2)}, u32[]{:S(2)}) collective-permute-start(f32[64,32,128]{2,1,0:T(8,128)} %all-to-all-done.1), channel_id=1, source_target_pairs={{0,64},{64,0},{1,65},{65,1},{2,66},{66,2},{3,67},{67,3},{4,68},{68... | collective-permute-start | bytes 3145736 | tf_op jit(solution)/shard_map/ppermute | solution.py:255
  161.5 3.2 %collective-permute-start.17 = (f32[3,40,8,128]{3,2,1,0:T(8,128)S(1)}, f32[3,40,8,128]{3,2,1,0:T(8,128)S(1)}, u32[]{:S(2)}, u32[]{:S(2)}) collective-permute-start(f32[3,40,8,128]{3,2,1,0:T(8,128)S(1)} %copy_add_fusion), channel_id=1, source_target_pairs={{0,64},{64,0},{1,65},{65,1},{2,66},{66,2},{3,67},{67,3},{4,68},{68... | collective-permute-start | bytes 1474568 | tf_op jit(solution)/shard_map/ppermute | solution.py:255
  (7 other events, 5.3 us)

commit v2 on v0

v2 whole, which is shorter than its diff:
```python
import jax
import jax.numpy as jnp
from jax import lax
from jax.experimental import pallas as pl
from jax.experimental.pallas import tpu as pltpu
from jax.sharding import PartitionSpec as P

SUBSTEPS = 4
COURANT = 0.3
DIFFUSION = 0.08
UNIT = 1.0 / 12.0

BLK = 8
OWN = 40
EDGE = 8
EXT = OWN + EDGE
ROWS = 7 * BLK
CHUNK = 24
WIND_BLOCKS = ((0, 5), (0, 5), (1, 4), (1, 4))
MASS_BLOCKS = ((0, 5), (1, 4), (1, 4), (2, 3))
FIELD = OWN * BLK
RIM = EDGE * BLK
COLS = BLK * 128
GROUP = 128
PAD = GROUP - 3 * OWN
STRIPE = 256
MIB = 1024 * 1024
F32 = jnp.float32
BF = jnp.bfloat16


def roll(values, steps, axis):
    return pltpu.roll(values, steps % values.shape[axis], axis)


def across_matrix():
    source = lax.broadcasted_iota(jnp.int32, (256, 128), 0)
    target = lax.broadcasted_iota(jnp.int32, (256, 128), 1)
    apart = (source - target) & 127
    near = jnp.where(apart == 1, 8.0, 0.0) - jnp.where(apart == 127, 8.0, 0.0)
    far = jnp.where(apart == 126, 1.0, 0.0) - jnp.where(apart == 2, 1.0, 0.0)
    return (near + far).astype(BF)


def across(values, matrix):
    flat = values.reshape(-1, 128)
    high = flat.astype(BF)
    low = (flat - high.astype(F32)).astype(BF)
    return dot(jnp.concatenate([high, low], axis=1), matrix[...]).reshape(values.shape)


def along(ref, levels, row):
    def take(steps):
        return ref[levels, row + steps : row + steps + BLK, :]

    return 8.0 * (take(1) - take(-1)) - (take(2) - take(-2))


def vertical(ref, k, row):
    v = ref[pl.ds(k, CHUNK + 4), row : row + BLK, :]
    near = v[3 : 3 + CHUNK] + v[1 : 1 + CHUNK]
    far = v[4 : 4 + CHUNK] + v[0:CHUNK]
    return (1.0 - 30.0 * UNIT * DIFFUSION) * v[2 : 2 + CHUNK] + (UNIT * DIFFUSION) * (16.0 * near - far)


def edge_masks():
    i = lax.broadcasted_iota(jnp.int32, (1, BLK, 128), 1)

    def at(row, value):
        return jnp.where(i == row, value, 0.0)

    return at(4, -8.0), at(4, 1.0) + at(5, 1.0), at(3, 8.0), at(3, -1.0) + at(2, -1.0)


def crossing(values, masks):
    m1, m2, m3, m4 = masks
    return (
        m1 * roll(values, 1, 1)
        + m2 * roll(values, 2, 1)
        + m3 * roll(values, -1, 1)
        + m4 * roll(values, -2, 1)
    )


def quarter_turn(quarter):
    cosine = jnp.where(quarter == 0, 1.0, 0.0) - jnp.where(quarter == 2, 1.0, 0.0)
    sine = jnp.where(quarter == 1, 1.0, 0.0) - jnp.where(quarter == 3, 1.0, 0.0)
    return cosine, sine


def clear(ref):
    levels = ref.shape[0]
    zeros = jnp.zeros((levels, BLK, 128), F32)
    ref[:, 0:BLK, :] = zeros
    ref[:, ROWS - BLK : ROWS, :] = zeros


def clear_levels(ref):
    for level in (0, 1, EXT + 2, EXT + 3):
        ref[level] = jnp.zeros((ROWS, 128), F32)


def spread(src, start, count, dst, level, row, scale=None):
    def body(i, _):
        rows = src[pl.ds(pl.multiple_of(start + i * 16, 16), 16), :].astype(F32)
        if scale is not None:
            rows = rows * scale
        dst[pl.ds(level + 2 * i, 2), row : row + BLK, :] = rows.reshape(2, BLK, 128)
        return 0

    lax.fori_loop(0, count // 2, body, 0, unroll=4)


def static_rows(sec):
    return 16 + 16 * sec, 32 - 16 * sec, 24 + 8 * sec, 40 - 24 * sec


def spread_rims(sec, lev, odd, a, b, a_edge, b_edge, partner, partner_edge, own_col, other_col, fields):
    partner_row, other_row, _, _ = static_rows(sec)
    own_level, edge_level = EDGE * lev, OWN * (1 - lev)

    def sides(low, high, low_edge, high_edge):
        for n, (dst, shift, scale) in enumerate(fields):
            for src, edge, row in ((low, low_edge, BLK), (high, high_edge, 5 * BLK)):
                spread(src, n * FIELD, OWN, dst, own_level + shift, row, scale)
                spread(edge, n * RIM, EDGE, dst, edge_level + shift, row, scale)

    pl.when(odd)(lambda: sides(a, b, a_edge, b_edge))
    pl.when(jnp.logical_not(odd))(lambda: sides(b, a, b_edge, a_edge))
    for n, (dst, shift, scale) in enumerate(fields):
        spread(partner, n * FIELD, OWN, dst, own_level + shift, partner_row, scale)
        spread(partner_edge, n * RIM, EDGE, dst, edge_level + shift, partner_row, scale)
        start = BLK * GROUP + n * RIM
        spread(other_col, start, EDGE, dst, edge_level + shift, other_row, scale)
        spread(own_col, start, EDGE, dst, edge_level + shift, 3 * BLK, scale)


def chunk_range(step, lev):
    trim = 2 * step // CHUNK
    return trim * lev, EXT // CHUNK - trim * (1 - lev)


def column_rows(ref, row, start, stride, step, fill):
    fields = [ref[pl.ds(n * step + start + row, OWN, stride=stride), :] for n in range(3)]
    return jnp.concatenate([*fields, jnp.full((PAD, 128), fill, F32)], axis=0).astype(BF)


def pack_kernel(turn_ref, state_ref, sound_ref, rows_ref, edge_ref, column_ref):
    sec, lev = lax.axis_index("sec"), lax.axis_index("lev")

    def run(row):
        for n in range(4):
            src = state_ref[n * OWN * 16 : (n + 1) * OWN * 16, :] if n < 3 else sound_ref[...]
            field = src.reshape(OWN, 16, 128)[:, row : row + BLK, :].reshape(FIELD, 128)
            rows_ref[n * FIELD : (n + 1) * FIELD, :] = field.astype(BF)
        for r in range(BLK):
            column_ref[r * GROUP : (r + 1) * GROUP, :] = column_rows(state_ref, r, row, 16, OWN * 16, 1.0)

    for half in range(2):
        pl.when(sec == half)(lambda half=half: run(BLK * half))
    for n in range(4):
        start = pl.multiple_of(n * FIELD + (FIELD - RIM) * (1 - lev), 16)
        rim = rows_ref[pl.ds(start, RIM), :]
        edge_ref[n * RIM : (n + 1) * RIM, :] = rim
        column_ref[BLK * GROUP + n * RIM : BLK * GROUP + (n + 1) * RIM, :] = rim
    i = lax.broadcasted_iota(jnp.int32, (16, 128), 0)
    factors = jnp.zeros((16, 128), F32)
    for n, value in enumerate((*quarter_turn(turn_ref[0, 0]), *quarter_turn(turn_ref[0, 1]))):
        factors = jnp.where(i == n, value, factors)
    rows_ref[4 * FIELD :, :] = factors.astype(BF)


def forward_kernel(
    turn_ref, state_ref, sound_ref, target_ref, tendency_ref,
    a, b, a_edge, b_edge, partner, partner_edge, own_col, other_col,
    resid_ref, rows_ref, edge_ref, column_ref, c_ref, factor_ref, pa, pb, u, v, matrix,
):
    section, lev = lax.axis_index("sec"), lax.axis_index("lev")
    odd = lax.rem(lax.axis_index("tile"), 2) == 1
    own_level = EDGE * lev
    for ref in (pa, pb, u, v, c_ref):
        clear(ref)
    clear_levels(pa)
    clear_levels(pb)
    cos_low, sin_low = quarter_turn(turn_ref[0, 0])
    cos_high, sin_high = quarter_turn(turn_ref[0, 1])
    below = lax.broadcasted_iota(jnp.int32, (BLK, 128), 0) < 4

    def factors(low, high):
        low = low[4 * FIELD :, :].astype(F32)
        high = high[4 * FIELD :, :].astype(F32)
        factor_ref[0] = jnp.where(below, cos_low, low[2:3, :]) - 1.0
        factor_ref[1] = jnp.where(below, sin_low, low[3:4, :])
        factor_ref[2] = jnp.where(below, high[0:1, :], cos_high) - 1.0
        factor_ref[3] = jnp.where(below, high[1:2, :], sin_high)

    pl.when(odd)(lambda: factors(a, b))
    pl.when(jnp.logical_not(odd))(lambda: factors(b, a))
    masks = edge_masks()
    matrix[...] = across_matrix()

    def run(sec):
        unit = COURANT * UNIT
        spread_rims(
            sec, lev, odd, a, b, a_edge, b_edge, partner, partner_edge, own_col, other_col,
            ((pa, 2, None), (u, 0, None), (v, 0, None), (c_ref, 0, unit)),
        )
        _, _, near_edge, far_edge = static_rows(sec)
        tile_row = 24 - 8 * sec
        for n, (dst, shift) in enumerate(((pa, 2), (u, 0), (v, 0))):
            field = state_ref[n * OWN * 16 : (n + 1) * OWN * 16, :].reshape(OWN, 16, 128)
            dst[pl.ds(own_level + shift, OWN), tile_row : tile_row + 16, :] = field
        field = unit * sound_ref[...].reshape(OWN, 16, 128)
        c_ref[pl.ds(own_level, OWN), tile_row : tile_row + 16, :] = field
        near_factor, far_factor = (0, 2) if sec == 0 else (2, 0)
        for step in range(SUBSTEPS):
            old, new = (pa, pb) if step % 2 == 0 else (pb, pa)

            def body(i, _, step=step, old=old, new=new):
                k = i * CHUNK
                levels = pl.ds(k, CHUNK)
                inner = pl.ds(k + 2, CHUNK)
                first, last = WIND_BLOCKS[step]
                wide = slice(BLK + BLK * first, BLK + BLK * last)
                slopes = across(old[inner, wide, :], matrix)
                for block in range(first, last):
                    row = BLK + BLK * block
                    rows = slice(row, row + BLK)
                    c = c_ref[levels, rows, :]
                    u[levels, rows, :] = u[levels, rows, :] - c * along(old, inner, row)
                    at = BLK * (block - first)
                    v[levels, rows, :] = v[levels, rows, :] - c * slopes[:, at : at + BLK, :]
                first, last = MASS_BLOCKS[step]
                narrow = slice(BLK + BLK * first, BLK + BLK * last)
                slopes = across(v[levels, narrow, :], matrix)
                for block in range(first, last):
                    row = BLK + BLK * block
                    rows = slice(row, row + BLK)
                    at = BLK * (block - first)
                    spread_uv = along(u, levels, row) + slopes[:, at : at + BLK, :]
                    new[inner, rows, :] = vertical(old, k, row) - c_ref[levels, rows, :] * spread_uv
                for edge, f in ((near_edge, near_factor), (far_edge, far_factor))[: 2 if step < 2 else 1]:
                    rows = slice(edge - 4, edge + 4)
                    delta = factor_ref[f] * u[levels, rows, :] - factor_ref[f + 1] * v[levels, rows, :]
                    new[inner, rows, :] = new[inner, rows, :] - c_ref[levels, rows, :] * crossing(delta, masks)
                return 0

            lax.fori_loop(*chunk_range(step, lev), body, 0)
        final = pa if SUBSTEPS % 2 == 0 else pb
        mine = slice(BLK * sec, BLK * sec + BLK)
        for n, (src, shift) in enumerate(((final, 2), (u, 0), (v, 0))):
            evolved = src[pl.ds(own_level + shift, OWN), 3 * BLK : 4 * BLK, :]
            goal = target_ref[n * OWN * 16 : (n + 1) * OWN * 16, :].reshape(OWN, 16, 128)[:, mine, :]
            packed = slice(n * FIELD, (n + 1) * FIELD)
            resid = evolved.reshape(FIELD, 128) + tendency_ref[packed, :] - goal.reshape(FIELD, 128)
            resid_ref[packed, :] = resid
            rows_ref[packed, :] = resid.astype(BF)

    for sec in range(2):
        pl.when(section == sec)(lambda sec=sec: run(sec))
    for r in range(BLK):
        column_ref[r * GROUP : (r + 1) * GROUP, :] = column_rows(resid_ref, r, 0, BLK, FIELD, 0.0)
    for n in range(3):
        start = pl.multiple_of(n * FIELD + (FIELD - RIM) * (1 - lev), 16)
        rim = rows_ref[pl.ds(start, RIM), :]
        edge_ref[n * RIM : (n + 1) * RIM, :] = rim
        column_ref[BLK * GROUP + n * RIM : BLK * GROUP + (n + 1) * RIM, :] = rim


def adjoint_kernel(
    resid_ref, other_ref, input_grad_ref, c_ref, factor_ref,
    a, b, a_edge, b_edge, partner, partner_edge, own_col, other_col,
    out_ref, pa, pb, u, v, matrix, w,
):
    section, lev = lax.axis_index("sec"), lax.axis_index("lev")
    odd = lax.rem(lax.axis_index("tile"), 2) == 1
    own_level = EDGE * lev
    for ref in (pa, pb, u, v, w):
        clear(ref)
    clear_levels(pa)
    clear_levels(pb)
    masks = edge_masks()
    matrix[...] = across_matrix()
    whole = pl.ds(0, CHUNK)

    def run(sec):
        spread_rims(
            sec, lev, odd, a, b, a_edge, b_edge, partner, partner_edge, own_col, other_col,
            ((pa, 2, None), (u, 0, None), (v, 0, None)),
        )
        _, other_row, near_edge, far_edge = static_rows(sec)
        for n, (dst, shift) in enumerate(((pa, 2), (u, 0), (v, 0))):
            at = pl.ds(own_level + shift, OWN)
            packed = slice(n * FIELD, (n + 1) * FIELD)
            dst[at, 3 * BLK : 4 * BLK, :] = resid_ref[packed, :].reshape(OWN, BLK, 128)
            dst[at, other_row : other_row + BLK, :] = other_ref[packed, :].reshape(OWN, BLK, 128)
        near_factor, far_factor = (0, 2) if sec == 0 else (2, 0)
        for step in range(SUBSTEPS):
            old, new = (pa, pb) if step % 2 == 0 else (pb, pa)
            first, last = WIND_BLOCKS[step]
            wide = slice(BLK + BLK * max(first - 1, 0), BLK + BLK * min(last + 1, 5))
            first, last = MASS_BLOCKS[step]
            narrow = slice(BLK + BLK * max(first - 1, 0), BLK + BLK * min(last + 1, 5))

            def body(i, _, step=step, old=old, new=new, wide=wide, narrow=narrow):
                k = i * CHUNK
                levels = pl.ds(k, CHUNK)
                inner = pl.ds(k + 2, CHUNK)
                w[:, wide, :] = c_ref[levels, wide, :] * old[inner, wide, :]
                first, last = WIND_BLOCKS[step]
                slopes = across(w[:, BLK + BLK * first : BLK + BLK * last, :], matrix)
                for block in range(first, last):
                    row = BLK + BLK * block
                    rows = slice(row, row + BLK)
                    u[levels, rows, :] = u[levels, rows, :] + along(w, whole, row)
                    at = BLK * (block - first)
                    v[levels, rows, :] = v[levels, rows, :] + slopes[:, at : at + BLK, :]
                for edge, f in ((near_edge, near_factor), (far_edge, far_factor))[: 2 if step < 2 else 1]:
                    rows = slice(edge - 4, edge + 4)
                    cross = crossing(w[:, rows, :], masks)
                    u[levels, rows, :] = u[levels, rows, :] + factor_ref[f] * cross
                    v[levels, rows, :] = v[levels, rows, :] - factor_ref[f + 1] * cross
                w[:, narrow, :] = c_ref[levels, narrow, :] * u[levels, narrow, :]
                first, last = MASS_BLOCKS[step]
                rows = slice(BLK + BLK * first, BLK + BLK * last)
                slopes = across(c_ref[levels, rows, :] * v[levels, rows, :], matrix)
                for block in range(first, last):
                    row = BLK + BLK * block
                    at = BLK * (block - first)
                    spread_uv = along(w, whole, row) + slopes[:, at : at + BLK, :]
                    new[inner, row : row + BLK, :] = vertical(old, k, row) + spread_uv
                return 0

            lax.fori_loop(*chunk_range(step, lev), body, 0)

    for sec in range(2):
        pl.when(section == sec)(lambda sec=sec: run(sec))
    final = pa if SUBSTEPS % 2 == 0 else pb
    for n, (src, shift) in enumerate(((final, 2), (u, 0), (v, 0))):
        packed = slice(n * FIELD, (n + 1) * FIELD)
        adjoint = src[pl.ds(own_level + shift, OWN), 3 * BLK : 4 * BLK, :].reshape(FIELD, 128)
        out_ref[packed, :] = adjoint + input_grad_ref[packed, :]


def dot(left, right):
    return lax.dot_general(left, right, (((1,), (0,)), ((), ())), preferred_element_type=F32)


def dot_columns(left, right):
    return lax.dot_general(left, right, (((1,), (1,)), ((), ())), preferred_element_type=F32)


def silu_and_slope(values):
    sigma = 0.5 * jnp.tanh(0.5 * values) + 0.5
    silu = values * sigma
    return silu.astype(BF), sigma + silu * (1.0 - sigma)


def both_groups(out_ref, own_ref, other_ref):
    for r in range(BLK):
        cols = slice(r * 128, (r + 1) * 128)
        out_ref[:GROUP, cols] = own_ref[r * GROUP : (r + 1) * GROUP, :]
        out_ref[GROUP:, cols] = other_ref[r * GROUP : (r + 1) * GROUP, :]


def to_fields(out_ref, start, values):
    for r in range(values.shape[1] // 128):
        for n in range(3):
            rows = pl.ds(n * FIELD + start // 128 + r, OWN, stride=BLK)
            out_ref[rows, :] = values[n * OWN : (n + 1) * OWN, r * 128 : (r + 1) * 128]


def network_kernel(
    own_ref, other_ref, first_t_ref, bias_ref, second_t_ref, third_t_ref,
    feat_ref, one_ref, two_ref, slope_one_ref, slope_two_ref, tendency_ref,
):
    both_groups(feat_ref, own_ref, other_ref)
    for start in range(0, COLS, STRIPE):
        cols = slice(start, start + STRIPE)
        one, slope = silu_and_slope(dot(first_t_ref[...], feat_ref[:, cols]) + bias_ref[...])
        one_ref[:, cols] = one
        slope_one_ref[:, cols] = slope
        two, slope = silu_and_slope(dot(second_t_ref[...], one))
        two_ref[:, cols] = two
        slope_two_ref[:, cols] = slope
        to_fields(tendency_ref, start, dot(third_t_ref[:GROUP, :], two))


def unit_gradients(out_ref, start, feat_ref, resid_ref, one_ref, two_ref, err_one_ref, err_two_ref):
    units = pl.ds(pl.multiple_of(start, 128), 128)
    feats, hid = feat_ref.shape[0], one_ref.shape[0]
    out_ref[:feats, :] = dot_columns(feat_ref[...], err_one_ref[units, :])
    out_ref[feats : feats + hid, :] = dot_columns(one_ref[...], err_two_ref[units, :])
    out_ref[feats + hid :, :] = dot_columns(resid_ref[...], two_ref[units, :])


def back_kernel(
    own_ref, other_ref, feat_ref, third_ref, second_ref, one_ref, two_ref, slope_one_ref, slope_two_ref,
    resid_ref, err_one_ref, err_two_ref, given_ref,
):
    both_groups(resid_ref, own_ref, other_ref)
    for start in range(0, COLS, STRIPE):
        cols = slice(start, start + STRIPE)
        err_two = (dot(third_ref[...], resid_ref[:, cols]) * slope_two_ref[:, cols]).astype(BF)
        err_two_ref[:, cols] = err_two
        err_one_ref[:, cols] = (dot(second_ref[...], err_two) * slope_one_ref[:, cols]).astype(BF)
    start = 256 * lax.axis_index("lev") + 128 * (1 - lax.axis_index("sec"))
    unit_gradients(given_ref, start, feat_ref, resid_ref, one_ref, two_ref, err_one_ref, err_two_ref)


def kept_kernel(
    resid_ref, feat_ref, first_ref, one_ref, two_ref, err_one_ref, err_two_ref, kept_ref, input_grad_ref
):
    start = 256 * lax.axis_index("lev") + 128 * lax.axis_index("sec")
    unit_gradients(kept_ref, start, feat_ref, resid_ref, one_ref, two_ref, err_one_ref, err_two_ref)
    for start in range(0, COLS, STRIPE):
        to_fields(input_grad_ref, start, dot(first_ref[:GROUP, :], err_one_ref[:, start : start + STRIPE]))


def spread_gradients_kernel(own_ref, partner_ref, first_ref, bias_ref, second_ref, third_t_ref):
    section = lax.axis_index("sec")
    hid = second_ref.shape[0]
    share = own_ref.shape[1]

    def feature_rows(out, row, lanes, lev, values):
        group, at = divmod(row, GROUP)
        if at < 3 * OWN:
            field, level = divmod(at, OWN)
            to = (2 * field + (lev + group) % 2) * OWN + level
            out[to : to + 8, lanes] = values

    def run(sec):
        for tile in range(own_ref.shape[0] // 2):
            for part in range(0, share, 8):
                row = tile * share + part
                for lev in range(2):
                    for core, src in ((sec, own_ref), (1 - sec, partner_ref)):
                        lanes = slice(256 * lev + 128 * core, 256 * lev + 128 * core + 128)
                        values = src[2 * tile + lev, part : part + 8, :]
                        if row < 2 * GROUP:
                            feature_rows(first_ref, row, lanes, lev, values)
                            if row == 3 * OWN:
                                bias_ref[:, lanes] = values
                        elif row < 2 * GROUP + hid:
                            second_ref[row - 2 * GROUP : row - 2 * GROUP + 8, lanes] = values
                        else:
                            feature_rows(third_t_ref, row - 2 * GROUP - hid, lanes, lev, values)

    for sec in range(2):
        pl.when(section == sec)(lambda sec=sec: run(sec))


def call(kernel, n_smem, operands, outs, scratch=(), flops=0, moved=0):
    def whole(value):
        return pl.BlockSpec(value.shape, lambda i: (0,) * len(value.shape), pipeline_mode=pl.Buffered(1))

    smem = pl.BlockSpec(memory_space=pltpu.SMEM)
    return pl.pallas_call(
        kernel,
        grid=(1,),
        out_shape=outs,
        in_specs=[smem] * n_smem + [whole(value) for value in operands[n_smem:]],
        out_specs=jax.tree.map(whole, outs),
        scratch_shapes=list(scratch),
        compiler_params=pltpu.CompilerParams(vmem_limit_bytes=60 * MIB),
        cost_estimate=pl.CostEstimate(flops=flops, bytes_accessed=moved, transcendentals=0),
    )(*operands)


def stencil_scratch(extra=()):
    mass = pltpu.VMEM((EXT + 4, ROWS, 128), F32)
    wind = pltpu.VMEM((EXT, ROWS, 128), F32)
    return [mass, mass, wind, wind, pltpu.VMEM((256, 128), BF), *extra]


def shape(*dims, dtype=F32):
    return jax.ShapeDtypeStruct(dims, dtype)


def swap(value, axis):
    return lax.ppermute(value, axis, [(0, 1), (1, 0)])


def strip_swaps(value, edges, tiles):
    first = [(t, t ^ 1) for t in range(tiles)]
    second = [(t, ((t + 1) ^ 1) - 1) for t in range(1, tiles - 1)]

    def cross(pairs):
        return [(2 * a + lev, 2 * b + 1 - lev) for a, b in pairs for lev in range(2)]

    return (
        lax.ppermute(value, "tile", first),
        lax.ppermute(value, "tile", second),
        lax.ppermute(edges, ("tile", "lev"), cross(first)),
        lax.ppermute(edges, ("tile", "lev"), cross(second)),
    )


def local(state, sound, target, edge_turn, w_first, b_first, w_second, w_third):
    sec, lev = lax.axis_index("sec"), lax.axis_index("lev")
    tiles = lax.axis_size("tile")
    hid, feats = w_second.shape[0], 2 * GROUP
    odd = lax.rem(lax.axis_index("tile"), 2) == 1
    second_swap = (sec == 0) == odd

    def by_group(weights):
        weights = weights.reshape(3, 2, OWN, hid).transpose(1, 0, 2, 3).reshape(2, 3 * OWN, hid)
        weights = jnp.pad(weights, ((0, 0), (0, PAD), (0, 0)))
        weights = jnp.where(lev == 0, weights, weights[::-1])
        return weights.reshape(feats, hid)

    state, sound, target = state.reshape(-1, 128), sound.reshape(-1, 128), target.reshape(-1, 128)
    rows, edges, columns = call(
        pack_kernel, 1, (edge_turn, state, sound),
        (shape(4 * FIELD + 16, 128, dtype=BF), shape(4 * RIM, 128, dtype=BF), shape(BLK * GROUP + 4 * RIM, 128, dtype=BF)),
    )
    own_col = swap(columns, "lev")
    a, b, a_edge, b_edge = strip_swaps(rows, edges, tiles)

    first, third_t = by_group(w_first), by_group(w_third.T)
    feat, one, two, slope_one, slope_two, tendency = call(
        network_kernel, 0, (columns, own_col, first.T, b_first[:, None], w_second.T, third_t),
        (shape(feats, COLS, dtype=BF), shape(hid, COLS, dtype=BF), shape(hid, COLS, dtype=BF), shape(hid, COLS), shape(hid, COLS), shape(3 * FIELD, 128)),
    )

    a, b, a_edge, b_edge, tendency = lax.optimization_barrier((a, b, a_edge, b_edge, tendency))
    partner = swap(jnp.where(second_swap, b, a), "sec")
    partner_edge = swap(jnp.where(second_swap, b_edge, a_edge), "sec")
    other_col = swap(own_col, "sec")
    resid, r_rows, r_edges, r_columns, coeff, factors = call(
        forward_kernel, 1,
        (edge_turn, state, sound, target, tendency, a, b, a_edge, b_edge, partner, partner_edge, own_col, other_col),
        (shape(3 * FIELD, 128), shape(3 * FIELD, 128, dtype=BF), shape(3 * RIM, 128, dtype=BF), shape(BLK * GROUP + 3 * RIM, 128, dtype=BF), shape(EXT, ROWS, 128), shape(4, BLK, 128)),
        stencil_scratch(), moved=20_000_000,
    )

    r_own_col = swap(r_columns, "lev")
    r_other = swap(resid, "sec")
    r_a, r_b, r_a_edge, r_b_edge = strip_swaps(r_rows, r_edges, tiles)

    r_own_col, r_a, r_b, r_a_edge, r_b_edge = lax.optimization_barrier((r_own_col, r_a, r_b, r_a_edge, r_b_edge))

    n_rows = 2 * feats + hid
    resid_cols, err_one, err_two, given = call(
        back_kernel, 0, (r_columns, r_own_col, feat, third_t.T, w_second, one, two, slope_one, slope_two),
        (shape(feats, COLS, dtype=BF), shape(hid, COLS, dtype=BF), shape(hid, COLS, dtype=BF), shape(n_rows, 128)),
    )
    received = swap(given, "sec")
    kept, input_grad = call(
        kept_kernel, 0, (resid_cols, feat, first, one, two, err_one, err_two),
        (shape(n_rows, 128), shape(3 * FIELD, 128)),
    )
    share = n_rows // tiles
    partial = (kept + received).astype(BF).reshape(tiles, share, 128)
    parts = lax.all_to_all(partial, "tile", 0, 0)
    total = jnp.sum(parts.astype(F32), axis=0) / (COLS * 2 * tiles)
    everywhere = jnp.broadcast_to(total[None], (2 * tiles, share, 128))
    gathered = lax.all_to_all(everywhere, ("tile", "lev"), 0, 0)

    r_partner = swap(jnp.where(second_swap, r_b, r_a), "sec")
    r_partner_edge = swap(jnp.where(second_swap, r_b_edge, r_a_edge), "sec")
    r_other_col = swap(r_own_col, "sec")
    mine = call(
        adjoint_kernel, 0,
        (resid, r_other, input_grad, coeff, factors, r_a, r_b, r_a_edge, r_b_edge, r_partner, r_partner_edge, r_own_col, r_other_col),
        shape(3 * FIELD, 128), stencil_scratch((pltpu.VMEM((CHUNK, ROWS, 128), F32),)), moved=20_000_000,
    )
    mine, gathered = lax.optimization_barrier((mine, gathered))
    theirs = swap(mine, "sec")
    mine, theirs = mine.reshape(3, OWN, BLK, 128), theirs.reshape(3, OWN, BLK, 128)
    state_grad = jnp.concatenate(
        [jnp.where(sec == 0, mine, theirs), jnp.where(sec == 0, theirs, mine)], axis=2
    )
    g_first, g_bias, g_second, g_third_t = call(
        spread_gradients_kernel, 0, (gathered, swap(gathered, "sec")),
        (shape(6 * OWN, hid), shape(8, hid), shape(hid, hid), shape(6 * OWN, hid)),
    )
    return (state_grad, g_first, g_bias[0], g_second, g_third_t.T)


def solution(mesh):
    placed = (
        P(None, "lev", "tile", None),
        P("lev", "tile", None),
        P(None, "lev", "tile", None),
        P("tile", None),
        P(),
        P(),
        P(),
        P(),
    )
    return jax.shard_map(
        local,
        mesh=mesh,
        in_specs=placed,
        out_specs=(P(None, "lev", "tile", None), P(), P(), P(), P()),
        check_vma=False,
    )
```

time: 658 us -> 134 us (0.20); the launches traced: 647 us -> 133 us
  local copies, waits for them, and re-layouts: 165 us -> 12.3 us
  starting transfers between devices: 184 us -> 42.3 us
  other arithmetic: 107 us -> 4.17 us
  blocking collectives: 90.8 us -> 17.3 us
  waiting for transfers between devices: 67.4 us -> 14.9 us
  Pallas kernels: 0 us -> 41 us
  between operations: 21.8 us -> 0.92 us
  matrix products: 10.9 us -> 0 us
    ppermute x49 -> x20, starting transfers between devices: 164 us -> 36.5 us  [the longest x2 14.2 us: strip_swaps(): lax.ppermute(edges, ('tile', 'lev'), cross(first))]
    psum x1 -> x0, blocking collectives: 90.8 us -> none  [local(): lax.psum((grad_first, grad_bias, grad_second, grad_third), ('sec', 'tile'...]
    slice x96 -> x1, local copies, waits for them, and re-layouts: 89 us -> 1.3 us  [local(): return (state_grad, g_first, g_bias[0], g_second, g_third_t.T)]
    pallas_call x0 -> x7, Pallas kernels: none -> 41 us  [call(): pl.pallas_call(kernel, grid=(1,), out_shape=outs, in_specs=[smem] * n_sme...]
    ppermute x16 -> x0, local copies, waits for them, and re-layouts: 33.5 us -> none  [the longest x8 16.1 us: from_behind(): lax.ppermute(value, axis, [(source, source + steps) for source in range(f...]
    psum x2 -> x0, waiting for transfers between devices: 29.5 us -> none  [the longest x1 23.2 us: local(): state_grad = lax.psum(adjoint + placed, 'sec')]
    mul x8 -> x0, other arithmetic: 26.5 us -> none  [the longest x2 11.7 us: adjoint_step(): spread_x = diff_padded_t(coeff * grad_x, 1)]
    ppermute x49 -> x20, waiting for transfers between devices: 37.2 us -> 11.4 us  [the longest x12 9.74 us: swap(): return lax.ppermute(value, axis, [(0, 1), (1, 0)])]
  transfers between devices with their start and end apart: 55 -> 21, of which waited for: 16 -> 8; matrix products, arithmetic and copies ran while one was open for 36% -> 6% of each run, Pallas kernels for 0% -> 15%
where the time goes in v2:
time: 134 us; the launch traced here: 133 us
  starting transfers between devices  42.3 us (32%)
  Pallas kernels  41 us (31%)
  blocking collectives  17.3 us (13%)
  waiting for transfers between devices  14.9 us (11%)
  local copies, waits for them, and re-layouts  12.3 us (9%)
  other arithmetic  4.17 us (3%)
    pallas_call x7, Pallas kernels, call(): pl.pallas_call(kernel, grid=(1,), out_shape=outs, in_specs=[smem] * n_sme...  41 us
    all_to_all x1, blocking collectives, local(): parts = lax.all_to_all(partial, 'tile', 0, 0)  17.3 us
    ppermute x2, starting transfers between devices, strip_swaps(): lax.ppermute(edges, ('tile', 'lev'), cross(first))  14.2 us
    ppermute x12, starting transfers between devices, swap(): return lax.ppermute(value, axis, [(0, 1), (1, 0)])  14 us
    ppermute x12, waiting for transfers between devices, swap(): return lax.ppermute(value, axis, [(0, 1), (1, 0)])  9.74 us
    all_to_all x1, starting transfers between devices, local(): gathered = lax.all_to_all(everywhere, ('tile', 'lev'), 0, 0)  5.81 us
    ppermute x2, starting transfers between devices, strip_swaps(): lax.ppermute(value, 'tile', first)  5.49 us
    unnamed x51, local copies, waits for them, and re-layouts  5.36 us
  transfers between devices with their start and end apart: 21, of which 8 were waited for; matrix products, arithmetic and copies ran while one was open for 6% of the time, Pallas kernels for 15%

profile of v2, /device:TPU:1, one launch (start us, length us, event | category | flops | bytes accessed | tf_op | source)
XLA Modules:
  0.0 132.9 jit_solution(7991429788320132435)
XLA Ops:
  0.6 2.4 %shard_map.119 = (bf16[1296,128]{1,0:T(8,128)(2,1)}, bf16[256,128]{1,0:T(8,128)(2,1)}, bf16[1280,128]{1,0:T(8,128)(2,1)}) custom-call(s32[1,2]{1,0:T(1,128)} %turn_ref.3, f32[1920,128]{1,0:T(8,128)} %bitcast.25, f32[640,128]{1,0:T(8,128)} %bitcast.34), custom_call_target="tpu_custom_call" | custom-call | tf_op jit(solution)/shard_map/pallas_call | solution.py:458
  3.0 0.8 collective-permute-start.1
  3.8 5.4 %collective-permute-start = (bf16[1296,128]{1,0:T(8,128)(2,1)}, bf16[1296,128]{1,0:T(8,128)(2,1)S(1)}, u32[]{:S(2)}, u32[]{:S(2)}) collective-permute-start(bf16[1296,128]{1,0:T(8,128)(2,1)} %get-tuple-element.42), channel_id=1, source_target_pairs={{0,2},{2,0},{4,6},{6,4},{8,10},{10,8},{12,14},{14,12},{16,18},{18,... | collective-permute-start | bytes 995336 | tf_op jit(solution)/shard_map/ppermute | solution.py:492
  9.2 2.9 %collective-permute-start.4 = (bf16[1280,128]{1,0:T(8,128)(2,1)}, bf16[1280,128]{1,0:T(8,128)(2,1)S(1)}, u32[]{:S(2)}, u32[]{:S(2)}) collective-permute-start(bf16[1280,128]{1,0:T(8,128)(2,1)} %get-tuple-element.44.own_ref), channel_id=1, source_target_pairs={{0,1},{1,0},{2,3},{3,2},{4,5},{5,4},{6,7},{7,6},{8,9},{9,8},{10,11... | collective-permute-start | bytes 983048 | tf_op jit(solution)/shard_map/ppermute | solution.py:481
  12.1 0.7 collective-permute-start.3
  12.8 5.1 %collective-permute-start.2 = (bf16[256,128]{1,0:T(8,128)(2,1)}, bf16[256,128]{1,0:T(8,128)(2,1)S(1)}, u32[]{:S(2)}, u32[]{:S(2)}) collective-permute-start(bf16[256,128]{1,0:T(8,128)(2,1)} %get-tuple-element.43), channel_id=1, source_target_pairs={{0,3},{1,2},{2,1},{3,0},{4,7},{5,6},{6,5},{7,4},{8,11},{9,10},{10,... | collective-permute-start | bytes 196616 | tf_op jit(solution)/shard_map/ppermute | solution.py:494
  17.9 1.0 copy.19
  18.9 1.0 copy.21
  19.9 0.8 reverse_select_fusion
  20.7 0.9 copy.23.first_t_ref
  21.6 0.9 copy.24.bias_ref
  22.4 1.0 copy.20
  23.4 2.9 %collective-permute-done.4.other_ref.own_col = bf16[1280,128]{1,0:T(8,128)(2,1)S(1)} collective-permute-done((bf16[1280,128]{1,0:T(8,128)(2,1)}, bf16[1280,128]{1,0:T(8,128)(2,1)S(1)}, u32[]{:S(2)}, u32[]{:S(2)}) %collective-permute-start.4) | collective-permute-done | bytes 327712 | tf_op jit(solution)/shard_map/ppermute | solution.py:481
  26.4 0.8 copy-done.6
  27.2 6.6 %shard_map.120 = (bf16[256,1024]{1,0:T(8,128)(2,1)}, bf16[512,1024]{1,0:T(8,128)(2,1)}, bf16[512,1024]{1,0:T(8,128)(2,1)}, f32[512,1024]{1,0:T(8,128)}, f32[512,1024]{1,0:T(8,128)}, /*index=5*/f32[960,128]{1,0:T(8,128)}) custom-call(bf16[1280,128]{1,0:T(8,128)(2,1)} %get-tuple-element.44.own_ref, bf16[1280,128]{1,0:T(8,128)(2,1)} %copy-done.6, ...), custom_call_target="tpu_custom_call" | custom-call | tf_op jit(solution)/shard_map/pallas_call | solution.py:458
  33.9 2.6 %collective-permute-start.5 = (bf16[1296,128]{1,0:T(8,128)(2,1)S(1)}, bf16[1296,128]{1,0:T(8,128)(2,1)S(1)}, u32[]{:S(2)}, u32[]{:S(2)}) collective-permute-start(bf16[1296,128]{1,0:T(8,128)(2,1)S(1)} %broadcast_select_fusion), channel_id=1, source_target_pairs={{0,64},{64,0},{1,65},{65,1},{2,66},{66,2},{3,67},{67,3},{4,68},{68... | collective-permute-start | bytes 995336 | tf_op jit(solution)/shard_map/ppermute | solution.py:481
  36.6 0.5 collective-permute-start.6
  37.1 1.2 collective-permute-done.6.partner_edge
  38.5 0.5 copy-done.22
  39.4 9.8 %shard_map.121 = (f32[960,128]{1,0:T(8,128)}, bf16[960,128]{1,0:T(8,128)(2,1)}, bf16[192,128]{1,0:T(8,128)(2,1)}, bf16[1216,128]{1,0:T(8,128)(2,1)}, f32[48,56,128]{2,1,0:T(8,128)}, /*index=5*/f32[4,8,128]{2,1,0:T(8,128)}) custom-call(s32[1,2]{1,0:T(1,128)} %turn_ref.3, f32[1920,128]{1,0:T(8,128)} %bitcast.26, f32[640,128]{1,0:T(8,128)} %bitcast.35, ...), custom_call_target="tpu_custom_call" | custom-call | bytes 20000000 | tf_op jit(solution)/shard_map/pallas_call | solution.py:458
  49.2 1.7 %collective-permute-start.9 = (bf16[1216,128]{1,0:T(8,128)(2,1)}, bf16[1216,128]{1,0:T(8,128)(2,1)S(1)}, u32[]{:S(2)}, u32[]{:S(2)}) collective-permute-start(bf16[1216,128]{1,0:T(8,128)(2,1)} %get-tuple-element.52.own_ref), channel_id=1, source_target_pairs={{0,1},{1,0},{2,3},{3,2},{4,5},{5,4},{6,7},{7,6},{8,9},{9,8},{10,11... | collective-permute-start | bytes 933896 | tf_op jit(solution)/shard_map/ppermute | solution.py:481
  50.9 0.7 collective-permute-start.11
  51.6 0.7 collective-permute-start.13
  52.3 9.1 %collective-permute-start.12 = (bf16[192,128]{1,0:T(8,128)(2,1)}, bf16[192,128]{1,0:T(8,128)(2,1)S(1)}, u32[]{:S(2)}, u32[]{:S(2)}) collective-permute-start(bf16[192,128]{1,0:T(8,128)(2,1)} %get-tuple-element.54), channel_id=1, source_target_pairs={{0,3},{1,2},{2,1},{3,0},{4,7},{5,6},{6,5},{7,4},{8,11},{9,10},{10,... | collective-permute-start | bytes 147464 | tf_op jit(solution)/shard_map/ppermute | solution.py:494
  61.5 0.8 copy.26
  62.3 1.6 %collective-permute-done.12.a_edge = bf16[192,128]{1,0:T(8,128)(2,1)S(1)} collective-permute-done((bf16[192,128]{1,0:T(8,128)(2,1)}, bf16[192,128]{1,0:T(8,128)(2,1)S(1)}, u32[]{:S(2)}, u32[]{:S(2)}) %collective-permute-start.12) | collective-permute-done | bytes 49184 | tf_op jit(solution)/shard_map/ppermute | solution.py:494
  63.9 0.9 collective-permute-done.9.other_ref.own_col
  64.8 0.7 copy-done.7
  65.5 6.1 %shard_map.122 = (bf16[256,1024]{1,0:T(8,128)(2,1)}, bf16[512,1024]{1,0:T(8,128)(2,1)}, bf16[512,1024]{1,0:T(8,128)(2,1)}, f32[1024,128]{1,0:T(8,128)}) custom-call(bf16[1216,128]{1,0:T(8,128)(2,1)} %get-tuple-element.52.own_ref, bf16[1216,128]{1,0:T(8,128)(2,1)} %copy-done.7, bf16[256,1024]{1,0:T(8,128)(2,1)} %get-tuple-element.56.feat_ref, ...), custom_call_target="tpu_custom_call" | custom-call | tf_op jit(solution)/shard_map/pallas_call | solution.py:458
  71.7 1.3 collective-permute-start.17
  72.9 4.3 %shard_map.123 = (f32[1024,128]{1,0:T(8,128)}, f32[960,128]{1,0:T(8,128)}) custom-call(bf16[256,1024]{1,0:T(8,128)(2,1)} %get-tuple-element.61.resid_ref, bf16[256,1024]{1,0:T(8,128)(2,1)} %get-tuple-element.56.feat_ref, bf16[256,512]{1,0:T(8,128)(2,1)} %bitcast.30, bf16[512,1024]{1,0:T(8,128)(2,1)} %get-tuple-element.57.one_ref, ...), custom_call_target="tpu_custom_call" | custom-call | tf_op jit(solution)/shard_map/pallas_call | solution.py:458
  77.2 1.1 add_convert_fusion
  78.3 17.3 %all_to_all.10 = bf16[32,32,128]{2,1,0:T(8,128)(2,1)S(1)} all-to-all(bf16[32,32,128]{2,1,0:T(8,128)(2,1)S(1)} %bitcast.37), channel_id=1, replica_groups=mesh['sec'=2,'tile'=32,'lev'=2] {'tile'}, dimensions={0} | all-to-all | bytes 524288 | tf_op jit(solution)/shard_map/all_to_all | solution.py:555
  95.7 1.1 broadcast_in_dim.10
  96.8 5.8 %all-to-all-start.1 = ((f32[64,32,128]{2,1,0:T(8,128)}), f32[64,32,128]{2,1,0:T(8,128)S(1)}, u32[]{:S(2)}, u32[]{:S(2)}) async-start(f32[64,32,128]{2,1,0:T(8,128)} %broadcast_in_dim.10), calls=%async_computation.1 | async-start | bytes 2097152 | tf_op jit(solution)/shard_map/all_to_all | solution.py:558
  102.6 1.6 %collective-permute-start.8 = (f32[960,128]{1,0:T(8,128)S(1)}, f32[960,128]{1,0:T(8,128)S(1)}, u32[]{:S(2)}, u32[]{:S(2)}) collective-permute-start(f32[960,128]{1,0:T(8,128)S(1)} %copy-done.12), channel_id=1, source_target_pairs={{0,64},{64,0},{1,65},{65,1},{2,66},{66,2},{3,67},{67,3},{4,68},{68... | collective-permute-start | bytes 1474568 | tf_op jit(solution)/shard_map/ppermute | solution.py:481
  104.3 0.5 collective-permute-start.14
  105.0 1.5 %collective-permute-done.15.partner_edge = bf16[192,128]{1,0:T(8,128)(2,1)S(1)} collective-permute-done((bf16[192,128]{1,0:T(8,128)(2,1)S(1)}, bf16[192,128]{1,0:T(8,128)(2,1)S(1)}, u32[]{:S(2)}, u32[]{:S(2)}) %collective-permute-start.15) | collective-permute-done | bytes 49184 | tf_op jit(solution)/shard_map/ppermute | solution.py:481
  106.5 0.6 copy-done.23
  107.5 8.8 %shard_map.124 = f32[960,128]{1,0:T(8,128)} custom-call(f32[960,128]{1,0:T(8,128)} %get-tuple-element.51.resid_ref, f32[960,128]{1,0:T(8,128)} %copy-done.13, f32[960,128]{1,0:T(8,128)} %get-tuple-element.64.input_grad_ref, f32[48,56,128]{2,1,0:T(8,128)} %get-tuple-element.65.c_ref, f32[4,8,128]{2,1,0:T(8,128)} %get-tuple-element.66.factor_ref, ...), custom_call_target="tpu_custom_call" | custom-call | bytes 20000000 | tf_op jit(solution)/shard_map/pallas_call | solution.py:458
  116.2 3.5 %all-to-all-done.1.own_ref = f32[64,32,128]{2,1,0:T(8,128)S(1)} async-done(((f32[64,32,128]{2,1,0:T(8,128)}), f32[64,32,128]{2,1,0:T(8,128)S(1)}, u32[]{:S(2)}, u32[]{:S(2)}) %all-to-all-start.1) | async-done | bytes 1048608 | tf_op jit(solution)/shard_map/all_to_all | solution.py:558
  119.8 2.7 %collective-permute-start.19 = (f32[64,32,128]{2,1,0:T(8,128)S(1)}, f32[64,32,128]{2,1,0:T(8,128)S(1)}, u32[]{:S(2)}, u32[]{:S(2)}) collective-permute-start(f32[64,32,128]{2,1,0:T(8,128)S(1)} %all-to-all-done.1.own_ref), channel_id=1, source_target_pairs={{0,64},{64,0},{1,65},{65,1},{2,66},{66,2},{3,67},{67,3},{4,68},{68... | collective-permute-start | bytes 3145736 | tf_op jit(solution)/shard_map/ppermute | solution.py:481
  122.5 3.1 %collective-permute-done.18 = f32[960,128]{1,0:T(8,128)S(1)} collective-permute-done((f32[960,128]{1,0:T(8,128)}, f32[960,128]{1,0:T(8,128)S(1)}, u32[]{:S(2)}, u32[]{:S(2)}) %collective-permute-start.18) | collective-permute-done | bytes 491552 | tf_op jit(solution)/shard_map/ppermute | solution.py:481
  125.5 1.1 broadcast_select_fusion.3
  126.6 1.0 pad_maximum_fusion
  127.6 1.0 copy-done.9
  128.6 3.0 %shard_map.125 = (f32[240,512]{1,0:T(8,128)}, f32[8,512]{1,0:T(8,128)}, f32[512,512]{1,0:T(8,128)}, f32[240,512]{1,0:T(8,128)}) custom-call(f32[64,32,128]{2,1,0:T(8,128)} %copy-done, f32[64,32,128]{2,1,0:T(8,128)} %copy-done.9), custom_call_target="tpu_custom_call" | custom-call | tf_op jit(solution)/shard_map/pallas_call | solution.py:458
  131.6 1.3 slice.3
  (72 shorter events, 1.6 us)
Async XLA Ops:
  3.0 18.6 %copy-start.24 = (f32[512]{0:T(512)S(1)}, f32[512]{0:T(512)}, u32[]{:S(2)}) copy-start(f32[512]{0:T(512)} %param.13) | copy-start | bytes 6148
  3.0 19.4 %copy-start.3 = (bf16[512,512]{1,0:T(8,128)(2,1)S(1)}, bf16[512,512]{1,0:T(8,128)(2,1)}, u32[]{:S(2)}) copy-start(bf16[512,512]{1,0:T(8,128)(2,1)} %second_ref.1) | copy-start | bytes 1572868
  3.0 30.8 %collective-permute-start.1 = (bf16[1296,128]{1,0:T(8,128)(2,1)}, bf16[1296,128]{1,0:T(8,128)(2,1)S(1)}, u32[]{:S(2)}, u32[]{:S(2)}) collective-permute-start(bf16[1296,128]{1,0:T(8,128)(2,1)} %get-tuple-element.42), channel_id=1, source_target_pairs={{2,4},{4,2},{6,8},{8,6},{10,12},{12,10},{14,16},{16,14},{18,20},{2... | collective-permute-start | bytes 995336 | tf_op jit(solution)/shard_map/ppermute | solution.py:493
  3.8 30.0 %collective-permute-start = (bf16[1296,128]{1,0:T(8,128)(2,1)}, bf16[1296,128]{1,0:T(8,128)(2,1)S(1)}, u32[]{:S(2)}, u32[]{:S(2)}) collective-permute-start(bf16[1296,128]{1,0:T(8,128)(2,1)} %get-tuple-element.42), channel_id=1, source_target_pairs={{0,2},{2,0},{4,6},{6,4},{8,10},{10,8},{12,14},{14,12},{16,18},{18,... | collective-permute-start | bytes 995336 | tf_op jit(solution)/shard_map/ppermute | solution.py:492
  9.2 17.1 %collective-permute-start.4 = (bf16[1280,128]{1,0:T(8,128)(2,1)}, bf16[1280,128]{1,0:T(8,128)(2,1)S(1)}, u32[]{:S(2)}, u32[]{:S(2)}) collective-permute-start(bf16[1280,128]{1,0:T(8,128)(2,1)} %get-tuple-element.44.own_ref), channel_id=1, source_target_pairs={{0,1},{1,0},{2,3},{3,2},{4,5},{5,4},{6,7},{7,6},{8,9},{9,8},{10,11... | collective-permute-start | bytes 983048 | tf_op jit(solution)/shard_map/ppermute | solution.py:481
  12.1 21.6 %collective-permute-start.3 = (bf16[256,128]{1,0:T(8,128)(2,1)}, bf16[256,128]{1,0:T(8,128)(2,1)S(1)}, u32[]{:S(2)}, u32[]{:S(2)}) collective-permute-start(bf16[256,128]{1,0:T(8,128)(2,1)} %get-tuple-element.43), channel_id=1, source_target_pairs={{2,5},{3,4},{4,3},{5,2},{6,9},{7,8},{8,7},{9,6},{10,13},{11,12},{1... | collective-permute-start | bytes 196616 | tf_op jit(solution)/shard_map/ppermute | solution.py:495
  12.8 21.0 %collective-permute-start.2 = (bf16[256,128]{1,0:T(8,128)(2,1)}, bf16[256,128]{1,0:T(8,128)(2,1)S(1)}, u32[]{:S(2)}, u32[]{:S(2)}) collective-permute-start(bf16[256,128]{1,0:T(8,128)(2,1)} %get-tuple-element.43), channel_id=1, source_target_pairs={{0,3},{1,2},{2,1},{3,0},{4,7},{5,6},{6,5},{7,4},{8,11},{9,10},{10,... | collective-permute-start | bytes 196616 | tf_op jit(solution)/shard_map/ppermute | solution.py:494
  20.7 13.2 %copy-start.2 = (bf16[2,128,512]{2,1,0:T(8,128)(2,1)}, bf16[2,128,512]{2,1,0:T(8,128)(2,1)S(1)}, u32[]{:S(2)}) copy-start(bf16[2,128,512]{2,1,0:T(8,128)(2,1)S(1)} %get-tuple-element.82) | copy-start | bytes 786436
  26.4 0.8 copy-start.6
  33.8 4.7 %copy-start.17 = (bf16[256,128]{1,0:T(8,128)(2,1)}, bf16[256,128]{1,0:T(8,128)(2,1)S(1)}, u32[]{:S(2)}) copy-start(bf16[256,128]{1,0:T(8,128)(2,1)S(1)} %collective-permute-done.3.b_edge) | copy-start | bytes 196612
  33.8 4.7 %copy-start.18 = (bf16[256,128]{1,0:T(8,128)(2,1)}, bf16[256,128]{1,0:T(8,128)(2,1)S(1)}, u32[]{:S(2)}) copy-start(bf16[256,128]{1,0:T(8,128)(2,1)S(1)} %collective-permute-done.2.a_edge) | copy-start | bytes 196612
  33.8 4.6 %copy-start.4 = (bf16[1296,128]{1,0:T(8,128)(2,1)}, bf16[1296,128]{1,0:T(8,128)(2,1)S(1)}, u32[]{:S(2)}) copy-start(bf16[1296,128]{1,0:T(8,128)(2,1)S(1)} %collective-permute-done.1.b) | copy-start | bytes 995332
  33.8 4.6 %copy-start.5 = (bf16[1296,128]{1,0:T(8,128)(2,1)}, bf16[1296,128]{1,0:T(8,128)(2,1)S(1)}, u32[]{:S(2)}) copy-start(bf16[1296,128]{1,0:T(8,128)(2,1)S(1)} %collective-permute-done.a) | copy-start | bytes 995332
  33.9 4.5 %collective-permute-start.5 = (bf16[1296,128]{1,0:T(8,128)(2,1)S(1)}, bf16[1296,128]{1,0:T(8,128)(2,1)S(1)}, u32[]{:S(2)}, u32[]{:S(2)}) collective-permute-start(bf16[1296,128]{1,0:T(8,128)(2,1)S(1)} %broadcast_select_fusion), channel_id=1, source_target_pairs={{0,64},{64,0},{1,65},{65,1},{2,66},{66,2},{3,67},{67,3},{4,68},{68... | collective-permute-start | bytes 995336 | tf_op jit(solution)/shard_map/ppermute | solution.py:481
  36.5 1.9 %collective-permute-start.7 = (bf16[1280,128]{1,0:T(8,128)(2,1)}, bf16[1280,128]{1,0:T(8,128)(2,1)S(1)}, u32[]{:S(2)}, u32[]{:S(2)}) collective-permute-start(bf16[1280,128]{1,0:T(8,128)(2,1)} %copy-done.6), channel_id=1, source_target_pairs={{0,64},{64,0},{1,65},{65,1},{2,66},{66,2},{3,67},{67,3},{4,68},{68... | collective-permute-start | bytes 983048 | tf_op jit(solution)/shard_map/ppermute | solution.py:481
  36.6 1.7 %collective-permute-start.6 = (bf16[256,128]{1,0:T(8,128)(2,1)S(1)}, bf16[256,128]{1,0:T(8,128)(2,1)S(1)}, u32[]{:S(2)}, u32[]{:S(2)}) collective-permute-start(bf16[256,128]{1,0:T(8,128)(2,1)S(1)} %broadcast_select_fusion.4), channel_id=1, source_target_pairs={{0,64},{64,0},{1,65},{65,1},{2,66},{66,2},{3,67},{67,3},{4,68},{68... | collective-permute-start | bytes 196616 | tf_op jit(solution)/shard_map/ppermute | solution.py:481
  38.3 0.6 copy-start.22
  38.4 0.8 copy-start.15
  38.4 0.9 copy-start.14
  39.4 22.1 %copy-start.1 = (bf16[2,128,512]{2,1,0:T(8,128)(2,1)S(1)}, bf16[2,128,512]{2,1,0:T(8,128)(2,1)}, u32[]{:S(2)}) copy-start(bf16[2,128,512]{2,1,0:T(8,128)(2,1)} %get-tuple-element.81) | copy-start | bytes 786436
  49.2 15.6 %collective-permute-start.9 = (bf16[1216,128]{1,0:T(8,128)(2,1)}, bf16[1216,128]{1,0:T(8,128)(2,1)S(1)}, u32[]{:S(2)}, u32[]{:S(2)}) collective-permute-start(bf16[1216,128]{1,0:T(8,128)(2,1)} %get-tuple-element.52.own_ref), channel_id=1, source_target_pairs={{0,1},{1,0},{2,3},{3,2},{4,5},{5,4},{6,7},{7,6},{8,9},{9,8},{10,11... | collective-permute-start | bytes 933896 | tf_op jit(solution)/shard_map/ppermute | solution.py:481
  50.9 13.0 %collective-permute-start.11 = (bf16[960,128]{1,0:T(8,128)(2,1)}, bf16[960,128]{1,0:T(8,128)(2,1)S(1)}, u32[]{:S(2)}, u32[]{:S(2)}) collective-permute-start(bf16[960,128]{1,0:T(8,128)(2,1)} %get-tuple-element.53), channel_id=1, source_target_pairs={{2,4},{4,2},{6,8},{8,6},{10,12},{12,10},{14,16},{16,14},{18,20},{2... | collective-permute-start | bytes 737288 | tf_op jit(solution)/shard_map/ppermute | solution.py:493
  51.6 12.4 %collective-permute-start.10 = (bf16[960,128]{1,0:T(8,128)(2,1)}, bf16[960,128]{1,0:T(8,128)(2,1)S(1)}, u32[]{:S(2)}, u32[]{:S(2)}) collective-permute-start(bf16[960,128]{1,0:T(8,128)(2,1)} %get-tuple-element.53), channel_id=1, source_target_pairs={{0,2},{2,0},{4,6},{6,4},{8,10},{10,8},{12,14},{14,12},{16,18},{18,... | collective-permute-start | bytes 737288 | tf_op jit(solution)/shard_map/ppermute | solution.py:492
  51.6 10.7 %collective-permute-start.13 = (bf16[192,128]{1,0:T(8,128)(2,1)}, bf16[192,128]{1,0:T(8,128)(2,1)S(1)}, u32[]{:S(2)}, u32[]{:S(2)}) collective-permute-start(bf16[192,128]{1,0:T(8,128)(2,1)} %get-tuple-element.54), channel_id=1, source_target_pairs={{2,5},{3,4},{4,3},{5,2},{6,9},{7,8},{8,7},{9,6},{10,13},{11,12},{1... | collective-permute-start | bytes 147464 | tf_op jit(solution)/shard_map/ppermute | solution.py:495
  52.3 11.6 %collective-permute-start.12 = (bf16[192,128]{1,0:T(8,128)(2,1)}, bf16[192,128]{1,0:T(8,128)(2,1)S(1)}, u32[]{:S(2)}, u32[]{:S(2)}) collective-permute-start(bf16[192,128]{1,0:T(8,128)(2,1)} %get-tuple-element.54), channel_id=1, source_target_pairs={{0,3},{1,2},{2,1},{3,0},{4,7},{5,6},{6,5},{7,4},{8,11},{9,10},{10,... | collective-permute-start | bytes 147464 | tf_op jit(solution)/shard_map/ppermute | solution.py:494
  62.3 42.5 %copy-start.20 = (bf16[192,128]{1,0:T(8,128)(2,1)}, bf16[192,128]{1,0:T(8,128)(2,1)S(1)}, u32[]{:S(2)}) copy-start(bf16[192,128]{1,0:T(8,128)(2,1)S(1)} %collective-permute-done.13.b_edge) | copy-start | bytes 147460
  63.9 40.9 %copy-start.21 = (bf16[192,128]{1,0:T(8,128)(2,1)}, bf16[192,128]{1,0:T(8,128)(2,1)S(1)}, u32[]{:S(2)}) copy-start(bf16[192,128]{1,0:T(8,128)(2,1)S(1)} %collective-permute-done.12.a_edge) | copy-start | bytes 147460
  63.9 40.3 %copy-start.10 = (bf16[960,128]{1,0:T(8,128)(2,1)}, bf16[960,128]{1,0:T(8,128)(2,1)S(1)}, u32[]{:S(2)}) copy-start(bf16[960,128]{1,0:T(8,128)(2,1)S(1)} %collective-permute-done.11.b) | copy-start | bytes 737284
  63.9 40.3 %copy-start.11 = (bf16[960,128]{1,0:T(8,128)(2,1)}, bf16[960,128]{1,0:T(8,128)(2,1)S(1)}, u32[]{:S(2)}) copy-start(bf16[960,128]{1,0:T(8,128)(2,1)S(1)} %collective-permute-done.10.a) | copy-start | bytes 737284
  64.8 0.7 copy-start.7
  71.7 5.5 %collective-permute-start.17 = (f32[1024,128]{1,0:T(8,128)}, f32[1024,128]{1,0:T(8,128)S(1)}, u32[]{:S(2)}, u32[]{:S(2)}) collective-permute-start(f32[1024,128]{1,0:T(8,128)} %get-tuple-element.72), channel_id=1, source_target_pairs={{0,64},{64,0},{1,65},{65,1},{2,66},{66,2},{3,67},{67,3},{4,68},{68... | collective-permute-start | bytes 1572872 | tf_op jit(solution)/shard_map/ppermute | solution.py:481
  78.3 24.3 %copy-start.12 = (f32[960,128]{1,0:T(8,128)S(1)}, f32[960,128]{1,0:T(8,128)}, u32[]{:S(2)}) copy-start(f32[960,128]{1,0:T(8,128)} %get-tuple-element.51.resid_ref) | copy-start | bytes 1474564
  78.3 25.8 %copy-start.8 = (bf16[1216,128]{1,0:T(8,128)(2,1)S(1)}, bf16[1216,128]{1,0:T(8,128)(2,1)}, u32[]{:S(2)}) copy-start(bf16[1216,128]{1,0:T(8,128)(2,1)} %copy-done.7) | copy-start | bytes 933892
  96.8 23.0 %all-to-all-start.1 = ((f32[64,32,128]{2,1,0:T(8,128)}), f32[64,32,128]{2,1,0:T(8,128)S(1)}, u32[]{:S(2)}, u32[]{:S(2)}) async-start(f32[64,32,128]{2,1,0:T(8,128)} %broadcast_in_dim.10), calls=%async_computation.1 | async-start | bytes 2097152 | tf_op jit(solution)/shard_map/all_to_all | solution.py:558
  102.6 3.9 %collective-permute-start.8 = (f32[960,128]{1,0:T(8,128)S(1)}, f32[960,128]{1,0:T(8,128)S(1)}, u32[]{:S(2)}, u32[]{:S(2)}) collective-permute-start(f32[960,128]{1,0:T(8,128)S(1)} %copy-done.12), channel_id=1, source_target_pairs={{0,64},{64,0},{1,65},{65,1},{2,66},{66,2},{3,67},{67,3},{4,68},{68... | collective-permute-start | bytes 1474568 | tf_op jit(solution)/shard_map/ppermute | solution.py:481
  104.1 2.4 %collective-permute-start.16 = (bf16[1216,128]{1,0:T(8,128)(2,1)S(1)}, bf16[1216,128]{1,0:T(8,128)(2,1)S(1)}, u32[]{:S(2)}, u32[]{:S(2)}) collective-permute-start(bf16[1216,128]{1,0:T(8,128)(2,1)S(1)} %copy-done.8), channel_id=1, source_target_pairs={{0,64},{64,0},{1,65},{65,1},{2,66},{66,2},{3,67},{67,3},{4,68},{68... | collective-permute-start | bytes 933896 | tf_op jit(solution)/shard_map/ppermute | solution.py:481
  104.3 2.2 %collective-permute-start.14 = (bf16[960,128]{1,0:T(8,128)(2,1)S(1)}, bf16[960,128]{1,0:T(8,128)(2,1)S(1)}, u32[]{:S(2)}, u32[]{:S(2)}) collective-permute-start(bf16[960,128]{1,0:T(8,128)(2,1)S(1)} %broadcast_select_fusion.1), channel_id=1, source_target_pairs={{0,64},{64,0},{1,65},{65,1},{2,66},{66,2},{3,67},{67,3},{4,68},{68... | collective-permute-start | bytes 737288 | tf_op jit(solution)/shard_map/ppermute | solution.py:481
  104.8 1.7 %collective-permute-start.15 = (bf16[192,128]{1,0:T(8,128)(2,1)S(1)}, bf16[192,128]{1,0:T(8,128)(2,1)S(1)}, u32[]{:S(2)}, u32[]{:S(2)}) collective-permute-start(bf16[192,128]{1,0:T(8,128)(2,1)S(1)} %broadcast_select_fusion.5), channel_id=1, source_target_pairs={{0,64},{64,0},{1,65},{65,1},{2,66},{66,2},{3,67},{67,3},{4,68},{68... | collective-permute-start | bytes 147464 | tf_op jit(solution)/shard_map/ppermute | solution.py:481
  106.5 0.6 copy-start.23
  106.5 0.8 copy-start.13
  106.5 0.9 copy-start.19
  106.5 0.9 copy-start.16
  119.8 7.9 %copy-start = (f32[64,32,128]{2,1,0:T(8,128)}, f32[64,32,128]{2,1,0:T(8,128)S(1)}, u32[]{:S(2)}) copy-start(f32[64,32,128]{2,1,0:T(8,128)S(1)} %all-to-all-done.1.own_ref) | copy-start | bytes 3145732
  119.8 7.9 %collective-permute-start.19 = (f32[64,32,128]{2,1,0:T(8,128)S(1)}, f32[64,32,128]{2,1,0:T(8,128)S(1)}, u32[]{:S(2)}, u32[]{:S(2)}) collective-permute-start(f32[64,32,128]{2,1,0:T(8,128)S(1)} %all-to-all-done.1.own_ref), channel_id=1, source_target_pairs={{0,64},{64,0},{1,65},{65,1},{2,66},{66,2},{3,67},{67,3},{4,68},{68... | collective-permute-start | bytes 3145736 | tf_op jit(solution)/shard_map/ppermute | solution.py:481
  122.4 3.1 %collective-permute-start.18 = (f32[960,128]{1,0:T(8,128)}, f32[960,128]{1,0:T(8,128)S(1)}, u32[]{:S(2)}, u32[]{:S(2)}) collective-permute-start(f32[960,128]{1,0:T(8,128)} %shard_map.124), channel_id=1, source_target_pairs={{0,64},{64,0},{1,65},{65,1},{2,66},{66,2},{3,67},{67,3},{4,68},{68... | collective-permute-start | bytes 1474568 | tf_op jit(solution)/shard_map/ppermute | solution.py:481
  127.6 1.0 copy-start.9

commit v3 on v2

--- a/solution.py
+++ b/solution.py
@@ -23,8 +23,9 @@
 COLS = BLK * 128
 GROUP = 128
 PAD = GROUP - 3 * OWN
-STRIPE = 256
+STRIPE = 512
 MIB = 1024 * 1024
+LONG = 20_000_000_000
 F32 = jnp.float32
 BF = jnp.bfloat16
 
@@ -112,27 +113,20 @@
 
 
 def static_rows(sec):
-    return 16 + 16 * sec, 32 - 16 * sec, 24 + 8 * sec, 40 - 24 * sec
-
-
-def spread_rims(sec, lev, odd, a, b, a_edge, b_edge, partner, partner_edge, own_col, other_col, fields):
-    partner_row, other_row, _, _ = static_rows(sec)
+    return 32 - 16 * sec, 24 + 8 * sec, 40 - 24 * sec
+
+
+def spread_rims(sec, lev, near, far, partner, rims, partner_rims, own_edge, other_edge, fields):
     own_level, edge_level = EDGE * lev, OWN * (1 - lev)
-
-    def sides(low, high, low_edge, high_edge):
-        for n, (dst, shift, scale) in enumerate(fields):
-            for src, edge, row in ((low, low_edge, BLK), (high, high_edge, 5 * BLK)):
-                spread(src, n * FIELD, OWN, dst, own_level + shift, row, scale)
-                spread(edge, n * RIM, EDGE, dst, edge_level + shift, row, scale)
-
-    pl.when(odd)(lambda: sides(a, b, a_edge, b_edge))
-    pl.when(jnp.logical_not(odd))(lambda: sides(b, a, b_edge, a_edge))
+    count = len(fields)
+    rows = (8, 16, 40) if sec == 0 else (40, 32, 8)
+    sources = ((far, rims, count * RIM, rows[0]), (near, rims, 0, rows[1]), (partner, partner_rims, 0, rows[2]))
     for n, (dst, shift, scale) in enumerate(fields):
-        spread(partner, n * FIELD, OWN, dst, own_level + shift, partner_row, scale)
-        spread(partner_edge, n * RIM, EDGE, dst, edge_level + shift, partner_row, scale)
-        start = BLK * GROUP + n * RIM
-        spread(other_col, start, EDGE, dst, edge_level + shift, other_row, scale)
-        spread(own_col, start, EDGE, dst, edge_level + shift, 3 * BLK, scale)
+        for src, edge, start, row in sources:
+            spread(src, n * FIELD, OWN, dst, own_level + shift, row, scale)
+            spread(edge, start + n * RIM, EDGE, dst, edge_level + shift, row, scale)
+        for (edge, start), row in ((own_edge, 3 * BLK), (other_edge, static_rows(sec)[0])):
+            spread(edge, start + n * RIM, EDGE, dst, edge_level + shift, row, scale)
 
 
 def chunk_range(step, lev):
@@ -145,38 +139,66 @@
     return jnp.concatenate([*fields, jnp.full((PAD, 128), fill, F32)], axis=0).astype(BF)
 
 
-def pack_kernel(turn_ref, state_ref, sound_ref, rows_ref, edge_ref, column_ref):
+def by_group(out_ref, weights_ref, lev, bias_ref=None):
+    hid = out_ref.shape[1]
+    values = weights_ref[...].astype(F32)
+    padding = jnp.zeros((PAD, hid), F32)
+    own_padding = padding
+    if bias_ref is not None:
+        rest = bias_ref[...]
+        row = lax.broadcasted_iota(jnp.int32, (PAD, hid), 0)
+        for n in range(3):
+            part = rest.astype(BF).astype(F32)
+            own_padding = jnp.where(row == n, part, own_padding)
+            rest = rest - part
+    groups = [[values[(2 * n + g) * OWN : (2 * n + g + 1) * OWN] for n in range(3)] for g in range(2)]
+    for group in range(2):
+
+        def run(group=group):
+            parts = [*groups[group], own_padding, *groups[1 - group], padding]
+            out_ref[...] = jnp.concatenate(parts, axis=0).astype(BF)
+
+        pl.when(lev == group)(run)
+
+
+def pack_kernel(
+    turn_ref, state_ref, sound_ref, first_ref, third_t_ref, bias_ref,
+    near_ref, far_ref, edge_ref, column_ref, first_out_ref, third_out_ref,
+):
     sec, lev = lax.axis_index("sec"), lax.axis_index("lev")
-
-    def run(row):
-        for n in range(4):
-            src = state_ref[n * OWN * 16 : (n + 1) * OWN * 16, :] if n < 3 else sound_ref[...]
-            field = src.reshape(OWN, 16, 128)[:, row : row + BLK, :].reshape(FIELD, 128)
-            rows_ref[n * FIELD : (n + 1) * FIELD, :] = field.astype(BF)
-        for r in range(BLK):
-            column_ref[r * GROUP : (r + 1) * GROUP, :] = column_rows(state_ref, r, row, 16, OWN * 16, 1.0)
-
+    by_group(first_out_ref, first_ref, lev, bias_ref)
+    by_group(third_out_ref, third_t_ref, lev)
     for half in range(2):
-        pl.when(sec == half)(lambda half=half: run(BLK * half))
+
+        def run(half=half):
+            for n in range(4):
+                src = state_ref[n * OWN * 16 : (n + 1) * OWN * 16, :] if n < 3 else sound_ref[...]
+                for out, block in ((near_ref, half), (far_ref, 1 - half)):
+                    field = src.reshape(OWN, 16, 128)[:, block * BLK : block * BLK + BLK, :]
+                    out[n * FIELD : (n + 1) * FIELD, :] = field.reshape(FIELD, 128).astype(BF)
+            for r in range(BLK):
+                features = column_rows(state_ref, r, BLK * half, 16, OWN * 16, 1.0)
+                column_ref[r * GROUP : (r + 1) * GROUP, :] = features
+
+        pl.when(sec == half)(run)
     for n in range(4):
         start = pl.multiple_of(n * FIELD + (FIELD - RIM) * (1 - lev), 16)
-        rim = rows_ref[pl.ds(start, RIM), :]
-        edge_ref[n * RIM : (n + 1) * RIM, :] = rim
-        column_ref[BLK * GROUP + n * RIM : BLK * GROUP + (n + 1) * RIM, :] = rim
+        edge_ref[n * RIM : (n + 1) * RIM, :] = near_ref[pl.ds(start, RIM), :]
+        edge_ref[(4 + n) * RIM : (5 + n) * RIM, :] = far_ref[pl.ds(start, RIM), :]
+    column_ref[BLK * GROUP :, :] = edge_ref[...]
     i = lax.broadcasted_iota(jnp.int32, (16, 128), 0)
     factors = jnp.zeros((16, 128), F32)
     for n, value in enumerate((*quarter_turn(turn_ref[0, 0]), *quarter_turn(turn_ref[0, 1]))):
         factors = jnp.where(i == n, value, factors)
-    rows_ref[4 * FIELD :, :] = factors.astype(BF)
+    near_ref[4 * FIELD :, :] = factors.astype(BF)
 
 
 def forward_kernel(
     turn_ref, state_ref, sound_ref, target_ref, tendency_ref,
-    a, b, a_edge, b_edge, partner, partner_edge, own_col, other_col,
+    near, far, partner, rims, partner_rims, own_col,
     resid_ref, rows_ref, edge_ref, column_ref, c_ref, factor_ref, pa, pb, u, v, matrix,
 ):
     section, lev = lax.axis_index("sec"), lax.axis_index("lev")
-    odd = lax.rem(lax.axis_index("tile"), 2) == 1
     own_level = EDGE * lev
     for ref in (pa, pb, u, v, c_ref):
         clear(ref)
@@ -194,18 +216,19 @@
         factor_ref[2] = jnp.where(below, high[0:1, :], cos_high) - 1.0
         factor_ref[3] = jnp.where(below, high[1:2, :], sin_high)
 
-    pl.when(odd)(lambda: factors(a, b))
-    pl.when(jnp.logical_not(odd))(lambda: factors(b, a))
+    pl.when(section == 0)(lambda: factors(near, partner))
+    pl.when(section == 1)(lambda: factors(partner, near))
     masks = edge_masks()
     matrix[...] = across_matrix()
 
     def run(sec):
         unit = COURANT * UNIT
         spread_rims(
-            sec, lev, odd, a, b, a_edge, b_edge, partner, partner_edge, own_col, other_col,
+            sec, lev, near, far, partner, rims, partner_rims,
+            (own_col, BLK * GROUP), (own_col, BLK * GROUP + 4 * RIM),
             ((pa, 2, None), (u, 0, None), (v, 0, None), (c_ref, 0, unit)),
         )
-        _, _, near_edge, far_edge = static_rows(sec)
+        _, near_edge, far_edge = static_rows(sec)
         tile_row = 24 - 8 * sec
         for n, (dst, shift) in enumerate(((pa, 2), (u, 0), (v, 0))):
             field = state_ref[n * OWN * 16 : (n + 1) * OWN * 16, :].reshape(OWN, 16, 128)
@@ -269,11 +292,10 @@
 
 def adjoint_kernel(
     resid_ref, other_ref, input_grad_ref, c_ref, factor_ref,
-    a, b, a_edge, b_edge, partner, partner_edge, own_col, other_col,
+    near, far, partner, rims, partner_rims, own_col, other_col,
     out_ref, pa, pb, u, v, matrix, w,
 ):
     section, lev = lax.axis_index("sec"), lax.axis_index("lev")
-    odd = lax.rem(lax.axis_index("tile"), 2) == 1
     own_level = EDGE * lev
     for ref in (pa, pb, u, v, w):
         clear(ref)
@@ -285,10 +307,11 @@
 
     def run(sec):
         spread_rims(
-            sec, lev, odd, a, b, a_edge, b_edge, partner, partner_edge, own_col, other_col,
+            sec, lev, near, far, partner, rims, partner_rims,
+            (own_col, BLK * GROUP), (other_col, BLK * GROUP),
             ((pa, 2, None), (u, 0, None), (v, 0, None)),
         )
-        _, other_row, near_edge, far_edge = static_rows(sec)
+        other_row, near_edge, far_edge = static_rows(sec)
         for n, (dst, shift) in enumerate(((pa, 2), (u, 0), (v, 0))):
             at = pl.ds(own_level + shift, OWN)
             packed = slice(n * FIELD, (n + 1) * FIELD)
@@ -346,6 +369,10 @@
     return lax.dot_general(left, right, (((1,), (0,)), ((), ())), preferred_element_type=F32)
 
 
+def dot_t(left, right):
+    return lax.dot_general(left, right, (((0,), (0,)), ((), ())), preferred_element_type=F32)
+
+
 def dot_columns(left, right):
     return lax.dot_general(left, right, (((1,), (1,)), ((), ())), preferred_element_type=F32)
 
@@ -356,65 +383,90 @@
     return silu.astype(BF), sigma + silu * (1.0 - sigma)
 
 
-def both_groups(out_ref, own_ref, other_ref):
-    for r in range(BLK):
-        cols = slice(r * 128, (r + 1) * 128)
-        out_ref[:GROUP, cols] = own_ref[r * GROUP : (r + 1) * GROUP, :]
-        out_ref[GROUP:, cols] = other_ref[r * GROUP : (r + 1) * GROUP, :]
-
-
-def to_fields(out_ref, start, values):
-    for r in range(values.shape[1] // 128):
+def both_groups(own_ref, other_ref):
+    parts = [
+        jnp.concatenate([ref[r * GROUP : (r + 1) * GROUP, :] for ref in (own_ref, other_ref)], axis=0)
+        for r in range(STRIPE // 128)
+    ]
+    return jnp.concatenate(parts, axis=1)
+
+
+def to_fields(out_ref, first, values):
+    for r in range(STRIPE // 128):
         for n in range(3):
-            rows = pl.ds(n * FIELD + start // 128 + r, OWN, stride=BLK)
+            rows = pl.ds(n * FIELD + first + r, OWN, stride=BLK)
             out_ref[rows, :] = values[n * OWN : (n + 1) * OWN, r * 128 : (r + 1) * 128]
 
 
 def network_kernel(
-    own_ref, other_ref, first_t_ref, bias_ref, second_t_ref, third_t_ref,
+    own_ref, other_ref, first_ref, second_ref, third_t_ref,
     feat_ref, one_ref, two_ref, slope_one_ref, slope_two_ref, tendency_ref,
 ):
-    both_groups(feat_ref, own_ref, other_ref)
+    feat = both_groups(own_ref, other_ref)
+    feat_ref[...] = feat
+    one, slope = silu_and_slope(dot_t(first_ref[...], feat))
+    one_ref[...] = one
+    slope_one_ref[...] = slope
+    two, slope = silu_and_slope(dot_t(second_ref[...], one))
+    two_ref[...] = two
+    slope_two_ref[...] = slope
+    to_fields(tendency_ref, pl.program_id(0) * (STRIPE // 128), dot(third_t_ref[:GROUP, :], two))
+
+
+def gather_kernel(own_ref, other_ref, out_ref):
     for start in range(0, COLS, STRIPE):
-        cols = slice(start, start + STRIPE)
-        one, slope = silu_and_slope(dot(first_t_ref[...], feat_ref[:, cols]) + bias_ref[...])
-        one_ref[:, cols] = one
-        slope_one_ref[:, cols] = slope
-        two, slope = silu_and_slope(dot(second_t_ref[...], one))
-        two_ref[:, cols] = two
-        slope_two_ref[:, cols] = slope
-        to_fields(tendency_ref, start, dot(third_t_ref[:GROUP, :], two))
-
-
-def unit_gradients(out_ref, start, feat_ref, resid_ref, one_ref, two_ref, err_one_ref, err_two_ref):
-    units = pl.ds(pl.multiple_of(start, 128), 128)
+        rows = slice(start // 128 * GROUP, (start + STRIPE) // 128 * GROUP)
+        out_ref[:, start : start + STRIPE] = both_groups(own_ref.at[rows, :], other_ref.at[rows, :])
+
+
+def back_kernel(
+    resid_ref, feat_ref, third_t_ref, second_ref, first_ref, one_ref, two_ref, slope_one_ref, slope_two_ref,
+    given_ref, kept_ref, input_grad_ref, err_one_ref, err_two_ref, total_ref,
+):
+    step = pl.program_id(0)
+    resid = resid_ref[...]
+    err_two = (dot_t(third_t_ref[...], resid) * slope_two_ref[...]).astype(BF)
+    err_two_ref[...] = err_two
+    err_one = (dot(second_ref[...], err_two) * slope_one_ref[...]).astype(BF)
+    err_one_ref[...] = err_one
+    to_fields(input_grad_ref, step * (STRIPE // 128), dot(first_ref[:GROUP, :], err_one))
     feats, hid = feat_ref.shape[0], one_ref.shape[0]
-    out_ref[:feats, :] = dot_columns(feat_ref[...], err_one_ref[units, :])
-    out_ref[feats : feats + hid, :] = dot_columns(one_ref[...], err_two_ref[units, :])
-    out_ref[feats + hid :, :] = dot_columns(resid_ref[...], two_ref[units, :])
-
-
-def back_kernel(
-    own_ref, other_ref, feat_ref, third_ref, second_ref, one_ref, two_ref, slope_one_ref, slope_two_ref,
-    resid_ref, err_one_ref, err_two_ref, given_ref,
-):
-    both_groups(resid_ref, own_ref, other_ref)
-    for start in range(0, COLS, STRIPE):
-        cols = slice(start, start + STRIPE)
-        err_two = (dot(third_ref[...], resid_ref[:, cols]) * slope_two_ref[:, cols]).astype(BF)
-        err_two_ref[:, cols] = err_two
-        err_one_ref[:, cols] = (dot(second_ref[...], err_two) * slope_one_ref[:, cols]).astype(BF)
-    start = 256 * lax.axis_index("lev") + 128 * (1 - lax.axis_index("sec"))
-    unit_gradients(given_ref, start, feat_ref, resid_ref, one_ref, two_ref, err_one_ref, err_two_ref)
-
-
-def kept_kernel(
-    resid_ref, feat_ref, first_ref, one_ref, two_ref, err_one_ref, err_two_ref, kept_ref, input_grad_ref
-):
-    start = 256 * lax.axis_index("lev") + 128 * lax.axis_index("sec")
-    unit_gradients(kept_ref, start, feat_ref, resid_ref, one_ref, two_ref, err_one_ref, err_two_ref)
-    for start in range(0, COLS, STRIPE):
-        to_fields(input_grad_ref, start, dot(first_ref[:GROUP, :], err_one_ref[:, start : start + STRIPE]))
+    half = pl.ds(pl.multiple_of(256 * lax.axis_index("lev"), 256), 256)
+
+    def clear_total():
+        total_ref[...] = jnp.zeros(total_ref.shape, F32)
+
+    pl.when(step == 0)(clear_total)
+
+    def add(rows, left, right):
+        total_ref[rows, :] = total_ref[rows, :] + dot_columns(left, right)
+
+    add(slice(0, feats), feat_ref[...], err_one_ref[half, :])
+    add(slice(feats, feats + hid), one_ref[...], err_two_ref[half, :])
+    add(slice(feats + hid, 2 * feats + hid), resid, two_ref[half, :])
+
+    def finish():
+        for sec in range(2):
+
+            def share(sec=sec):
+                kept_ref[...] = total_ref[:, 128 * sec : 128 * sec + 128]
+                given_ref[...] = total_ref[:, 128 - 128 * sec : 256 - 128 * sec].astype(BF)
+
+            pl.when(lax.axis_index("sec") == sec)(share)
+
+    pl.when(step == COLS // STRIPE - 1)(finish)
+
+
+def place_rows_kernel(mine_ref, theirs_ref, out_ref):
+    for sec in range(2):
+
+        def run(sec=sec):
+            for n in range(3):
+                packed = slice(n * FIELD, (n + 1) * FIELD)
+                for core, ref in ((sec, mine_ref), (1 - sec, theirs_ref)):
+                    out_ref[n, :, BLK * core : BLK * core + BLK, :] = ref[packed, :].reshape(OWN, BLK, 128)
+
+        pl.when(lax.axis_index("sec") == sec)(run)
 
 
 def spread_gradients_kernel(own_ref, partner_ref, first_ref, bias_ref, second_ref, third_t_ref):
@@ -430,40 +482,51 @@
             out[to : to + 8, lanes] = values
 
     def run(sec):
-        for tile in range(own_ref.shape[0] // 2):
+        blocks = [(tile, lev, core) for tile in range(own_ref.shape[0] // 2) for lev in range(2) for core in range(2)]
+        for tile, lev, core in blocks:
+            lanes = slice(256 * lev + 128 * core, 256 * lev + 128 * core + 128)
+            block = (own_ref if core == sec else partner_ref)[2 * tile + lev].astype(F32)
             for part in range(0, share, 8):
                 row = tile * share + part
-                for lev in range(2):
-                    for core, src in ((sec, own_ref), (1 - sec, partner_ref)):
-                        lanes = slice(256 * lev + 128 * core, 256 * lev + 128 * core + 128)
-                        values = src[2 * tile + lev, part : part + 8, :]
-                        if row < 2 * GROUP:
-                            feature_rows(first_ref, row, lanes, lev, values)
-                            if row == 3 * OWN:
-                                bias_ref[:, lanes] = values
-                        elif row < 2 * GROUP + hid:
-                            second_ref[row - 2 * GROUP : row - 2 * GROUP + 8, lanes] = values
-                        else:
-                            feature_rows(third_t_ref, row - 2 * GROUP - hid, lanes, lev, values)
+                values = block[part : part + 8, :]
+                if row < 2 * GROUP:
+                    feature_rows(first_ref, row, lanes, lev, values)
+                    if row == 3 * OWN:
+                        bias_ref[:, lanes] = values[:1, :]
+                elif row < 2 * GROUP + hid:
+                    second_ref[row - 2 * GROUP : row - 2 * GROUP + 8, lanes] = values
+                else:
+                    feature_rows(third_t_ref, row - 2 * GROUP - hid, lanes, lev, values)
 
     for sec in range(2):
         pl.when(section == sec)(lambda sec=sec: run(sec))
 
 
-def call(kernel, n_smem, operands, outs, scratch=(), flops=0, moved=0):
-    def whole(value):
-        return pl.BlockSpec(value.shape, lambda i: (0,) * len(value.shape), pipeline_mode=pl.Buffered(1))
+def whole(value):
+    return pl.BlockSpec(value.shape, lambda i: (0,) * len(value.shape), pipeline_mode=pl.Buffered(1))
+
+
+def stripes(value, along):
+    if along:
+        return pl.BlockSpec((value.shape[0], STRIPE), lambda i: (0, i))
+    return pl.BlockSpec((STRIPE // 128 * GROUP, 128), lambda i: (i, 0))
+
+
+def call(kernel, n_smem, operands, outs, scratch=(), flops=0, steps=1, in_along=None, out_along=None):
+    def specs(values, along):
+        along = along or [None] * len(values)
+        return [whole(v) if at is None else stripes(v, at) for v, at in zip(values, along, strict=True)]
 
     smem = pl.BlockSpec(memory_space=pltpu.SMEM)
     return pl.pallas_call(
         kernel,
-        grid=(1,),
+        grid=(steps,),
         out_shape=outs,
-        in_specs=[smem] * n_smem + [whole(value) for value in operands[n_smem:]],
-        out_specs=jax.tree.map(whole, outs),
+        in_specs=[smem] * n_smem + specs(operands[n_smem:], in_along),
+        out_specs=specs(outs, out_along),
         scratch_shapes=list(scratch),
         compiler_params=pltpu.CompilerParams(vmem_limit_bytes=60 * MIB),
-        cost_estimate=pl.CostEstimate(flops=flops, bytes_accessed=moved, transcendentals=0),
+        cost_estimate=pl.CostEstimate(flops=flops, bytes_accessed=0, transcendentals=0),
     )(*operands)
 
 
@@ -481,101 +544,84 @@
     return lax.ppermute(value, axis, [(0, 1), (1, 0)])
 
 
-def strip_swaps(value, edges, tiles):
-    first = [(t, t ^ 1) for t in range(tiles)]
-    second = [(t, ((t + 1) ^ 1) - 1) for t in range(1, tiles - 1)]
-
-    def cross(pairs):
-        return [(2 * a + lev, 2 * b + 1 - lev) for a, b in pairs for lev in range(2)]
-
+def strip_swaps(near, far, edges, tiles):
+    pairs = [(tiles + t, t + 1) for t in range(tiles - 1)]
+    pairs += [(b, a) for a, b in pairs]
+    cross = [(2 * a + lev, 2 * b + 1 - lev) for a, b in pairs for lev in range(2)]
     return (
-        lax.ppermute(value, "tile", first),
-        lax.ppermute(value, "tile", second),
-        lax.ppermute(edges, ("tile", "lev"), cross(first)),
-        lax.ppermute(edges, ("tile", "lev"), cross(second)),
+        lax.ppermute(near, ("sec", "tile"), pairs),
+        lax.ppermute(far, ("sec", "tile"), pairs),
+        lax.ppermute(edges, ("sec", "tile", "lev"), cross),
     )
 
 
 def local(state, sound, target, edge_turn, w_first, b_first, w_second, w_third):
-    sec, lev = lax.axis_index("sec"), lax.axis_index("lev")
     tiles = lax.axis_size("tile")
     hid, feats = w_second.shape[0], 2 * GROUP
-    odd = lax.rem(lax.axis_index("tile"), 2) == 1
-    second_swap = (sec == 0) == odd
-
-    def by_group(weights):
-        weights = weights.reshape(3, 2, OWN, hid).transpose(1, 0, 2, 3).reshape(2, 3 * OWN, hid)
-        weights = jnp.pad(weights, ((0, 0), (0, PAD), (0, 0)))
-        weights = jnp.where(lev == 0, weights, weights[::-1])
-        return weights.reshape(feats, hid)
 
     state, sound, target = state.reshape(-1, 128), sound.reshape(-1, 128), target.reshape(-1, 128)
-    rows, edges, columns = call(
-        pack_kernel, 1, (edge_turn, state, sound),
-        (shape(4 * FIELD + 16, 128, dtype=BF), shape(4 * RIM, 128, dtype=BF), shape(BLK * GROUP + 4 * RIM, 128, dtype=BF)),
+    near, far, edges, columns, first, third_t = call(
+        pack_kernel, 1, (edge_turn, state, sound, w_first, w_third.T, b_first[None]),
+        (shape(4 * FIELD + 16, 128, dtype=BF), shape(4 * FIELD, 128, dtype=BF), shape(8 * RIM, 128, dtype=BF), shape(BLK * GROUP + 8 * RIM, 128, dtype=BF), shape(feats, hid, dtype=BF), shape(feats, hid, dtype=BF)),
     )
     own_col = swap(columns, "lev")
-    a, b, a_edge, b_edge = strip_swaps(rows, edges, tiles)
-
-    first, third_t = by_group(w_first), by_group(w_third.T)
+    near, far, rims = strip_swaps(near, far, edges, tiles)
+
+    activations = (shape(feats, COLS, dtype=BF), shape(hid, COLS, dtype=BF), shape(hid, COLS, dtype=BF), shape(hid, COLS), shape(hid, COLS))
     feat, one, two, slope_one, slope_two, tendency = call(
-        network_kernel, 0, (columns, own_col, first.T, b_first[:, None], w_second.T, third_t),
-        (shape(feats, COLS, dtype=BF), shape(hid, COLS, dtype=BF), shape(hid, COLS, dtype=BF), shape(hid, COLS), shape(hid, COLS), shape(3 * FIELD, 128)),
-    )
-
-    a, b, a_edge, b_edge, tendency = lax.optimization_barrier((a, b, a_edge, b_edge, tendency))
-    partner = swap(jnp.where(second_swap, b, a), "sec")
-    partner_edge = swap(jnp.where(second_swap, b_edge, a_edge), "sec")
-    other_col = swap(own_col, "sec")
+        network_kernel, 0, (columns, own_col, first, w_second, third_t),
+        (*activations, shape(3 * FIELD, 128)),
+        steps=COLS // STRIPE, flops=LONG, in_along=(0, 0, None, None, None), out_along=(1, 1, 1, 1, 1, None),
+    )
+
+    near, far, rims, tendency = lax.optimization_barrier((near, far, rims, tendency))
     resid, r_rows, r_edges, r_columns, coeff, factors = call(
         forward_kernel, 1,
-        (edge_turn, state, sound, target, tendency, a, b, a_edge, b_edge, partner, partner_edge, own_col, other_col),
+        (edge_turn, state, sound, target, tendency, near, far, swap(near, "sec"), rims, swap(rims, "sec"), own_col),
         (shape(3 * FIELD, 128), shape(3 * FIELD, 128, dtype=BF), shape(3 * RIM, 128, dtype=BF), shape(BLK * GROUP + 3 * RIM, 128, dtype=BF), shape(EXT, ROWS, 128), shape(4, BLK, 128)),
-        stencil_scratch(), moved=20_000_000,
+        stencil_scratch(), flops=LONG,
     )
 
     r_own_col = swap(r_columns, "lev")
     r_other = swap(resid, "sec")
-    r_a, r_b, r_a_edge, r_b_edge = strip_swaps(r_rows, r_edges, tiles)
-
-    r_own_col, r_a, r_b, r_a_edge, r_b_edge = lax.optimization_barrier((r_own_col, r_a, r_b, r_a_edge, r_b_edge))
+    both_edges = jnp.concatenate([r_edges, swap(r_edges, "sec")], axis=0)
+    r_near, r_far, r_rims = strip_swaps(r_rows, swap(r_rows, "sec"), both_edges, tiles)
+    (resid_cols,) = call(
+        gather_kernel, 0, (r_columns, r_own_col), (shape(feats, COLS, dtype=BF),), flops=LONG
+    )
+    resid_cols, r_near, r_far, r_rims = lax.optimization_barrier((resid_cols, r_near, r_far, r_rims))
 
     n_rows = 2 * feats + hid
-    resid_cols, err_one, err_two, given = call(
-        back_kernel, 0, (r_columns, r_own_col, feat, third_t.T, w_second, one, two, slope_one, slope_two),
-        (shape(feats, COLS, dtype=BF), shape(hid, COLS, dtype=BF), shape(hid, COLS, dtype=BF), shape(n_rows, 128)),
+    given, kept, input_grad = call(
+        back_kernel, 0, (resid_cols, feat, third_t, w_second, first, one, two, slope_one, slope_two),
+        (shape(n_rows, 128, dtype=BF), shape(n_rows, 128), shape(3 * FIELD, 128)),
+        (pltpu.VMEM((hid, STRIPE), BF), pltpu.VMEM((hid, STRIPE), BF), pltpu.VMEM((n_rows, 256), F32)),
+        flops=LONG, steps=COLS // STRIPE, in_along=(1, 1, None, None, None, 1, 1, 1, 1),
+    )
+    r_partner, r_partner_rims, r_other_col = swap(r_near, "sec"), swap(r_rims, "sec"), swap(r_own_col, "sec")
+    given, r_other, r_partner, r_partner_rims, r_other_col = lax.optimization_barrier(
+        (given, r_other, r_partner, r_partner_rims, r_other_col)
     )
     received = swap(given, "sec")
-    kept, input_grad = call(
-        kept_kernel, 0, (resid_cols, feat, first, one, two, err_one, err_two),
-        (shape(n_rows, 128), shape(3 * FIELD, 128)),
-    )
     share = n_rows // tiles
-    partial = (kept + received).astype(BF).reshape(tiles, share, 128)
+    partial = (kept + received.astype(F32)).astype(BF).reshape(tiles, share, 128)
     parts = lax.all_to_all(partial, "tile", 0, 0)
     total = jnp.sum(parts.astype(F32), axis=0) / (COLS * 2 * tiles)
-    everywhere = jnp.broadcast_to(total[None], (2 * tiles, share, 128))
+    (mine,) = call(
+        adjoint_kernel, 0,
+        (resid, r_other, input_grad, coeff, factors, r_near, r_far, r_partner, r_rims, r_partner_rims, r_own_col, r_other_col),
+        (shape(3 * FIELD, 128),), stencil_scratch((pltpu.VMEM((CHUNK, ROWS, 128), F32),)), flops=LONG,
+    )
+    total, mine = lax.optimization_barrier((total, mine))
+    everywhere = jnp.broadcast_to(total.astype(BF)[None], (2 * tiles, share, 128))
     gathered = lax.all_to_all(everywhere, ("tile", "lev"), 0, 0)
-
-    r_partner = swap(jnp.where(second_swap, r_b, r_a), "sec")
-    r_partner_edge = swap(jnp.where(second_swap, r_b_edge, r_a_edge), "sec")
-    r_other_col = swap(r_own_col, "sec")
-    mine = call(
-        adjoint_kernel, 0,
-        (resid, r_other, input_grad, coeff, factors, r_a, r_b, r_a_edge, r_b_edge, r_partner, r_partner_edge, r_own_col, r_other_col),
-        shape(3 * FIELD, 128), stencil_scratch((pltpu.VMEM((CHUNK, ROWS, 128), F32),)), moved=20_000_000,
-    )
-    mine, gathered = lax.optimization_barrier((mine, gathered))
-    theirs = swap(mine, "sec")
-    mine, theirs = mine.reshape(3, OWN, BLK, 128), theirs.reshape(3, OWN, BLK, 128)
-    state_grad = jnp.concatenate(
-        [jnp.where(sec == 0, mine, theirs), jnp.where(sec == 0, theirs, mine)], axis=2
-    )
+    (state_grad,) = call(place_rows_kernel, 0, (mine, swap(mine, "sec")), (shape(3, OWN, 2 * BLK, 128),))
+    state_grad, gathered = lax.optimization_barrier((state_grad, gathered))
     g_first, g_bias, g_second, g_third_t = call(
         spread_gradients_kernel, 0, (gathered, swap(gathered, "sec")),
-        (shape(6 * OWN, hid), shape(8, hid), shape(hid, hid), shape(6 * OWN, hid)),
-    )
-    return (state_grad, g_first, g_bias[0], g_second, g_third_t.T)
+        (shape(6 * OWN, hid), shape(1, hid), shape(hid, hid), shape(6 * OWN, hid)),
+    )
+    return (state_grad, g_first, g_bias.reshape(hid), g_second, g_third_t.T)
 
 
 def solution(mesh):

time: 134 us -> 120 us (0.90)
  blocking collectives: 17.3 us -> 0 us
  starting transfers between devices: 42.3 us -> 53.4 us
  local copies, waits for them, and re-layouts: 12.3 us -> 4.72 us
  waiting for transfers between devices: 14.9 us -> 17.4 us
  other arithmetic: 4.17 us -> 2.67 us
    all_to_all x1 -> x0, blocking collectives: 17.3 us -> none  [local(): parts = lax.all_to_all(partial, 'tile', 0, 0)]
    all_to_all x0 -> x1, starting transfers between devices: none -> 14.1 us  [local(): parts = lax.all_to_all(partial, 'tile', 0, 0)]
    ppermute x8 -> x6, starting transfers between devices: 22.5 us -> 19 us  [the longest x2 7.52 us: strip_swaps(): lax.ppermute(edges, ('sec', 'tile', 'lev'), cross)]
    ppermute x12 -> x13, waiting for transfers between devices: 9.74 us -> 6.31 us  [swap(): return lax.ppermute(value, axis, [(0, 1), (1, 0)])]
    ppermute x8 -> x6, waiting for transfers between devices: 1.62 us -> 4.89 us  [the longest x2 2.63 us: strip_swaps(): lax.ppermute(far, ('sec', 'tile'), pairs)]
    transpose x3 -> x0, local copies, waits for them, and re-layouts: 2.79 us -> none  [the longest x2 1.92 us: by_group(): weights.reshape(3, 2, OWN, hid).transpose(1, 0, 2, 3)]
    all_to_all x1, starting transfers between devices: 5.81 us -> 8.59 us  [local(): gathered = lax.all_to_all(everywhere, ('tile', 'lev'), 0, 0)]
    all_to_all x1, waiting for transfers between devices: 3.53 us -> 6.24 us  [local(): gathered = lax.all_to_all(everywhere, ('tile', 'lev'), 0, 0)]
  transfers between devices with their start and end apart: 21 -> 21, of which waited for: 8 -> 8; matrix products, arithmetic and copies ran while one was open for 6% -> 1% of each run, Pallas kernels for 15% -> 21%
where the time goes in v3:
time: 120 us; the launch traced here: 119 us
  starting transfers between devices  53.4 us (44%)
  Pallas kernels  39.9 us (33%)
  waiting for transfers between devices  17.4 us (14%)
  local copies, waits for them, and re-layouts  4.72 us (4%)
  other arithmetic  2.67 us (2%)
    pallas_call x8, Pallas kernels, call(): pl.pallas_call(kernel, grid=(steps,), out_shape=outs, in_specs=[smem] * n...  39.9 us
    all_to_all x1, starting transfers between devices, local(): parts = lax.all_to_all(partial, 'tile', 0, 0)  14.1 us
    ppermute x13, starting transfers between devices, swap(): return lax.ppermute(value, axis, [(0, 1), (1, 0)])  11.7 us
    all_to_all x1, starting transfers between devices, local(): gathered = lax.all_to_all(everywhere, ('tile', 'lev'), 0, 0)  8.59 us
    ppermute x2, starting transfers between devices, strip_swaps(): lax.ppermute(edges, ('sec', 'tile', 'lev'), cross)  7.52 us
    ppermute x2, starting transfers between devices, strip_swaps(): lax.ppermute(near, ('sec', 'tile'), pairs)  7.18 us
    ppermute x13, waiting for transfers between devices, swap(): return lax.ppermute(value, axis, [(0, 1), (1, 0)])  6.31 us
    all_to_all x1, waiting for transfers between devices, local(): gathered = lax.all_to_all(everywhere, ('tile', 'lev'), 0, 0)  6.24 us
  transfers between devices with their start and end apart: 21, of which 8 were waited for; matrix products, arithmetic and copies ran while one was open for 1% of the time, Pallas kernels for 21%

profile of v3, /device:TPU:1, one launch (start us, length us, event | category | flops | bytes accessed | tf_op | source)
XLA Modules:
  0.0 119.1 jit_solution(1363812989108512698)
XLA Ops:
  0.6 3.0 %shard_map.119 = (bf16[1296,128]{1,0:T(8,128)(2,1)}, bf16[1280,128]{1,0:T(8,128)(2,1)}, bf16[512,128]{1,0:T(8,128)(2,1)}, bf16[1536,128]{1,0:T(8,128)(2,1)}, bf1...) custom-call(s32[1,2]{1,0:T(1,128)} %turn_ref.3, f32[1920,128]{1,0:T(8,128)} %bitcast.8, f32[640,128]{1,0:T(8,128)} %bitcast.10, ...), custom_call_target="tpu_custom_call" | custom-call | tf_op jit(solution)/shard_map/pallas_call | solution.py:521
  3.6 3.8 %collective-permute-start.3 = (bf16[1536,128]{1,0:T(8,128)(2,1)}, bf16[1536,128]{1,0:T(8,128)(2,1)S(1)}, u32[]{:S(2)}, u32[]{:S(2)}) collective-permute-start(bf16[1536,128]{1,0:T(8,128)(2,1)} %get-tuple-element.50.own_ref), channel_id=1, source_target_pairs={{0,1},{1,0},{2,3},{3,2},{4,5},{5,4},{6,7},{7,6},{8,9},{9,8},{10,11... | collective-permute-start | bytes 1179656 | tf_op jit(solution)/shard_map/ppermute | solution.py:544
  7.4 4.1 %collective-permute-start.2 = (bf16[512,128]{1,0:T(8,128)(2,1)}, bf16[512,128]{1,0:T(8,128)(2,1)S(1)}, u32[]{:S(2)}, u32[]{:S(2)}) collective-permute-start(bf16[512,128]{1,0:T(8,128)(2,1)} %get-tuple-element.49), channel_id=1, source_target_pairs={{64,3},{65,2},{66,5},{67,4},{68,7},{69,6},{70,9},{71,8},{72,11},{7... | collective-permute-start | bytes 393224 | tf_op jit(solution)/shard_map/ppermute | solution.py:554
  11.5 2.2 %collective-permute-start.1 = (bf16[1280,128]{1,0:T(8,128)(2,1)}, bf16[1280,128]{1,0:T(8,128)(2,1)S(1)}, u32[]{:S(2)}, u32[]{:S(2)}) collective-permute-start(bf16[1280,128]{1,0:T(8,128)(2,1)} %get-tuple-element.48), channel_id=1, source_target_pairs={{64,2},{66,4},{68,6},{70,8},{72,10},{74,12},{76,14},{78,16},{80,18... | collective-permute-start | bytes 983048 | tf_op jit(solution)/shard_map/ppermute | solution.py:553
  13.7 3.4 %collective-permute-start = (bf16[1296,128]{1,0:T(8,128)(2,1)}, bf16[1296,128]{1,0:T(8,128)(2,1)S(1)}, u32[]{:S(2)}, u32[]{:S(2)}) collective-permute-start(bf16[1296,128]{1,0:T(8,128)(2,1)} %get-tuple-element.47), channel_id=1, source_target_pairs={{64,2},{66,4},{68,6},{70,8},{72,10},{74,12},{76,14},{78,16},{80,18... | collective-permute-start | bytes 995336 | tf_op jit(solution)/shard_map/ppermute | solution.py:552
  17.1 0.7 copy-done.4
  17.9 5.0 %shard_map.120 = (bf16[256,1024]{1,0:T(8,128)(2,1)}, bf16[512,1024]{1,0:T(8,128)(2,1)}, bf16[512,1024]{1,0:T(8,128)(2,1)}, f32[512,1024]{1,0:T(8,128)}, f32[512,1024]{1,0:T(8,128)}, /*index=5*/f32[960,128]{1,0:T(8,128)}) custom-call(bf16[1536,128]{1,0:T(8,128)(2,1)} %get-tuple-element.50.own_ref, bf16[1536,128]{1,0:T(8,128)(2,1)} %copy-done.4, ...), custom_call_target="tpu_custom_call" | custom-call | flops 20000000000 | tf_op jit(solution)/shard_map/pallas_call | solution.py:521
  22.9 0.0 collective-permute-done.2.rims
  22.9 0.0 collective-permute-done.1.far
  22.9 2.2 %collective-permute-done.near = bf16[1296,128]{1,0:T(8,128)(2,1)S(1)} collective-permute-done((bf16[1296,128]{1,0:T(8,128)(2,1)}, bf16[1296,128]{1,0:T(8,128)(2,1)S(1)}, u32[]{:S(2)}, u32[]{:S(2)}) %collective-permute-start) | collective-permute-done | bytes 331808 | tf_op jit(solution)/shard_map/ppermute | solution.py:552
  25.1 0.0 collective-permute-start.4
  25.1 0.5 collective-permute-start.5
  25.6 1.3 %collective-permute-done.5.partner_rims = bf16[512,128]{1,0:T(8,128)(2,1)S(1)} collective-permute-done((bf16[512,128]{1,0:T(8,128)(2,1)S(1)}, bf16[512,128]{1,0:T(8,128)(2,1)S(1)}, u32[]{:S(2)}, u32[]{:S(2)}) %collective-permute-start.5) | collective-permute-done | bytes 131104 | tf_op jit(solution)/shard_map/ppermute | solution.py:544
  27.0 0.6 copy-done.14
  27.6 0.1 copy-done.6
  27.7 9.8 %shard_map.121 = (f32[960,128]{1,0:T(8,128)}, bf16[960,128]{1,0:T(8,128)(2,1)}, bf16[192,128]{1,0:T(8,128)(2,1)}, bf16[1216,128]{1,0:T(8,128)(2,1)}, f32[48,56,128]{2,1,0:T(8,128)}, /*index=5*/f32[4,8,128]{2,1,0:T(8,128)}) custom-call(s32[1,2]{1,0:T(1,128)} %turn_ref.3, f32[1920,128]{1,0:T(8,128)} %bitcast.9, f32[640,128]{1,0:T(8,128)} %bitcast.11, ...), custom_call_target="tpu_custom_call" | custom-call | flops 20000000000 | tf_op jit(solution)/shard_map/pallas_call | solution.py:521
  37.5 3.0 %collective-permute-start.6 = (bf16[1216,128]{1,0:T(8,128)(2,1)}, bf16[1216,128]{1,0:T(8,128)(2,1)S(1)}, u32[]{:S(2)}, u32[]{:S(2)}) collective-permute-start(bf16[1216,128]{1,0:T(8,128)(2,1)} %get-tuple-element.58.own_ref), channel_id=1, source_target_pairs={{0,1},{1,0},{2,3},{3,2},{4,5},{5,4},{6,7},{7,6},{8,9},{9,8},{10,11... | collective-permute-start | bytes 933896 | tf_op jit(solution)/shard_map/ppermute | solution.py:544
  40.5 0.4 collective-permute-start.8
  40.8 0.1 collective-permute-start.10
  41.0 3.8 %collective-permute-start.7 = (bf16[960,128]{1,0:T(8,128)(2,1)}, bf16[960,128]{1,0:T(8,128)(2,1)S(1)}, u32[]{:S(2)}, u32[]{:S(2)}) collective-permute-start(bf16[960,128]{1,0:T(8,128)(2,1)} %get-tuple-element.59), channel_id=1, source_target_pairs={{64,2},{66,4},{68,6},{70,8},{72,10},{74,12},{76,14},{78,16},{80,18... | collective-permute-start | bytes 737288 | tf_op jit(solution)/shard_map/ppermute | solution.py:552
  44.8 0.1 collective-permute-start.12
  44.9 0.8 pad_maximum_fusion
  45.7 3.4 %collective-permute-start.11 = (bf16[384,128]{1,0:T(8,128)(2,1)S(1)}, bf16[384,128]{1,0:T(8,128)(2,1)S(1)}, u32[]{:S(2)}, u32[]{:S(2)}) collective-permute-start(bf16[384,128]{1,0:T(8,128)(2,1)S(1)} %pad_maximum_fusion), channel_id=1, source_target_pairs={{64,3},{65,2},{66,5},{67,4},{68,7},{69,6},{70,9},{71,8},{72,11},{7... | collective-permute-start | bytes 294920 | tf_op jit(solution)/shard_map/ppermute | solution.py:554
  49.1 2.2 %collective-permute-start.9 = (bf16[960,128]{1,0:T(8,128)(2,1)S(1)}, bf16[960,128]{1,0:T(8,128)(2,1)S(1)}, u32[]{:S(2)}, u32[]{:S(2)}) collective-permute-start(bf16[960,128]{1,0:T(8,128)(2,1)S(1)} %collective-permute-done.8), channel_id=1, source_target_pairs={{64,2},{66,4},{68,6},{70,8},{72,10},{74,12},{76,14},{78,16},{80,18... | collective-permute-start | bytes 737288 | tf_op jit(solution)/shard_map/ppermute | solution.py:553
  51.3 0.7 copy-done.8
  52.0 1.9 %shard_map.122.resid_ref = bf16[256,1024]{1,0:T(8,128)(2,1)} custom-call(bf16[1216,128]{1,0:T(8,128)(2,1)} %get-tuple-element.58.own_ref, bf16[1216,128]{1,0:T(8,128)(2,1)} %copy-done.8), custom_call_target="tpu_custom_call" | custom-call | flops 20000000000 | tf_op jit(solution)/shard_map/pallas_call | solution.py:521
  53.9 0.1 collective-permute-done.11.rims
  54.0 2.6 %collective-permute-done.9.far = bf16[960,128]{1,0:T(8,128)(2,1)S(1)} collective-permute-done((bf16[960,128]{1,0:T(8,128)(2,1)S(1)}, bf16[960,128]{1,0:T(8,128)(2,1)S(1)}, u32[]{:S(2)}, u32[]{:S(2)}) %collective-permute-start.9) | collective-permute-done | bytes 245792 | tf_op jit(solution)/shard_map/ppermute | solution.py:553
  56.6 0.5 collective-permute-start.13
  57.1 6.5 %shard_map.123 = (bf16[1024,128]{1,0:T(8,128)(2,1)}, f32[1024,128]{1,0:T(8,128)}, f32[960,128]{1,0:T(8,128)}) custom-call(bf16[256,1024]{1,0:T(8,128)(2,1)} %shard_map.122.resid_ref, bf16[256,1024]{1,0:T(8,128)(2,1)} %get-tuple-element.62.feat_ref, bf16[256,512]{1,0:T(8,128)(2,1)} %get-tuple-element.52.third_t_ref, bf16[512,512]{1,0:T(8,128)(2,1)} %second_ref.3, ...), custom_call_target="tpu_custom_call" | custom-call | flops 20000000000 | tf_op jit(solution)/shard_map/pallas_call | solution.py:521
  63.7 0.0 copy-start.3
  63.7 0.0 copy-start.9
  63.7 0.1 collective-permute-start.16
  63.8 1.7 %collective-permute-done.16 = bf16[1024,128]{1,0:T(8,128)(2,1)S(1)} collective-permute-done((bf16[1024,128]{1,0:T(8,128)(2,1)}, bf16[1024,128]{1,0:T(8,128)(2,1)S(1)}, u32[]{:S(2)}, u32[]{:S(2)}) %collective-permute-start.16) | collective-permute-done | bytes 262176 | tf_op jit(solution)/shard_map/ppermute | solution.py:544
  65.6 1.8 %add_convert_fusion = bf16[1024,128]{1,0:T(8,128)(2,1)} fusion(f32[1024,128]{1,0:T(8,128)} %get-tuple-element.67, bf16[1024,128]{1,0:T(8,128)(2,1)S(1)} %collective-permute-done.16), kind=kLoop, calls=%fused_computation.1 | loop fusion | flops 393216 | bytes 1048576 | tf_op jit(solution)/shard_map/convert_element_type | solution.py:607
  67.4 14.1 %all-to-all-start = ((bf16[32,32,128]{2,1,0:T(8,128)(2,1)}), bf16[32,32,128]{2,1,0:T(8,128)(2,1)S(1)}, u32[]{:S(2)}, u32[]{:S(2)}) async-start(bf16[32,32,128]{2,1,0:T(8,128)(2,1)} %bitcast.5), calls=%async_computation | async-start | bytes 524288 | tf_op jit(solution)/shard_map/all_to_all | solution.py:608
  81.5 8.8 %shard_map.124.mine_ref = f32[960,128]{1,0:T(8,128)} custom-call(f32[960,128]{1,0:T(8,128)} %get-tuple-element.69.resid_ref, f32[960,128]{1,0:T(8,128)} %copy-done.3, f32[960,128]{1,0:T(8,128)} %get-tuple-element.74.input_grad_ref, f32[48,56,128]{2,1,0:T(8,128)} %get-tuple-element.75.c_ref, f32[4,8,128]{2,1,0:T(8,128)} %get-tuple-element.76.factor_ref, ...), custom_call_target="tpu_custom_call" | custom-call | flops 20000000000 | tf_op jit(solution)/shard_map/pallas_call | solution.py:521
  90.4 0.9 broadcast_in_dim.10
  91.3 8.6 %all-to-all-start.1 = ((bf16[64,32,128]{2,1,0:T(8,128)(2,1)}), bf16[64,32,128]{2,1,0:T(8,128)(2,1)S(1)}, u32[]{:S(2)}, u32[]{:S(2)}) async-start(bf16[64,32,128]{2,1,0:T(8,128)(2,1)} %broadcast_in_dim.10), calls=%async_computation.1 | async-start | bytes 1048576 | tf_op jit(solution)/shard_map/all_to_all | solution.py:617
  99.9 1.1 collective-permute-start.17
  101.0 1.7 %collective-permute-done.17.theirs_ref = f32[960,128]{1,0:T(8,128)S(1)} collective-permute-done((f32[960,128]{1,0:T(8,128)}, f32[960,128]{1,0:T(8,128)S(1)}, u32[]{:S(2)}, u32[]{:S(2)}) %collective-permute-start.17) | collective-permute-done | bytes 491552 | tf_op jit(solution)/shard_map/ppermute | solution.py:544
  102.7 0.8 copy-done.2
  103.4 2.2 %shard_map.125 = f32[3,40,16,128]{3,2,1,0:T(8,128)} custom-call(f32[960,128]{1,0:T(8,128)} %shard_map.124.mine_ref, f32[960,128]{1,0:T(8,128)} %copy-done.2), custom_call_target="tpu_custom_call" | custom-call | tf_op jit(solution)/shard_map/pallas_call | solution.py:521
  105.6 6.2 %all-to-all-done.1.own_ref = bf16[64,32,128]{2,1,0:T(8,128)(2,1)S(1)} async-done(((bf16[64,32,128]{2,1,0:T(8,128)(2,1)}), bf16[64,32,128]{2,1,0:T(8,128)(2,1)S(1)}, u32[]{:S(2)}, u32[]{:S(2)}) %all-to-all-start.1) | async-done | bytes 524320 | tf_op jit(solution)/shard_map/all_to_all | solution.py:617
  111.9 2.2 %collective-permute-start.18 = (bf16[64,32,128]{2,1,0:T(8,128)(2,1)S(1)}, bf16[64,32,128]{2,1,0:T(8,128)(2,1)S(1)}, u32[]{:S(2)}, u32[]{:S(2)}) collective-permute-start(bf16[64,32,128]{2,1,0:T(8,128)(2,1)S(1)} %all-to-all-done.1.own_ref), channel_id=1, source_target_pairs={{0,64},{64,0},{1,65},{65,1},{2,66},{66,2},{3,67},{67,3},{4,68},{68... | collective-permute-start | bytes 1572872 | tf_op jit(solution)/shard_map/ppermute | solution.py:544
  114.1 1.5 %collective-permute-done.18.partner_ref = bf16[64,32,128]{2,1,0:T(8,128)(2,1)S(1)} collective-permute-done((bf16[64,32,128]{2,1,0:T(8,128)(2,1)S(1)}, bf16[64,32,128]{2,1,0:T(8,128)(2,1)S(1)}, u32[]{:S(2)}, u32[]{:S(2)}) %collective-permute-start.18) | collective-permute-done | bytes 524320 | tf_op jit(solution)/shard_map/ppermute | solution.py:544
  115.6 0.8 copy-done.1
  116.5 2.6 %shard_map.126 = (f32[240,512]{1,0:T(8,128)}, f32[1,512]{1,0:T(1,128)}, f32[512,512]{1,0:T(8,128)}, f32[240,512]{1,0:T(8,128)}) custom-call(bf16[64,32,128]{2,1,0:T(8,128)(2,1)} %copy-done, bf16[64,32,128]{2,1,0:T(8,128)(2,1)} %copy-done.1), custom_call_target="tpu_custom_call" | custom-call | tf_op jit(solution)/shard_map/pallas_call | solution.py:521
  (41 shorter events, 0.1 us)
Async XLA Ops:
  3.6 13.5 %collective-permute-start.3 = (bf16[1536,128]{1,0:T(8,128)(2,1)}, bf16[1536,128]{1,0:T(8,128)(2,1)S(1)}, u32[]{:S(2)}, u32[]{:S(2)}) collective-permute-start(bf16[1536,128]{1,0:T(8,128)(2,1)} %get-tuple-element.50.own_ref), channel_id=1, source_target_pairs={{0,1},{1,0},{2,3},{3,2},{4,5},{5,4},{6,7},{7,6},{8,9},{9,8},{10,11... | collective-permute-start | bytes 1179656 | tf_op jit(solution)/shard_map/ppermute | solution.py:544
  7.4 15.5 %collective-permute-start.2 = (bf16[512,128]{1,0:T(8,128)(2,1)}, bf16[512,128]{1,0:T(8,128)(2,1)S(1)}, u32[]{:S(2)}, u32[]{:S(2)}) collective-permute-start(bf16[512,128]{1,0:T(8,128)(2,1)} %get-tuple-element.49), channel_id=1, source_target_pairs={{64,3},{65,2},{66,5},{67,4},{68,7},{69,6},{70,9},{71,8},{72,11},{7... | collective-permute-start | bytes 393224 | tf_op jit(solution)/shard_map/ppermute | solution.py:554
  11.5 11.4 %collective-permute-start.1 = (bf16[1280,128]{1,0:T(8,128)(2,1)}, bf16[1280,128]{1,0:T(8,128)(2,1)S(1)}, u32[]{:S(2)}, u32[]{:S(2)}) collective-permute-start(bf16[1280,128]{1,0:T(8,128)(2,1)} %get-tuple-element.48), channel_id=1, source_target_pairs={{64,2},{66,4},{68,6},{70,8},{72,10},{74,12},{76,14},{78,16},{80,18... | collective-permute-start | bytes 983048 | tf_op jit(solution)/shard_map/ppermute | solution.py:553
  13.7 11.4 %collective-permute-start = (bf16[1296,128]{1,0:T(8,128)(2,1)}, bf16[1296,128]{1,0:T(8,128)(2,1)S(1)}, u32[]{:S(2)}, u32[]{:S(2)}) collective-permute-start(bf16[1296,128]{1,0:T(8,128)(2,1)} %get-tuple-element.47), channel_id=1, source_target_pairs={{64,2},{66,4},{68,6},{70,8},{72,10},{74,12},{76,14},{78,16},{80,18... | collective-permute-start | bytes 995336 | tf_op jit(solution)/shard_map/ppermute | solution.py:552
  17.1 0.7 copy-start.4
  22.9 4.0 %copy-start.13 = (bf16[512,128]{1,0:T(8,128)(2,1)}, bf16[512,128]{1,0:T(8,128)(2,1)S(1)}, u32[]{:S(2)}) copy-start(bf16[512,128]{1,0:T(8,128)(2,1)S(1)} %collective-permute-done.2.rims) | copy-start | bytes 393220
  22.9 4.0 %copy-start.7 = (bf16[1280,128]{1,0:T(8,128)(2,1)}, bf16[1280,128]{1,0:T(8,128)(2,1)S(1)}, u32[]{:S(2)}) copy-start(bf16[1280,128]{1,0:T(8,128)(2,1)S(1)} %collective-permute-done.1.far) | copy-start | bytes 983044
  25.1 1.9 %copy-start.5 = (bf16[1296,128]{1,0:T(8,128)(2,1)}, bf16[1296,128]{1,0:T(8,128)(2,1)S(1)}, u32[]{:S(2)}) copy-start(bf16[1296,128]{1,0:T(8,128)(2,1)S(1)} %collective-permute-done.near) | copy-start | bytes 995332
  25.1 1.8 %collective-permute-start.4 = (bf16[1296,128]{1,0:T(8,128)(2,1)S(1)}, bf16[1296,128]{1,0:T(8,128)(2,1)S(1)}, u32[]{:S(2)}, u32[]{:S(2)}) collective-permute-start(bf16[1296,128]{1,0:T(8,128)(2,1)S(1)} %collective-permute-done.near), channel_id=1, source_target_pairs={{0,64},{64,0},{1,65},{65,1},{2,66},{66,2},{3,67},{67,3},{4,68},{68... | collective-permute-start | bytes 995336 | tf_op jit(solution)/shard_map/ppermute | solution.py:544
  25.1 1.8 %collective-permute-start.5 = (bf16[512,128]{1,0:T(8,128)(2,1)S(1)}, bf16[512,128]{1,0:T(8,128)(2,1)S(1)}, u32[]{:S(2)}, u32[]{:S(2)}) collective-permute-start(bf16[512,128]{1,0:T(8,128)(2,1)S(1)} %collective-permute-done.2.rims), channel_id=1, source_target_pairs={{0,64},{64,0},{1,65},{65,1},{2,66},{66,2},{3,67},{67,3},{4,68},{68... | collective-permute-start | bytes 393224 | tf_op jit(solution)/shard_map/ppermute | solution.py:544
  26.9 0.7 copy-start.14
  26.9 0.8 copy-start.6
  37.5 13.7 %collective-permute-start.6 = (bf16[1216,128]{1,0:T(8,128)(2,1)}, bf16[1216,128]{1,0:T(8,128)(2,1)S(1)}, u32[]{:S(2)}, u32[]{:S(2)}) collective-permute-start(bf16[1216,128]{1,0:T(8,128)(2,1)} %get-tuple-element.58.own_ref), channel_id=1, source_target_pairs={{0,1},{1,0},{2,3},{3,2},{4,5},{5,4},{6,7},{7,6},{8,9},{9,8},{10,11... | collective-permute-start | bytes 933896 | tf_op jit(solution)/shard_map/ppermute | solution.py:544
  40.5 8.6 %collective-permute-start.8 = (bf16[960,128]{1,0:T(8,128)(2,1)}, bf16[960,128]{1,0:T(8,128)(2,1)S(1)}, u32[]{:S(2)}, u32[]{:S(2)}) collective-permute-start(bf16[960,128]{1,0:T(8,128)(2,1)} %get-tuple-element.59), channel_id=1, source_target_pairs={{0,64},{64,0},{1,65},{65,1},{2,66},{66,2},{3,67},{67,3},{4,68},{68... | collective-permute-start | bytes 737288 | tf_op jit(solution)/shard_map/ppermute | solution.py:544
  40.8 4.0 %collective-permute-start.10 = (bf16[192,128]{1,0:T(8,128)(2,1)}, bf16[192,128]{1,0:T(8,128)(2,1)S(1)}, u32[]{:S(2)}, u32[]{:S(2)}) collective-permute-start(bf16[192,128]{1,0:T(8,128)(2,1)} %get-tuple-element.60), channel_id=1, source_target_pairs={{0,64},{64,0},{1,65},{65,1},{2,66},{66,2},{3,67},{67,3},{4,68},{68... | collective-permute-start | bytes 147464 | tf_op jit(solution)/shard_map/ppermute | solution.py:544
  41.0 13.0 %collective-permute-start.7 = (bf16[960,128]{1,0:T(8,128)(2,1)}, bf16[960,128]{1,0:T(8,128)(2,1)S(1)}, u32[]{:S(2)}, u32[]{:S(2)}) collective-permute-start(bf16[960,128]{1,0:T(8,128)(2,1)} %get-tuple-element.59), channel_id=1, source_target_pairs={{64,2},{66,4},{68,6},{70,8},{72,10},{74,12},{76,14},{78,16},{80,18... | collective-permute-start | bytes 737288 | tf_op jit(solution)/shard_map/ppermute | solution.py:552
  44.8 18.9 %collective-permute-start.12 = (f32[960,128]{1,0:T(8,128)}, f32[960,128]{1,0:T(8,128)S(1)}, u32[]{:S(2)}, u32[]{:S(2)}) collective-permute-start(f32[960,128]{1,0:T(8,128)} %get-tuple-element.69.resid_ref), channel_id=1, source_target_pairs={{0,64},{64,0},{1,65},{65,1},{2,66},{66,2},{3,67},{67,3},{4,68},{68... | collective-permute-start | bytes 1474568 | tf_op jit(solution)/shard_map/ppermute | solution.py:544
  45.7 8.3 %collective-permute-start.11 = (bf16[384,128]{1,0:T(8,128)(2,1)S(1)}, bf16[384,128]{1,0:T(8,128)(2,1)S(1)}, u32[]{:S(2)}, u32[]{:S(2)}) collective-permute-start(bf16[384,128]{1,0:T(8,128)(2,1)S(1)} %pad_maximum_fusion), channel_id=1, source_target_pairs={{64,3},{65,2},{66,5},{67,4},{68,7},{69,6},{70,9},{71,8},{72,11},{7... | collective-permute-start | bytes 294920 | tf_op jit(solution)/shard_map/ppermute | solution.py:554
  49.1 7.6 %collective-permute-start.9 = (bf16[960,128]{1,0:T(8,128)(2,1)S(1)}, bf16[960,128]{1,0:T(8,128)(2,1)S(1)}, u32[]{:S(2)}, u32[]{:S(2)}) collective-permute-start(bf16[960,128]{1,0:T(8,128)(2,1)S(1)} %collective-permute-done.8), channel_id=1, source_target_pairs={{64,2},{66,4},{68,6},{70,8},{72,10},{74,12},{76,14},{78,16},{80,18... | collective-permute-start | bytes 737288 | tf_op jit(solution)/shard_map/ppermute | solution.py:553
  51.3 0.7 copy-start.8
  53.9 9.8 %collective-permute-start.15 = (bf16[1216,128]{1,0:T(8,128)(2,1)}, bf16[1216,128]{1,0:T(8,128)(2,1)S(1)}, u32[]{:S(2)}, u32[]{:S(2)}) collective-permute-start(bf16[1216,128]{1,0:T(8,128)(2,1)} %copy-done.8), channel_id=1, source_target_pairs={{0,64},{64,0},{1,65},{65,1},{2,66},{66,2},{3,67},{67,3},{4,68},{68... | collective-permute-start | bytes 933896 | tf_op jit(solution)/shard_map/ppermute | solution.py:544
  54.0 9.6 %copy-start.15 = (bf16[384,128]{1,0:T(8,128)(2,1)}, bf16[384,128]{1,0:T(8,128)(2,1)S(1)}, u32[]{:S(2)}) copy-start(bf16[384,128]{1,0:T(8,128)(2,1)S(1)} %collective-permute-done.11.rims) | copy-start | bytes 294916
  54.0 9.6 %copy-start.10 = (bf16[960,128]{1,0:T(8,128)(2,1)}, bf16[960,128]{1,0:T(8,128)(2,1)S(1)}, u32[]{:S(2)}) copy-start(bf16[960,128]{1,0:T(8,128)(2,1)S(1)} %collective-permute-done.7.near) | copy-start | bytes 737284
  56.6 7.0 %copy-start.11 = (bf16[960,128]{1,0:T(8,128)(2,1)}, bf16[960,128]{1,0:T(8,128)(2,1)S(1)}, u32[]{:S(2)}) copy-start(bf16[960,128]{1,0:T(8,128)(2,1)S(1)} %collective-permute-done.9.far) | copy-start | bytes 737284
  56.6 7.0 %collective-permute-start.14 = (bf16[384,128]{1,0:T(8,128)(2,1)S(1)}, bf16[384,128]{1,0:T(8,128)(2,1)S(1)}, u32[]{:S(2)}, u32[]{:S(2)}) collective-permute-start(bf16[384,128]{1,0:T(8,128)(2,1)S(1)} %collective-permute-done.11.rims), channel_id=1, source_target_pairs={{0,64},{64,0},{1,65},{65,1},{2,66},{66,2},{3,67},{67,3},{4,68},{68... | collective-permute-start | bytes 294920 | tf_op jit(solution)/shard_map/ppermute | solution.py:544
  56.6 7.1 %collective-permute-start.13 = (bf16[960,128]{1,0:T(8,128)(2,1)S(1)}, bf16[960,128]{1,0:T(8,128)(2,1)S(1)}, u32[]{:S(2)}, u32[]{:S(2)}) collective-permute-start(bf16[960,128]{1,0:T(8,128)(2,1)S(1)} %collective-permute-done.7.near), channel_id=1, source_target_pairs={{0,64},{64,0},{1,65},{65,1},{2,66},{66,2},{3,67},{67,3},{4,68},{68... | collective-permute-start | bytes 737288 | tf_op jit(solution)/shard_map/ppermute | solution.py:544
  63.7 17.8 %copy-start.3 = (f32[960,128]{1,0:T(8,128)}, f32[960,128]{1,0:T(8,128)S(1)}, u32[]{:S(2)}) copy-start(f32[960,128]{1,0:T(8,128)S(1)} %collective-permute-done.12.other_ref) | copy-start | bytes 1474564
  63.7 17.8 %copy-start.16 = (bf16[384,128]{1,0:T(8,128)(2,1)}, bf16[384,128]{1,0:T(8,128)(2,1)S(1)}, u32[]{:S(2)}) copy-start(bf16[384,128]{1,0:T(8,128)(2,1)S(1)} %collective-permute-done.14.partner_rims) | copy-start | bytes 294916
  63.7 17.8 %copy-start.9 = (bf16[1216,128]{1,0:T(8,128)(2,1)}, bf16[1216,128]{1,0:T(8,128)(2,1)S(1)}, u32[]{:S(2)}) copy-start(bf16[1216,128]{1,0:T(8,128)(2,1)S(1)} %collective-permute-done.15.other_col) | copy-start | bytes 933892
  63.7 17.8 %copy-start.12 = (bf16[960,128]{1,0:T(8,128)(2,1)}, bf16[960,128]{1,0:T(8,128)(2,1)S(1)}, u32[]{:S(2)}) copy-start(bf16[960,128]{1,0:T(8,128)(2,1)S(1)} %collective-permute-done.13.partner) | copy-start | bytes 737284
  63.7 1.8 %collective-permute-start.16 = (bf16[1024,128]{1,0:T(8,128)(2,1)}, bf16[1024,128]{1,0:T(8,128)(2,1)S(1)}, u32[]{:S(2)}, u32[]{:S(2)}) collective-permute-start(bf16[1024,128]{1,0:T(8,128)(2,1)} %get-tuple-element.72), channel_id=1, source_target_pairs={{0,64},{64,0},{1,65},{65,1},{2,66},{66,2},{3,67},{67,3},{4,68},{68... | collective-permute-start | bytes 786440 | tf_op jit(solution)/shard_map/ppermute | solution.py:544
  67.4 23.0 %all-to-all-start = ((bf16[32,32,128]{2,1,0:T(8,128)(2,1)}), bf16[32,32,128]{2,1,0:T(8,128)(2,1)S(1)}, u32[]{:S(2)}, u32[]{:S(2)}) async-start(bf16[32,32,128]{2,1,0:T(8,128)(2,1)} %bitcast.5), calls=%async_computation | async-start | bytes 524288 | tf_op jit(solution)/shard_map/all_to_all | solution.py:608
  91.3 20.6 %all-to-all-start.1 = ((bf16[64,32,128]{2,1,0:T(8,128)(2,1)}), bf16[64,32,128]{2,1,0:T(8,128)(2,1)S(1)}, u32[]{:S(2)}, u32[]{:S(2)}) async-start(bf16[64,32,128]{2,1,0:T(8,128)(2,1)} %broadcast_in_dim.10), calls=%async_computation.1 | async-start | bytes 1048576 | tf_op jit(solution)/shard_map/all_to_all | solution.py:617
  99.9 2.8 %collective-permute-start.17 = (f32[960,128]{1,0:T(8,128)}, f32[960,128]{1,0:T(8,128)S(1)}, u32[]{:S(2)}, u32[]{:S(2)}) collective-permute-start(f32[960,128]{1,0:T(8,128)} %shard_map.124.mine_ref), channel_id=1, source_target_pairs={{0,64},{64,0},{1,65},{65,1},{2,66},{66,2},{3,67},{67,3},{4,68},{68... | collective-permute-start | bytes 1474568 | tf_op jit(solution)/shard_map/ppermute | solution.py:544
  102.7 0.8 copy-start.2
  111.9 3.8 %copy-start = (bf16[64,32,128]{2,1,0:T(8,128)(2,1)}, bf16[64,32,128]{2,1,0:T(8,128)(2,1)S(1)}, u32[]{:S(2)}) copy-start(bf16[64,32,128]{2,1,0:T(8,128)(2,1)S(1)} %all-to-all-done.1.own_ref) | copy-start | bytes 1572868
  111.9 3.8 %collective-permute-start.18 = (bf16[64,32,128]{2,1,0:T(8,128)(2,1)S(1)}, bf16[64,32,128]{2,1,0:T(8,128)(2,1)S(1)}, u32[]{:S(2)}, u32[]{:S(2)}) collective-permute-start(bf16[64,32,128]{2,1,0:T(8,128)(2,1)S(1)} %all-to-all-done.1.own_ref), channel_id=1, source_target_pairs={{0,64},{64,0},{1,65},{65,1},{2,66},{66,2},{3,67},{67,3},{4,68},{68... | collective-permute-start | bytes 1572872 | tf_op jit(solution)/shard_map/ppermute | solution.py:544
  115.6 0.8 copy-start.1

commit v4 on v3

--- a/solution.py
+++ b/solution.py
@@ -15,11 +15,11 @@
 EDGE = 8
 EXT = OWN + EDGE
 ROWS = 7 * BLK
-CHUNK = 24
 WIND_BLOCKS = ((0, 5), (0, 5), (1, 4), (1, 4))
 MASS_BLOCKS = ((0, 5), (1, 4), (1, 4), (2, 3))
 FIELD = OWN * BLK
 RIM = EDGE * BLK
+NEAR_EDGE, FAR_EDGE = 6, 2
 COLS = BLK * 128
 GROUP = 128
 PAD = GROUP - 3 * OWN
@@ -57,11 +57,11 @@
     return 8.0 * (take(1) - take(-1)) - (take(2) - take(-2))
 
 
-def vertical(ref, k, row):
-    v = ref[pl.ds(k, CHUNK + 4), row : row + BLK, :]
-    near = v[3 : 3 + CHUNK] + v[1 : 1 + CHUNK]
-    far = v[4 : 4 + CHUNK] + v[0:CHUNK]
-    return (1.0 - 30.0 * UNIT * DIFFUSION) * v[2 : 2 + CHUNK] + (UNIT * DIFFUSION) * (16.0 * near - far)
+def vertical(ref, k, size, row):
+    v = ref[pl.ds(k, size + 4), row : row + BLK, :]
+    near = v[3 : 3 + size] + v[1 : 1 + size]
+    far = v[4 : 4 + size] + v[0:size]
+    return (1.0 - 30.0 * UNIT * DIFFUSION) * v[2 : 2 + size] + (UNIT * DIFFUSION) * (16.0 * near - far)
 
 
 def edge_masks():
@@ -109,29 +109,44 @@
         dst[pl.ds(level + 2 * i, 2), row : row + BLK, :] = rows.reshape(2, BLK, 128)
         return 0
 
-    lax.fori_loop(0, count // 2, body, 0, unroll=4)
+    if count > EDGE:
+        lax.fori_loop(0, count // 2, body, 0, unroll=20)
+    else:
+        for i in range(count // 2):
+            body(i, 0)
+
+
+def spread_column_edge(columns, n, dst, level, row, lev, scale=None):
+    if n == 3:
+        spread(columns, BLK * GROUP, EDGE, dst, level, row, scale)
+        return
+    skip = n * OWN % 16
+    for r in range(BLK):
+        start = pl.multiple_of(r * GROUP + n * OWN - skip + (OWN - EDGE) * lev, 16)
+        values = columns[pl.ds(start, 16), :].astype(F32)
+        dst[pl.ds(level, EDGE), row + r, :] = values[skip : skip + EDGE, :]
 
 
 def static_rows(sec):
     return 32 - 16 * sec, 24 + 8 * sec, 40 - 24 * sec
 
 
-def spread_rims(sec, lev, near, far, partner, rims, partner_rims, own_edge, other_edge, fields):
+def spread_rims(sec, lev, strip, partner, rims, partner_rims, own_col, other_col, fields):
     own_level, edge_level = EDGE * lev, OWN * (1 - lev)
     count = len(fields)
-    rows = (8, 16, 40) if sec == 0 else (40, 32, 8)
-    sources = ((far, rims, count * RIM, rows[0]), (near, rims, 0, rows[1]), (partner, partner_rims, 0, rows[2]))
+    far_start = strip.shape[0] - count * FIELD
+    far_row, near_row, partner_row = (8, 16, 40) if sec == 0 else (40, 32, 8)
+    near_level, far_level = edge_level + (EDGE - NEAR_EDGE) * lev, edge_level + (EDGE - FAR_EDGE) * lev
     for n, (dst, shift, scale) in enumerate(fields):
-        for src, edge, start, row in sources:
-            spread(src, n * FIELD, OWN, dst, own_level + shift, row, scale)
-            spread(edge, start + n * RIM, EDGE, dst, edge_level + shift, row, scale)
-        for (edge, start), row in ((own_edge, 3 * BLK), (other_edge, static_rows(sec)[0])):
-            spread(edge, start + n * RIM, EDGE, dst, edge_level + shift, row, scale)
-
-
-def chunk_range(step, lev):
-    trim = 2 * step // CHUNK
-    return trim * lev, EXT // CHUNK - trim * (1 - lev)
+        dst[pl.ds(edge_level + shift, EDGE), :, :] = jnp.zeros((EDGE, ROWS, 128), F32)
+        spread(strip, far_start + n * FIELD, OWN, dst, own_level + shift, far_row, scale)
+        spread(strip, n * FIELD, OWN, dst, own_level + shift, near_row, scale)
+        spread(partner, n * FIELD, OWN, dst, own_level + shift, partner_row, scale)
+        spread(rims, n * RIM, NEAR_EDGE, dst, near_level + shift, near_row, scale)
+        spread(partner_rims, n * RIM, NEAR_EDGE, dst, near_level + shift, partner_row, scale)
+        spread(rims, n * RIM + NEAR_EDGE * BLK, FAR_EDGE, dst, far_level + shift, far_row, scale)
+        for columns, row in ((own_col, 3 * BLK), (other_col, static_rows(sec)[0])):
+            spread_column_edge(columns, n, dst, edge_level + shift, row, lev, scale)
 
 
 def column_rows(ref, row, start, stride, step, fill):
@@ -161,42 +176,50 @@
         pl.when(lev == group)(run)
 
 
+def corner(edge_ref, n, near_ref, near, far_ref, far, lev):
+    for src, start, at, levels in ((near_ref, near, 0, NEAR_EDGE), (far_ref, far, NEAR_EDGE, FAR_EDGE)):
+        rows = pl.ds(pl.multiple_of(start + (OWN - levels) * BLK * (1 - lev), 16), levels * BLK)
+        edge_ref[n * RIM + at * BLK : n * RIM + (at + levels) * BLK, :] = src[rows, :]
+
+
 def pack_kernel(
     turn_ref, state_ref, sound_ref, first_ref, third_t_ref, bias_ref,
-    near_ref, far_ref, edge_ref, column_ref, first_out_ref, third_out_ref,
+    strip_ref, edge_ref, column_ref, first_out_ref, third_out_ref,
 ):
     sec, lev = lax.axis_index("sec"), lax.axis_index("lev")
     by_group(first_out_ref, first_ref, lev, bias_ref)
     by_group(third_out_ref, third_t_ref, lev)
+    far_start = 4 * FIELD + 16
     for half in range(2):
 
         def run(half=half):
             for n in range(4):
                 src = state_ref[n * OWN * 16 : (n + 1) * OWN * 16, :] if n < 3 else sound_ref[...]
-                for out, block in ((near_ref, half), (far_ref, 1 - half)):
+                for at, block in ((n * FIELD, half), (far_start + n * FIELD, 1 - half)):
                     field = src.reshape(OWN, 16, 128)[:, block * BLK : block * BLK + BLK, :]
-                    out[n * FIELD : (n + 1) * FIELD, :] = field.reshape(FIELD, 128).astype(BF)
+                    strip_ref[at : at + FIELD, :] = field.reshape(FIELD, 128).astype(BF)
             for r in range(BLK):
                 features = column_rows(state_ref, r, BLK * half, 16, OWN * 16, 1.0)
                 column_ref[r * GROUP : (r + 1) * GROUP, :] = features
 
         pl.when(sec == half)(run)
     for n in range(4):
-        start = pl.multiple_of(n * FIELD + (FIELD - RIM) * (1 - lev), 16)
-        edge_ref[n * RIM : (n + 1) * RIM, :] = near_ref[pl.ds(start, RIM), :]
-        edge_ref[(4 + n) * RIM : (5 + n) * RIM, :] = far_ref[pl.ds(start, RIM), :]
-    column_ref[BLK * GROUP :, :] = edge_ref[...]
+        near, far = n * FIELD, far_start + n * FIELD
+        if n == 3:
+            start = pl.multiple_of(near + (FIELD - RIM) * (1 - lev), 16)
+            column_ref[BLK * GROUP :, :] = strip_ref[pl.ds(start, RIM), :]
+        corner(edge_ref, n, strip_ref, near, strip_ref, far, lev)
     i = lax.broadcasted_iota(jnp.int32, (16, 128), 0)
     factors = jnp.zeros((16, 128), F32)
     for n, value in enumerate((*quarter_turn(turn_ref[0, 0]), *quarter_turn(turn_ref[0, 1]))):
         factors = jnp.where(i == n, value, factors)
-    near_ref[4 * FIELD :, :] = factors.astype(BF)
+    strip_ref[4 * FIELD : far_start, :] = factors.astype(BF)
 
 
 def forward_kernel(
-    turn_ref, state_ref, sound_ref, target_ref, tendency_ref,
-    near, far, partner, rims, partner_rims, own_col,
-    resid_ref, rows_ref, edge_ref, column_ref, c_ref, factor_ref, pa, pb, u, v, matrix,
+    turn_ref, state_ref, sound_ref, tendency_ref,
+    strip, partner, rims, partner_rims, own_col, other_col,
+    resid_ref, rows_ref, column_ref, c_ref, factor_ref, pa, pb, u, v, matrix,
 ):
     section, lev = lax.axis_index("sec"), lax.axis_index("lev")
     own_level = EDGE * lev
@@ -209,23 +232,22 @@
     below = lax.broadcasted_iota(jnp.int32, (BLK, 128), 0) < 4
 
     def factors(low, high):
-        low = low[4 * FIELD :, :].astype(F32)
-        high = high[4 * FIELD :, :].astype(F32)
+        low = low[4 * FIELD : 4 * FIELD + 16, :].astype(F32)
+        high = high[4 * FIELD : 4 * FIELD + 16, :].astype(F32)
         factor_ref[0] = jnp.where(below, cos_low, low[2:3, :]) - 1.0
         factor_ref[1] = jnp.where(below, sin_low, low[3:4, :])
         factor_ref[2] = jnp.where(below, high[0:1, :], cos_high) - 1.0
         factor_ref[3] = jnp.where(below, high[1:2, :], sin_high)
 
-    pl.when(section == 0)(lambda: factors(near, partner))
-    pl.when(section == 1)(lambda: factors(partner, near))
+    pl.when(section == 0)(lambda: factors(strip, partner))
+    pl.when(section == 1)(lambda: factors(partner, strip))
     masks = edge_masks()
     matrix[...] = across_matrix()
 
     def run(sec):
         unit = COURANT * UNIT
         spread_rims(
-            sec, lev, near, far, partner, rims, partner_rims,
-            (own_col, BLK * GROUP), (own_col, BLK * GROUP + 4 * RIM),
+            sec, lev, strip, partner, rims, partner_rims, own_col, other_col,
             ((pa, 2, None), (u, 0, None), (v, 0, None), (c_ref, 0, unit)),
         )
         _, near_edge, far_edge = static_rows(sec)
@@ -239,10 +261,10 @@
         for step in range(SUBSTEPS):
             old, new = (pa, pb) if step % 2 == 0 else (pb, pa)
 
-            def body(i, _, step=step, old=old, new=new):
-                k = i * CHUNK
-                levels = pl.ds(k, CHUNK)
-                inner = pl.ds(k + 2, CHUNK)
+            def body(step=step, old=old, new=new):
+                k, size = 0, EXT
+                levels = pl.ds(k, size)
+                inner = pl.ds(k + 2, size)
                 first, last = WIND_BLOCKS[step]
                 wide = slice(BLK + BLK * first, BLK + BLK * last)
                 slopes = across(old[inner, wide, :], matrix)
@@ -261,21 +283,18 @@
                     rows = slice(row, row + BLK)
                     at = BLK * (block - first)
                     spread_uv = along(u, levels, row) + slopes[:, at : at + BLK, :]
-                    new[inner, rows, :] = vertical(old, k, row) - c_ref[levels, rows, :] * spread_uv
+                    new[inner, rows, :] = vertical(old, k, size, row) - c_ref[levels, rows, :] * spread_uv
                 for edge, f in ((near_edge, near_factor), (far_edge, far_factor))[: 2 if step < 2 else 1]:
                     rows = slice(edge - 4, edge + 4)
                     delta = factor_ref[f] * u[levels, rows, :] - factor_ref[f + 1] * v[levels, rows, :]
                     new[inner, rows, :] = new[inner, rows, :] - c_ref[levels, rows, :] * crossing(delta, masks)
-                return 0
-
-            lax.fori_loop(*chunk_range(step, lev), body, 0)
+
+            body()
         final = pa if SUBSTEPS % 2 == 0 else pb
-        mine = slice(BLK * sec, BLK * sec + BLK)
         for n, (src, shift) in enumerate(((final, 2), (u, 0), (v, 0))):
             evolved = src[pl.ds(own_level + shift, OWN), 3 * BLK : 4 * BLK, :]
-            goal = target_ref[n * OWN * 16 : (n + 1) * OWN * 16, :].reshape(OWN, 16, 128)[:, mine, :]
             packed = slice(n * FIELD, (n + 1) * FIELD)
-            resid = evolved.reshape(FIELD, 128) + tendency_ref[packed, :] - goal.reshape(FIELD, 128)
+            resid = evolved.reshape(FIELD, 128) + tendency_ref[packed, :]
             resid_ref[packed, :] = resid
             rows_ref[packed, :] = resid.astype(BF)
 
@@ -283,16 +302,11 @@
         pl.when(section == sec)(lambda sec=sec: run(sec))
     for r in range(BLK):
         column_ref[r * GROUP : (r + 1) * GROUP, :] = column_rows(resid_ref, r, 0, BLK, FIELD, 0.0)
-    for n in range(3):
-        start = pl.multiple_of(n * FIELD + (FIELD - RIM) * (1 - lev), 16)
-        rim = rows_ref[pl.ds(start, RIM), :]
-        edge_ref[n * RIM : (n + 1) * RIM, :] = rim
-        column_ref[BLK * GROUP + n * RIM : BLK * GROUP + (n + 1) * RIM, :] = rim
 
 
 def adjoint_kernel(
     resid_ref, other_ref, input_grad_ref, c_ref, factor_ref,
-    near, far, partner, rims, partner_rims, own_col, other_col,
+    strip, partner, rims, partner_rims, own_col, other_col,
     out_ref, pa, pb, u, v, matrix, w,
 ):
     section, lev = lax.axis_index("sec"), lax.axis_index("lev")
@@ -303,12 +317,10 @@
     clear_levels(pb)
     masks = edge_masks()
     matrix[...] = across_matrix()
-    whole = pl.ds(0, CHUNK)
 
     def run(sec):
         spread_rims(
-            sec, lev, near, far, partner, rims, partner_rims,
-            (own_col, BLK * GROUP), (other_col, BLK * GROUP),
+            sec, lev, strip, partner, rims, partner_rims, own_col, other_col,
             ((pa, 2, None), (u, 0, None), (v, 0, None)),
         )
         other_row, near_edge, far_edge = static_rows(sec)
@@ -325,13 +337,14 @@
             first, last = MASS_BLOCKS[step]
             narrow = slice(BLK + BLK * max(first - 1, 0), BLK + BLK * min(last + 1, 5))
 
-            def body(i, _, step=step, old=old, new=new, wide=wide, narrow=narrow):
-                k = i * CHUNK
-                levels = pl.ds(k, CHUNK)
-                inner = pl.ds(k + 2, CHUNK)
-                w[:, wide, :] = c_ref[levels, wide, :] * old[inner, wide, :]
+            def body(step=step, old=old, new=new, wide=wide, narrow=narrow):
+                k, size = 0, EXT
+                whole = pl.ds(0, size)
+                levels = pl.ds(k, size)
+                inner = pl.ds(k + 2, size)
+                w[whole, wide, :] = c_ref[levels, wide, :] * old[inner, wide, :]
                 first, last = WIND_BLOCKS[step]
-                slopes = across(w[:, BLK + BLK * first : BLK + BLK * last, :], matrix)
+                slopes = across(w[whole, BLK + BLK * first : BLK + BLK * last, :], matrix)
                 for block in range(first, last):
                     row = BLK + BLK * block
                     rows = slice(row, row + BLK)
@@ -340,10 +353,10 @@
                     v[levels, rows, :] = v[levels, rows, :] + slopes[:, at : at + BLK, :]
                 for edge, f in ((near_edge, near_factor), (far_edge, far_factor))[: 2 if step < 2 else 1]:
                     rows = slice(edge - 4, edge + 4)
-                    cross = crossing(w[:, rows, :], masks)
+                    cross = crossing(w[whole, rows, :], masks)
                     u[levels, rows, :] = u[levels, rows, :] + factor_ref[f] * cross
                     v[levels, rows, :] = v[levels, rows, :] - factor_ref[f + 1] * cross
-                w[:, narrow, :] = c_ref[levels, narrow, :] * u[levels, narrow, :]
+                w[whole, narrow, :] = c_ref[levels, narrow, :] * u[levels, narrow, :]
                 first, last = MASS_BLOCKS[step]
                 rows = slice(BLK + BLK * first, BLK + BLK * last)
                 slopes = across(c_ref[levels, rows, :] * v[levels, rows, :], matrix)
@@ -351,10 +364,9 @@
                     row = BLK + BLK * block
                     at = BLK * (block - first)
                     spread_uv = along(w, whole, row) + slopes[:, at : at + BLK, :]
-                    new[inner, row : row + BLK, :] = vertical(old, k, row) + spread_uv
-                return 0
-
-            lax.fori_loop(*chunk_range(step, lev), body, 0)
+                    new[inner, row : row + BLK, :] = vertical(old, k, size, row) + spread_uv
+
+            body()
 
     for sec in range(2):
         pl.when(section == sec)(lambda sec=sec: run(sec))
@@ -391,15 +403,17 @@
     return jnp.concatenate(parts, axis=1)
 
 
-def to_fields(out_ref, first, values):
+def to_fields(out_ref, first, values, minus_ref=None, minus_first=None):
     for r in range(STRIPE // 128):
         for n in range(3):
-            rows = pl.ds(n * FIELD + first + r, OWN, stride=BLK)
-            out_ref[rows, :] = values[n * OWN : (n + 1) * OWN, r * 128 : (r + 1) * 128]
+            value = values[n * OWN : (n + 1) * OWN, r * 128 : (r + 1) * 128]
+            if minus_ref is not None:
+                value = value - minus_ref[pl.ds(n * OWN * 16 + minus_first + r, OWN, stride=16), :]
+            out_ref[pl.ds(n * FIELD + first + r, OWN, stride=BLK), :] = value
 
 
 def network_kernel(
-    own_ref, other_ref, first_ref, second_ref, third_t_ref,
+    own_ref, other_ref, first_ref, second_ref, third_t_ref, target_ref,
     feat_ref, one_ref, two_ref, slope_one_ref, slope_two_ref, tendency_ref,
 ):
     feat = both_groups(own_ref, other_ref)
@@ -410,21 +424,17 @@
     two, slope = silu_and_slope(dot_t(second_ref[...], one))
     two_ref[...] = two
     slope_two_ref[...] = slope
-    to_fields(tendency_ref, pl.program_id(0) * (STRIPE // 128), dot(third_t_ref[:GROUP, :], two))
-
-
-def gather_kernel(own_ref, other_ref, out_ref):
-    for start in range(0, COLS, STRIPE):
-        rows = slice(start // 128 * GROUP, (start + STRIPE) // 128 * GROUP)
-        out_ref[:, start : start + STRIPE] = both_groups(own_ref.at[rows, :], other_ref.at[rows, :])
+    row = pl.program_id(0) * (STRIPE // 128)
+    at = BLK * lax.axis_index("sec") + row
+    to_fields(tendency_ref, row, dot(third_t_ref[:GROUP, :], two), target_ref, at)
 
 
 def back_kernel(
-    resid_ref, feat_ref, third_t_ref, second_ref, first_ref, one_ref, two_ref, slope_one_ref, slope_two_ref,
+    own_ref, other_ref, feat_ref, third_t_ref, second_ref, first_ref, one_ref, two_ref, slope_one_ref, slope_two_ref,
     given_ref, kept_ref, input_grad_ref, err_one_ref, err_two_ref, total_ref,
 ):
     step = pl.program_id(0)
-    resid = resid_ref[...]
+    resid = both_groups(own_ref, other_ref)
     err_two = (dot_t(third_t_ref[...], resid) * slope_two_ref[...]).astype(BF)
     err_two_ref[...] = err_two
     err_one = (dot(second_ref[...], err_two) * slope_one_ref[...]).astype(BF)
@@ -455,6 +465,26 @@
             pl.when(lax.axis_index("sec") == sec)(share)
 
     pl.when(step == COLS // STRIPE - 1)(finish)
+
+
+def join_kernel(near_ref, far_ref, strip_ref, edge_ref):
+    strip_ref[: 3 * FIELD, :] = near_ref[...]
+    strip_ref[3 * FIELD :, :] = far_ref[...]
+    for n in range(3):
+        corner(edge_ref, n, near_ref, n * FIELD, far_ref, n * FIELD, lax.axis_index("lev"))
+
+
+def add_kernel(kept_ref, received_ref, out_ref):
+    out_ref[...] = (kept_ref[...] + received_ref[...].astype(F32)).astype(BF)
+
+
+def mean_kernel(parts_ref, out_ref):
+    total = parts_ref[0].astype(F32)
+    for tile in range(1, parts_ref.shape[0]):
+        total = total + parts_ref[tile].astype(F32)
+    mean = (total / (COLS * out_ref.shape[0])).astype(BF)
+    for device in range(out_ref.shape[0]):
+        out_ref[device] = mean
 
 
 def place_rows_kernel(mine_ref, theirs_ref, out_ref):
@@ -512,10 +542,14 @@
     return pl.BlockSpec((STRIPE // 128 * GROUP, 128), lambda i: (i, 0))
 
 
-def call(kernel, n_smem, operands, outs, scratch=(), flops=0, steps=1, in_along=None, out_along=None):
+def first_rows(rows, value):
+    return pl.BlockSpec((rows, *value.shape[1:]), lambda i: (0,) * len(value.shape), pipeline_mode=pl.Buffered(1))
+
+
+def call(kernel, n_smem, operands, outs, scratch=(), flops=0, limit=60, steps=1, in_along=None, out_along=None):
     def specs(values, along):
         along = along or [None] * len(values)
-        return [whole(v) if at is None else stripes(v, at) for v, at in zip(values, along, strict=True)]
+        return [whole(v) if at is None else first_rows(at, v) if at > 1 else stripes(v, at) for v, at in zip(values, along, strict=True)]
 
     smem = pl.BlockSpec(memory_space=pltpu.SMEM)
     return pl.pallas_call(
@@ -525,7 +559,7 @@
         in_specs=[smem] * n_smem + specs(operands[n_smem:], in_along),
         out_specs=specs(outs, out_along),
         scratch_shapes=list(scratch),
-        compiler_params=pltpu.CompilerParams(vmem_limit_bytes=60 * MIB),
+        compiler_params=pltpu.CompilerParams(vmem_limit_bytes=limit * MIB),
         cost_estimate=pl.CostEstimate(flops=flops, bytes_accessed=0, transcendentals=0),
     )(*operands)
 
@@ -544,15 +578,11 @@
     return lax.ppermute(value, axis, [(0, 1), (1, 0)])
 
 
-def strip_swaps(near, far, edges, tiles):
+def strip_swaps(strip, edges, tiles):
     pairs = [(tiles + t, t + 1) for t in range(tiles - 1)]
     pairs += [(b, a) for a, b in pairs]
     cross = [(2 * a + lev, 2 * b + 1 - lev) for a, b in pairs for lev in range(2)]
-    return (
-        lax.ppermute(near, ("sec", "tile"), pairs),
-        lax.ppermute(far, ("sec", "tile"), pairs),
-        lax.ppermute(edges, ("sec", "tile", "lev"), cross),
-    )
+    return lax.ppermute(strip, ("sec", "tile"), pairs), lax.ppermute(edges, ("sec", "tile", "lev"), cross)
 
 
 def local(state, sound, target, edge_turn, w_first, b_first, w_second, w_third):
@@ -560,66 +590,64 @@
     hid, feats = w_second.shape[0], 2 * GROUP
 
     state, sound, target = state.reshape(-1, 128), sound.reshape(-1, 128), target.reshape(-1, 128)
-    near, far, edges, columns, first, third_t = call(
+    strip, edges, columns, first, third_t = call(
         pack_kernel, 1, (edge_turn, state, sound, w_first, w_third.T, b_first[None]),
-        (shape(4 * FIELD + 16, 128, dtype=BF), shape(4 * FIELD, 128, dtype=BF), shape(8 * RIM, 128, dtype=BF), shape(BLK * GROUP + 8 * RIM, 128, dtype=BF), shape(feats, hid, dtype=BF), shape(feats, hid, dtype=BF)),
+        (shape(8 * FIELD + 16, 128, dtype=BF), shape(4 * RIM, 128, dtype=BF), shape(BLK * GROUP + RIM, 128, dtype=BF), shape(feats, hid, dtype=BF), shape(feats, hid, dtype=BF)),
     )
     own_col = swap(columns, "lev")
-    near, far, rims = strip_swaps(near, far, edges, tiles)
+    strip, rims = strip_swaps(strip, edges, tiles)
 
     activations = (shape(feats, COLS, dtype=BF), shape(hid, COLS, dtype=BF), shape(hid, COLS, dtype=BF), shape(hid, COLS), shape(hid, COLS))
     feat, one, two, slope_one, slope_two, tendency = call(
-        network_kernel, 0, (columns, own_col, first, w_second, third_t),
+        network_kernel, 0, (columns, own_col, first, w_second, third_t, target),
         (*activations, shape(3 * FIELD, 128)),
-        steps=COLS // STRIPE, flops=LONG, in_along=(0, 0, None, None, None), out_along=(1, 1, 1, 1, 1, None),
-    )
-
-    near, far, rims, tendency = lax.optimization_barrier((near, far, rims, tendency))
-    resid, r_rows, r_edges, r_columns, coeff, factors = call(
+        steps=COLS // STRIPE, flops=LONG, in_along=(0, 0, None, None, None, None), out_along=(1, 1, 1, 1, 1, None),
+    )
+
+    other_col = swap(own_col, "sec")
+    strip, rims, tendency = lax.optimization_barrier((strip, rims, tendency))
+    resid, r_rows, r_columns, coeff, factors = call(
         forward_kernel, 1,
-        (edge_turn, state, sound, target, tendency, near, far, swap(near, "sec"), rims, swap(rims, "sec"), own_col),
-        (shape(3 * FIELD, 128), shape(3 * FIELD, 128, dtype=BF), shape(3 * RIM, 128, dtype=BF), shape(BLK * GROUP + 3 * RIM, 128, dtype=BF), shape(EXT, ROWS, 128), shape(4, BLK, 128)),
-        stencil_scratch(), flops=LONG,
+        (edge_turn, state, sound, tendency, strip, swap(strip, "sec"), rims, swap(rims, "sec"), own_col, other_col),
+        (shape(3 * FIELD, 128), shape(3 * FIELD, 128, dtype=BF), shape(BLK * GROUP, 128, dtype=BF), shape(EXT, ROWS, 128), shape(4, BLK, 128)),
+        stencil_scratch(), flops=LONG, in_along=(*[None] * 4, 4 * FIELD + 16, *[None] * 4),
     )
 
     r_own_col = swap(r_columns, "lev")
     r_other = swap(resid, "sec")
-    both_edges = jnp.concatenate([r_edges, swap(r_edges, "sec")], axis=0)
-    r_near, r_far, r_rims = strip_swaps(r_rows, swap(r_rows, "sec"), both_edges, tiles)
-    (resid_cols,) = call(
-        gather_kernel, 0, (r_columns, r_own_col), (shape(feats, COLS, dtype=BF),), flops=LONG
-    )
-    resid_cols, r_near, r_far, r_rims = lax.optimization_barrier((resid_cols, r_near, r_far, r_rims))
-
+    r_strip, r_edges = call(
+        join_kernel, 0, (r_rows, swap(r_rows, "sec")),
+        (shape(6 * FIELD, 128, dtype=BF), shape(3 * RIM, 128, dtype=BF)), limit=16,
+    )
+    r_strip, r_rims = strip_swaps(r_strip, r_edges, tiles)
     n_rows = 2 * feats + hid
     given, kept, input_grad = call(
-        back_kernel, 0, (resid_cols, feat, third_t, w_second, first, one, two, slope_one, slope_two),
+        back_kernel, 0, (r_columns, r_own_col, feat, third_t, w_second, first, one, two, slope_one, slope_two),
         (shape(n_rows, 128, dtype=BF), shape(n_rows, 128), shape(3 * FIELD, 128)),
         (pltpu.VMEM((hid, STRIPE), BF), pltpu.VMEM((hid, STRIPE), BF), pltpu.VMEM((n_rows, 256), F32)),
-        flops=LONG, steps=COLS // STRIPE, in_along=(1, 1, None, None, None, 1, 1, 1, 1),
-    )
-    r_partner, r_partner_rims, r_other_col = swap(r_near, "sec"), swap(r_rims, "sec"), swap(r_own_col, "sec")
-    given, r_other, r_partner, r_partner_rims, r_other_col = lax.optimization_barrier(
-        (given, r_other, r_partner, r_partner_rims, r_other_col)
-    )
+        flops=LONG, steps=COLS // STRIPE, in_along=(0, 0, 1, None, None, None, 1, 1, 1, 1),
+    )
+    given, r_strip, r_rims = lax.optimization_barrier((given, r_strip, r_rims))
+    r_partner, r_partner_rims, r_other_col = swap(r_strip, "sec"), swap(r_rims, "sec"), swap(r_own_col, "sec")
     received = swap(given, "sec")
     share = n_rows // tiles
-    partial = (kept + received.astype(F32)).astype(BF).reshape(tiles, share, 128)
+    (partial,) = call(add_kernel, 0, (kept, received), (shape(n_rows, 128, dtype=BF),), limit=16)
+    partial = partial.reshape(tiles, share, 128)
     parts = lax.all_to_all(partial, "tile", 0, 0)
-    total = jnp.sum(parts.astype(F32), axis=0) / (COLS * 2 * tiles)
     (mine,) = call(
         adjoint_kernel, 0,
-        (resid, r_other, input_grad, coeff, factors, r_near, r_far, r_partner, r_rims, r_partner_rims, r_own_col, r_other_col),
-        (shape(3 * FIELD, 128),), stencil_scratch((pltpu.VMEM((CHUNK, ROWS, 128), F32),)), flops=LONG,
-    )
-    total, mine = lax.optimization_barrier((total, mine))
-    everywhere = jnp.broadcast_to(total.astype(BF)[None], (2 * tiles, share, 128))
+        (resid, r_other, input_grad, coeff, factors, r_strip, r_partner, r_rims, r_partner_rims, r_own_col, r_other_col),
+        (shape(3 * FIELD, 128),), stencil_scratch((pltpu.VMEM((EXT, ROWS, 128), F32),)), flops=LONG,
+        in_along=(*[None] * 6, 3 * FIELD, *[None] * 4),
+    )
+    parts, mine = lax.optimization_barrier((parts, mine))
+    (everywhere,) = call(mean_kernel, 0, (parts,), (shape(2 * tiles, share, 128, dtype=BF),), limit=16)
     gathered = lax.all_to_all(everywhere, ("tile", "lev"), 0, 0)
-    (state_grad,) = call(place_rows_kernel, 0, (mine, swap(mine, "sec")), (shape(3, OWN, 2 * BLK, 128),))
+    (state_grad,) = call(place_rows_kernel, 0, (mine, swap(mine, "sec")), (shape(3, OWN, 2 * BLK, 128),), limit=16)
     state_grad, gathered = lax.optimization_barrier((state_grad, gathered))
     g_first, g_bias, g_second, g_third_t = call(
         spread_gradients_kernel, 0, (gathered, swap(gathered, "sec")),
-        (shape(6 * OWN, hid), shape(1, hid), shape(hid, hid), shape(6 * OWN, hid)),
+        (shape(6 * OWN, hid), shape(1, hid), shape(hid, hid), shape(6 * OWN, hid)), limit=16,
     )
     return (state_grad, g_first, g_bias.reshape(hid), g_second, g_third_t.T)
 

time: 120 us -> 110 us (0.917)
  starting transfers between devices: 53.4 us -> 47.8 us
  Pallas kernels: 39.9 us -> 35.3 us
  other arithmetic: 2.67 us -> 0 us
  waiting for transfers between devices: 17.4 us -> 20 us
    ppermute x4 -> x2, starting transfers between devices: 11.5 us -> 4.56 us  [strip_swaps(): lax.ppermute(strip, ('sec', 'tile'), pairs)]
    pallas_call x8 -> x10, Pallas kernels: 39.9 us -> 35.3 us  [call(): pl.pallas_call(kernel, grid=(steps,), out_shape=outs, in_specs=[smem] * n...]
    unnamed x34 -> x32, local copies, waits for them, and re-layouts: 3.86 us -> 5.84 us
    all_to_all x1, waiting for transfers between devices: 6.24 us -> 8.1 us  [local(): gathered = lax.all_to_all(everywhere, ('tile', 'lev'), 0, 0)]
    convert_element_type x1 -> x0, other arithmetic: 1.81 us -> none  [local(): (kept + received.astype(F32)).astype(BF).reshape(tiles, share, 128)]
    ppermute x13, waiting for transfers between devices: 6.31 us -> 7.82 us  [swap(): return lax.ppermute(value, axis, [(0, 1), (1, 0)])]
    all_to_all x1, starting transfers between devices: 8.59 us -> 9.83 us  [local(): gathered = lax.all_to_all(everywhere, ('tile', 'lev'), 0, 0)]
    ppermute x4 -> x2, waiting for transfers between devices: 4.81 us -> 4.12 us  [strip_swaps(): lax.ppermute(strip, ('sec', 'tile'), pairs)]
  transfers between devices with their start and end apart: 21 -> 19, of which waited for: 8 -> 9; matrix products, arithmetic and copies ran while one was open for 1% -> 0% of each run, Pallas kernels for 21% -> 20%
where the time goes in v4:
time: 110 us
  starting transfers between devices  47.8 us (43%)
  Pallas kernels  35.3 us (32%)
  waiting for transfers between devices  20 us (18%)
  local copies, waits for them, and re-layouts  5.84 us (5%)
    pallas_call x10, Pallas kernels, call(): pl.pallas_call(kernel, grid=(steps,), out_shape=outs, in_specs=[smem] * n...  35.3 us
    all_to_all x1, starting transfers between devices, local(): parts = lax.all_to_all(partial, 'tile', 0, 0)  13 us
    ppermute x13, starting transfers between devices, swap(): return lax.ppermute(value, axis, [(0, 1), (1, 0)])  12.9 us
    all_to_all x1, starting transfers between devices, local(): gathered = lax.all_to_all(everywhere, ('tile', 'lev'), 0, 0)  9.83 us
    all_to_all x1, waiting for transfers between devices, local(): gathered = lax.all_to_all(everywhere, ('tile', 'lev'), 0, 0)  8.1 us
    ppermute x13, waiting for transfers between devices, swap(): return lax.ppermute(value, axis, [(0, 1), (1, 0)])  7.82 us
    ppermute x2, starting transfers between devices, strip_swaps(): lax.ppermute(edges, ('sec', 'tile', 'lev'), cross)  7.46 us
    unnamed x32, local copies, waits for them, and re-layouts  5.84 us
  transfers between devices with their start and end apart: 19, of which 9 were waited for; matrix products, arithmetic and copies ran while one was open for 0% of the time, Pallas kernels for 20%

profile of v4, /device:TPU:1, one launch (start us, length us, event | category | flops | bytes accessed | tf_op | source)
XLA Modules:
  0.0 109.8 jit_solution(12443922773404942115)
XLA Ops:
  0.6 2.9 %shard_map.119 = (bf16[2576,128]{1,0:T(8,128)(2,1)}, bf16[256,128]{1,0:T(8,128)(2,1)}, bf16[1088,128]{1,0:T(8,128)(2,1)}, bf16[256,512]{1,0:T(8,128)(2,1)}, bf16[256,512]{1,0:T(8,128)(2,1)}) custom-call(s32[1,2]{1,0:T(1,128)} %turn_ref.3, f32[1920,128]{1,0:T(8,128)} %bitcast.8, f32[640,128]{1,0:T(8,128)} %bitcast.10, bf16[240,512]{1,0:T(8,128)(2,1)} %first_ref.1, ...), custom_call_target="tpu_custom_call" | custom-call | tf_op jit(solution)/shard_map/pallas_call | solution.py:555
  3.5 3.8 %collective-permute-start.2 = (bf16[1088,128]{1,0:T(8,128)(2,1)}, bf16[1088,128]{1,0:T(8,128)(2,1)S(1)}, u32[]{:S(2)}, u32[]{:S(2)}) collective-permute-start(bf16[1088,128]{1,0:T(8,128)(2,1)} %get-tuple-element.42.own_ref), channel_id=1, source_target_pairs={{0,1},{1,0},{2,3},{3,2},{4,5},{5,4},{6,7},{7,6},{8,9},{9,8},{10,11... | collective-permute-start | bytes 835592 | tf_op jit(solution)/shard_map/ppermute | solution.py:578
  7.3 4.1 %collective-permute-start.1 = (bf16[256,128]{1,0:T(8,128)(2,1)}, bf16[256,128]{1,0:T(8,128)(2,1)S(1)}, u32[]{:S(2)}, u32[]{:S(2)}) collective-permute-start(bf16[256,128]{1,0:T(8,128)(2,1)} %get-tuple-element.41), channel_id=1, source_target_pairs={{64,3},{65,2},{66,5},{67,4},{68,7},{69,6},{70,9},{71,8},{72,11},{7... | collective-permute-start | bytes 196616 | tf_op jit(solution)/shard_map/ppermute | solution.py:585
  11.4 2.2 %collective-permute-start = (bf16[2576,128]{1,0:T(8,128)(2,1)}, bf16[2576,128]{1,0:T(8,128)(2,1)S(1)}, u32[]{:S(2)}, u32[]{:S(2)}) collective-permute-start(bf16[2576,128]{1,0:T(8,128)(2,1)} %get-tuple-element.40), channel_id=1, source_target_pairs={{64,2},{66,4},{68,6},{70,8},{72,10},{74,12},{76,14},{78,16},{80,18... | collective-permute-start | bytes 1978376 | tf_op jit(solution)/shard_map/ppermute | solution.py:585
  13.6 0.0 collective-permute-done.2.other_ref.own_col
  13.6 0.7 copy-done.8
  14.3 5.4 %shard_map.120 = (bf16[256,1024]{1,0:T(8,128)(2,1)}, bf16[512,1024]{1,0:T(8,128)(2,1)}, bf16[512,1024]{1,0:T(8,128)(2,1)}, f32[512,1024]{1,0:T(8,128)}, f32[512,1024]{1,0:T(8,128)}, /*index=5*/f32[960,128]{1,0:T(8,128)}) custom-call(bf16[1088,128]{1,0:T(8,128)(2,1)} %get-tuple-element.42.own_ref, bf16[1088,128]{1,0:T(8,128)(2,1)} %copy-done.8, ...), custom_call_target="tpu_custom_call" | custom-call | flops 20000000000 | tf_op jit(solution)/shard_map/pallas_call | solution.py:555
  19.7 3.9 %collective-permute-done.strip = bf16[2576,128]{1,0:T(8,128)(2,1)S(1)} collective-permute-done((bf16[2576,128]{1,0:T(8,128)(2,1)}, bf16[2576,128]{1,0:T(8,128)(2,1)S(1)}, u32[]{:S(2)}, u32[]{:S(2)}) %collective-permute-start) | collective-permute-done | bytes 659488 | tf_op jit(solution)/shard_map/ppermute | solution.py:585
  23.6 0.0 collective-permute-start.3
  23.6 0.5 collective-permute-start.5
  24.1 0.0 collective-permute-start.4
  24.1 1.9 %collective-permute-done.5.other_col = bf16[1088,128]{1,0:T(8,128)(2,1)S(1)} collective-permute-done((bf16[1088,128]{1,0:T(8,128)(2,1)}, bf16[1088,128]{1,0:T(8,128)(2,1)S(1)}, u32[]{:S(2)}, u32[]{:S(2)}) %collective-permute-start.5) | collective-permute-done | bytes 278560 | tf_op jit(solution)/shard_map/ppermute | solution.py:578
  26.0 0.2 collective-permute-done.4.partner_rims
  26.2 0.5 copy-done.9
  26.8 0.1 copy-done.13
  26.8 0.8 copy-done.4
  27.6 7.8 %shard_map.121 = (f32[960,128]{1,0:T(8,128)}, bf16[960,128]{1,0:T(8,128)(2,1)}, bf16[1024,128]{1,0:T(8,128)(2,1)}, f32[48,56,128]{2,1,0:T(8,128)}, f32[4,8,128]{2,1,0:T(8,128)}) custom-call(s32[1,2]{1,0:T(1,128)} %turn_ref.3, f32[1920,128]{1,0:T(8,128)} %bitcast.9, f32[640,128]{1,0:T(8,128)} %bitcast.11, f32[960,128]{1,0:T(8,128)} %get-tuple-element.46.tendency_ref, ...), custom_call_target="tpu_custom_call" | custom-call | flops 20000000000 | tf_op jit(solution)/shard_map/pallas_call | solution.py:555
  35.5 3.6 %collective-permute-start.6 = (bf16[1024,128]{1,0:T(8,128)(2,1)}, bf16[1024,128]{1,0:T(8,128)(2,1)S(1)}, u32[]{:S(2)}, u32[]{:S(2)}) collective-permute-start(bf16[1024,128]{1,0:T(8,128)(2,1)} %get-tuple-element.49.own_ref), channel_id=1, source_target_pairs={{0,1},{1,0},{2,3},{3,2},{4,5},{5,4},{6,7},{7,6},{8,9},{9,8},{10,11... | collective-permute-start | bytes 786440 | tf_op jit(solution)/shard_map/ppermute | solution.py:578
  39.1 0.6 collective-permute-start.7
  39.7 1.3 %collective-permute-done.7.far_ref = bf16[960,128]{1,0:T(8,128)(2,1)S(1)} collective-permute-done((bf16[960,128]{1,0:T(8,128)(2,1)}, bf16[960,128]{1,0:T(8,128)(2,1)S(1)}, u32[]{:S(2)}, u32[]{:S(2)}) %collective-permute-start.7) | collective-permute-done | bytes 245792 | tf_op jit(solution)/shard_map/ppermute | solution.py:578
  41.1 0.9 copy-done.2
  42.0 3.3 %collective-permute-start.9 = (bf16[192,128]{1,0:T(8,128)(2,1)S(1)}, bf16[192,128]{1,0:T(8,128)(2,1)S(1)}, u32[]{:S(2)}, u32[]{:S(2)}) collective-permute-start(bf16[192,128]{1,0:T(8,128)(2,1)S(1)} %get-tuple-element.59), channel_id=1, source_target_pairs={{64,3},{65,2},{66,5},{67,4},{68,7},{69,6},{70,9},{71,8},{72,11},{7... | collective-permute-start | bytes 147464 | tf_op jit(solution)/shard_map/ppermute | solution.py:585
  45.4 2.4 %collective-permute-start.8 = (bf16[1920,128]{1,0:T(8,128)(2,1)S(1)}, bf16[1920,128]{1,0:T(8,128)(2,1)S(1)}, u32[]{:S(2)}, u32[]{:S(2)}) collective-permute-start(bf16[1920,128]{1,0:T(8,128)(2,1)S(1)} %get-tuple-element.58), channel_id=1, source_target_pairs={{64,2},{66,4},{68,6},{70,8},{72,10},{74,12},{76,14},{78,16},{80,18... | collective-permute-start | bytes 1474568 | tf_op jit(solution)/shard_map/ppermute | solution.py:585
  47.8 0.7 copy-done.10
  48.5 6.7 %shard_map.122 = (bf16[1024,128]{1,0:T(8,128)(2,1)}, f32[1024,128]{1,0:T(8,128)}, f32[960,128]{1,0:T(8,128)}) custom-call(bf16[1024,128]{1,0:T(8,128)(2,1)} %get-tuple-element.49.own_ref, bf16[1024,128]{1,0:T(8,128)(2,1)} %copy-done.10, bf16[256,1024]{1,0:T(8,128)(2,1)} %get-tuple-element.50.feat_ref, bf16[256,512]{1,0:T(8,128)(2,1)} %get-tuple-element.44.third_t_ref, ...), custom_call_target="tpu_custom_call" | custom-call | flops 20000000000 | tf_op jit(solution)/shard_map/pallas_call | solution.py:555
  55.3 0.3 collective-permute-done.8.strip
  55.5 0.5 collective-permute-start.10
  56.0 0.0 collective-permute-start.14
  56.0 0.5 collective-permute-start.13
  56.5 1.1 %collective-permute-done.10.received_ref = bf16[1024,128]{1,0:T(8,128)(2,1)S(1)} collective-permute-done((bf16[1024,128]{1,0:T(8,128)(2,1)}, bf16[1024,128]{1,0:T(8,128)(2,1)S(1)}, u32[]{:S(2)}, u32[]{:S(2)}) %collective-permute-start.10) | collective-permute-done | bytes 262176 | tf_op jit(solution)/shard_map/ppermute | solution.py:578
  57.7 1.0 copy-done
  58.7 0.7 shard_map.124
  59.5 13.0 %all-to-all-start = ((bf16[32,32,128]{2,1,0:T(8,128)(2,1)}), bf16[32,32,128]{2,1,0:T(8,128)(2,1)S(1)}, u32[]{:S(2)}, u32[]{:S(2)}) async-start(bf16[32,32,128]{2,1,0:T(8,128)(2,1)} %bitcast.5), calls=%async_computation | async-start | bytes 524288 | tf_op jit(solution)/shard_map/all_to_all | solution.py:636
  72.5 0.0 copy-start.5
  72.6 0.0 copy-start.7
  72.6 0.7 copy-done.5
  73.3 0.1 copy-done.11
  73.4 0.2 copy-done.7
  73.6 8.4 %shard_map.125.mine_ref = f32[960,128]{1,0:T(8,128)} custom-call(f32[960,128]{1,0:T(8,128)} %get-tuple-element.61.resid_ref, f32[960,128]{1,0:T(8,128)} %copy-done.5, f32[960,128]{1,0:T(8,128)} %get-tuple-element.62.input_grad_ref, f32[48,56,128]{2,1,0:T(8,128)} %get-tuple-element.63.c_ref, f32[4,8,128]{2,1,0:T(8,128)} %get-tuple-element.64.factor_ref, ...), custom_call_target="tpu_custom_call" | custom-call | flops 20000000000 | tf_op jit(solution)/shard_map/pallas_call | solution.py:555
  81.9 0.9 shard_map.127
  82.8 9.8 %all-to-all-start.1 = ((bf16[64,32,128]{2,1,0:T(8,128)(2,1)}), bf16[64,32,128]{2,1,0:T(8,128)(2,1)S(1)}, u32[]{:S(2)}, u32[]{:S(2)}) async-start(bf16[64,32,128]{2,1,0:T(8,128)(2,1)} %shard_map.127), calls=%async_computation.1 | async-start | bytes 1048576 | tf_op jit(solution)/shard_map/all_to_all | solution.py:645
  92.6 1.1 %collective-permute-start.15 = (f32[960,128]{1,0:T(8,128)}, f32[960,128]{1,0:T(8,128)S(1)}, u32[]{:S(2)}, u32[]{:S(2)}) collective-permute-start(f32[960,128]{1,0:T(8,128)} %shard_map.125.mine_ref), channel_id=1, source_target_pairs={{0,64},{64,0},{1,65},{65,1},{2,66},{66,2},{3,67},{67,3},{4,68},{68... | collective-permute-start | bytes 1474568 | tf_op jit(solution)/shard_map/ppermute | solution.py:578
  93.8 1.7 %collective-permute-done.15.theirs_ref = f32[960,128]{1,0:T(8,128)S(1)} collective-permute-done((f32[960,128]{1,0:T(8,128)}, f32[960,128]{1,0:T(8,128)S(1)}, u32[]{:S(2)}, u32[]{:S(2)}) %collective-permute-start.15) | collective-permute-done | bytes 491552 | tf_op jit(solution)/shard_map/ppermute | solution.py:578
  95.5 1.0 shard_map.126
  96.5 8.1 %all-to-all-done.1.own_ref = bf16[64,32,128]{2,1,0:T(8,128)(2,1)S(1)} async-done(((bf16[64,32,128]{2,1,0:T(8,128)(2,1)}), bf16[64,32,128]{2,1,0:T(8,128)(2,1)S(1)}, u32[]{:S(2)}, u32[]{:S(2)}) %all-to-all-start.1) | async-done | bytes 524320 | tf_op jit(solution)/shard_map/all_to_all | solution.py:645
  104.6 2.3 %collective-permute-start.16 = (bf16[64,32,128]{2,1,0:T(8,128)(2,1)S(1)}, bf16[64,32,128]{2,1,0:T(8,128)(2,1)S(1)}, u32[]{:S(2)}, u32[]{:S(2)}) collective-permute-start(bf16[64,32,128]{2,1,0:T(8,128)(2,1)S(1)} %all-to-all-done.1.own_ref), channel_id=1, source_target_pairs={{0,64},{64,0},{1,65},{65,1},{2,66},{66,2},{3,67},{67,3},{4,68},{68... | collective-permute-start | bytes 1572872 | tf_op jit(solution)/shard_map/ppermute | solution.py:578
  106.9 1.5 %collective-permute-done.16.partner_ref = bf16[64,32,128]{2,1,0:T(8,128)(2,1)S(1)} collective-permute-done((bf16[64,32,128]{2,1,0:T(8,128)(2,1)S(1)}, bf16[64,32,128]{2,1,0:T(8,128)(2,1)S(1)}, u32[]{:S(2)}, u32[]{:S(2)}) %collective-permute-start.16) | collective-permute-done | bytes 524320 | tf_op jit(solution)/shard_map/ppermute | solution.py:578
  108.4 1.4 %shard_map.128 = (f32[240,512]{1,0:T(8,128)}, f32[1,512]{1,0:T(1,128)}, f32[512,512]{1,0:T(8,128)}, f32[240,512]{1,0:T(8,128)}) custom-call(bf16[64,32,128]{2,1,0:T(8,128)(2,1)S(1)} %all-to-all-done.1.own_ref, bf16[64,32,128]{2,1,0:T(8,128)(2,1)S(1)} %collective-permute-done.16.partner_ref), custom_call_target="tpu_custom_call" | custom-call | tf_op jit(solution)/shard_map/pallas_call | solution.py:555
  (32 shorter events, 0.1 us)
Async XLA Ops:
  3.5 10.1 %collective-permute-start.2 = (bf16[1088,128]{1,0:T(8,128)(2,1)}, bf16[1088,128]{1,0:T(8,128)(2,1)S(1)}, u32[]{:S(2)}, u32[]{:S(2)}) collective-permute-start(bf16[1088,128]{1,0:T(8,128)(2,1)} %get-tuple-element.42.own_ref), channel_id=1, source_target_pairs={{0,1},{1,0},{2,3},{3,2},{4,5},{5,4},{6,7},{7,6},{8,9},{9,8},{10,11... | collective-permute-start | bytes 835592 | tf_op jit(solution)/shard_map/ppermute | solution.py:578
  7.3 12.4 %collective-permute-start.1 = (bf16[256,128]{1,0:T(8,128)(2,1)}, bf16[256,128]{1,0:T(8,128)(2,1)S(1)}, u32[]{:S(2)}, u32[]{:S(2)}) collective-permute-start(bf16[256,128]{1,0:T(8,128)(2,1)} %get-tuple-element.41), channel_id=1, source_target_pairs={{64,3},{65,2},{66,5},{67,4},{68,7},{69,6},{70,9},{71,8},{72,11},{7... | collective-permute-start | bytes 196616 | tf_op jit(solution)/shard_map/ppermute | solution.py:585
  11.4 12.2 %collective-permute-start = (bf16[2576,128]{1,0:T(8,128)(2,1)}, bf16[2576,128]{1,0:T(8,128)(2,1)S(1)}, u32[]{:S(2)}, u32[]{:S(2)}) collective-permute-start(bf16[2576,128]{1,0:T(8,128)(2,1)} %get-tuple-element.40), channel_id=1, source_target_pairs={{64,2},{66,4},{68,6},{70,8},{72,10},{74,12},{76,14},{78,16},{80,18... | collective-permute-start | bytes 1978376 | tf_op jit(solution)/shard_map/ppermute | solution.py:585
  13.6 0.7 copy-start.8
  19.7 6.5 %copy-start.12 = (bf16[256,128]{1,0:T(8,128)(2,1)}, bf16[256,128]{1,0:T(8,128)(2,1)S(1)}, u32[]{:S(2)}) copy-start(bf16[256,128]{1,0:T(8,128)(2,1)S(1)} %collective-permute-done.1.rims) | copy-start | bytes 196612
  23.6 2.6 %copy-start.3 = (bf16[2576,128]{1,0:T(8,128)(2,1)}, bf16[2576,128]{1,0:T(8,128)(2,1)S(1)}, u32[]{:S(2)}) copy-start(bf16[2576,128]{1,0:T(8,128)(2,1)S(1)} %collective-permute-done.strip) | copy-start | bytes 1978372
  23.6 2.6 %collective-permute-start.3 = (bf16[2576,128]{1,0:T(8,128)(2,1)S(1)}, bf16[2576,128]{1,0:T(8,128)(2,1)S(1)}, u32[]{:S(2)}, u32[]{:S(2)}) collective-permute-start(bf16[2576,128]{1,0:T(8,128)(2,1)S(1)} %collective-permute-done.strip), channel_id=1, source_target_pairs={{0,64},{64,0},{1,65},{65,1},{2,66},{66,2},{3,67},{67,3},{4,68},{68... | collective-permute-start | bytes 1978376 | tf_op jit(solution)/shard_map/ppermute | solution.py:578
  23.6 2.4 %collective-permute-start.5 = (bf16[1088,128]{1,0:T(8,128)(2,1)}, bf16[1088,128]{1,0:T(8,128)(2,1)S(1)}, u32[]{:S(2)}, u32[]{:S(2)}) collective-permute-start(bf16[1088,128]{1,0:T(8,128)(2,1)} %copy-done.8), channel_id=1, source_target_pairs={{0,64},{64,0},{1,65},{65,1},{2,66},{66,2},{3,67},{67,3},{4,68},{68... | collective-permute-start | bytes 835592 | tf_op jit(solution)/shard_map/ppermute | solution.py:578
  24.1 2.1 %collective-permute-start.4 = (bf16[256,128]{1,0:T(8,128)(2,1)S(1)}, bf16[256,128]{1,0:T(8,128)(2,1)S(1)}, u32[]{:S(2)}, u32[]{:S(2)}) collective-permute-start(bf16[256,128]{1,0:T(8,128)(2,1)S(1)} %collective-permute-done.1.rims), channel_id=1, source_target_pairs={{0,64},{64,0},{1,65},{65,1},{2,66},{66,2},{3,67},{67,3},{4,68},{68... | collective-permute-start | bytes 196616 | tf_op jit(solution)/shard_map/ppermute | solution.py:578
  26.0 0.7 copy-start.9
  26.2 0.6 copy-start.13
  26.8 0.8 copy-start.4
  35.5 12.3 %collective-permute-start.6 = (bf16[1024,128]{1,0:T(8,128)(2,1)}, bf16[1024,128]{1,0:T(8,128)(2,1)S(1)}, u32[]{:S(2)}, u32[]{:S(2)}) collective-permute-start(bf16[1024,128]{1,0:T(8,128)(2,1)} %get-tuple-element.49.own_ref), channel_id=1, source_target_pairs={{0,1},{1,0},{2,3},{3,2},{4,5},{5,4},{6,7},{7,6},{8,9},{9,8},{10,11... | collective-permute-start | bytes 786440 | tf_op jit(solution)/shard_map/ppermute | solution.py:578
  39.1 1.9 %collective-permute-start.7 = (bf16[960,128]{1,0:T(8,128)(2,1)}, bf16[960,128]{1,0:T(8,128)(2,1)S(1)}, u32[]{:S(2)}, u32[]{:S(2)}) collective-permute-start(bf16[960,128]{1,0:T(8,128)(2,1)} %get-tuple-element.57.near_ref), channel_id=1, source_target_pairs={{0,64},{64,0},{1,65},{65,1},{2,66},{66,2},{3,67},{67,3},{4,68},{68... | collective-permute-start | bytes 737288 | tf_op jit(solution)/shard_map/ppermute | solution.py:578
  39.7 32.8 %collective-permute-start.11 = (f32[960,128]{1,0:T(8,128)}, f32[960,128]{1,0:T(8,128)S(1)}, u32[]{:S(2)}, u32[]{:S(2)}) collective-permute-start(f32[960,128]{1,0:T(8,128)} %get-tuple-element.61.resid_ref), channel_id=1, source_target_pairs={{0,64},{64,0},{1,65},{65,1},{2,66},{66,2},{3,67},{67,3},{4,68},{68... | collective-permute-start | bytes 1474568 | tf_op jit(solution)/shard_map/ppermute | solution.py:578
  41.1 0.9 copy-start.2
  42.0 13.2 %collective-permute-start.9 = (bf16[192,128]{1,0:T(8,128)(2,1)S(1)}, bf16[192,128]{1,0:T(8,128)(2,1)S(1)}, u32[]{:S(2)}, u32[]{:S(2)}) collective-permute-start(bf16[192,128]{1,0:T(8,128)(2,1)S(1)} %get-tuple-element.59), channel_id=1, source_target_pairs={{64,3},{65,2},{66,5},{67,4},{68,7},{69,6},{70,9},{71,8},{72,11},{7... | collective-permute-start | bytes 147464 | tf_op jit(solution)/shard_map/ppermute | solution.py:585
  45.4 10.1 %collective-permute-start.8 = (bf16[1920,128]{1,0:T(8,128)(2,1)S(1)}, bf16[1920,128]{1,0:T(8,128)(2,1)S(1)}, u32[]{:S(2)}, u32[]{:S(2)}) collective-permute-start(bf16[1920,128]{1,0:T(8,128)(2,1)S(1)} %get-tuple-element.58), channel_id=1, source_target_pairs={{64,2},{66,4},{68,6},{70,8},{72,10},{74,12},{76,14},{78,16},{80,18... | collective-permute-start | bytes 1474568 | tf_op jit(solution)/shard_map/ppermute | solution.py:585
  47.8 0.7 copy-start.10
  55.2 17.3 %copy-start.14 = (bf16[192,128]{1,0:T(8,128)(2,1)}, bf16[192,128]{1,0:T(8,128)(2,1)S(1)}, u32[]{:S(2)}) copy-start(bf16[192,128]{1,0:T(8,128)(2,1)S(1)} %collective-permute-done.9.rims) | copy-start | bytes 147460
  55.5 17.1 %copy-start.6 = (bf16[1920,128]{1,0:T(8,128)(2,1)}, bf16[1920,128]{1,0:T(8,128)(2,1)S(1)}, u32[]{:S(2)}) copy-start(bf16[1920,128]{1,0:T(8,128)(2,1)S(1)} %collective-permute-done.8.strip) | copy-start | bytes 1474564
  55.5 17.1 %collective-permute-start.12 = (bf16[1920,128]{1,0:T(8,128)(2,1)S(1)}, bf16[1920,128]{1,0:T(8,128)(2,1)S(1)}, u32[]{:S(2)}, u32[]{:S(2)}) collective-permute-start(bf16[1920,128]{1,0:T(8,128)(2,1)S(1)} %collective-permute-done.8.strip), channel_id=1, source_target_pairs={{0,64},{64,0},{1,65},{65,1},{2,66},{66,2},{3,67},{67,3},{4,68},{68... | collective-permute-start | bytes 1474568 | tf_op jit(solution)/shard_map/ppermute | solution.py:578
  55.5 2.2 %collective-permute-start.10 = (bf16[1024,128]{1,0:T(8,128)(2,1)}, bf16[1024,128]{1,0:T(8,128)(2,1)S(1)}, u32[]{:S(2)}, u32[]{:S(2)}) collective-permute-start(bf16[1024,128]{1,0:T(8,128)(2,1)} %get-tuple-element.60), channel_id=1, source_target_pairs={{0,64},{64,0},{1,65},{65,1},{2,66},{66,2},{3,67},{67,3},{4,68},{68... | collective-permute-start | bytes 786440 | tf_op jit(solution)/shard_map/ppermute | solution.py:578
  56.0 16.5 %collective-permute-start.14 = (bf16[1024,128]{1,0:T(8,128)(2,1)}, bf16[1024,128]{1,0:T(8,128)(2,1)S(1)}, u32[]{:S(2)}, u32[]{:S(2)}) collective-permute-start(bf16[1024,128]{1,0:T(8,128)(2,1)} %copy-done.10), channel_id=1, source_target_pairs={{0,64},{64,0},{1,65},{65,1},{2,66},{66,2},{3,67},{67,3},{4,68},{68... | collective-permute-start | bytes 786440 | tf_op jit(solution)/shard_map/ppermute | solution.py:578
  56.0 16.5 %collective-permute-start.13 = (bf16[192,128]{1,0:T(8,128)(2,1)S(1)}, bf16[192,128]{1,0:T(8,128)(2,1)S(1)}, u32[]{:S(2)}, u32[]{:S(2)}) collective-permute-start(bf16[192,128]{1,0:T(8,128)(2,1)S(1)} %collective-permute-done.9.rims), channel_id=1, source_target_pairs={{0,64},{64,0},{1,65},{65,1},{2,66},{66,2},{3,67},{67,3},{4,68},{68... | collective-permute-start | bytes 147464 | tf_op jit(solution)/shard_map/ppermute | solution.py:578
  57.7 1.0 copy-start
  59.5 22.5 %all-to-all-start = ((bf16[32,32,128]{2,1,0:T(8,128)(2,1)}), bf16[32,32,128]{2,1,0:T(8,128)(2,1)S(1)}, u32[]{:S(2)}, u32[]{:S(2)}) async-start(bf16[32,32,128]{2,1,0:T(8,128)(2,1)} %bitcast.5), calls=%async_computation | async-start | bytes 524288 | tf_op jit(solution)/shard_map/all_to_all | solution.py:636
  72.5 0.8 copy-start.5
  72.5 0.9 copy-start.11
  72.6 0.8 copy-start.15
  72.6 1.0 copy-start.7
  81.9 13.5 %copy-start.1 = (f32[960,128]{1,0:T(8,128)S(1)}, f32[960,128]{1,0:T(8,128)}, u32[]{:S(2)}) copy-start(f32[960,128]{1,0:T(8,128)} %shard_map.125.mine_ref) | copy-start | bytes 1474564
  82.8 21.8 %all-to-all-start.1 = ((bf16[64,32,128]{2,1,0:T(8,128)(2,1)}), bf16[64,32,128]{2,1,0:T(8,128)(2,1)S(1)}, u32[]{:S(2)}, u32[]{:S(2)}) async-start(bf16[64,32,128]{2,1,0:T(8,128)(2,1)} %shard_map.127), calls=%async_computation.1 | async-start | bytes 1048576 | tf_op jit(solution)/shard_map/all_to_all | solution.py:645
  92.6 2.8 %collective-permute-start.15 = (f32[960,128]{1,0:T(8,128)}, f32[960,128]{1,0:T(8,128)S(1)}, u32[]{:S(2)}, u32[]{:S(2)}) collective-permute-start(f32[960,128]{1,0:T(8,128)} %shard_map.125.mine_ref), channel_id=1, source_target_pairs={{0,64},{64,0},{1,65},{65,1},{2,66},{66,2},{3,67},{67,3},{4,68},{68... | collective-permute-start | bytes 1474568 | tf_op jit(solution)/shard_map/ppermute | solution.py:578
  104.6 3.8 %collective-permute-start.16 = (bf16[64,32,128]{2,1,0:T(8,128)(2,1)S(1)}, bf16[64,32,128]{2,1,0:T(8,128)(2,1)S(1)}, u32[]{:S(2)}, u32[]{:S(2)}) collective-permute-start(bf16[64,32,128]{2,1,0:T(8,128)(2,1)S(1)} %all-to-all-done.1.own_ref), channel_id=1, source_target_pairs={{0,64},{64,0},{1,65},{65,1},{2,66},{66,2},{3,67},{67,3},{4,68},{68... | collective-permute-start | bytes 1572872 | tf_op jit(solution)/shard_map/ppermute | solution.py:578

commit v5 on v4

--- a/solution.py
+++ b/solution.py
@@ -546,7 +546,7 @@
     return pl.BlockSpec((rows, *value.shape[1:]), lambda i: (0,) * len(value.shape), pipeline_mode=pl.Buffered(1))
 
 
-def call(kernel, n_smem, operands, outs, scratch=(), flops=0, limit=60, steps=1, in_along=None, out_along=None):
+def call(kernel, n_smem, operands, outs, scratch=(), flops=0, limit=40, steps=1, in_along=None, out_along=None):
     def specs(values, along):
         along = along or [None] * len(values)
         return [whole(v) if at is None else first_rows(at, v) if at > 1 else stripes(v, at) for v, at in zip(values, along, strict=True)]
@@ -593,6 +593,7 @@
     strip, edges, columns, first, third_t = call(
         pack_kernel, 1, (edge_turn, state, sound, w_first, w_third.T, b_first[None]),
         (shape(8 * FIELD + 16, 128, dtype=BF), shape(4 * RIM, 128, dtype=BF), shape(BLK * GROUP + RIM, 128, dtype=BF), shape(feats, hid, dtype=BF), shape(feats, hid, dtype=BF)),
+        limit=60,
     )
     own_col = swap(columns, "lev")
     strip, rims = strip_swaps(strip, edges, tiles)
@@ -627,24 +628,23 @@
         (pltpu.VMEM((hid, STRIPE), BF), pltpu.VMEM((hid, STRIPE), BF), pltpu.VMEM((n_rows, 256), F32)),
         flops=LONG, steps=COLS // STRIPE, in_along=(0, 0, 1, None, None, None, 1, 1, 1, 1),
     )
-    given, r_strip, r_rims = lax.optimization_barrier((given, r_strip, r_rims))
-    r_partner, r_partner_rims, r_other_col = swap(r_strip, "sec"), swap(r_rims, "sec"), swap(r_own_col, "sec")
     received = swap(given, "sec")
     share = n_rows // tiles
     (partial,) = call(add_kernel, 0, (kept, received), (shape(n_rows, 128, dtype=BF),), limit=16)
     partial = partial.reshape(tiles, share, 128)
     parts = lax.all_to_all(partial, "tile", 0, 0)
+    (everywhere,) = call(mean_kernel, 0, (parts,), (shape(2 * tiles, share, 128, dtype=BF),), limit=16)
+    everywhere, coeff, r_strip, r_rims = lax.optimization_barrier((everywhere, coeff, r_strip, r_rims))
+    r_partner, r_partner_rims, r_other_col = swap(r_strip, "sec"), swap(r_rims, "sec"), swap(r_own_col, "sec")
+    gathered = lax.all_to_all(everywhere, ("tile", "lev"), 0, 0)
     (mine,) = call(
         adjoint_kernel, 0,
         (resid, r_other, input_grad, coeff, factors, r_strip, r_partner, r_rims, r_partner_rims, r_own_col, r_other_col),
-        (shape(3 * FIELD, 128),), stencil_scratch((pltpu.VMEM((EXT, ROWS, 128), F32),)), flops=LONG,
+        (shape(3 * FIELD, 128),), stencil_scratch((pltpu.VMEM((EXT, ROWS, 128), F32),)), flops=LONG, limit=60,
         in_along=(*[None] * 6, 3 * FIELD, *[None] * 4),
     )
-    parts, mine = lax.optimization_barrier((parts, mine))
-    (everywhere,) = call(mean_kernel, 0, (parts,), (shape(2 * tiles, share, 128, dtype=BF),), limit=16)
-    gathered = lax.all_to_all(everywhere, ("tile", "lev"), 0, 0)
-    (state_grad,) = call(place_rows_kernel, 0, (mine, swap(mine, "sec")), (shape(3, OWN, 2 * BLK, 128),), limit=16)
-    state_grad, gathered = lax.optimization_barrier((state_grad, gathered))
+    theirs, gathered = lax.optimization_barrier((swap(mine, "sec"), gathered))
+    (state_grad,) = call(place_rows_kernel, 0, (mine, theirs), (shape(3, OWN, 2 * BLK, 128),), limit=16)
     g_first, g_bias, g_second, g_third_t = call(
         spread_gradients_kernel, 0, (gathered, swap(gathered, "sec")),
         (shape(6 * OWN, hid), shape(1, hid), shape(hid, hid), shape(6 * OWN, hid)), limit=16,

time: 110 us -> 99.3 us (0.903)
  Pallas kernels: 35.3 us -> 26.8 us
  starting transfers between devices: 47.8 us -> 45.3 us
  waiting for transfers between devices: 20 us -> 17.7 us
  local copies, waits for them, and re-layouts: 5.84 us -> 7.92 us
    pallas_call x10, Pallas kernels: 35.3 us -> 26.8 us  [call(): pl.pallas_call(kernel, grid=(steps,), out_shape=outs, in_specs=[smem] * n...]
    all_to_all x1, waiting for transfers between devices: 8.1 us -> 2.55 us  [local(): gathered = lax.all_to_all(everywhere, ('tile', 'lev'), 0, 0)]
    all_to_all x1, waiting for transfers between devices: 0.01 us -> 4.91 us  [local(): parts = lax.all_to_all(partial, 'tile', 0, 0)]
    ppermute x2, waiting for transfers between devices: 4.12 us -> 1.87 us  [strip_swaps(): lax.ppermute(strip, ('sec', 'tile'), pairs)]
    unnamed x32 -> x44, local copies, waits for them, and re-layouts: 5.84 us -> 7.92 us
    all_to_all x1, starting transfers between devices: 13 us -> 11.3 us  [local(): parts = lax.all_to_all(partial, 'tile', 0, 0)]
  transfers between devices with their start and end apart: 19 -> 19, of which waited for: 9 -> 6; matrix products, arithmetic and copies ran while one was open for 0% -> 0% of each run, Pallas kernels for 20% -> 17%
where the time goes in v5:
time: 99.3 us; the launch traced here: 98.7 us
  starting transfers between devices  45.3 us (46%)
  Pallas kernels  26.8 us (27%)
  waiting for transfers between devices  17.7 us (18%)
  local copies, waits for them, and re-layouts  7.92 us (8%)
    pallas_call x10, Pallas kernels, call(): pl.pallas_call(kernel, grid=(steps,), out_shape=outs, in_specs=[smem] * n...  26.8 us
    ppermute x13, starting transfers between devices, swap(): return lax.ppermute(value, axis, [(0, 1), (1, 0)])  12.2 us
    all_to_all x1, starting transfers between devices, local(): parts = lax.all_to_all(partial, 'tile', 0, 0)  11.3 us
    all_to_all x1, starting transfers between devices, local(): gathered = lax.all_to_all(everywhere, ('tile', 'lev'), 0, 0)  8.96 us
    ppermute x13, waiting for transfers between devices, swap(): return lax.ppermute(value, axis, [(0, 1), (1, 0)])  8.39 us
    unnamed x44, local copies, waits for them, and re-layouts  7.92 us
    ppermute x2, starting transfers between devices, strip_swaps(): lax.ppermute(edges, ('sec', 'tile', 'lev'), cross)  7.25 us
    ppermute x2, starting transfers between devices, strip_swaps(): lax.ppermute(strip, ('sec', 'tile'), pairs)  5.6 us
  transfers between devices with their start and end apart: 19, of which 6 were waited for; matrix products, arithmetic and copies ran while one was open for 0% of the time, Pallas kernels for 17%

profile of v5, /device:TPU:1, one launch (start us, length us, event | category | flops | bytes accessed | tf_op | source)
XLA Modules:
  0.0 98.7 jit_solution(10030788456296425107)
XLA Ops:
  0.6 2.9 %shard_map.119 = (bf16[2576,128]{1,0:T(8,128)(2,1)}, bf16[256,128]{1,0:T(8,128)(2,1)}, bf16[1088,128]{1,0:T(8,128)(2,1)}, bf16[256,512]{1,0:T(8,128)(2,1)}, bf16[256,512]{1,0:T(8,128)(2,1)}) custom-call(s32[1,2]{1,0:T(1,128)} %turn_ref.3, f32[1920,128]{1,0:T(8,128)} %bitcast.8, f32[640,128]{1,0:T(8,128)} %bitcast.10, bf16[240,512]{1,0:T(8,128)(2,1)} %first_ref.1, ...), custom_call_target="tpu_custom_call" | custom-call | tf_op jit(solution)/shard_map/pallas_call | solution.py:555
  3.5 3.8 %collective-permute-start.2 = (bf16[1088,128]{1,0:T(8,128)(2,1)}, bf16[1088,128]{1,0:T(8,128)(2,1)S(1)}, u32[]{:S(2)}, u32[]{:S(2)}) collective-permute-start(bf16[1088,128]{1,0:T(8,128)(2,1)} %get-tuple-element.41.own_ref), channel_id=1, source_target_pairs={{0,1},{1,0},{2,3},{3,2},{4,5},{5,4},{6,7},{7,6},{8,9},{9,8},{10,11... | collective-permute-start | bytes 835592 | tf_op jit(solution)/shard_map/ppermute | solution.py:578
  7.3 4.1 %collective-permute-start.1 = (bf16[256,128]{1,0:T(8,128)(2,1)}, bf16[256,128]{1,0:T(8,128)(2,1)S(1)}, u32[]{:S(2)}, u32[]{:S(2)}) collective-permute-start(bf16[256,128]{1,0:T(8,128)(2,1)} %get-tuple-element.40), channel_id=1, source_target_pairs={{64,3},{65,2},{66,5},{67,4},{68,7},{69,6},{70,9},{71,8},{72,11},{7... | collective-permute-start | bytes 196616 | tf_op jit(solution)/shard_map/ppermute | solution.py:585
  11.4 2.2 %collective-permute-start = (bf16[2576,128]{1,0:T(8,128)(2,1)}, bf16[2576,128]{1,0:T(8,128)(2,1)S(1)}, u32[]{:S(2)}, u32[]{:S(2)}) collective-permute-start(bf16[2576,128]{1,0:T(8,128)(2,1)} %get-tuple-element.39), channel_id=1, source_target_pairs={{64,2},{66,4},{68,6},{70,8},{72,10},{74,12},{76,14},{78,16},{80,18... | collective-permute-start | bytes 1978376 | tf_op jit(solution)/shard_map/ppermute | solution.py:585
  13.6 0.0 collective-permute-done.2.other_ref.own_col
  13.6 0.0 copy-start.4
  13.6 1.2 %copy-done.4 = f32[3,40,16,128]{3,2,1,0:T(8,128)S(1)} copy-done((f32[3,40,16,128]{3,2,1,0:T(8,128)S(1)}, f32[3,40,16,128]{3,2,1,0:T(8,128)}, u32[]{:S(2)}) %copy-start.4) | copy-done | bytes 983064
  14.8 1.0 %copy-done.5 = bf16[512,512]{1,0:T(8,128)(2,1)S(1)} copy-done((bf16[512,512]{1,0:T(8,128)(2,1)S(1)}, bf16[512,512]{1,0:T(8,128)(2,1)}, u32[]{:S(2)}) %copy-start.5) | copy-done | bytes 524312
  15.9 1.0 copy-done.8
  16.8 0.9 copy-done.10
  17.8 0.9 copy-done.12
  18.7 3.0 %shard_map.120 = (bf16[256,1024]{1,0:T(8,128)(2,1)S(1)}, bf16[512,1024]{1,0:T(8,128)(2,1)S(1)}, bf16[512,1024]{1,0:T(8,128)(2,1)S(1)}, f32[512,1024]{1,0:T(8,128...) custom-call(bf16[1088,128]{1,0:T(8,128)(2,1)S(1)} %copy-done.8, ...), custom_call_target="tpu_custom_call" | custom-call | flops 20000000000 | tf_op jit(solution)/shard_map/pallas_call | solution.py:555
  21.7 1.9 %collective-permute-done.strip = bf16[2576,128]{1,0:T(8,128)(2,1)S(1)} collective-permute-done((bf16[2576,128]{1,0:T(8,128)(2,1)}, bf16[2576,128]{1,0:T(8,128)(2,1)S(1)}, u32[]{:S(2)}, u32[]{:S(2)}) %collective-permute-start) | collective-permute-done | bytes 659488 | tf_op jit(solution)/shard_map/ppermute | solution.py:585
  23.6 0.5 collective-permute-start.5
  24.1 0.1 collective-permute-start.4
  24.2 1.9 %collective-permute-done.5.other_col = bf16[1088,128]{1,0:T(8,128)(2,1)S(1)} collective-permute-done((bf16[1088,128]{1,0:T(8,128)(2,1)S(1)}, bf16[1088,128]{1,0:T(8,128)(2,1)S(1)}, u32[]{:S(2)}, u32[]{:S(2)}) %collective-permute-start.5) | collective-permute-done | bytes 278560 | tf_op jit(solution)/shard_map/ppermute | solution.py:578
  26.1 0.1 collective-permute-done.4.partner_rims
  26.2 5.2 %shard_map.121 = (f32[960,128]{1,0:T(8,128)S(1)}, bf16[960,128]{1,0:T(8,128)(2,1)S(1)}, bf16[1024,128]{1,0:T(8,128)(2,1)S(1)}, f32[48,56,128]{2,1,0:T(8,128)S(1)}, f32[4,8,128]{2,1,0:T(8,128)S(1)}) custom-call(s32[1,2]{1,0:T(1,128)S(1)} %copy-done.3, f32[1920,128]{1,0:T(8,128)S(1)} %bitcast.9, f32[640,128]{1,0:T(8,128)S(1)} %bitcast.11, ...), custom_call_target="tpu_custom_call" | custom-call | flops 20000000000 | tf_op jit(solution)/shard_map/pallas_call | solution.py:555
  31.4 0.0 copy-start.7
  31.5 3.9 %collective-permute-start.7 = (bf16[1024,128]{1,0:T(8,128)(2,1)S(1)}, bf16[1024,128]{1,0:T(8,128)(2,1)S(1)}, u32[]{:S(2)}, u32[]{:S(2)}) collective-permute-start(bf16[1024,128]{1,0:T(8,128)(2,1)S(1)} %get-tuple-element.49.own_ref), channel_id=1, source_target_pairs={{0,1},{1,0},{2,3},{3,2},{4,5},{5,4},{6,7},{7,6},{8,9},{9,8},{10,11... | collective-permute-start | bytes 786440 | tf_op jit(solution)/shard_map/ppermute | solution.py:578
  35.4 0.3 collective-permute-start.9
  35.7 6.3 %collective-permute-done.7.other_ref.own_col = bf16[1024,128]{1,0:T(8,128)(2,1)S(1)} collective-permute-done((bf16[1024,128]{1,0:T(8,128)(2,1)S(1)}, bf16[1024,128]{1,0:T(8,128)(2,1)S(1)}, u32[]{:S(2)}, u32[]{:S(2)}) %collective-permute-start.7) | collective-permute-done | bytes 262176 | tf_op jit(solution)/shard_map/ppermute | solution.py:578
  42.0 3.3 %shard_map.122 = (bf16[1024,128]{1,0:T(8,128)(2,1)S(1)}, f32[1024,128]{1,0:T(8,128)S(1)}, f32[960,128]{1,0:T(8,128)S(1)}) custom-call(bf16[1024,128]{1,0:T(8,128)(2,1)S(1)} %get-tuple-element.49.own_ref, bf16[1024,128]{1,0:T(8,128)(2,1)S(1)} %collective-permute-done.7.other_ref.own_col, bf16[256,1024]{1,0:T(8,128)(2,1)S(1)} %get-tuple-element.50.feat_ref, ...), custom_call_target="tpu_custom_call" | custom-call | flops 20000000000 | tf_op jit(solution)/shard_map/pallas_call | solution.py:555
  45.3 0.0 copy-start.14
  45.4 0.8 copy-done.14
  46.1 0.6 collective-permute-start.8
  46.8 3.4 %collective-permute-start.10 = (bf16[1920,128]{1,0:T(8,128)(2,1)S(1)}, bf16[1920,128]{1,0:T(8,128)(2,1)S(1)}, u32[]{:S(2)}, u32[]{:S(2)}) collective-permute-start(bf16[1920,128]{1,0:T(8,128)(2,1)S(1)} %get-tuple-element.60), channel_id=1, source_target_pairs={{64,2},{66,4},{68,6},{70,8},{72,10},{74,12},{76,14},{78,16},{80,18... | collective-permute-start | bytes 1474568 | tf_op jit(solution)/shard_map/ppermute | solution.py:585
  50.2 0.7 shard_map.123
  51.0 11.3 %all-to-all-start = ((bf16[32,32,128]{2,1,0:T(8,128)(2,1)}), bf16[32,32,128]{2,1,0:T(8,128)(2,1)S(1)}, u32[]{:S(2)}, u32[]{:S(2)}) async-start(bf16[32,32,128]{2,1,0:T(8,128)(2,1)} %bitcast.5), calls=%async_computation | async-start | bytes 524288 | tf_op jit(solution)/shard_map/all_to_all | solution.py:635
  62.3 3.1 %collective-permute-start.11 = (bf16[192,128]{1,0:T(8,128)(2,1)S(1)}, bf16[192,128]{1,0:T(8,128)(2,1)S(1)}, u32[]{:S(2)}, u32[]{:S(2)}) collective-permute-start(bf16[192,128]{1,0:T(8,128)(2,1)S(1)} %get-tuple-element.61), channel_id=1, source_target_pairs={{64,3},{65,2},{66,5},{67,4},{68,7},{69,6},{70,9},{71,8},{72,11},{7... | collective-permute-start | bytes 147464 | tf_op jit(solution)/shard_map/ppermute | solution.py:585
  65.4 0.1 collective-permute-start.6
  65.5 4.9 %all-to-all-done.parts_ref = bf16[32,32,128]{2,1,0:T(8,128)(2,1)S(1)} async-done(((bf16[32,32,128]{2,1,0:T(8,128)(2,1)}), bf16[32,32,128]{2,1,0:T(8,128)(2,1)S(1)}, u32[]{:S(2)}, u32[]{:S(2)}) %all-to-all-start) | async-done | bytes 262176 | tf_op jit(solution)/shard_map/all_to_all | solution.py:635
  70.4 0.9 shard_map.124
  71.3 0.1 collective-permute-start.12
  71.4 0.5 collective-permute-start.14
  71.9 0.1 collective-permute-start.13
  72.0 9.0 %all-to-all-start.1 = ((bf16[64,32,128]{2,1,0:T(8,128)(2,1)}), bf16[64,32,128]{2,1,0:T(8,128)(2,1)S(1)}, u32[]{:S(2)}, u32[]{:S(2)}) async-start(bf16[64,32,128]{2,1,0:T(8,128)(2,1)} %shard_map.124), calls=%async_computation.1 | async-start | bytes 1048576 | tf_op jit(solution)/shard_map/all_to_all | solution.py:639
  81.0 0.0 copy-start.17
  81.1 0.7 copy-done.17
  81.7 0.1 copy-done.19
  81.9 0.2 copy-done.18
  82.0 8.3 %shard_map.126.mine_ref = f32[960,128]{1,0:T(8,128)} custom-call(f32[960,128]{1,0:T(8,128)} %copy-done.7, f32[960,128]{1,0:T(8,128)} %copy-done.17, f32[960,128]{1,0:T(8,128)} %copy-done.14, f32[48,56,128]{2,1,0:T(8,128)} %copy-done.13, f32[4,8,128]{2,1,0:T(8,128)} %copy-done.15, bf16[1920,128]{1,0:T(8,128)(2,1)} %copy-done.16, ...), custom_call_target="tpu_custom_call" | custom-call | flops 20000000000 | tf_op jit(solution)/shard_map/pallas_call | solution.py:555
  90.4 0.6 collective-permute-start.15
  91.0 2.5 %all-to-all-done.1.own_ref = bf16[64,32,128]{2,1,0:T(8,128)(2,1)S(1)} async-done(((bf16[64,32,128]{2,1,0:T(8,128)(2,1)}), bf16[64,32,128]{2,1,0:T(8,128)(2,1)S(1)}, u32[]{:S(2)}, u32[]{:S(2)}) %all-to-all-start.1) | async-done | bytes 524320 | tf_op jit(solution)/shard_map/all_to_all | solution.py:639
  93.5 1.7 %collective-permute-start.16 = (bf16[64,32,128]{2,1,0:T(8,128)(2,1)S(1)}, bf16[64,32,128]{2,1,0:T(8,128)(2,1)S(1)}, u32[]{:S(2)}, u32[]{:S(2)}) collective-permute-start(bf16[64,32,128]{2,1,0:T(8,128)(2,1)S(1)} %all-to-all-done.1.own_ref), channel_id=1, source_target_pairs={{0,64},{64,0},{1,65},{65,1},{2,66},{66,2},{3,67},{67,3},{4,68},{68... | collective-permute-start | bytes 1572872 | tf_op jit(solution)/shard_map/ppermute | solution.py:578
  95.2 1.0 %copy-done.1 = f32[960,128]{1,0:T(8,128)S(1)} copy-done((f32[960,128]{1,0:T(8,128)S(1)}, f32[960,128]{1,0:T(8,128)}, u32[]{:S(2)}) %copy-start.1) | copy-done | bytes 491544
  96.2 1.0 %shard_map.127 = f32[3,40,16,128]{3,2,1,0:T(8,128)} custom-call(f32[960,128]{1,0:T(8,128)S(1)} %copy-done.1, f32[960,128]{1,0:T(8,128)S(1)} %collective-permute-done.15.theirs_ref), custom_call_target="tpu_custom_call" | custom-call | tf_op jit(solution)/shard_map/pallas_call | solution.py:555
  97.2 1.4 %shard_map.128 = (f32[240,512]{1,0:T(8,128)}, f32[1,512]{1,0:T(1,128)}, f32[512,512]{1,0:T(8,128)}, f32[240,512]{1,0:T(8,128)}) custom-call(bf16[64,32,128]{2,1,0:T(8,128)(2,1)S(1)} %all-to-all-done.1.own_ref, bf16[64,32,128]{2,1,0:T(8,128)(2,1)S(1)} %collective-permute-done.16.partner_ref), custom_call_target="tpu_custom_call" | custom-call | tf_op jit(solution)/shard_map/pallas_call | solution.py:555
  (44 shorter events, 0.1 us)
Async XLA Ops:
  3.5 10.1 %collective-permute-start.2 = (bf16[1088,128]{1,0:T(8,128)(2,1)}, bf16[1088,128]{1,0:T(8,128)(2,1)S(1)}, u32[]{:S(2)}, u32[]{:S(2)}) collective-permute-start(bf16[1088,128]{1,0:T(8,128)(2,1)} %get-tuple-element.41.own_ref), channel_id=1, source_target_pairs={{0,1},{1,0},{2,3},{3,2},{4,5},{5,4},{6,7},{7,6},{8,9},{9,8},{10,11... | collective-permute-start | bytes 835592 | tf_op jit(solution)/shard_map/ppermute | solution.py:578
  7.3 14.4 %collective-permute-start.1 = (bf16[256,128]{1,0:T(8,128)(2,1)}, bf16[256,128]{1,0:T(8,128)(2,1)S(1)}, u32[]{:S(2)}, u32[]{:S(2)}) collective-permute-start(bf16[256,128]{1,0:T(8,128)(2,1)} %get-tuple-element.40), channel_id=1, source_target_pairs={{64,3},{65,2},{66,5},{67,4},{68,7},{69,6},{70,9},{71,8},{72,11},{7... | collective-permute-start | bytes 196616 | tf_op jit(solution)/shard_map/ppermute | solution.py:585
  11.4 12.2 %collective-permute-start = (bf16[2576,128]{1,0:T(8,128)(2,1)}, bf16[2576,128]{1,0:T(8,128)(2,1)S(1)}, u32[]{:S(2)}, u32[]{:S(2)}) collective-permute-start(bf16[2576,128]{1,0:T(8,128)(2,1)} %get-tuple-element.39), channel_id=1, source_target_pairs={{64,2},{66,4},{68,6},{70,8},{72,10},{74,12},{76,14},{78,16},{80,18... | collective-permute-start | bytes 1978376 | tf_op jit(solution)/shard_map/ppermute | solution.py:585
  13.6 1.2 %copy-start.4 = (f32[3,40,16,128]{3,2,1,0:T(8,128)S(1)}, f32[3,40,16,128]{3,2,1,0:T(8,128)}, u32[]{:S(2)}) copy-start(f32[3,40,16,128]{3,2,1,0:T(8,128)} %param.10) | copy-start | bytes 2949124
  14.8 1.0 %copy-start.5 = (bf16[512,512]{1,0:T(8,128)(2,1)S(1)}, bf16[512,512]{1,0:T(8,128)(2,1)}, u32[]{:S(2)}) copy-start(bf16[512,512]{1,0:T(8,128)(2,1)} %second_ref.3) | copy-start | bytes 1572868
  15.9 1.0 copy-start.8
  16.8 0.9 copy-start.10
  17.8 0.9 copy-start.12
  18.7 7.5 %copy-start = (f32[3,40,16,128]{3,2,1,0:T(8,128)S(1)}, f32[3,40,16,128]{3,2,1,0:T(8,128)}, u32[]{:S(2)}) copy-start(f32[3,40,16,128]{3,2,1,0:T(8,128)} %param.8) | copy-start | bytes 2949124
  18.7 7.5 %copy-start.2 = (f32[40,16,128]{2,1,0:T(8,128)S(1)}, f32[40,16,128]{2,1,0:T(8,128)}, u32[]{:S(2)}) copy-start(f32[40,16,128]{2,1,0:T(8,128)} %param.9) | copy-start | bytes 983044
  18.7 7.5 %copy-start.3 = (s32[1,2]{1,0:T(1,128)S(1)}, s32[1,2]{1,0:T(1,128)}, u32[]{:S(2)}) copy-start(s32[1,2]{1,0:T(1,128)} %turn_ref.3) | copy-start | bytes 28
  23.6 18.4 %copy-start.6 = (bf16[512,512]{1,0:T(8,128)(2,1)S(1)}, bf16[512,512]{1,0:T(8,128)(2,1)}, u32[]{:S(2)}) copy-start(bf16[512,512]{1,0:T(8,128)(2,1)} %second_ref.3) | copy-start | bytes 1572868
  23.6 18.4 %copy-start.11 = (bf16[256,512]{1,0:T(8,128)(2,1)S(1)}, bf16[256,512]{1,0:T(8,128)(2,1)}, u32[]{:S(2)}) copy-start(bf16[256,512]{1,0:T(8,128)(2,1)} %get-tuple-element.42.first_ref) | copy-start | bytes 786436
  23.6 2.6 %collective-permute-start.3 = (bf16[2576,128]{1,0:T(8,128)(2,1)S(1)}, bf16[2576,128]{1,0:T(8,128)(2,1)S(1)}, u32[]{:S(2)}, u32[]{:S(2)}) collective-permute-start(bf16[2576,128]{1,0:T(8,128)(2,1)S(1)} %collective-permute-done.strip), channel_id=1, source_target_pairs={{0,64},{64,0},{1,65},{65,1},{2,66},{66,2},{3,67},{67,3},{4,68},{68... | collective-permute-start | bytes 1978376 | tf_op jit(solution)/shard_map/ppermute | solution.py:578
  23.6 2.5 %collective-permute-start.5 = (bf16[1088,128]{1,0:T(8,128)(2,1)S(1)}, bf16[1088,128]{1,0:T(8,128)(2,1)S(1)}, u32[]{:S(2)}, u32[]{:S(2)}) collective-permute-start(bf16[1088,128]{1,0:T(8,128)(2,1)S(1)} %collective-permute-done.2.other_ref.own_col), channel_id=1, source_target_pairs={{0,64},{64,0},{1,65},{65,1},{2,66},{66,2},{3,67},{67,3},{4,68},{68... | collective-permute-start | bytes 835592 | tf_op jit(solution)/shard_map/ppermute | solution.py:578
  24.1 2.1 %collective-permute-start.4 = (bf16[256,128]{1,0:T(8,128)(2,1)S(1)}, bf16[256,128]{1,0:T(8,128)(2,1)S(1)}, u32[]{:S(2)}, u32[]{:S(2)}) collective-permute-start(bf16[256,128]{1,0:T(8,128)(2,1)S(1)} %collective-permute-done.1.rims), channel_id=1, source_target_pairs={{0,64},{64,0},{1,65},{65,1},{2,66},{66,2},{3,67},{67,3},{4,68},{68... | collective-permute-start | bytes 196616 | tf_op jit(solution)/shard_map/ppermute | solution.py:578
  31.4 13.9 %copy-start.13 = (f32[48,56,128]{2,1,0:T(8,128)}, f32[48,56,128]{2,1,0:T(8,128)S(1)}, u32[]{:S(2)}) copy-start(f32[48,56,128]{2,1,0:T(8,128)S(1)} %get-tuple-element.62.c_ref) | copy-start | bytes 4128772
  31.4 13.9 %copy-start.15 = (f32[4,8,128]{2,1,0:T(8,128)}, f32[4,8,128]{2,1,0:T(8,128)S(1)}, u32[]{:S(2)}) copy-start(f32[4,8,128]{2,1,0:T(8,128)S(1)} %get-tuple-element.63.factor_ref) | copy-start | bytes 49156
  31.4 34.0 %copy-start.7 = (f32[960,128]{1,0:T(8,128)}, f32[960,128]{1,0:T(8,128)S(1)}, u32[]{:S(2)}) copy-start(f32[960,128]{1,0:T(8,128)S(1)} %get-tuple-element.48.resid_ref) | copy-start | bytes 1474564
  31.5 10.6 %collective-permute-start.7 = (bf16[1024,128]{1,0:T(8,128)(2,1)S(1)}, bf16[1024,128]{1,0:T(8,128)(2,1)S(1)}, u32[]{:S(2)}, u32[]{:S(2)}) collective-permute-start(bf16[1024,128]{1,0:T(8,128)(2,1)S(1)} %get-tuple-element.49.own_ref), channel_id=1, source_target_pairs={{0,1},{1,0},{2,3},{3,2},{4,5},{5,4},{6,7},{7,6},{8,9},{9,8},{10,11... | collective-permute-start | bytes 786440 | tf_op jit(solution)/shard_map/ppermute | solution.py:578
  35.4 11.4 %collective-permute-start.9 = (bf16[960,128]{1,0:T(8,128)(2,1)S(1)}, bf16[960,128]{1,0:T(8,128)(2,1)S(1)}, u32[]{:S(2)}, u32[]{:S(2)}) collective-permute-start(bf16[960,128]{1,0:T(8,128)(2,1)S(1)} %get-tuple-element.59.near_ref), channel_id=1, source_target_pairs={{0,64},{64,0},{1,65},{65,1},{2,66},{66,2},{3,67},{67,3},{4,68},{68... | collective-permute-start | bytes 737288 | tf_op jit(solution)/shard_map/ppermute | solution.py:578
  42.0 29.4 %copy-start.9 = (bf16[1024,128]{1,0:T(8,128)(2,1)}, bf16[1024,128]{1,0:T(8,128)(2,1)S(1)}, u32[]{:S(2)}) copy-start(bf16[1024,128]{1,0:T(8,128)(2,1)S(1)} %collective-permute-done.7.other_ref.own_col) | copy-start | bytes 786436
  45.3 0.8 copy-start.14
  46.1 4.1 %collective-permute-start.8 = (bf16[1024,128]{1,0:T(8,128)(2,1)S(1)}, bf16[1024,128]{1,0:T(8,128)(2,1)S(1)}, u32[]{:S(2)}, u32[]{:S(2)}) collective-permute-start(bf16[1024,128]{1,0:T(8,128)(2,1)S(1)} %get-tuple-element.57), channel_id=1, source_target_pairs={{0,64},{64,0},{1,65},{65,1},{2,66},{66,2},{3,67},{67,3},{4,68},{68... | collective-permute-start | bytes 786440 | tf_op jit(solution)/shard_map/ppermute | solution.py:578
  46.8 24.5 %collective-permute-start.10 = (bf16[1920,128]{1,0:T(8,128)(2,1)S(1)}, bf16[1920,128]{1,0:T(8,128)(2,1)S(1)}, u32[]{:S(2)}, u32[]{:S(2)}) collective-permute-start(bf16[1920,128]{1,0:T(8,128)(2,1)S(1)} %get-tuple-element.60), channel_id=1, source_target_pairs={{64,2},{66,4},{68,6},{70,8},{72,10},{74,12},{76,14},{78,16},{80,18... | collective-permute-start | bytes 1474568 | tf_op jit(solution)/shard_map/ppermute | solution.py:585
  51.0 19.4 %all-to-all-start = ((bf16[32,32,128]{2,1,0:T(8,128)(2,1)}), bf16[32,32,128]{2,1,0:T(8,128)(2,1)S(1)}, u32[]{:S(2)}, u32[]{:S(2)}) async-start(bf16[32,32,128]{2,1,0:T(8,128)(2,1)} %bitcast.5), calls=%async_computation | async-start | bytes 524288 | tf_op jit(solution)/shard_map/all_to_all | solution.py:635
  62.3 9.0 %collective-permute-start.11 = (bf16[192,128]{1,0:T(8,128)(2,1)S(1)}, bf16[192,128]{1,0:T(8,128)(2,1)S(1)}, u32[]{:S(2)}, u32[]{:S(2)}) collective-permute-start(bf16[192,128]{1,0:T(8,128)(2,1)S(1)} %get-tuple-element.61), channel_id=1, source_target_pairs={{64,3},{65,2},{66,5},{67,4},{68,7},{69,6},{70,9},{71,8},{72,11},{7... | collective-permute-start | bytes 147464 | tf_op jit(solution)/shard_map/ppermute | solution.py:585
  65.4 15.6 %collective-permute-start.6 = (f32[960,128]{1,0:T(8,128)S(1)}, f32[960,128]{1,0:T(8,128)S(1)}, u32[]{:S(2)}, u32[]{:S(2)}) collective-permute-start(f32[960,128]{1,0:T(8,128)S(1)} %get-tuple-element.48.resid_ref), channel_id=1, source_target_pairs={{0,64},{64,0},{1,65},{65,1},{2,66},{66,2},{3,67},{67,3},{4,68},{68... | collective-permute-start | bytes 1474568 | tf_op jit(solution)/shard_map/ppermute | solution.py:578
  71.3 9.8 %copy-start.20 = (bf16[192,128]{1,0:T(8,128)(2,1)}, bf16[192,128]{1,0:T(8,128)(2,1)S(1)}, u32[]{:S(2)}) copy-start(bf16[192,128]{1,0:T(8,128)(2,1)S(1)} %collective-permute-done.11.rims) | copy-start | bytes 147460
  71.3 9.8 %copy-start.16 = (bf16[1920,128]{1,0:T(8,128)(2,1)}, bf16[1920,128]{1,0:T(8,128)(2,1)S(1)}, u32[]{:S(2)}) copy-start(bf16[1920,128]{1,0:T(8,128)(2,1)S(1)} %collective-permute-done.10.strip) | copy-start | bytes 1474564
  71.3 9.7 %collective-permute-start.12 = (bf16[1920,128]{1,0:T(8,128)(2,1)S(1)}, bf16[1920,128]{1,0:T(8,128)(2,1)S(1)}, u32[]{:S(2)}, u32[]{:S(2)}) collective-permute-start(bf16[1920,128]{1,0:T(8,128)(2,1)S(1)} %collective-permute-done.10.strip), channel_id=1, source_target_pairs={{0,64},{64,0},{1,65},{65,1},{2,66},{66,2},{3,67},{67,3},{4,68},{68... | collective-permute-start | bytes 1474568 | tf_op jit(solution)/shard_map/ppermute | solution.py:578
  71.4 9.6 %collective-permute-start.14 = (bf16[1024,128]{1,0:T(8,128)(2,1)S(1)}, bf16[1024,128]{1,0:T(8,128)(2,1)S(1)}, u32[]{:S(2)}, u32[]{:S(2)}) collective-permute-start(bf16[1024,128]{1,0:T(8,128)(2,1)S(1)} %collective-permute-done.7.other_ref.own_col), channel_id=1, source_target_pairs={{0,64},{64,0},{1,65},{65,1},{2,66},{66,2},{3,67},{67,3},{4,68},{68... | collective-permute-start | bytes 786440 | tf_op jit(solution)/shard_map/ppermute | solution.py:578
  71.9 9.1 %collective-permute-start.13 = (bf16[192,128]{1,0:T(8,128)(2,1)S(1)}, bf16[192,128]{1,0:T(8,128)(2,1)S(1)}, u32[]{:S(2)}, u32[]{:S(2)}) collective-permute-start(bf16[192,128]{1,0:T(8,128)(2,1)S(1)} %collective-permute-done.11.rims), channel_id=1, source_target_pairs={{0,64},{64,0},{1,65},{65,1},{2,66},{66,2},{3,67},{67,3},{4,68},{68... | collective-permute-start | bytes 147464 | tf_op jit(solution)/shard_map/ppermute | solution.py:578
  72.0 21.5 %all-to-all-start.1 = ((bf16[64,32,128]{2,1,0:T(8,128)(2,1)}), bf16[64,32,128]{2,1,0:T(8,128)(2,1)S(1)}, u32[]{:S(2)}, u32[]{:S(2)}) async-start(bf16[64,32,128]{2,1,0:T(8,128)(2,1)} %shard_map.124), calls=%async_computation.1 | async-start | bytes 1048576 | tf_op jit(solution)/shard_map/all_to_all | solution.py:639
  81.0 0.8 copy-start.17
  81.0 0.9 copy-start.19
  81.0 0.9 copy-start.21
  81.0 1.0 %copy-start.18 = (bf16[1920,128]{1,0:T(8,128)(2,1)}, bf16[1920,128]{1,0:T(8,128)(2,1)S(1)}, u32[]{:S(2)}) copy-start(bf16[1920,128]{1,0:T(8,128)(2,1)S(1)} %collective-permute-done.12.partner) | copy-start | bytes 1474564
  90.4 3.2 %collective-permute-start.15 = (f32[960,128]{1,0:T(8,128)}, f32[960,128]{1,0:T(8,128)S(1)}, u32[]{:S(2)}, u32[]{:S(2)}) collective-permute-start(f32[960,128]{1,0:T(8,128)} %shard_map.126.mine_ref), channel_id=1, source_target_pairs={{0,64},{64,0},{1,65},{65,1},{2,66},{66,2},{3,67},{67,3},{4,68},{68... | collective-permute-start | bytes 1474568 | tf_op jit(solution)/shard_map/ppermute | solution.py:578
  93.5 3.7 %collective-permute-start.16 = (bf16[64,32,128]{2,1,0:T(8,128)(2,1)S(1)}, bf16[64,32,128]{2,1,0:T(8,128)(2,1)S(1)}, u32[]{:S(2)}, u32[]{:S(2)}) collective-permute-start(bf16[64,32,128]{2,1,0:T(8,128)(2,1)S(1)} %all-to-all-done.1.own_ref), channel_id=1, source_target_pairs={{0,64},{64,0},{1,65},{65,1},{2,66},{66,2},{3,67},{67,3},{4,68},{68... | collective-permute-start | bytes 1572872 | tf_op jit(solution)/shard_map/ppermute | solution.py:578
  95.2 1.0 %copy-start.1 = (f32[960,128]{1,0:T(8,128)S(1)}, f32[960,128]{1,0:T(8,128)}, u32[]{:S(2)}) copy-start(f32[960,128]{1,0:T(8,128)} %shard_map.126.mine_ref) | copy-start | bytes 1474564

commit v6 on v5

--- a/solution.py
+++ b/solution.py
@@ -621,6 +621,8 @@
         (shape(6 * FIELD, 128, dtype=BF), shape(3 * RIM, 128, dtype=BF)), limit=16,
     )
     r_strip, r_rims = strip_swaps(r_strip, r_edges, tiles)
+    r_own_col, r_rims = lax.optimization_barrier((r_own_col, r_rims))
+
     n_rows = 2 * feats + hid
     given, kept, input_grad = call(
         back_kernel, 0, (r_columns, r_own_col, feat, third_t, w_second, first, one, two, slope_one, slope_two),
@@ -633,8 +635,8 @@
     (partial,) = call(add_kernel, 0, (kept, received), (shape(n_rows, 128, dtype=BF),), limit=16)
     partial = partial.reshape(tiles, share, 128)
     parts = lax.all_to_all(partial, "tile", 0, 0)
-    (everywhere,) = call(mean_kernel, 0, (parts,), (shape(2 * tiles, share, 128, dtype=BF),), limit=16)
-    everywhere, coeff, r_strip, r_rims = lax.optimization_barrier((everywhere, coeff, r_strip, r_rims))
+    (everywhere,) = call(mean_kernel, 0, (parts,), (shape(2 * tiles, share, 128, dtype=BF),), limit=16, flops=LONG)
+    everywhere, coeff = lax.optimization_barrier((everywhere, coeff))
     r_partner, r_partner_rims, r_other_col = swap(r_strip, "sec"), swap(r_rims, "sec"), swap(r_own_col, "sec")
     gathered = lax.all_to_all(everywhere, ("tile", "lev"), 0, 0)
     (mine,) = call(

time: 99.3 us -> 96.2 us (0.969)
  starting transfers between devices: 45.3 us -> 43.1 us
    ppermute x13, waiting for transfers between devices: 8.39 us -> 3.86 us  [swap(): return lax.ppermute(value, axis, [(0, 1), (1, 0)])]
    all_to_all x1, starting transfers between devices: 8.96 us -> 4.69 us  [local(): gathered = lax.all_to_all(everywhere, ('tile', 'lev'), 0, 0)]
    all_to_all x1, waiting for transfers between devices: 4.91 us -> 7.67 us  [local(): parts = lax.all_to_all(partial, 'tile', 0, 0)]
    ppermute x2, waiting for transfers between devices: 0.01 us -> 2.14 us  [strip_swaps(): lax.ppermute(edges, ('sec', 'tile', 'lev'), cross)]
    ppermute x2, starting transfers between devices: 7.25 us -> 8.85 us  [strip_swaps(): lax.ppermute(edges, ('sec', 'tile', 'lev'), cross)]
    all_to_all x1, waiting for transfers between devices: 2.55 us -> 1.49 us  [local(): gathered = lax.all_to_all(everywhere, ('tile', 'lev'), 0, 0)]
    unnamed x44 -> x42, local copies, waits for them, and re-layouts: 7.92 us -> 7.76 us
  transfers between devices with their start and end apart: 19 -> 19, of which waited for: 6 -> 8; matrix products, arithmetic and copies ran while one was open for 0% -> 0% of each run, Pallas kernels for 17% -> 15%
where the time goes in v6:
time: 96.2 us; the launch traced here: 95.6 us
  starting transfers between devices  43.1 us (45%)
  Pallas kernels  26.8 us (28%)
  waiting for transfers between devices  17 us (18%)
  local copies, waits for them, and re-layouts  7.76 us (8%)
    pallas_call x10, Pallas kernels, call(): pl.pallas_call(kernel, grid=(steps,), out_shape=outs, in_specs=[smem] * n...  26.8 us
    ppermute x13, starting transfers between devices, swap(): return lax.ppermute(value, axis, [(0, 1), (1, 0)])  12.3 us
    all_to_all x1, starting transfers between devices, local(): parts = lax.all_to_all(partial, 'tile', 0, 0)  11.2 us
    ppermute x2, starting transfers between devices, strip_swaps(): lax.ppermute(edges, ('sec', 'tile', 'lev'), cross)  8.85 us
    unnamed x42, local copies, waits for them, and re-layouts  7.76 us
    all_to_all x1, waiting for transfers between devices, local(): parts = lax.all_to_all(partial, 'tile', 0, 0)  7.67 us
    ppermute x2, starting transfers between devices, strip_swaps(): lax.ppermute(strip, ('sec', 'tile'), pairs)  6.1 us
    all_to_all x1, starting transfers between devices, local(): gathered = lax.all_to_all(everywhere, ('tile', 'lev'), 0, 0)  4.69 us
  transfers between devices with their start and end apart: 19, of which 8 were waited for; matrix products, arithmetic and copies ran while one was open for 0% of the time, Pallas kernels for 15%

profile of v6, /device:TPU:1, one launch (start us, length us, event | category | flops | bytes accessed | tf_op | source)
XLA Modules:
  0.0 95.6 jit_solution(4896694760754000374)
XLA Ops:
  0.6 2.9 %shard_map.119 = (bf16[2576,128]{1,0:T(8,128)(2,1)}, bf16[256,128]{1,0:T(8,128)(2,1)}, bf16[1088,128]{1,0:T(8,128)(2,1)}, bf16[256,512]{1,0:T(8,128)(2,1)}, bf16[256,512]{1,0:T(8,128)(2,1)}) custom-call(s32[1,2]{1,0:T(1,128)} %turn_ref.3, f32[1920,128]{1,0:T(8,128)} %bitcast.8, f32[640,128]{1,0:T(8,128)} %bitcast.10, bf16[240,512]{1,0:T(8,128)(2,1)} %first_ref.1, ...), custom_call_target="tpu_custom_call" | custom-call | tf_op jit(solution)/shard_map/pallas_call | solution.py:555
  3.5 3.8 %collective-permute-start.2 = (bf16[1088,128]{1,0:T(8,128)(2,1)}, bf16[1088,128]{1,0:T(8,128)(2,1)S(1)}, u32[]{:S(2)}, u32[]{:S(2)}) collective-permute-start(bf16[1088,128]{1,0:T(8,128)(2,1)} %get-tuple-element.41.own_ref), channel_id=1, source_target_pairs={{0,1},{1,0},{2,3},{3,2},{4,5},{5,4},{6,7},{7,6},{8,9},{9,8},{10,11... | collective-permute-start | bytes 835592 | tf_op jit(solution)/shard_map/ppermute | solution.py:578
  7.3 4.1 %collective-permute-start.1 = (bf16[256,128]{1,0:T(8,128)(2,1)}, bf16[256,128]{1,0:T(8,128)(2,1)S(1)}, u32[]{:S(2)}, u32[]{:S(2)}) collective-permute-start(bf16[256,128]{1,0:T(8,128)(2,1)} %get-tuple-element.40), channel_id=1, source_target_pairs={{64,3},{65,2},{66,5},{67,4},{68,7},{69,6},{70,9},{71,8},{72,11},{7... | collective-permute-start | bytes 196616 | tf_op jit(solution)/shard_map/ppermute | solution.py:585
  11.4 2.2 %collective-permute-start = (bf16[2576,128]{1,0:T(8,128)(2,1)}, bf16[2576,128]{1,0:T(8,128)(2,1)S(1)}, u32[]{:S(2)}, u32[]{:S(2)}) collective-permute-start(bf16[2576,128]{1,0:T(8,128)(2,1)} %get-tuple-element.39), channel_id=1, source_target_pairs={{64,2},{66,4},{68,6},{70,8},{72,10},{74,12},{76,14},{78,16},{80,18... | collective-permute-start | bytes 1978376 | tf_op jit(solution)/shard_map/ppermute | solution.py:585
  13.6 0.0 collective-permute-done.2.other_ref.own_col
  13.6 0.0 copy-start.4
  13.6 1.2 %copy-done.4 = f32[3,40,16,128]{3,2,1,0:T(8,128)S(1)} copy-done((f32[3,40,16,128]{3,2,1,0:T(8,128)S(1)}, f32[3,40,16,128]{3,2,1,0:T(8,128)}, u32[]{:S(2)}) %copy-start.4) | copy-done | bytes 983064
  14.8 1.0 %copy-done.5 = bf16[512,512]{1,0:T(8,128)(2,1)S(1)} copy-done((bf16[512,512]{1,0:T(8,128)(2,1)S(1)}, bf16[512,512]{1,0:T(8,128)(2,1)}, u32[]{:S(2)}) %copy-start.5) | copy-done | bytes 524312
  15.9 1.0 copy-done.8
  16.8 0.9 copy-done.10
  17.8 0.9 copy-done.11
  18.7 3.0 %shard_map.120 = (bf16[256,1024]{1,0:T(8,128)(2,1)S(1)}, bf16[512,1024]{1,0:T(8,128)(2,1)S(1)}, bf16[512,1024]{1,0:T(8,128)(2,1)S(1)}, f32[512,1024]{1,0:T(8,128...) custom-call(bf16[1088,128]{1,0:T(8,128)(2,1)S(1)} %copy-done.8, ...), custom_call_target="tpu_custom_call" | custom-call | flops 20000000000 | tf_op jit(solution)/shard_map/pallas_call | solution.py:555
  21.7 1.9 %collective-permute-done.strip = bf16[2576,128]{1,0:T(8,128)(2,1)S(1)} collective-permute-done((bf16[2576,128]{1,0:T(8,128)(2,1)}, bf16[2576,128]{1,0:T(8,128)(2,1)S(1)}, u32[]{:S(2)}, u32[]{:S(2)}) %collective-permute-start) | collective-permute-done | bytes 659488 | tf_op jit(solution)/shard_map/ppermute | solution.py:585
  23.6 0.5 collective-permute-start.5
  24.1 2.0 %collective-permute-done.5.other_col = bf16[1088,128]{1,0:T(8,128)(2,1)S(1)} collective-permute-done((bf16[1088,128]{1,0:T(8,128)(2,1)S(1)}, bf16[1088,128]{1,0:T(8,128)(2,1)S(1)}, u32[]{:S(2)}, u32[]{:S(2)}) %collective-permute-start.5) | collective-permute-done | bytes 278560 | tf_op jit(solution)/shard_map/ppermute | solution.py:578
  26.1 0.1 collective-permute-done.4.partner_rims
  26.2 5.2 %shard_map.121 = (f32[960,128]{1,0:T(8,128)S(1)}, bf16[960,128]{1,0:T(8,128)(2,1)S(1)}, bf16[1024,128]{1,0:T(8,128)(2,1)S(1)}, f32[48,56,128]{2,1,0:T(8,128)S(1)}, f32[4,8,128]{2,1,0:T(8,128)S(1)}) custom-call(s32[1,2]{1,0:T(1,128)S(1)} %copy-done.3, f32[1920,128]{1,0:T(8,128)S(1)} %bitcast.9, f32[640,128]{1,0:T(8,128)S(1)} %bitcast.11, ...), custom_call_target="tpu_custom_call" | custom-call | flops 20000000000 | tf_op jit(solution)/shard_map/pallas_call | solution.py:555
  31.4 0.6 copy-done.14
  32.0 0.0 collective-permute-start.8
  32.1 3.7 %collective-permute-start.7 = (bf16[1024,128]{1,0:T(8,128)(2,1)S(1)}, bf16[1024,128]{1,0:T(8,128)(2,1)S(1)}, u32[]{:S(2)}, u32[]{:S(2)}) collective-permute-start(bf16[1024,128]{1,0:T(8,128)(2,1)S(1)} %get-tuple-element.49.own_ref), channel_id=1, source_target_pairs={{0,1},{1,0},{2,3},{3,2},{4,5},{5,4},{6,7},{7,6},{8,9},{9,8},{10,11... | collective-permute-start | bytes 786440 | tf_op jit(solution)/shard_map/ppermute | solution.py:578
  35.8 4.7 %collective-permute-start.9 = (bf16[192,128]{1,0:T(8,128)(2,1)S(1)}, bf16[192,128]{1,0:T(8,128)(2,1)S(1)}, u32[]{:S(2)}, u32[]{:S(2)}) collective-permute-start(bf16[192,128]{1,0:T(8,128)(2,1)S(1)} %get-tuple-element.51), channel_id=1, source_target_pairs={{64,3},{65,2},{66,5},{67,4},{68,7},{69,6},{70,9},{71,8},{72,11},{7... | collective-permute-start | bytes 147464 | tf_op jit(solution)/shard_map/ppermute | solution.py:585
  40.5 1.5 %collective-permute-done.7.other_ref.own_col = bf16[1024,128]{1,0:T(8,128)(2,1)S(1)} collective-permute-done((bf16[1024,128]{1,0:T(8,128)(2,1)S(1)}, bf16[1024,128]{1,0:T(8,128)(2,1)S(1)}, u32[]{:S(2)}, u32[]{:S(2)}) %collective-permute-start.7) | collective-permute-done | bytes 262176 | tf_op jit(solution)/shard_map/ppermute | solution.py:578
  42.1 2.1 %collective-permute-done.9.rims = bf16[192,128]{1,0:T(8,128)(2,1)S(1)} collective-permute-done((bf16[192,128]{1,0:T(8,128)(2,1)S(1)}, bf16[192,128]{1,0:T(8,128)(2,1)S(1)}, u32[]{:S(2)}, u32[]{:S(2)}) %collective-permute-start.9) | collective-permute-done | bytes 49184 | tf_op jit(solution)/shard_map/ppermute | solution.py:585
  44.2 3.3 %shard_map.123 = (bf16[1024,128]{1,0:T(8,128)(2,1)S(1)}, f32[1024,128]{1,0:T(8,128)S(1)}, f32[960,128]{1,0:T(8,128)S(1)}) custom-call(bf16[1024,128]{1,0:T(8,128)(2,1)S(1)} %get-tuple-element.49.own_ref, bf16[1024,128]{1,0:T(8,128)(2,1)S(1)} %collective-permute-done.7.other_ref.own_col, bf16[256,1024]{1,0:T(8,128)(2,1)S(1)} %get-tuple-element.53.feat_ref, ...), custom_call_target="tpu_custom_call" | custom-call | flops 20000000000 | tf_op jit(solution)/shard_map/pallas_call | solution.py:555
  47.5 0.0 copy-start.13
  47.5 0.1 collective-permute-start.10
  47.6 3.9 %collective-permute-start.11 = (bf16[1920,128]{1,0:T(8,128)(2,1)S(1)}, bf16[1920,128]{1,0:T(8,128)(2,1)S(1)}, u32[]{:S(2)}, u32[]{:S(2)}) collective-permute-start(bf16[1920,128]{1,0:T(8,128)(2,1)S(1)} %get-tuple-element.64), channel_id=1, source_target_pairs={{64,2},{66,4},{68,6},{70,8},{72,10},{74,12},{76,14},{78,16},{80,18... | collective-permute-start | bytes 1474568 | tf_op jit(solution)/shard_map/ppermute | solution.py:585
  51.6 0.7 shard_map.124
  52.3 11.2 %all-to-all-start = ((bf16[32,32,128]{2,1,0:T(8,128)(2,1)}), bf16[32,32,128]{2,1,0:T(8,128)(2,1)S(1)}, u32[]{:S(2)}, u32[]{:S(2)}) async-start(bf16[32,32,128]{2,1,0:T(8,128)(2,1)} %bitcast.5), calls=%async_computation | async-start | bytes 524288 | tf_op jit(solution)/shard_map/all_to_all | solution.py:637
  63.6 0.1 collective-permute-start.6
  63.7 0.5 collective-permute-start.14
  64.2 0.1 collective-permute-start.13
  64.3 0.4 collective-permute-start.12
  64.7 7.7 %all-to-all-done.parts_ref = bf16[32,32,128]{2,1,0:T(8,128)(2,1)S(1)} async-done(((bf16[32,32,128]{2,1,0:T(8,128)(2,1)}), bf16[32,32,128]{2,1,0:T(8,128)(2,1)S(1)}, u32[]{:S(2)}, u32[]{:S(2)}) %all-to-all-start) | async-done | bytes 262176 | tf_op jit(solution)/shard_map/all_to_all | solution.py:637
  72.3 0.9 shard_map.125
  73.2 4.7 %all-to-all-start.1 = ((bf16[64,32,128]{2,1,0:T(8,128)(2,1)}), bf16[64,32,128]{2,1,0:T(8,128)(2,1)S(1)}, u32[]{:S(2)}, u32[]{:S(2)}) async-start(bf16[64,32,128]{2,1,0:T(8,128)(2,1)} %shard_map.125), calls=%async_computation.1 | async-start | bytes 1048576 | tf_op jit(solution)/shard_map/all_to_all | solution.py:641
  78.0 0.6 copy-done.20
  78.5 0.2 copy-done.16
  78.7 0.1 copy-done.18
  78.8 0.2 copy-done.17
  79.0 8.3 %shard_map.126.mine_ref = f32[960,128]{1,0:T(8,128)} custom-call(f32[960,128]{1,0:T(8,128)} %copy-done.7, f32[960,128]{1,0:T(8,128)} %copy-done.16, f32[960,128]{1,0:T(8,128)} %copy-done.13, f32[48,56,128]{2,1,0:T(8,128)} %copy-done.12, f32[4,8,128]{2,1,0:T(8,128)} %copy-done.14, bf16[1920,128]{1,0:T(8,128)(2,1)} %copy-done.15, ...), custom_call_target="tpu_custom_call" | custom-call | flops 20000000000 | tf_op jit(solution)/shard_map/pallas_call | solution.py:555
  87.3 1.0 %collective-permute-start.15 = (f32[960,128]{1,0:T(8,128)}, f32[960,128]{1,0:T(8,128)S(1)}, u32[]{:S(2)}, u32[]{:S(2)}) collective-permute-start(f32[960,128]{1,0:T(8,128)} %shard_map.126.mine_ref), channel_id=1, source_target_pairs={{0,64},{64,0},{1,65},{65,1},{2,66},{66,2},{3,67},{67,3},{4,68},{68... | collective-permute-start | bytes 1474568 | tf_op jit(solution)/shard_map/ppermute | solution.py:578
  88.3 1.5 %all-to-all-done.1.own_ref = bf16[64,32,128]{2,1,0:T(8,128)(2,1)S(1)} async-done(((bf16[64,32,128]{2,1,0:T(8,128)(2,1)}), bf16[64,32,128]{2,1,0:T(8,128)(2,1)S(1)}, u32[]{:S(2)}, u32[]{:S(2)}) %all-to-all-start.1) | async-done | bytes 524320 | tf_op jit(solution)/shard_map/all_to_all | solution.py:641
  89.8 0.2 collective-permute-done.15.theirs_ref
  90.0 2.1 %collective-permute-start.16 = (bf16[64,32,128]{2,1,0:T(8,128)(2,1)S(1)}, bf16[64,32,128]{2,1,0:T(8,128)(2,1)S(1)}, u32[]{:S(2)}, u32[]{:S(2)}) collective-permute-start(bf16[64,32,128]{2,1,0:T(8,128)(2,1)S(1)} %all-to-all-done.1.own_ref), channel_id=1, source_target_pairs={{0,64},{64,0},{1,65},{65,1},{2,66},{66,2},{3,67},{67,3},{4,68},{68... | collective-permute-start | bytes 1572872 | tf_op jit(solution)/shard_map/ppermute | solution.py:578
  92.1 1.0 %copy-done.1 = f32[960,128]{1,0:T(8,128)S(1)} copy-done((f32[960,128]{1,0:T(8,128)S(1)}, f32[960,128]{1,0:T(8,128)}, u32[]{:S(2)}) %copy-start.1) | copy-done | bytes 491544
  93.2 1.0 %shard_map.127 = f32[3,40,16,128]{3,2,1,0:T(8,128)} custom-call(f32[960,128]{1,0:T(8,128)S(1)} %copy-done.1, f32[960,128]{1,0:T(8,128)S(1)} %collective-permute-done.15.theirs_ref), custom_call_target="tpu_custom_call" | custom-call | tf_op jit(solution)/shard_map/pallas_call | solution.py:555
  94.2 1.4 %shard_map.128 = (f32[240,512]{1,0:T(8,128)}, f32[1,512]{1,0:T(1,128)}, f32[512,512]{1,0:T(8,128)}, f32[240,512]{1,0:T(8,128)}) custom-call(bf16[64,32,128]{2,1,0:T(8,128)(2,1)S(1)} %all-to-all-done.1.own_ref, bf16[64,32,128]{2,1,0:T(8,128)(2,1)S(1)} %collective-permute-done.16.partner_ref), custom_call_target="tpu_custom_call" | custom-call | tf_op jit(solution)/shard_map/pallas_call | solution.py:555
  (42 shorter events, 0.1 us)
Async XLA Ops:
  3.5 10.1 %collective-permute-start.2 = (bf16[1088,128]{1,0:T(8,128)(2,1)}, bf16[1088,128]{1,0:T(8,128)(2,1)S(1)}, u32[]{:S(2)}, u32[]{:S(2)}) collective-permute-start(bf16[1088,128]{1,0:T(8,128)(2,1)} %get-tuple-element.41.own_ref), channel_id=1, source_target_pairs={{0,1},{1,0},{2,3},{3,2},{4,5},{5,4},{6,7},{7,6},{8,9},{9,8},{10,11... | collective-permute-start | bytes 835592 | tf_op jit(solution)/shard_map/ppermute | solution.py:578
  7.3 14.4 %collective-permute-start.1 = (bf16[256,128]{1,0:T(8,128)(2,1)}, bf16[256,128]{1,0:T(8,128)(2,1)S(1)}, u32[]{:S(2)}, u32[]{:S(2)}) collective-permute-start(bf16[256,128]{1,0:T(8,128)(2,1)} %get-tuple-element.40), channel_id=1, source_target_pairs={{64,3},{65,2},{66,5},{67,4},{68,7},{69,6},{70,9},{71,8},{72,11},{7... | collective-permute-start | bytes 196616 | tf_op jit(solution)/shard_map/ppermute | solution.py:585
  11.4 12.2 %collective-permute-start = (bf16[2576,128]{1,0:T(8,128)(2,1)}, bf16[2576,128]{1,0:T(8,128)(2,1)S(1)}, u32[]{:S(2)}, u32[]{:S(2)}) collective-permute-start(bf16[2576,128]{1,0:T(8,128)(2,1)} %get-tuple-element.39), channel_id=1, source_target_pairs={{64,2},{66,4},{68,6},{70,8},{72,10},{74,12},{76,14},{78,16},{80,18... | collective-permute-start | bytes 1978376 | tf_op jit(solution)/shard_map/ppermute | solution.py:585
  13.6 1.2 %copy-start.4 = (f32[3,40,16,128]{3,2,1,0:T(8,128)S(1)}, f32[3,40,16,128]{3,2,1,0:T(8,128)}, u32[]{:S(2)}) copy-start(f32[3,40,16,128]{3,2,1,0:T(8,128)} %param.10) | copy-start | bytes 2949124
  14.8 1.0 %copy-start.5 = (bf16[512,512]{1,0:T(8,128)(2,1)S(1)}, bf16[512,512]{1,0:T(8,128)(2,1)}, u32[]{:S(2)}) copy-start(bf16[512,512]{1,0:T(8,128)(2,1)} %second_ref.3) | copy-start | bytes 1572868
  15.9 1.0 copy-start.8
  16.8 0.9 copy-start.10
  17.8 0.9 copy-start.11
  18.7 7.5 %copy-start = (f32[3,40,16,128]{3,2,1,0:T(8,128)S(1)}, f32[3,40,16,128]{3,2,1,0:T(8,128)}, u32[]{:S(2)}) copy-start(f32[3,40,16,128]{3,2,1,0:T(8,128)} %param.8) | copy-start | bytes 2949124
  18.7 7.5 %copy-start.2 = (f32[40,16,128]{2,1,0:T(8,128)S(1)}, f32[40,16,128]{2,1,0:T(8,128)}, u32[]{:S(2)}) copy-start(f32[40,16,128]{2,1,0:T(8,128)} %param.9) | copy-start | bytes 983044
  18.7 7.5 %copy-start.3 = (s32[1,2]{1,0:T(1,128)S(1)}, s32[1,2]{1,0:T(1,128)}, u32[]{:S(2)}) copy-start(s32[1,2]{1,0:T(1,128)} %turn_ref.3) | copy-start | bytes 28
  23.6 20.6 %copy-start.6 = (bf16[512,512]{1,0:T(8,128)(2,1)S(1)}, bf16[512,512]{1,0:T(8,128)(2,1)}, u32[]{:S(2)}) copy-start(bf16[512,512]{1,0:T(8,128)(2,1)} %second_ref.3) | copy-start | bytes 1572868
  23.6 2.6 %collective-permute-start.3 = (bf16[2576,128]{1,0:T(8,128)(2,1)S(1)}, bf16[2576,128]{1,0:T(8,128)(2,1)S(1)}, u32[]{:S(2)}, u32[]{:S(2)}) collective-permute-start(bf16[2576,128]{1,0:T(8,128)(2,1)S(1)} %collective-permute-done.strip), channel_id=1, source_target_pairs={{0,64},{64,0},{1,65},{65,1},{2,66},{66,2},{3,67},{67,3},{4,68},{68... | collective-permute-start | bytes 1978376 | tf_op jit(solution)/shard_map/ppermute | solution.py:578
  23.6 2.5 %collective-permute-start.5 = (bf16[1088,128]{1,0:T(8,128)(2,1)S(1)}, bf16[1088,128]{1,0:T(8,128)(2,1)S(1)}, u32[]{:S(2)}, u32[]{:S(2)}) collective-permute-start(bf16[1088,128]{1,0:T(8,128)(2,1)S(1)} %collective-permute-done.2.other_ref.own_col), channel_id=1, source_target_pairs={{0,64},{64,0},{1,65},{65,1},{2,66},{66,2},{3,67},{67,3},{4,68},{68... | collective-permute-start | bytes 835592 | tf_op jit(solution)/shard_map/ppermute | solution.py:578
  24.1 2.1 %collective-permute-start.4 = (bf16[256,128]{1,0:T(8,128)(2,1)S(1)}, bf16[256,128]{1,0:T(8,128)(2,1)S(1)}, u32[]{:S(2)}, u32[]{:S(2)}) collective-permute-start(bf16[256,128]{1,0:T(8,128)(2,1)S(1)} %collective-permute-done.1.rims), channel_id=1, source_target_pairs={{0,64},{64,0},{1,65},{65,1},{2,66},{66,2},{3,67},{67,3},{4,68},{68... | collective-permute-start | bytes 196616 | tf_op jit(solution)/shard_map/ppermute | solution.py:578
  31.4 0.6 copy-start.14
  32.0 15.5 %copy-start.12 = (f32[48,56,128]{2,1,0:T(8,128)}, f32[48,56,128]{2,1,0:T(8,128)S(1)}, u32[]{:S(2)}) copy-start(f32[48,56,128]{2,1,0:T(8,128)S(1)} %get-tuple-element.62.c_ref) | copy-start | bytes 4128772
  32.0 31.5 %copy-start.7 = (f32[960,128]{1,0:T(8,128)}, f32[960,128]{1,0:T(8,128)S(1)}, u32[]{:S(2)}) copy-start(f32[960,128]{1,0:T(8,128)S(1)} %get-tuple-element.48.resid_ref) | copy-start | bytes 1474564
  32.0 3.7 %collective-permute-start.8 = (bf16[960,128]{1,0:T(8,128)(2,1)S(1)}, bf16[960,128]{1,0:T(8,128)(2,1)S(1)}, u32[]{:S(2)}, u32[]{:S(2)}) collective-permute-start(bf16[960,128]{1,0:T(8,128)(2,1)S(1)} %get-tuple-element.50.near_ref), channel_id=1, source_target_pairs={{0,64},{64,0},{1,65},{65,1},{2,66},{66,2},{3,67},{67,3},{4,68},{68... | collective-permute-start | bytes 737288 | tf_op jit(solution)/shard_map/ppermute | solution.py:578
  32.1 10.0 %collective-permute-start.7 = (bf16[1024,128]{1,0:T(8,128)(2,1)S(1)}, bf16[1024,128]{1,0:T(8,128)(2,1)S(1)}, u32[]{:S(2)}, u32[]{:S(2)}) collective-permute-start(bf16[1024,128]{1,0:T(8,128)(2,1)S(1)} %get-tuple-element.49.own_ref), channel_id=1, source_target_pairs={{0,1},{1,0},{2,3},{3,2},{4,5},{5,4},{6,7},{7,6},{8,9},{9,8},{10,11... | collective-permute-start | bytes 786440 | tf_op jit(solution)/shard_map/ppermute | solution.py:578
  35.8 8.4 %collective-permute-start.9 = (bf16[192,128]{1,0:T(8,128)(2,1)S(1)}, bf16[192,128]{1,0:T(8,128)(2,1)S(1)}, u32[]{:S(2)}, u32[]{:S(2)}) collective-permute-start(bf16[192,128]{1,0:T(8,128)(2,1)S(1)} %get-tuple-element.51), channel_id=1, source_target_pairs={{64,3},{65,2},{66,5},{67,4},{68,7},{69,6},{70,9},{71,8},{72,11},{7... | collective-permute-start | bytes 147464 | tf_op jit(solution)/shard_map/ppermute | solution.py:585
  42.1 21.6 %copy-start.9 = (bf16[1024,128]{1,0:T(8,128)(2,1)}, bf16[1024,128]{1,0:T(8,128)(2,1)S(1)}, u32[]{:S(2)}) copy-start(bf16[1024,128]{1,0:T(8,128)(2,1)S(1)} %collective-permute-done.7.other_ref.own_col) | copy-start | bytes 786436
  44.2 19.9 %copy-start.19 = (bf16[192,128]{1,0:T(8,128)(2,1)}, bf16[192,128]{1,0:T(8,128)(2,1)S(1)}, u32[]{:S(2)}) copy-start(bf16[192,128]{1,0:T(8,128)(2,1)S(1)} %collective-permute-done.9.rims) | copy-start | bytes 147460
  47.5 4.8 %copy-start.13 = (f32[960,128]{1,0:T(8,128)}, f32[960,128]{1,0:T(8,128)S(1)}, u32[]{:S(2)}) copy-start(f32[960,128]{1,0:T(8,128)S(1)} %get-tuple-element.58.input_grad_ref) | copy-start | bytes 1474564
  47.5 4.0 %collective-permute-start.10 = (bf16[1024,128]{1,0:T(8,128)(2,1)S(1)}, bf16[1024,128]{1,0:T(8,128)(2,1)S(1)}, u32[]{:S(2)}, u32[]{:S(2)}) collective-permute-start(bf16[1024,128]{1,0:T(8,128)(2,1)S(1)} %get-tuple-element.60), channel_id=1, source_target_pairs={{0,64},{64,0},{1,65},{65,1},{2,66},{66,2},{3,67},{67,3},{4,68},{68... | collective-permute-start | bytes 786440 | tf_op jit(solution)/shard_map/ppermute | solution.py:578
  47.6 16.6 %collective-permute-start.11 = (bf16[1920,128]{1,0:T(8,128)(2,1)S(1)}, bf16[1920,128]{1,0:T(8,128)(2,1)S(1)}, u32[]{:S(2)}, u32[]{:S(2)}) collective-permute-start(bf16[1920,128]{1,0:T(8,128)(2,1)S(1)} %get-tuple-element.64), channel_id=1, source_target_pairs={{64,2},{66,4},{68,6},{70,8},{72,10},{74,12},{76,14},{78,16},{80,18... | collective-permute-start | bytes 1474568 | tf_op jit(solution)/shard_map/ppermute | solution.py:585
  52.3 20.0 %all-to-all-start = ((bf16[32,32,128]{2,1,0:T(8,128)(2,1)}), bf16[32,32,128]{2,1,0:T(8,128)(2,1)S(1)}, u32[]{:S(2)}, u32[]{:S(2)}) async-start(bf16[32,32,128]{2,1,0:T(8,128)(2,1)} %bitcast.5), calls=%async_computation | async-start | bytes 524288 | tf_op jit(solution)/shard_map/all_to_all | solution.py:637
  63.6 14.4 %collective-permute-start.6 = (f32[960,128]{1,0:T(8,128)S(1)}, f32[960,128]{1,0:T(8,128)S(1)}, u32[]{:S(2)}, u32[]{:S(2)}) collective-permute-start(f32[960,128]{1,0:T(8,128)S(1)} %get-tuple-element.48.resid_ref), channel_id=1, source_target_pairs={{0,64},{64,0},{1,65},{65,1},{2,66},{66,2},{3,67},{67,3},{4,68},{68... | collective-permute-start | bytes 1474568 | tf_op jit(solution)/shard_map/ppermute | solution.py:578
  63.7 14.3 %collective-permute-start.14 = (bf16[1024,128]{1,0:T(8,128)(2,1)S(1)}, bf16[1024,128]{1,0:T(8,128)(2,1)S(1)}, u32[]{:S(2)}, u32[]{:S(2)}) collective-permute-start(bf16[1024,128]{1,0:T(8,128)(2,1)S(1)} %collective-permute-done.7.other_ref.own_col), channel_id=1, source_target_pairs={{0,64},{64,0},{1,65},{65,1},{2,66},{66,2},{3,67},{67,3},{4,68},{68... | collective-permute-start | bytes 786440 | tf_op jit(solution)/shard_map/ppermute | solution.py:578
  64.2 13.7 %collective-permute-start.13 = (bf16[192,128]{1,0:T(8,128)(2,1)S(1)}, bf16[192,128]{1,0:T(8,128)(2,1)S(1)}, u32[]{:S(2)}, u32[]{:S(2)}) collective-permute-start(bf16[192,128]{1,0:T(8,128)(2,1)S(1)} %collective-permute-done.9.rims), channel_id=1, source_target_pairs={{0,64},{64,0},{1,65},{65,1},{2,66},{66,2},{3,67},{67,3},{4,68},{68... | collective-permute-start | bytes 147464 | tf_op jit(solution)/shard_map/ppermute | solution.py:578
  64.3 8.9 %copy-start.15 = (bf16[1920,128]{1,0:T(8,128)(2,1)}, bf16[1920,128]{1,0:T(8,128)(2,1)S(1)}, u32[]{:S(2)}) copy-start(bf16[1920,128]{1,0:T(8,128)(2,1)S(1)} %collective-permute-done.11.strip) | copy-start | bytes 1474564
  64.3 13.7 %collective-permute-start.12 = (bf16[1920,128]{1,0:T(8,128)(2,1)S(1)}, bf16[1920,128]{1,0:T(8,128)(2,1)S(1)}, u32[]{:S(2)}, u32[]{:S(2)}) collective-permute-start(bf16[1920,128]{1,0:T(8,128)(2,1)S(1)} %collective-permute-done.11.strip), channel_id=1, source_target_pairs={{0,64},{64,0},{1,65},{65,1},{2,66},{66,2},{3,67},{67,3},{4,68},{68... | collective-permute-start | bytes 1474568 | tf_op jit(solution)/shard_map/ppermute | solution.py:578
  73.2 16.6 %all-to-all-start.1 = ((bf16[64,32,128]{2,1,0:T(8,128)(2,1)}), bf16[64,32,128]{2,1,0:T(8,128)(2,1)S(1)}, u32[]{:S(2)}, u32[]{:S(2)}) async-start(bf16[64,32,128]{2,1,0:T(8,128)(2,1)} %shard_map.125), calls=%async_computation.1 | async-start | bytes 1048576 | tf_op jit(solution)/shard_map/all_to_all | solution.py:641
  77.9 0.6 copy-start.20
  77.9 0.8 copy-start.16
  78.0 0.9 copy-start.18
  78.0 1.0 %copy-start.17 = (bf16[1920,128]{1,0:T(8,128)(2,1)}, bf16[1920,128]{1,0:T(8,128)(2,1)S(1)}, u32[]{:S(2)}) copy-start(bf16[1920,128]{1,0:T(8,128)(2,1)S(1)} %collective-permute-done.12.partner) | copy-start | bytes 1474564
  87.3 2.7 %collective-permute-start.15 = (f32[960,128]{1,0:T(8,128)}, f32[960,128]{1,0:T(8,128)S(1)}, u32[]{:S(2)}, u32[]{:S(2)}) collective-permute-start(f32[960,128]{1,0:T(8,128)} %shard_map.126.mine_ref), channel_id=1, source_target_pairs={{0,64},{64,0},{1,65},{65,1},{2,66},{66,2},{3,67},{67,3},{4,68},{68... | collective-permute-start | bytes 1474568 | tf_op jit(solution)/shard_map/ppermute | solution.py:578
  90.0 4.1 %collective-permute-start.16 = (bf16[64,32,128]{2,1,0:T(8,128)(2,1)S(1)}, bf16[64,32,128]{2,1,0:T(8,128)(2,1)S(1)}, u32[]{:S(2)}, u32[]{:S(2)}) collective-permute-start(bf16[64,32,128]{2,1,0:T(8,128)(2,1)S(1)} %all-to-all-done.1.own_ref), channel_id=1, source_target_pairs={{0,64},{64,0},{1,65},{65,1},{2,66},{66,2},{3,67},{67,3},{4,68},{68... | collective-permute-start | bytes 1572872 | tf_op jit(solution)/shard_map/ppermute | solution.py:578
  92.1 1.0 %copy-start.1 = (f32[960,128]{1,0:T(8,128)S(1)}, f32[960,128]{1,0:T(8,128)}, u32[]{:S(2)}) copy-start(f32[960,128]{1,0:T(8,128)} %shard_map.126.mine_ref) | copy-start | bytes 1474564

commit v7 on v6

--- a/solution.py
+++ b/solution.py
@@ -328,7 +328,7 @@
             at = pl.ds(own_level + shift, OWN)
             packed = slice(n * FIELD, (n + 1) * FIELD)
             dst[at, 3 * BLK : 4 * BLK, :] = resid_ref[packed, :].reshape(OWN, BLK, 128)
-            dst[at, other_row : other_row + BLK, :] = other_ref[packed, :].reshape(OWN, BLK, 128)
+            dst[at, other_row : other_row + BLK, :] = other_ref[packed, :].astype(F32).reshape(OWN, BLK, 128)
         near_factor, far_factor = (0, 2) if sec == 0 else (2, 0)
         for step in range(SUBSTEPS):
             old, new = (pa, pb) if step % 2 == 0 else (pb, pa)
@@ -615,9 +615,9 @@
     )
 
     r_own_col = swap(r_columns, "lev")
-    r_other = swap(resid, "sec")
+    r_other = swap(r_rows, "sec")
     r_strip, r_edges = call(
-        join_kernel, 0, (r_rows, swap(r_rows, "sec")),
+        join_kernel, 0, (r_rows, r_other),
         (shape(6 * FIELD, 128, dtype=BF), shape(3 * RIM, 128, dtype=BF)), limit=16,
     )
     r_strip, r_rims = strip_swaps(r_strip, r_edges, tiles)

time: 96.2 us -> 95.9 us (level)
    ppermute x13 -> x12, waiting for transfers between devices: 3.86 us -> 3.73 us  [swap(): return lax.ppermute(value, axis, [(0, 1), (1, 0)])]
    ppermute x13 -> x12, starting transfers between devices: 12.3 us -> 12.3 us  [swap(): return lax.ppermute(value, axis, [(0, 1), (1, 0)])]
  transfers between devices with their start and end apart: 19 -> 18, of which waited for: 8 -> 7; matrix products, arithmetic and copies ran while one was open for 0% -> 0% of each run, Pallas kernels for 15% -> 15%
where the time goes in v7:
time: 95.9 us; the launch traced here: 95.3 us
  starting transfers between devices  43.1 us (45%)
  Pallas kernels  26.8 us (28%)
  waiting for transfers between devices  17.5 us (18%)
  local copies, waits for them, and re-layouts  7.04 us (7%)
    pallas_call x10, Pallas kernels, call(): pl.pallas_call(kernel, grid=(steps,), out_shape=outs, in_specs=[smem] * n...  26.8 us
    ppermute x12, starting transfers between devices, swap(): return lax.ppermute(value, axis, [(0, 1), (1, 0)])  12.3 us
    all_to_all x1, starting transfers between devices, local(): parts = lax.all_to_all(partial, 'tile', 0, 0)  11.2 us
    ppermute x2, starting transfers between devices, strip_swaps(): lax.ppermute(edges, ('sec', 'tile', 'lev'), cross)  8.83 us
    all_to_all x1, waiting for transfers between devices, local(): parts = lax.all_to_all(partial, 'tile', 0, 0)  8.1 us
    unnamed x42, local copies, waits for them, and re-layouts  7.04 us
    ppermute x2, starting transfers between devices, strip_swaps(): lax.ppermute(strip, ('sec', 'tile'), pairs)  6.09 us
    all_to_all x1, starting transfers between devices, local(): gathered = lax.all_to_all(everywhere, ('tile', 'lev'), 0, 0)  4.68 us
  transfers between devices with their start and end apart: 18, of which 7 were waited for; matrix products, arithmetic and copies ran while one was open for 0% of the time, Pallas kernels for 15%

profile of v7, /device:TPU:1, one launch (start us, length us, event | category | flops | bytes accessed | tf_op | source)
XLA Modules:
  0.0 95.3 jit_solution(17654320947960653913)
XLA Ops:
  0.6 2.9 %shard_map.119 = (bf16[2576,128]{1,0:T(8,128)(2,1)}, bf16[256,128]{1,0:T(8,128)(2,1)}, bf16[1088,128]{1,0:T(8,128)(2,1)}, bf16[256,512]{1,0:T(8,128)(2,1)}, bf16[256,512]{1,0:T(8,128)(2,1)}) custom-call(s32[1,2]{1,0:T(1,128)} %turn_ref.3, f32[1920,128]{1,0:T(8,128)} %bitcast.8, f32[640,128]{1,0:T(8,128)} %bitcast.10, bf16[240,512]{1,0:T(8,128)(2,1)} %first_ref.1, ...), custom_call_target="tpu_custom_call" | custom-call | tf_op jit(solution)/shard_map/pallas_call | solution.py:555
  3.5 3.8 %collective-permute-start.2 = (bf16[1088,128]{1,0:T(8,128)(2,1)}, bf16[1088,128]{1,0:T(8,128)(2,1)S(1)}, u32[]{:S(2)}, u32[]{:S(2)}) collective-permute-start(bf16[1088,128]{1,0:T(8,128)(2,1)} %get-tuple-element.41.own_ref), channel_id=1, source_target_pairs={{0,1},{1,0},{2,3},{3,2},{4,5},{5,4},{6,7},{7,6},{8,9},{9,8},{10,11... | collective-permute-start | bytes 835592 | tf_op jit(solution)/shard_map/ppermute | solution.py:578
  7.3 4.1 %collective-permute-start.1 = (bf16[256,128]{1,0:T(8,128)(2,1)}, bf16[256,128]{1,0:T(8,128)(2,1)S(1)}, u32[]{:S(2)}, u32[]{:S(2)}) collective-permute-start(bf16[256,128]{1,0:T(8,128)(2,1)} %get-tuple-element.40), channel_id=1, source_target_pairs={{64,3},{65,2},{66,5},{67,4},{68,7},{69,6},{70,9},{71,8},{72,11},{7... | collective-permute-start | bytes 196616 | tf_op jit(solution)/shard_map/ppermute | solution.py:585
  11.4 2.2 %collective-permute-start = (bf16[2576,128]{1,0:T(8,128)(2,1)}, bf16[2576,128]{1,0:T(8,128)(2,1)S(1)}, u32[]{:S(2)}, u32[]{:S(2)}) collective-permute-start(bf16[2576,128]{1,0:T(8,128)(2,1)} %get-tuple-element.39), channel_id=1, source_target_pairs={{64,2},{66,4},{68,6},{70,8},{72,10},{74,12},{76,14},{78,16},{80,18... | collective-permute-start | bytes 1978376 | tf_op jit(solution)/shard_map/ppermute | solution.py:585
  13.6 0.0 collective-permute-done.2.other_ref.own_col
  13.6 0.0 copy-start.5
  13.6 1.2 %copy-done.5 = f32[3,40,16,128]{3,2,1,0:T(8,128)S(1)} copy-done((f32[3,40,16,128]{3,2,1,0:T(8,128)S(1)}, f32[3,40,16,128]{3,2,1,0:T(8,128)}, u32[]{:S(2)}) %copy-start.5) | copy-done | bytes 983064
  14.8 1.0 %copy-done.6 = bf16[512,512]{1,0:T(8,128)(2,1)S(1)} copy-done((bf16[512,512]{1,0:T(8,128)(2,1)S(1)}, bf16[512,512]{1,0:T(8,128)(2,1)}, u32[]{:S(2)}) %copy-start.6) | copy-done | bytes 524312
  15.9 1.0 %copy-done.8 = bf16[1088,128]{1,0:T(8,128)(2,1)S(1)} copy-done((bf16[1088,128]{1,0:T(8,128)(2,1)S(1)}, bf16[1088,128]{1,0:T(8,128)(2,1)}, u32[]{:S(2)}) %copy-start.8) | copy-done | bytes 278552
  16.8 0.9 copy-done.9
  17.8 0.9 copy-done.10
  18.7 3.0 %shard_map.120 = (bf16[256,1024]{1,0:T(8,128)(2,1)S(1)}, bf16[512,1024]{1,0:T(8,128)(2,1)S(1)}, bf16[512,1024]{1,0:T(8,128)(2,1)S(1)}, f32[512,1024]{1,0:T(8,128...) custom-call(bf16[1088,128]{1,0:T(8,128)(2,1)S(1)} %copy-done.8, ...), custom_call_target="tpu_custom_call" | custom-call | flops 20000000000 | tf_op jit(solution)/shard_map/pallas_call | solution.py:555
  21.7 0.0 collective-permute-done.1.rims
  21.7 1.9 %collective-permute-done.strip = bf16[2576,128]{1,0:T(8,128)(2,1)S(1)} collective-permute-done((bf16[2576,128]{1,0:T(8,128)(2,1)}, bf16[2576,128]{1,0:T(8,128)(2,1)S(1)}, u32[]{:S(2)}, u32[]{:S(2)}) %collective-permute-start) | collective-permute-done | bytes 659488 | tf_op jit(solution)/shard_map/ppermute | solution.py:585
  23.6 0.5 collective-permute-start.5
  24.1 0.0 collective-permute-start.4
  24.1 2.0 %collective-permute-done.5.other_col = bf16[1088,128]{1,0:T(8,128)(2,1)S(1)} collective-permute-done((bf16[1088,128]{1,0:T(8,128)(2,1)S(1)}, bf16[1088,128]{1,0:T(8,128)(2,1)S(1)}, u32[]{:S(2)}, u32[]{:S(2)}) %collective-permute-start.5) | collective-permute-done | bytes 278560 | tf_op jit(solution)/shard_map/ppermute | solution.py:578
  26.1 0.1 collective-permute-done.4.partner_rims
  26.2 5.2 %shard_map.121 = (f32[960,128]{1,0:T(8,128)S(1)}, bf16[960,128]{1,0:T(8,128)(2,1)S(1)}, bf16[1024,128]{1,0:T(8,128)(2,1)S(1)}, f32[48,56,128]{2,1,0:T(8,128)S(1)}, f32[4,8,128]{2,1,0:T(8,128)S(1)}) custom-call(s32[1,2]{1,0:T(1,128)S(1)} %copy-done.4, f32[1920,128]{1,0:T(8,128)S(1)} %bitcast.9, f32[640,128]{1,0:T(8,128)S(1)} %bitcast.11, ...), custom_call_target="tpu_custom_call" | custom-call | flops 20000000000 | tf_op jit(solution)/shard_map/pallas_call | solution.py:555
  31.4 0.0 copy-start.14
  31.5 0.3 collective-permute-start.6
  31.8 3.7 %collective-permute-start.7 = (bf16[1024,128]{1,0:T(8,128)(2,1)S(1)}, bf16[1024,128]{1,0:T(8,128)(2,1)S(1)}, u32[]{:S(2)}, u32[]{:S(2)}) collective-permute-start(bf16[1024,128]{1,0:T(8,128)(2,1)S(1)} %get-tuple-element.50.own_ref), channel_id=1, source_target_pairs={{0,1},{1,0},{2,3},{3,2},{4,5},{5,4},{6,7},{7,6},{8,9},{9,8},{10,11... | collective-permute-start | bytes 786440 | tf_op jit(solution)/shard_map/ppermute | solution.py:578
  35.5 4.7 %collective-permute-start.8 = (bf16[192,128]{1,0:T(8,128)(2,1)S(1)}, bf16[192,128]{1,0:T(8,128)(2,1)S(1)}, u32[]{:S(2)}, u32[]{:S(2)}) collective-permute-start(bf16[192,128]{1,0:T(8,128)(2,1)S(1)} %get-tuple-element.51), channel_id=1, source_target_pairs={{64,3},{65,2},{66,5},{67,4},{68,7},{69,6},{70,9},{71,8},{72,11},{7... | collective-permute-start | bytes 147464 | tf_op jit(solution)/shard_map/ppermute | solution.py:585
  40.2 1.6 %collective-permute-done.7.other_ref.own_col = bf16[1024,128]{1,0:T(8,128)(2,1)S(1)} collective-permute-done((bf16[1024,128]{1,0:T(8,128)(2,1)S(1)}, bf16[1024,128]{1,0:T(8,128)(2,1)S(1)}, u32[]{:S(2)}, u32[]{:S(2)}) %collective-permute-start.7) | collective-permute-done | bytes 262176 | tf_op jit(solution)/shard_map/ppermute | solution.py:578
  41.8 2.1 %collective-permute-done.8.rims = bf16[192,128]{1,0:T(8,128)(2,1)S(1)} collective-permute-done((bf16[192,128]{1,0:T(8,128)(2,1)S(1)}, bf16[192,128]{1,0:T(8,128)(2,1)S(1)}, u32[]{:S(2)}, u32[]{:S(2)}) %collective-permute-start.8) | collective-permute-done | bytes 49184 | tf_op jit(solution)/shard_map/ppermute | solution.py:585
  43.9 3.3 %shard_map.123 = (bf16[1024,128]{1,0:T(8,128)(2,1)S(1)}, f32[1024,128]{1,0:T(8,128)S(1)}, f32[960,128]{1,0:T(8,128)S(1)}) custom-call(bf16[1024,128]{1,0:T(8,128)(2,1)S(1)} %get-tuple-element.50.own_ref, bf16[1024,128]{1,0:T(8,128)(2,1)S(1)} %collective-permute-done.7.other_ref.own_col, bf16[256,1024]{1,0:T(8,128)(2,1)S(1)} %get-tuple-element.53.feat_ref, ...), custom_call_target="tpu_custom_call" | custom-call | flops 20000000000 | tf_op jit(solution)/shard_map/pallas_call | solution.py:555
  47.3 0.0 copy-start.13
  47.3 0.1 collective-permute-start.9
  47.4 3.9 %collective-permute-start.10 = (bf16[1920,128]{1,0:T(8,128)(2,1)S(1)}, bf16[1920,128]{1,0:T(8,128)(2,1)S(1)}, u32[]{:S(2)}, u32[]{:S(2)}) collective-permute-start(bf16[1920,128]{1,0:T(8,128)(2,1)S(1)} %get-tuple-element.64), channel_id=1, source_target_pairs={{64,2},{66,4},{68,6},{70,8},{72,10},{74,12},{76,14},{78,16},{80,18... | collective-permute-start | bytes 1474568 | tf_op jit(solution)/shard_map/ppermute | solution.py:585
  51.3 0.7 shard_map.124
  52.1 11.2 %all-to-all-start = ((bf16[32,32,128]{2,1,0:T(8,128)(2,1)}), bf16[32,32,128]{2,1,0:T(8,128)(2,1)S(1)}, u32[]{:S(2)}, u32[]{:S(2)}) async-start(bf16[32,32,128]{2,1,0:T(8,128)(2,1)} %bitcast.5), calls=%async_computation | async-start | bytes 524288 | tf_op jit(solution)/shard_map/all_to_all | solution.py:637
  63.3 0.1 collective-permute-start.13
  63.4 0.5 collective-permute-start.12
  63.9 0.1 collective-permute-start.11
  64.0 8.1 %all-to-all-done.parts_ref = bf16[32,32,128]{2,1,0:T(8,128)(2,1)S(1)} async-done(((bf16[32,32,128]{2,1,0:T(8,128)(2,1)}), bf16[32,32,128]{2,1,0:T(8,128)(2,1)S(1)}, u32[]{:S(2)}, u32[]{:S(2)}) %all-to-all-start) | async-done | bytes 262176 | tf_op jit(solution)/shard_map/all_to_all | solution.py:637
  72.1 0.9 shard_map.125
  72.9 4.7 %all-to-all-start.1 = ((bf16[64,32,128]{2,1,0:T(8,128)(2,1)}), bf16[64,32,128]{2,1,0:T(8,128)(2,1)S(1)}, u32[]{:S(2)}, u32[]{:S(2)}) async-start(bf16[64,32,128]{2,1,0:T(8,128)(2,1)} %shard_map.125), calls=%async_computation.1 | async-start | bytes 1048576 | tf_op jit(solution)/shard_map/all_to_all | solution.py:641
  77.7 0.6 copy-done.20
  78.3 0.1 copy-done.18
  78.4 0.2 copy-done.17
  78.6 8.3 %shard_map.126.mine_ref = f32[960,128]{1,0:T(8,128)} custom-call(f32[960,128]{1,0:T(8,128)} %copy-done.14, bf16[960,128]{1,0:T(8,128)(2,1)} %copy-done.3, f32[960,128]{1,0:T(8,128)} %copy-done.13, f32[48,56,128]{2,1,0:T(8,128)} %copy-done.12, f32[4,8,128]{2,1,0:T(8,128)} %copy-done.15, bf16[1920,128]{1,0:T(8,128)(2,1)} %copy-done.16, ...), custom_call_target="tpu_custom_call" | custom-call | flops 20000000000 | tf_op jit(solution)/shard_map/pallas_call | solution.py:555
  86.9 1.0 %collective-permute-start.14 = (f32[960,128]{1,0:T(8,128)}, f32[960,128]{1,0:T(8,128)S(1)}, u32[]{:S(2)}, u32[]{:S(2)}) collective-permute-start(f32[960,128]{1,0:T(8,128)} %shard_map.126.mine_ref), channel_id=1, source_target_pairs={{0,64},{64,0},{1,65},{65,1},{2,66},{66,2},{3,67},{67,3},{4,68},{68... | collective-permute-start | bytes 1474568 | tf_op jit(solution)/shard_map/ppermute | solution.py:578
  87.9 1.7 %all-to-all-done.1.own_ref = bf16[64,32,128]{2,1,0:T(8,128)(2,1)S(1)} async-done(((bf16[64,32,128]{2,1,0:T(8,128)(2,1)}), bf16[64,32,128]{2,1,0:T(8,128)(2,1)S(1)}, u32[]{:S(2)}, u32[]{:S(2)}) %all-to-all-start.1) | async-done | bytes 524320 | tf_op jit(solution)/shard_map/all_to_all | solution.py:641
  89.6 0.0 collective-permute-done.14.theirs_ref
  89.6 2.2 %collective-permute-start.15 = (bf16[64,32,128]{2,1,0:T(8,128)(2,1)S(1)}, bf16[64,32,128]{2,1,0:T(8,128)(2,1)S(1)}, u32[]{:S(2)}, u32[]{:S(2)}) collective-permute-start(bf16[64,32,128]{2,1,0:T(8,128)(2,1)S(1)} %all-to-all-done.1.own_ref), channel_id=1, source_target_pairs={{0,64},{64,0},{1,65},{65,1},{2,66},{66,2},{3,67},{67,3},{4,68},{68... | collective-permute-start | bytes 1572872 | tf_op jit(solution)/shard_map/ppermute | solution.py:578
  91.9 1.0 %copy-done.1 = f32[960,128]{1,0:T(8,128)S(1)} copy-done((f32[960,128]{1,0:T(8,128)S(1)}, f32[960,128]{1,0:T(8,128)}, u32[]{:S(2)}) %copy-start.1) | copy-done | bytes 491544
  92.9 1.0 %shard_map.127 = f32[3,40,16,128]{3,2,1,0:T(8,128)} custom-call(f32[960,128]{1,0:T(8,128)S(1)} %copy-done.1, f32[960,128]{1,0:T(8,128)S(1)} %collective-permute-done.14.theirs_ref), custom_call_target="tpu_custom_call" | custom-call | tf_op jit(solution)/shard_map/pallas_call | solution.py:555
  93.9 1.4 %shard_map.128 = (f32[240,512]{1,0:T(8,128)}, f32[1,512]{1,0:T(1,128)}, f32[512,512]{1,0:T(8,128)}, f32[240,512]{1,0:T(8,128)}) custom-call(bf16[64,32,128]{2,1,0:T(8,128)(2,1)S(1)} %all-to-all-done.1.own_ref, bf16[64,32,128]{2,1,0:T(8,128)(2,1)S(1)} %collective-permute-done.15.partner_ref), custom_call_target="tpu_custom_call" | custom-call | tf_op jit(solution)/shard_map/pallas_call | solution.py:555
  (40 shorter events, 0.1 us)
Async XLA Ops:
  3.5 10.1 %collective-permute-start.2 = (bf16[1088,128]{1,0:T(8,128)(2,1)}, bf16[1088,128]{1,0:T(8,128)(2,1)S(1)}, u32[]{:S(2)}, u32[]{:S(2)}) collective-permute-start(bf16[1088,128]{1,0:T(8,128)(2,1)} %get-tuple-element.41.own_ref), channel_id=1, source_target_pairs={{0,1},{1,0},{2,3},{3,2},{4,5},{5,4},{6,7},{7,6},{8,9},{9,8},{10,11... | collective-permute-start | bytes 835592 | tf_op jit(solution)/shard_map/ppermute | solution.py:578
  7.3 14.4 %collective-permute-start.1 = (bf16[256,128]{1,0:T(8,128)(2,1)}, bf16[256,128]{1,0:T(8,128)(2,1)S(1)}, u32[]{:S(2)}, u32[]{:S(2)}) collective-permute-start(bf16[256,128]{1,0:T(8,128)(2,1)} %get-tuple-element.40), channel_id=1, source_target_pairs={{64,3},{65,2},{66,5},{67,4},{68,7},{69,6},{70,9},{71,8},{72,11},{7... | collective-permute-start | bytes 196616 | tf_op jit(solution)/shard_map/ppermute | solution.py:585
  11.4 12.2 %collective-permute-start = (bf16[2576,128]{1,0:T(8,128)(2,1)}, bf16[2576,128]{1,0:T(8,128)(2,1)S(1)}, u32[]{:S(2)}, u32[]{:S(2)}) collective-permute-start(bf16[2576,128]{1,0:T(8,128)(2,1)} %get-tuple-element.39), channel_id=1, source_target_pairs={{64,2},{66,4},{68,6},{70,8},{72,10},{74,12},{76,14},{78,16},{80,18... | collective-permute-start | bytes 1978376 | tf_op jit(solution)/shard_map/ppermute | solution.py:585
  13.6 1.2 %copy-start.5 = (f32[3,40,16,128]{3,2,1,0:T(8,128)S(1)}, f32[3,40,16,128]{3,2,1,0:T(8,128)}, u32[]{:S(2)}) copy-start(f32[3,40,16,128]{3,2,1,0:T(8,128)} %param.10) | copy-start | bytes 2949124
  14.8 1.0 %copy-start.6 = (bf16[512,512]{1,0:T(8,128)(2,1)S(1)}, bf16[512,512]{1,0:T(8,128)(2,1)}, u32[]{:S(2)}) copy-start(bf16[512,512]{1,0:T(8,128)(2,1)} %second_ref.3) | copy-start | bytes 1572868
  15.9 1.0 %copy-start.8 = (bf16[1088,128]{1,0:T(8,128)(2,1)S(1)}, bf16[1088,128]{1,0:T(8,128)(2,1)}, u32[]{:S(2)}) copy-start(bf16[1088,128]{1,0:T(8,128)(2,1)} %get-tuple-element.41.own_ref) | copy-start | bytes 835588
  16.8 0.9 copy-start.9
  17.8 0.9 copy-start.10
  18.7 7.5 %copy-start = (f32[3,40,16,128]{3,2,1,0:T(8,128)S(1)}, f32[3,40,16,128]{3,2,1,0:T(8,128)}, u32[]{:S(2)}) copy-start(f32[3,40,16,128]{3,2,1,0:T(8,128)} %param.8) | copy-start | bytes 2949124
  18.7 7.5 %copy-start.2 = (f32[40,16,128]{2,1,0:T(8,128)S(1)}, f32[40,16,128]{2,1,0:T(8,128)}, u32[]{:S(2)}) copy-start(f32[40,16,128]{2,1,0:T(8,128)} %param.9) | copy-start | bytes 983044
  18.7 7.5 %copy-start.4 = (s32[1,2]{1,0:T(1,128)S(1)}, s32[1,2]{1,0:T(1,128)}, u32[]{:S(2)}) copy-start(s32[1,2]{1,0:T(1,128)} %turn_ref.3) | copy-start | bytes 28
  23.6 20.3 %copy-start.7 = (bf16[512,512]{1,0:T(8,128)(2,1)S(1)}, bf16[512,512]{1,0:T(8,128)(2,1)}, u32[]{:S(2)}) copy-start(bf16[512,512]{1,0:T(8,128)(2,1)} %second_ref.3) | copy-start | bytes 1572868
  23.6 2.6 %collective-permute-start.3 = (bf16[2576,128]{1,0:T(8,128)(2,1)S(1)}, bf16[2576,128]{1,0:T(8,128)(2,1)S(1)}, u32[]{:S(2)}, u32[]{:S(2)}) collective-permute-start(bf16[2576,128]{1,0:T(8,128)(2,1)S(1)} %collective-permute-done.strip), channel_id=1, source_target_pairs={{0,64},{64,0},{1,65},{65,1},{2,66},{66,2},{3,67},{67,3},{4,68},{68... | collective-permute-start | bytes 1978376 | tf_op jit(solution)/shard_map/ppermute | solution.py:578
  23.6 2.5 %collective-permute-start.5 = (bf16[1088,128]{1,0:T(8,128)(2,1)S(1)}, bf16[1088,128]{1,0:T(8,128)(2,1)S(1)}, u32[]{:S(2)}, u32[]{:S(2)}) collective-permute-start(bf16[1088,128]{1,0:T(8,128)(2,1)S(1)} %collective-permute-done.2.other_ref.own_col), channel_id=1, source_target_pairs={{0,64},{64,0},{1,65},{65,1},{2,66},{66,2},{3,67},{67,3},{4,68},{68... | collective-permute-start | bytes 835592 | tf_op jit(solution)/shard_map/ppermute | solution.py:578
  24.1 2.1 %collective-permute-start.4 = (bf16[256,128]{1,0:T(8,128)(2,1)S(1)}, bf16[256,128]{1,0:T(8,128)(2,1)S(1)}, u32[]{:S(2)}, u32[]{:S(2)}) collective-permute-start(bf16[256,128]{1,0:T(8,128)(2,1)S(1)} %collective-permute-done.1.rims), channel_id=1, source_target_pairs={{0,64},{64,0},{1,65},{65,1},{2,66},{66,2},{3,67},{67,3},{4,68},{68... | collective-permute-start | bytes 196616 | tf_op jit(solution)/shard_map/ppermute | solution.py:578
  31.4 15.8 %copy-start.12 = (f32[48,56,128]{2,1,0:T(8,128)}, f32[48,56,128]{2,1,0:T(8,128)S(1)}, u32[]{:S(2)}) copy-start(f32[48,56,128]{2,1,0:T(8,128)S(1)} %get-tuple-element.62.c_ref) | copy-start | bytes 4128772
  31.4 15.8 %copy-start.14 = (f32[960,128]{1,0:T(8,128)}, f32[960,128]{1,0:T(8,128)S(1)}, u32[]{:S(2)}) copy-start(f32[960,128]{1,0:T(8,128)S(1)} %get-tuple-element.48.resid_ref) | copy-start | bytes 1474564
  31.4 15.8 %copy-start.15 = (f32[4,8,128]{2,1,0:T(8,128)}, f32[4,8,128]{2,1,0:T(8,128)S(1)}, u32[]{:S(2)}) copy-start(f32[4,8,128]{2,1,0:T(8,128)S(1)} %get-tuple-element.63.factor_ref) | copy-start | bytes 49156
  31.5 4.0 %collective-permute-start.6 = (bf16[960,128]{1,0:T(8,128)(2,1)S(1)}, bf16[960,128]{1,0:T(8,128)(2,1)S(1)}, u32[]{:S(2)}, u32[]{:S(2)}) collective-permute-start(bf16[960,128]{1,0:T(8,128)(2,1)S(1)} %get-tuple-element.49.near_ref), channel_id=1, source_target_pairs={{0,64},{64,0},{1,65},{65,1},{2,66},{66,2},{3,67},{67,3},{4,68},{68... | collective-permute-start | bytes 737288 | tf_op jit(solution)/shard_map/ppermute | solution.py:578
  31.8 10.0 %collective-permute-start.7 = (bf16[1024,128]{1,0:T(8,128)(2,1)S(1)}, bf16[1024,128]{1,0:T(8,128)(2,1)S(1)}, u32[]{:S(2)}, u32[]{:S(2)}) collective-permute-start(bf16[1024,128]{1,0:T(8,128)(2,1)S(1)} %get-tuple-element.50.own_ref), channel_id=1, source_target_pairs={{0,1},{1,0},{2,3},{3,2},{4,5},{5,4},{6,7},{7,6},{8,9},{9,8},{10,11... | collective-permute-start | bytes 786440 | tf_op jit(solution)/shard_map/ppermute | solution.py:578
  35.5 11.8 %copy-start.3 = (bf16[960,128]{1,0:T(8,128)(2,1)}, bf16[960,128]{1,0:T(8,128)(2,1)S(1)}, u32[]{:S(2)}) copy-start(bf16[960,128]{1,0:T(8,128)(2,1)S(1)} %collective-permute-done.6.far_ref.other_ref) | copy-start | bytes 737284
  35.5 8.4 %collective-permute-start.8 = (bf16[192,128]{1,0:T(8,128)(2,1)S(1)}, bf16[192,128]{1,0:T(8,128)(2,1)S(1)}, u32[]{:S(2)}, u32[]{:S(2)}) collective-permute-start(bf16[192,128]{1,0:T(8,128)(2,1)S(1)} %get-tuple-element.51), channel_id=1, source_target_pairs={{64,3},{65,2},{66,5},{67,4},{68,7},{69,6},{70,9},{71,8},{72,11},{7... | collective-permute-start | bytes 147464 | tf_op jit(solution)/shard_map/ppermute | solution.py:585
  41.8 21.5 %copy-start.11 = (bf16[1024,128]{1,0:T(8,128)(2,1)}, bf16[1024,128]{1,0:T(8,128)(2,1)S(1)}, u32[]{:S(2)}) copy-start(bf16[1024,128]{1,0:T(8,128)(2,1)S(1)} %collective-permute-done.7.other_ref.own_col) | copy-start | bytes 786436
  43.9 19.4 %copy-start.19 = (bf16[192,128]{1,0:T(8,128)(2,1)}, bf16[192,128]{1,0:T(8,128)(2,1)S(1)}, u32[]{:S(2)}) copy-start(bf16[192,128]{1,0:T(8,128)(2,1)S(1)} %collective-permute-done.8.rims) | copy-start | bytes 147460
  47.3 4.8 %copy-start.13 = (f32[960,128]{1,0:T(8,128)}, f32[960,128]{1,0:T(8,128)S(1)}, u32[]{:S(2)}) copy-start(f32[960,128]{1,0:T(8,128)S(1)} %get-tuple-element.58.input_grad_ref) | copy-start | bytes 1474564
  47.3 4.0 %collective-permute-start.9 = (bf16[1024,128]{1,0:T(8,128)(2,1)S(1)}, bf16[1024,128]{1,0:T(8,128)(2,1)S(1)}, u32[]{:S(2)}, u32[]{:S(2)}) collective-permute-start(bf16[1024,128]{1,0:T(8,128)(2,1)S(1)} %get-tuple-element.60), channel_id=1, source_target_pairs={{0,64},{64,0},{1,65},{65,1},{2,66},{66,2},{3,67},{67,3},{4,68},{68... | collective-permute-start | bytes 786440 | tf_op jit(solution)/shard_map/ppermute | solution.py:578
  47.4 16.5 %collective-permute-start.10 = (bf16[1920,128]{1,0:T(8,128)(2,1)S(1)}, bf16[1920,128]{1,0:T(8,128)(2,1)S(1)}, u32[]{:S(2)}, u32[]{:S(2)}) collective-permute-start(bf16[1920,128]{1,0:T(8,128)(2,1)S(1)} %get-tuple-element.64), channel_id=1, source_target_pairs={{64,2},{66,4},{68,6},{70,8},{72,10},{74,12},{76,14},{78,16},{80,18... | collective-permute-start | bytes 1474568 | tf_op jit(solution)/shard_map/ppermute | solution.py:585
  52.1 20.0 %all-to-all-start = ((bf16[32,32,128]{2,1,0:T(8,128)(2,1)}), bf16[32,32,128]{2,1,0:T(8,128)(2,1)S(1)}, u32[]{:S(2)}, u32[]{:S(2)}) async-start(bf16[32,32,128]{2,1,0:T(8,128)(2,1)} %bitcast.5), calls=%async_computation | async-start | bytes 524288 | tf_op jit(solution)/shard_map/all_to_all | solution.py:637
  63.3 14.4 %collective-permute-start.13 = (bf16[1024,128]{1,0:T(8,128)(2,1)S(1)}, bf16[1024,128]{1,0:T(8,128)(2,1)S(1)}, u32[]{:S(2)}, u32[]{:S(2)}) collective-permute-start(bf16[1024,128]{1,0:T(8,128)(2,1)S(1)} %collective-permute-done.7.other_ref.own_col), channel_id=1, source_target_pairs={{0,64},{64,0},{1,65},{65,1},{2,66},{66,2},{3,67},{67,3},{4,68},{68... | collective-permute-start | bytes 786440 | tf_op jit(solution)/shard_map/ppermute | solution.py:578
  63.4 14.3 %collective-permute-start.12 = (bf16[192,128]{1,0:T(8,128)(2,1)S(1)}, bf16[192,128]{1,0:T(8,128)(2,1)S(1)}, u32[]{:S(2)}, u32[]{:S(2)}) collective-permute-start(bf16[192,128]{1,0:T(8,128)(2,1)S(1)} %collective-permute-done.8.rims), channel_id=1, source_target_pairs={{0,64},{64,0},{1,65},{65,1},{2,66},{66,2},{3,67},{67,3},{4,68},{68... | collective-permute-start | bytes 147464 | tf_op jit(solution)/shard_map/ppermute | solution.py:578
  63.9 9.1 %copy-start.16 = (bf16[1920,128]{1,0:T(8,128)(2,1)}, bf16[1920,128]{1,0:T(8,128)(2,1)S(1)}, u32[]{:S(2)}) copy-start(bf16[1920,128]{1,0:T(8,128)(2,1)S(1)} %collective-permute-done.10.strip) | copy-start | bytes 1474564
  63.9 13.8 %collective-permute-start.11 = (bf16[1920,128]{1,0:T(8,128)(2,1)S(1)}, bf16[1920,128]{1,0:T(8,128)(2,1)S(1)}, u32[]{:S(2)}, u32[]{:S(2)}) collective-permute-start(bf16[1920,128]{1,0:T(8,128)(2,1)S(1)} %collective-permute-done.10.strip), channel_id=1, source_target_pairs={{0,64},{64,0},{1,65},{65,1},{2,66},{66,2},{3,67},{67,3},{4,68},{68... | collective-permute-start | bytes 1474568 | tf_op jit(solution)/shard_map/ppermute | solution.py:578
  72.9 16.6 %all-to-all-start.1 = ((bf16[64,32,128]{2,1,0:T(8,128)(2,1)}), bf16[64,32,128]{2,1,0:T(8,128)(2,1)S(1)}, u32[]{:S(2)}, u32[]{:S(2)}) async-start(bf16[64,32,128]{2,1,0:T(8,128)(2,1)} %shard_map.125), calls=%async_computation.1 | async-start | bytes 1048576 | tf_op jit(solution)/shard_map/all_to_all | solution.py:641
  77.6 0.6 copy-start.20
  77.7 0.7 copy-start.18
  77.7 0.9 copy-start.17
  86.9 2.7 %collective-permute-start.14 = (f32[960,128]{1,0:T(8,128)}, f32[960,128]{1,0:T(8,128)S(1)}, u32[]{:S(2)}, u32[]{:S(2)}) collective-permute-start(f32[960,128]{1,0:T(8,128)} %shard_map.126.mine_ref), channel_id=1, source_target_pairs={{0,64},{64,0},{1,65},{65,1},{2,66},{66,2},{3,67},{67,3},{4,68},{68... | collective-permute-start | bytes 1474568 | tf_op jit(solution)/shard_map/ppermute | solution.py:578
  89.6 4.3 %collective-permute-start.15 = (bf16[64,32,128]{2,1,0:T(8,128)(2,1)S(1)}, bf16[64,32,128]{2,1,0:T(8,128)(2,1)S(1)}, u32[]{:S(2)}, u32[]{:S(2)}) collective-permute-start(bf16[64,32,128]{2,1,0:T(8,128)(2,1)S(1)} %all-to-all-done.1.own_ref), channel_id=1, source_target_pairs={{0,64},{64,0},{1,65},{65,1},{2,66},{66,2},{3,67},{67,3},{4,68},{68... | collective-permute-start | bytes 1572872 | tf_op jit(solution)/shard_map/ppermute | solution.py:578
  91.9 1.0 %copy-start.1 = (f32[960,128]{1,0:T(8,128)S(1)}, f32[960,128]{1,0:T(8,128)}, u32[]{:S(2)}) copy-start(f32[960,128]{1,0:T(8,128)} %shard_map.126.mine_ref) | copy-start | bytes 1474564
